TPU v7x, 32 devices: a whole 2x2x4 slice. The times are simulated.
32 devices in a mesh: shard: 16 (over z, x, core), rep: 2 (over y).
Axes of the slice: x: 2, y: 2, z: 4, core: 2. Of those that a mesh axis runs over, the one named last changes fastest.
Arguments:
- tokens: bfloat16 [64, 320, 1024], P(('shard', 'rep')), may hold values from -6 to 6
- kept: int32 [64], P(('shard', 'rep')), may hold values from 1 to 256, as said below
- attn_gain: bfloat16 [2, 1024], P(None, 'shard'), may hold values from 0.25 to 1.75
- attn_shift: bfloat16 [2, 1024], P(None, 'shard'), may hold values from -1.75 to 1.75
- qkv_weight: bfloat16 [2, 1024, 3072], P(None, 'shard'), may hold values from -0.1875 to 0.1875
- qv_bias: bfloat16 [2, 2048], P(None, 'shard'), may hold values from -1.75 to 1.75
- proj_weight: bfloat16 [2, 1024, 1024], P(None, 'shard'), may hold values from -1.5 to 1.5
- proj_bias: bfloat16 [2, 1024], P(None, 'shard'), may hold values from -1.75 to 1.75
- mlp_gain: bfloat16 [2, 1024], P(None, 'shard'), may hold values from 0.25 to 1.75
- mlp_shift: bfloat16 [2, 1024], P(None, 'shard'), may hold values from -1.75 to 1.75
- fc1_weight: bfloat16 [2, 1024, 4096], P(None, 'shard'), may hold values from -0.1875 to 0.1875
- fc1_bias: bfloat16 [2, 4096], P(None, 'shard'), may hold values from -1.75 to 1.75
- fc2_weight: bfloat16 [2, 4096, 1024], P(None, 'shard'), may hold values from -0.125 to 0.125
- fc2_bias: bfloat16 [2, 1024], P(None, 'shard'), may hold values from -1.75 to 1.75
- cotangent: bfloat16 [64, 320, 1024], P(('shard', 'rep')), may hold values from -6 to 6
Outputs:
- mixed: bfloat16 [64, 320, 1024], P(('shard', 'rep'))
- tokens_grad: float32 [64, 320, 1024], P(('shard', 'rep'))
- attn_gain_grad: float32 [2, 1024], P(None, 'shard')
- attn_shift_grad: float32 [2, 1024], P(None, 'shard')
- qkv_weight_grad: float32 [2, 1024, 3072], P(None, 'shard')
- qv_bias_grad: float32 [2, 2048], P(None, 'shard')
- proj_weight_grad: float32 [2, 1024, 1024], P(None, 'shard')
- proj_bias_grad: float32 [2, 1024], P(None, 'shard')
- mlp_gain_grad: float32 [2, 1024], P(None, 'shard')
- mlp_shift_grad: float32 [2, 1024], P(None, 'shard')
- fc1_weight_grad: float32 [2, 1024, 4096], P(None, 'shard')
- fc1_bias_grad: float32 [2, 4096], P(None, 'shard')
- fc2_weight_grad: float32 [2, 4096, 1024], P(None, 'shard')
- fc2_bias_grad: float32 [2, 1024], P(None, 'shard')
Inputs may be any that keep to these rules, and one draw needn't show every extreme that they name: kept[i] image slots of image i are live after its 64 buffer slots; some image keeps all 256.
All inputs are finite; a program needn't handle non-finite values.
Results may differ from a plain program's by a relative error of at most 0.018.
Values may be sent and summed in bfloat16 or wider, within the bound.
No kernel may reach another device: no remote copies, remote signals or barrier semaphores. Data moves between devices by JAX's collectives and lax.ppermute only.
A program may use at most 320 MiB of HBM per device.

v0:
```python
from functools import partial

import jax
import jax.numpy as jnp
from jax import lax
from jax.sharding import PartitionSpec as P

HEADS = 16
HEAD_DIM = 64
BUFFER = 64


EPS = 1e-06


def layer_norm(rows, gain, shift):
    mean = jnp.mean(rows, axis=-1, keepdims=True)
    centered = rows - mean
    spread = jnp.mean(centered * centered, axis=-1, keepdims=True)
    factor = lax.rsqrt(spread + EPS)
    normed = centered * factor
    return (normed * gain + shift, normed, factor)


def norm_back(grad_out, normed, factor, gain):
    gain_grad = jnp.sum(grad_out * normed, axis=0)
    shift_grad = jnp.sum(grad_out, axis=0)
    scaled = grad_out * gain
    inner = (
        scaled
        - jnp.mean(scaled, axis=-1, keepdims=True)
        - normed * jnp.mean(scaled * normed, axis=-1, keepdims=True)
    )
    return (factor * inner, gain_grad, shift_grad)


def scores_of(queries, keys_part, live, scale):
    scores = (
        jnp.einsum("bqhe,bkhe->bhqk", queries, keys_part, preferred_element_type=jnp.float32)
        * scale
    )
    return jnp.where(live[:, None, None, :], scores, -1e30)


def split_heads(projected, images, slots):
    split_view = projected.reshape(images, slots, 3, HEADS, HEAD_DIM)
    return (split_view[:, :, 0], split_view[:, :, 1], split_view[:, :, 2])


def layer_forward(state, weights, live):
    (
        attn_gain,
        attn_shift,
        qkv_weight,
        qv_bias,
        proj_weight,
        proj_bias,
        mlp_gain,
        mlp_shift,
        fc1_weight,
        fc1_bias,
        fc2_weight,
        fc2_bias,
    ) = weights
    images, slots, width = state.shape
    rows = state.reshape(images * slots, width)
    first_out, first_normed, first_factor = layer_norm(
        rows, attn_gain.astype(jnp.float32), attn_shift.astype(jnp.float32)
    )
    first_low = first_out.astype(jnp.bfloat16)
    qv_full = qv_bias.astype(jnp.float32)
    full_bias = jnp.concatenate(
        [qv_full[:width], jnp.zeros((width,), jnp.float32), qv_full[width:]]
    )
    projected = (
        jnp.dot(first_low, qkv_weight, preferred_element_type=jnp.float32) + full_bias
    ).astype(jnp.bfloat16)
    queries, keys_part, values = split_heads(projected, images, slots)
    scale = HEAD_DIM ** (-0.5)
    scores = scores_of(queries, keys_part, live, scale)
    peak = jnp.max(scores, axis=-1, keepdims=True)
    expo = jnp.exp(scores - peak)
    total = jnp.sum(expo, axis=-1, keepdims=True)
    probs = (expo / total).astype(jnp.bfloat16)
    log_total = peak + jnp.log(total)
    attended = jnp.einsum("bhqk,bkhe->bqhe", probs, values, preferred_element_type=jnp.float32)
    attended = attended.reshape(images * slots, width).astype(jnp.bfloat16)
    middle = (
        rows
        + jnp.dot(attended, proj_weight, preferred_element_type=jnp.float32)
        + proj_bias.astype(jnp.float32)
    )
    second_out, second_normed, second_factor = layer_norm(
        middle, mlp_gain.astype(jnp.float32), mlp_shift.astype(jnp.float32)
    )
    second_low = second_out.astype(jnp.bfloat16)
    hidden_pre = jnp.dot(
        second_low, fc1_weight, preferred_element_type=jnp.float32
    ) + fc1_bias.astype(jnp.float32)
    hidden_low = jax.nn.gelu(hidden_pre, approximate=False).astype(jnp.bfloat16)
    output = (
        middle
        + jnp.dot(hidden_low, fc2_weight, preferred_element_type=jnp.float32)
        + fc2_bias.astype(jnp.float32)
    )
    saved = (
        first_normed,
        first_factor,
        first_low,
        projected,
        log_total,
        attended,
        second_normed,
        second_factor,
        second_low,
        hidden_pre,
        hidden_low,
    )
    return (output.reshape(images, slots, width), saved)


def layer_backward(grad_state, weights, live, saved):
    (
        attn_gain,
        attn_shift,
        qkv_weight,
        qv_bias,
        proj_weight,
        proj_bias,
        mlp_gain,
        mlp_shift,
        fc1_weight,
        fc1_bias,
        fc2_weight,
        fc2_bias,
    ) = weights
    (
        first_normed,
        first_factor,
        first_low,
        projected,
        log_total,
        attended,
        second_normed,
        second_factor,
        second_low,
        hidden_pre,
        hidden_low,
    ) = saved
    images, slots, width = grad_state.shape
    grad_rows = grad_state.reshape(images * slots, width)
    out_low = grad_rows.astype(jnp.bfloat16)
    fc2_bias_grad = jnp.sum(out_low, axis=0, dtype=jnp.float32)
    fc2_weight_grad = jnp.einsum(
        "rf,rd->fd", hidden_low, out_low, preferred_element_type=jnp.float32
    )
    hidden_grad = jnp.einsum("rd,fd->rf", out_low, fc2_weight, preferred_element_type=jnp.float32)
    unused, gelu_back = jax.vjp(partial(jax.nn.gelu, approximate=False), hidden_pre)
    pre_low = gelu_back(hidden_grad)[0].astype(jnp.bfloat16)
    fc1_bias_grad = jnp.sum(pre_low, axis=0, dtype=jnp.float32)
    fc1_weight_grad = jnp.einsum(
        "rd,rf->df", second_low, pre_low, preferred_element_type=jnp.float32
    )
    second_grad = jnp.einsum("rf,df->rd", pre_low, fc1_weight, preferred_element_type=jnp.float32)
    mid_back, mlp_gain_grad, mlp_shift_grad = norm_back(
        second_grad, second_normed, second_factor, mlp_gain.astype(jnp.float32)
    )
    middle_grad = grad_rows + mid_back
    branch_low = middle_grad.astype(jnp.bfloat16)
    proj_bias_grad = jnp.sum(branch_low, axis=0, dtype=jnp.float32)
    proj_weight_grad = jnp.einsum(
        "rd,re->de", attended, branch_low, preferred_element_type=jnp.float32
    )
    attended_grad = jnp.einsum(
        "re,de->rd", branch_low, proj_weight, preferred_element_type=jnp.float32
    )
    attended_grad = attended_grad.astype(jnp.bfloat16).reshape(images, slots, HEADS, HEAD_DIM)
    queries, keys_part, values = split_heads(projected, images, slots)
    scale = HEAD_DIM ** (-0.5)
    scores = scores_of(queries, keys_part, live, scale)
    probs = jnp.exp(scores - log_total)
    prob_grad = jnp.einsum(
        "bqhe,bkhe->bhqk", attended_grad, values, preferred_element_type=jnp.float32
    )
    score_grad = (probs * (prob_grad - jnp.sum(probs * prob_grad, axis=-1, keepdims=True))).astype(
        jnp.bfloat16
    )
    query_grad = (
        jnp.einsum("bhqk,bkhe->bqhe", score_grad, keys_part, preferred_element_type=jnp.float32)
        * scale
    )
    key_grad = (
        jnp.einsum("bhqk,bqhe->bkhe", score_grad, queries, preferred_element_type=jnp.float32)
        * scale
    )
    value_grad = jnp.einsum(
        "bhqk,bqhe->bkhe",
        probs.astype(jnp.bfloat16),
        attended_grad,
        preferred_element_type=jnp.float32,
    )
    joined = (
        jnp.stack([query_grad, key_grad, value_grad], axis=2)
        .reshape(images * slots, 3 * width)
        .astype(jnp.bfloat16)
    )
    column_sums = jnp.sum(joined, axis=0, dtype=jnp.float32)
    qv_bias_grad = jnp.concatenate([column_sums[:width], column_sums[2 * width :]])
    qkv_weight_grad = jnp.einsum("rd,rc->dc", first_low, joined, preferred_element_type=jnp.float32)
    first_grad = jnp.einsum("rc,dc->rd", joined, qkv_weight, preferred_element_type=jnp.float32)
    first_back, attn_gain_grad, attn_shift_grad = norm_back(
        first_grad, first_normed, first_factor, attn_gain.astype(jnp.float32)
    )
    grad_in = middle_grad + first_back
    grads = (
        attn_gain_grad,
        attn_shift_grad,
        qkv_weight_grad,
        qv_bias_grad,
        proj_weight_grad,
        proj_bias_grad,
        mlp_gain_grad,
        mlp_shift_grad,
        fc1_weight_grad,
        fc1_bias_grad,
        fc2_weight_grad,
        fc2_bias_grad,
    )
    return (grad_in.reshape(images, slots, width), grads)


def per_device(
    tokens,
    kept,
    attn_gain,
    attn_shift,
    qkv_weight,
    qv_bias,
    proj_weight,
    proj_bias,
    mlp_gain,
    mlp_shift,
    fc1_weight,
    fc1_bias,
    fc2_weight,
    fc2_bias,
    cotangent,
):
    images, slots, width = tokens.shape
    layers = attn_gain.shape[0]
    live = lax.broadcasted_iota(jnp.int32, (images, slots), 1) < BUFFER + kept[:, None]
    state = tokens.astype(jnp.float32)
    held_weights = []
    saved_all = []
    for layer in range(layers):
        gathered = (
            lax.all_gather(attn_gain[layer], "shard", axis=0, tiled=True),
            lax.all_gather(attn_shift[layer], "shard", axis=0, tiled=True),
            lax.all_gather(qkv_weight[layer], "shard", axis=0, tiled=True),
            lax.all_gather(qv_bias[layer], "shard", axis=0, tiled=True),
            lax.all_gather(proj_weight[layer], "shard", axis=0, tiled=True),
            lax.all_gather(proj_bias[layer], "shard", axis=0, tiled=True),
            lax.all_gather(mlp_gain[layer], "shard", axis=0, tiled=True),
            lax.all_gather(mlp_shift[layer], "shard", axis=0, tiled=True),
            lax.all_gather(fc1_weight[layer], "shard", axis=0, tiled=True),
            lax.all_gather(fc1_bias[layer], "shard", axis=0, tiled=True),
            lax.all_gather(fc2_weight[layer], "shard", axis=0, tiled=True),
            lax.all_gather(fc2_bias[layer], "shard", axis=0, tiled=True),
        )
        held_weights.append(gathered)
        state, saved = layer_forward(state, gathered, live)
        saved_all.append(saved)
    mixed = jnp.where(live[:, :, None], state, 0.0).astype(jnp.bfloat16)
    grad_state = jnp.where(live[:, :, None], cotangent.astype(jnp.float32), 0.0)
    owned_grads = [None] * layers
    for layer in reversed(range(layers)):
        weights = (
            lax.all_gather(attn_gain[layer], "shard", axis=0, tiled=True),
            lax.all_gather(attn_shift[layer], "shard", axis=0, tiled=True),
            lax.all_gather(qkv_weight[layer], "shard", axis=0, tiled=True),
            lax.all_gather(qv_bias[layer], "shard", axis=0, tiled=True),
            lax.all_gather(proj_weight[layer], "shard", axis=0, tiled=True),
            lax.all_gather(proj_bias[layer], "shard", axis=0, tiled=True),
            lax.all_gather(mlp_gain[layer], "shard", axis=0, tiled=True),
            lax.all_gather(mlp_shift[layer], "shard", axis=0, tiled=True),
            lax.all_gather(fc1_weight[layer], "shard", axis=0, tiled=True),
            lax.all_gather(fc1_bias[layer], "shard", axis=0, tiled=True),
            lax.all_gather(fc2_weight[layer], "shard", axis=0, tiled=True),
            lax.all_gather(fc2_bias[layer], "shard", axis=0, tiled=True),
        )
        grad_state, grads = layer_backward(grad_state, weights, live, saved_all[layer])
        shares = (
            lax.psum_scatter(
                grads[0].astype(jnp.bfloat16), "shard", scatter_dimension=0, tiled=True
            ).astype(jnp.float32),
            lax.psum_scatter(
                grads[1].astype(jnp.bfloat16), "shard", scatter_dimension=0, tiled=True
            ).astype(jnp.float32),
            lax.psum_scatter(
                grads[2].astype(jnp.bfloat16), "shard", scatter_dimension=0, tiled=True
            ).astype(jnp.float32),
            lax.psum_scatter(
                grads[3].astype(jnp.bfloat16), "shard", scatter_dimension=0, tiled=True
            ).astype(jnp.float32),
            lax.psum_scatter(
                grads[4].astype(jnp.bfloat16), "shard", scatter_dimension=0, tiled=True
            ).astype(jnp.float32),
            lax.psum_scatter(
                grads[5].astype(jnp.bfloat16), "shard", scatter_dimension=0, tiled=True
            ).astype(jnp.float32),
            lax.psum_scatter(
                grads[6].astype(jnp.bfloat16), "shard", scatter_dimension=0, tiled=True
            ).astype(jnp.float32),
            lax.psum_scatter(
                grads[7].astype(jnp.bfloat16), "shard", scatter_dimension=0, tiled=True
            ).astype(jnp.float32),
            lax.psum_scatter(
                grads[8].astype(jnp.bfloat16), "shard", scatter_dimension=0, tiled=True
            ).astype(jnp.float32),
            lax.psum_scatter(
                grads[9].astype(jnp.bfloat16), "shard", scatter_dimension=0, tiled=True
            ).astype(jnp.float32),
            lax.psum_scatter(
                grads[10].astype(jnp.bfloat16), "shard", scatter_dimension=0, tiled=True
            ).astype(jnp.float32),
            lax.psum_scatter(
                grads[11].astype(jnp.bfloat16), "shard", scatter_dimension=0, tiled=True
            ).astype(jnp.float32),
        )
        owned_grads[layer] = (
            lax.psum(shares[0].astype(jnp.bfloat16), "rep").astype(jnp.float32),
            lax.psum(shares[1].astype(jnp.bfloat16), "rep").astype(jnp.float32),
            lax.psum(shares[2].astype(jnp.bfloat16), "rep").astype(jnp.float32),
            lax.psum(shares[3].astype(jnp.bfloat16), "rep").astype(jnp.float32),
            lax.psum(shares[4].astype(jnp.bfloat16), "rep").astype(jnp.float32),
            lax.psum(shares[5].astype(jnp.bfloat16), "rep").astype(jnp.float32),
            lax.psum(shares[6].astype(jnp.bfloat16), "rep").astype(jnp.float32),
            lax.psum(shares[7].astype(jnp.bfloat16), "rep").astype(jnp.float32),
            lax.psum(shares[8].astype(jnp.bfloat16), "rep").astype(jnp.float32),
            lax.psum(shares[9].astype(jnp.bfloat16), "rep").astype(jnp.float32),
            lax.psum(shares[10].astype(jnp.bfloat16), "rep").astype(jnp.float32),
            lax.psum(shares[11].astype(jnp.bfloat16), "rep").astype(jnp.float32),
        )
    outputs = tuple(
        (jnp.stack([owned_grads[layer][index] for layer in range(layers)]) for index in range(12))
    )
    return (mixed, grad_state) + tuple(outputs)


def solution(mesh):
    return jax.shard_map(
        per_device,
        mesh=mesh,
        in_specs=(
            P(("shard", "rep"), None, None),
            P(("shard", "rep")),
            P(None, "shard"),
            P(None, "shard"),
            P(None, "shard", None),
            P(None, "shard"),
            P(None, "shard", None),
            P(None, "shard"),
            P(None, "shard"),
            P(None, "shard"),
            P(None, "shard", None),
            P(None, "shard"),
            P(None, "shard", None),
            P(None, "shard"),
            P(("shard", "rep"), None, None),
        ),
        out_specs=(
            P(("shard", "rep"), None, None),
            P(("shard", "rep"), None, None),
            P(None, "shard"),
            P(None, "shard"),
            P(None, "shard", None),
            P(None, "shard"),
            P(None, "shard", None),
            P(None, "shard"),
            P(None, "shard"),
            P(None, "shard"),
            P(None, "shard", None),
            P(None, "shard"),
            P(None, "shard", None),
            P(None, "shard"),
        ),
        check_vma=False,
    )
```

profile of v0, /device:TPU:0, one launch (start us, length us, event | category | flops | bytes accessed | tf_op | source)
XLA Modules:
  0.0 1490.3 jit_solution(16787025607204131050)
XLA Ops:
  23.7 64.3 %all-reduce.29 = (bf16[1024]{0:T(1024)(128)(2,1)S(1)}, bf16[1024]{0:T(1024)(128)(2,1)S(1)}, bf16[1024]{0:T(1024)(128)(2,1)S(1)}, bf16[1024]{0:T(1024)(128)(2,1)S...) all-reduce(bf16[1024]{0:T(1024)(128)(2,1)S(1)} %dynamic-update-slic, ...), channel_id=3, replica_groups=mesh['shard'=16,'rep'=2] {'shard'}, use_global_device_ids=true, to_apply=%add.1 | all-reduce | flops 11264 | bytes 45056
  88.7 17.0 %all-gather.15 = bf16[1,2048]{1,0:T(2,128)(2,1)S(1)} all-gather(bf16[1,128]{1,0:T(2,128)(2,1)S(1)} %get-tuple-element.126), channel_id=17, replica_groups=mesh['shard'=16,'rep'=2] {'shard'}, dimensions={1}, use_global_device_ids=true | all-gather | bytes 4352 | tf_op jit(solution)/shard_map/all_gather | solution.py:260
  105.7 19.0 %all-gather.3 = bf16[1,2048]{1,0:T(2,128)(2,1)S(1)} all-gather(bf16[1,128]{1,0:T(2,128)(2,1)S(1)} %get-tuple-element.127), channel_id=5, replica_groups=mesh['shard'=16,'rep'=2] {'shard'}, dimensions={1}, use_global_device_ids=true | all-gather | bytes 4352 | tf_op jit(solution)/shard_map/all_gather | solution.py:260
  124.8 17.6 %all-gather.9 = bf16[1,4096]{1,0:T(2,128)(2,1)S(1)} all-gather(bf16[1,256]{1,0:T(2,128)(2,1)S(1)} %get-tuple-element.121), channel_id=11, replica_groups=mesh['shard'=16,'rep'=2] {'shard'}, dimensions={1}, use_global_device_ids=true | all-gather | bytes 8704 | tf_op jit(solution)/shard_map/all_gather | solution.py:266
  144.3 19.1 %all-gather.21 = bf16[1,4096]{1,0:T(2,128)(2,1)S(1)} all-gather(bf16[1,256]{1,0:T(2,128)(2,1)S(1)} %get-tuple-element.120), channel_id=23, replica_groups=mesh['shard'=16,'rep'=2] {'shard'}, dimensions={1}, use_global_device_ids=true | all-gather | bytes 8704 | tf_op jit(solution)/shard_map/all_gather | solution.py:266
  245.9 33.9 %multiply_convert_fusion.3 = (bf16[640,4096]{1,0:T(8,128)(2,1)}, f32[640,4096]{1,0:T(8,128)}, f32[640,4096]{1,0:T(8,128)}) fusion(f32[4096]{0:T(1024)S(1)} %bitcast.307, bf16[1,1024,4096]{2,1,0:T(8,128)(2,1)} %all-gather.37.cloned.1.call-done, f32[640,1024]{1,0:T(8,128)} %copy-done.12, f32[1024]{0:T(1024)S(1)} %convert_element_type.408, ...), kind=kOutput, calls=%fused_computation.35 | convolution fusion | flops 5545000960 | bytes 37254144 | tf_op jit(solution)/shard_map/dot_general | solution.py:97
  291.6 40.7 %all-gather.41.cloned.1.call-done = bf16[1,1024,3072]{2,1,0:T(8,128)(2,1)} async-done(((bf16[1,64,3072]{2,1,0:T(8,128)(2,1)}), bf16[1,1024,3072]{2,1,0:T(8,128)(2,1)}) %all-gather.41.cloned.1.call-update) | async-done | bytes 6291472 | tf_op jit(solution)/shard_map/all_gather | solution.py:259
  405.9 44.9 %all-gather.45.cloned.1.call-done = bf16[1,1024,4096]{2,1,0:T(8,128)(2,1)} async-done(((bf16[1,64,4096]{2,1,0:T(8,128)(2,1)}), bf16[1,1024,4096]{2,1,0:T(8,128)(2,1)}) %all-gather.45.cloned.1.call-update) | async-done | bytes 8388624 | tf_op jit(solution)/shard_map/all_gather | solution.py:265
  450.8 33.7 %multiply_convert_fusion.2 = (bf16[640,4096]{1,0:T(8,128)(2,1)}, f32[640,4096]{1,0:T(8,128)}, f32[640,4096]{1,0:T(8,128)}) fusion(f32[4096]{0:T(1024)S(1)} %bitcast.309, bf16[1,1024,4096]{2,1,0:T(8,128)(2,1)} %all-gather.45.cloned.1.call-done, f32[640,1024]{1,0:T(8,128)S(1)} %get-tuple-element.148, f32[1024]{0:T(1024)S(1)} %copy-done.82, ...), kind=kOutput, calls=%fused_computation.22 | convolution fusion | flops 5545000960 | bytes 37254144 | tf_op jit(solution)/shard_map/dot_general | solution.py:97
  484.5 42.2 %all-gather.47.cloned.1.call-done = bf16[1,4096,1024]{2,1,0:T(8,128)(2,1)} async-done(((bf16[1,256,1024]{2,1,0:T(8,128)(2,1)}), bf16[1,4096,1024]{2,1,0:T(8,128)(2,1)}) %all-gather.47.cloned.1.call-update) | async-done | bytes 8388624 | tf_op jit(solution)/shard_map/all_gather | solution.py:267
  526.7 18.3 %fusion.165 = (bf16[4096]{0:T(1024)(128)(2,1)}, bf16[640,4096]{1,0:T(8,128)(2,1)}) fusion(f32[640,4096]{1,0:T(8,128)} %get-tuple-element.93, bf16[640,1024]{1,0:T(8,128)(2,1)} %bitcast_convert_fusion, bf16[1,4096,1024]{2,1,0:T(8,128)(2,1)} %all-gather.47.cloned.1.call-done, f32[640,4096]{1,0:T(8,128)} %get-tuple-element.149, f32[4096]{0:T(1024)S(1)} %bitcast.310), kind=kOutput, calls=%fused_computation.281 | convolution fusion | flops 5410648064 | bytes 35938304 | tf_op jit(solution)/shard_map/rd,fd->rf/dot_general | solution.py:157
  569.2 17.7 %multiply_reduce_fusion.1 = (f32[2,16,320]{2,1,0:T(8,128)S(1)}, f32[2,16,320,320]{2,3,1,0:T(8,128)}) fusion(f32[2,16,320]{2,1,0:T(8,128)S(1)} %log_add_fusion.1, f32[2,16,320,320]{2,3,1,0:T(8,128)} %get-tuple-element.146, pred[2,320]{1,0:T(4,128)(4,1)S(1)} %iota_compare_fusion, bf16[2,320,16,64]{1,3,2,0:T(8,128)(2,1)} %copy.86, ...), kind=kOutput, calls=%fused_computation.4 | convolution fusion | flops 435804160 | bytes 28918400 | tf_op jit(solution)/shard_map/bqhe,bkhe->bhqk/dot_general | solution.py:182
  656.6 18.9 %fusion.166 = (bf16[4096]{0:T(1024)(128)(2,1)S(1)}, bf16[640,4096]{1,0:T(8,128)(2,1)}) fusion(f32[640,4096]{1,0:T(8,128)} %get-tuple-element.95, bf16[1,4096,1024]{2,1,0:T(8,128)(2,1)} %all-gather.39.cloned.1.call-done, f32[640,1024]{1,0:T(8,128)} %get-tuple-element.83, f32[640,4096]{1,0:T(8,128)} %get-tuple-element.142, f32[4096]{0:T(1024)S(1)} %bitcast.308), kind=kOutput, calls=%fused_computation.282 | convolution fusion | flops 5411303424 | bytes 37249024 | tf_op jit(solution)/shard_map/rd,fd->rf/dot_general | solution.py:157
  719.6 12.6 multiply_reduce_fusion
  732.2 12.0 multiply_convert_fusion
  790.0 12.5 convolution_convert_fusion.1
  803.2 12.0 convolution_convert_fusion
  853.9 60.5 %all-reduce.28 = (bf16[1024]{0:T(1024)(128)(2,1)S(1)}, bf16[1024]{0:T(1024)(128)(2,1)S(1)}, bf16[1024]{0:T(1024)(128)(2,1)S(1)}, bf16[1024]{0:T(1024)(128)(2,1)S...) all-reduce(bf16[1024]{0:T(1024)(128)(2,1)S(1)} %dynamic-update-slic, ...), channel_id=25, replica_groups=mesh['shard'=16,'rep'=2] {'shard'}, use_global_device_ids=true, to_apply=%add.11 | all-reduce | flops 25600 | bytes 102400
  923.7 30.3 %reduce-scatter.9.cloned.1.call-done = bf16[64,3072]{1,0:T(8,128)(2,1)} async-done(((bf16[1024,3072]{1,0:T(8,128)(2,1)}), bf16[64,3072]{1,0:T(8,128)(2,1)}) %reduce-scatter.9.cloned.1.call-update) | async-done | bytes 393232 | tf_op jit(solution)/shard_map/reduce_scatter | solution.py:299
  954.1 107.8 %reduce-scatter.17.cloned.1.call-done = bf16[64,4096]{1,0:T(8,128)(2,1)} async-done(((bf16[1024,4096]{1,0:T(8,128)(2,1)}), bf16[64,4096]{1,0:T(8,128)(2,1)}) %reduce-scatter.17.cloned.1.call-update) | async-done | bytes 524304 | tf_op jit(solution)/shard_map/reduce_scatter | solution.py:317
  1061.9 108.3 %reduce-scatter.19.cloned.1.call-done = bf16[64,4096]{1,0:T(8,128)(2,1)} async-done(((bf16[1024,4096]{1,0:T(8,128)(2,1)}), bf16[64,4096]{1,0:T(8,128)(2,1)}) %reduce-scatter.19.cloned.1.call-update) | async-done | bytes 524304 | tf_op jit(solution)/shard_map/reduce_scatter | solution.py:317
  1170.2 108.3 %reduce-scatter.21.cloned.1.call-done = bf16[256,1024]{1,0:T(8,128)(2,1)} async-done(((bf16[4096,1024]{1,0:T(8,128)(2,1)}), bf16[256,1024]{1,0:T(8,128)(2,1)}) %reduce-scatter.21.cloned.1.call-update) | async-done | bytes 524304 | tf_op jit(solution)/shard_map/reduce_scatter | solution.py:323
  1278.4 108.3 %reduce-scatter.23.cloned.1.call-done = bf16[256,1024]{1,0:T(8,128)(2,1)} async-done(((bf16[4096,1024]{1,0:T(8,128)(2,1)}), bf16[256,1024]{1,0:T(8,128)(2,1)}) %reduce-scatter.23.cloned.1.call-update) | async-done | bytes 524304 | tf_op jit(solution)/shard_map/reduce_scatter | solution.py:323
  1403.1 72.9 %all-reduce.34.cloned.1.call-done = (bf16[1,64,3072]{2,1,0:T(8,128)(2,1)}, bf16[1,64,3072]{2,1,0:T(8,128)(2,1)}, bf16[1,64,1024]{2,1,0:T(8,128)(2,1)}, bf16[1,64...) async-done(((bf16[1,64,3072]{2,1,0:T(8,128)(2,1)}, ...) | async-done | bytes 3145744 | tf_op jit(solution)/shard_map/psum | solution.py:333
  (433 shorter events, 439.2 us)
Async XLA Ops:
  7.2 160.4 %all-gather.33.cloned.1.call-start = ((), (), s32[]{:S(2)}) async-start(), calls=%async_computation.16 | async-start | bytes 6684672 | tf_op jit(solution)/shard_map/all_gather | solution.py:259
  9.3 230.9 %all-gather.35.cloned.1.call-start = ((), (), s32[]{:S(2)}) async-start(), calls=%async_computation.17 | async-start | bytes 2228224 | tf_op jit(solution)/shard_map/all_gather | solution.py:261
  11.1 234.7 %all-gather.37.cloned.1.call-start = ((), (), s32[]{:S(2)}) async-start(), calls=%async_computation.18 | async-start | bytes 8912896 | tf_op jit(solution)/shard_map/all_gather | solution.py:265
  13.5 150.5 %copy-start.28 = (bf16[2,320,1024]{2,1,0:T(8,128)(2,1)S(1)}, bf16[2,320,1024]{2,1,0:T(8,128)(2,1)}, u32[]{:S(2)}) copy-start(bf16[2,320,1024]{2,1,0:T(8,128)(2,1)} %param.29) | copy-start | bytes 3932164
  13.6 266.2 %all-gather.39.cloned.1.call-start = ((), (), s32[]{:S(2)}) async-start(), calls=%async_computation.19 | async-start | bytes 8912896 | tf_op jit(solution)/shard_map/all_gather | solution.py:267
  16.0 316.3 %all-gather.41.cloned.1.call-start = ((), (), s32[]{:S(2)}) async-start(), calls=%async_computation.20 | async-start | bytes 6684672 | tf_op jit(solution)/shard_map/all_gather | solution.py:259
  16.6 384.4 %all-gather.43.cloned.1.call-start = ((), (), s32[]{:S(2)}) async-start(), calls=%async_computation.21 | async-start | bytes 2228224 | tf_op jit(solution)/shard_map/all_gather | solution.py:261
  17.2 433.6 %all-gather.45.cloned.1.call-start = ((), (), s32[]{:S(2)}) async-start(), calls=%async_computation.22 | async-start | bytes 8912896 | tf_op jit(solution)/shard_map/all_gather | solution.py:265
  17.9 508.8 %all-gather.47.cloned.1.call-start = ((), (), s32[]{:S(2)}) async-start(), calls=%async_computation.23 | async-start | bytes 8912896 | tf_op jit(solution)/shard_map/all_gather | solution.py:267
  18.7 905.1 %reduce-scatter.15.cloned.1.call-start = ((), (), s32[]{:S(2)}) async-start(), calls=%async_computation.11 | async-start | bytes 2228224 | tf_op jit(solution)/shard_map/reduce_scatter | solution.py:305
  19.6 147.4 %copy-start.47 = (f32[640]{0:T(1024)}, f32[640]{0:T(1024)S(1)}, u32[]{:S(2)}) copy-start(f32[640]{0:T(1024)S(1)} %div.67) | copy-start | bytes 7684
  142.5 189.8 %copy-start.66 = (f32[1024]{0:T(1024)}, f32[1024]{0:T(1024)S(1)}, u32[]{:S(2)}) copy-start(f32[1024]{0:T(1024)S(1)} %convert_element_type.410) | copy-start | bytes 12292
  142.5 189.8 %copy-start.84 = (f32[1024]{0:T(1024)}, f32[1024]{0:T(1024)S(1)}, u32[]{:S(2)}) copy-start(f32[1024]{0:T(1024)S(1)} %convert_element_type.411) | copy-start | bytes 12292
  405.4 150.8 %copy-start.11 = (f32[640,1024]{1,0:T(8,128)}, f32[640,1024]{1,0:T(8,128)S(1)}, u32[]{:S(2)}) copy-start(f32[640,1024]{1,0:T(8,128)S(1)} %get-tuple-element.148) | copy-start | bytes 7864324
  405.4 150.8 %copy-start.55 = (f32[640]{0:T(1024)}, f32[640]{0:T(1024)S(1)}, u32[]{:S(2)}) copy-start(f32[640]{0:T(1024)S(1)} %broadcast_multiply_fusion.8) | copy-start | bytes 7684
  405.8 150.4 %copy-start.70 = (f32[640]{0:T(1024)}, f32[640]{0:T(1024)S(1)}, u32[]{:S(2)}) copy-start(f32[640]{0:T(1024)S(1)} %add_rsqrt_fusion) | copy-start | bytes 7684
  651.8 272.0 %reduce-scatter.13.cloned.1.call-start = ((), (), s32[]{:S(2)}) async-start(), calls=%async_computation.10 | async-start | bytes 2228224 | tf_op jit(solution)/shard_map/reduce_scatter | solution.py:305
  692.2 231.5 %reduce-scatter.11.cloned.1.call-start = ((), (), s32[]{:S(2)}) async-start(), calls=%async_computation.9 | async-start | bytes 6684672 | tf_op jit(solution)/shard_map/reduce_scatter | solution.py:299
  702.2 251.8 %reduce-scatter.9.cloned.1.call-start = ((), (), s32[]{:S(2)}) async-start(), calls=%async_computation.8 | async-start | bytes 6684672 | tf_op jit(solution)/shard_map/reduce_scatter | solution.py:299
  789.4 272.5 %reduce-scatter.17.cloned.1.call-start = ((), (), s32[]{:S(2)}) async-start(), calls=%async_computation.12 | async-start | bytes 8912896 | tf_op jit(solution)/shard_map/reduce_scatter | solution.py:317
  802.6 367.6 %reduce-scatter.19.cloned.1.call-start = ((), (), s32[]{:S(2)}) async-start(), calls=%async_computation.13 | async-start | bytes 8912896 | tf_op jit(solution)/shard_map/reduce_scatter | solution.py:317
  815.3 463.1 %reduce-scatter.21.cloned.1.call-start = ((), (), s32[]{:S(2)}) async-start(), calls=%async_computation.14 | async-start | bytes 8912896 | tf_op jit(solution)/shard_map/reduce_scatter | solution.py:323
  827.3 559.4 %reduce-scatter.23.cloned.1.call-start = ((), (), s32[]{:S(2)}) async-start(), calls=%async_computation.15 | async-start | bytes 8912896 | tf_op jit(solution)/shard_map/reduce_scatter | solution.py:323
  840.5 635.6 %all-reduce.34.cloned.1.call-start = ((), (), s32[]{:S(2)}) async-start(), calls=%async_computation.24 | async-start | bytes 6291456 | tf_op jit(solution)/shard_map/psum | solution.py:333
  (96 other events, 1808.4 us)
Sparse Core Ops, SparseCore 0:
  10.9 65.2 all-gather.32
  78.3 39.9 all-gather.34
  121.0 73.7 all-gather.36
  196.8 73.1 all-gather.38
  272.2 60.0 all-gather.40
  334.3 39.9 all-gather.42
  377.1 73.6 all-gather.44
  453.5 73.1 all-gather.46
  651.9 59.7 reduce-scatter.14
  716.3 60.5 reduce-scatter.12
  780.9 84.2 reduce-scatter.10
  869.5 84.5 reduce-scatter.8
  958.1 103.7 reduce-scatter.16
  1065.8 104.3 reduce-scatter.18
  1174.1 104.3 reduce-scatter.20
  1282.4 104.3 reduce-scatter.22
  1389.3 86.7 all-reduce.33
where the time goes:
time: 1500 us; the launch traced here: 1490 us
  waiting for transfers between devices  666 us (44%)
  matrix products  369 us (25%)
  blocking collectives  203 us (14%)
  local copies, waits for them, and re-layouts  150 us (10%)
  other arithmetic  82.6 us (6%)
  between operations  18.3 us (1%)
    reduce_scatter x2, waiting for transfers between devices, per_device(): lax.psum_scatter(grads[10].astype(jnp.bfloat16), 'shard', scatter_dimensi...  217 us
    reduce_scatter x2, waiting for transfers between devices, per_device(): lax.psum_scatter(grads[8].astype(jnp.bfloat16), 'shard', scatter_dimensio...  216 us
    unnamed x2, blocking collectives  125 us
    psum x1, waiting for transfers between devices, per_device(): lax.psum(shares[2].astype(jnp.bfloat16), 'rep').astype(jnp.float32)  72.9 us
    dot_general x2, matrix products, layer_forward(): jnp.dot(second_low, fc1_weight, preferred_element_type=jnp.float32)  67.6 us
    all_gather x2, waiting for transfers between devices, per_device(): lax.all_gather(fc1_weight[layer], 'shard', axis=0, tiled=True)  44.9 us
    unnamed x245, local copies, waits for them, and re-layouts  44.7 us
    all_gather x2, waiting for transfers between devices, per_device(): lax.all_gather(fc2_weight[layer], 'shard', axis=0, tiled=True)  42.2 us
  transfers between devices with their start and end apart: 17, of which 9 were waited for; matrix products, arithmetic and copies ran while one was open for 31% of the time, Pallas kernels for 0%

commit v1 on v0

v1 whole, which is shorter than its diff:
```python
from functools import partial

import jax
import jax.numpy as jnp
from jax import lax
from jax.experimental import pallas as pl
from jax.experimental.pallas import tpu as pltpu
from jax.sharding import PartitionSpec as P

HEADS = 16
HEAD_DIM = 64
BUFFER = 64
EPS = 1e-06
SCALE = HEAD_DIM ** (-0.5)
AX = ("shard", "rep")
BF = jnp.bfloat16
F32 = jnp.float32
LIMIT = 56 * 2**20
SMALL = ("ag", "as", "qvb", "pb", "mg", "ms", "f1b", "f2b")


class Plan:
    def __init__(self, mesh):
        self.shards = mesh.shape["shard"]
        self.rep = mesh.shape["rep"]
        self.chips = self.shards // 2
        self.ny = 2 if self.rep == 2 else 1
        self.bits = self.chips.bit_length() - 1

    def swap(self, v, flip_shard, flip_rep=0):
        pairs = []
        for s in range(self.shards):
            for y in range(self.rep):
                pairs.append((s * self.rep + y, (s ^ flip_shard) * self.rep + (y ^ flip_rep)))
        return lax.ppermute(v, AX, pairs)

    def core(self, v):
        return self.swap(v, 1)

    def flip(self, v, axis):
        if axis == 0:
            return self.swap(v, 0, 1)
        return self.swap(v, 2 << (self.bits - axis))


def dot(x, w):
    return lax.dot_general(x, w, (((1,), (0,)), ((), ())), preferred_element_type=F32)


def dot_t(x, w):
    return lax.dot_general(x, w, (((1,), (1,)), ((), ())), preferred_element_type=F32)


def t_dot(x, w):
    return lax.dot_general(x, w, (((0,), (0,)), ((), ())), preferred_element_type=F32)


def columns(width, first):
    return ("columns", width, first)


def row_call(body, where, kept, gathered, picks, blocked, whole, outs, images, slots, flops=0):
    in_specs, args = [], []
    for kind, width, first in picks:
        if kind == "columns":
            depth = gathered.shape[0]
            in_specs.append(pl.BlockSpec((depth, width), lambda i, w, k, f=first: (0, f + w[0])))
            args.append(gathered)
        else:
            view = gathered.reshape(HEADS // 2, 2, HEAD_DIM, gathered.shape[1])
            in_specs.append(pl.BlockSpec((HEADS // 2, None, HEAD_DIM, width), lambda i, w, k, f=first: (0, w[0], 0, f)))
            args.append(view)
    for v in blocked:
        if v.ndim == 2:
            in_specs.append(pl.BlockSpec((slots, v.shape[1]), lambda i, *_: (i, 0)))
        else:
            in_specs.append(pl.BlockSpec((1,) + v.shape[1:], lambda i, *_, n=v.ndim: (i,) + (0,) * (n - 1)))
        args.append(v)
    for v in whole:
        in_specs.append(pl.BlockSpec(v.shape, lambda i, *_, n=v.ndim: (0,) * n))
        args.append(v)
    out_specs, out_shape = [], []
    for kind, shape, dtype in outs:
        out_shape.append(jax.ShapeDtypeStruct(shape, dtype))
        if kind == "rows":
            out_specs.append(pl.BlockSpec((slots, shape[1]), lambda i, *_: (i, 0)))
        elif kind == "image":
            out_specs.append(pl.BlockSpec((1,) + shape[1:], lambda i, *_, n=len(shape): (i,) + (0,) * (n - 1)))
        else:
            out_specs.append(pl.BlockSpec(shape, lambda i, *_, n=len(shape): (0,) * n))
    n_p, n_b, n_in = len(picks), len(blocked), len(args)

    def kernel(where_ref, kept_ref, *refs):
        ins, res = refs[:n_in], refs[n_in:]
        body(kept_ref, ins[:n_p], ins[n_p : n_p + n_b], ins[n_p + n_b :], res)

    return pl.pallas_call(
        kernel,
        grid_spec=pltpu.PrefetchScalarGridSpec(
            num_scalar_prefetch=2, grid=(images,), in_specs=in_specs, out_specs=out_specs
        ),
        out_shape=out_shape,
        compiler_params=pltpu.CompilerParams(vmem_limit_bytes=LIMIT),
        cost_estimate=pl.CostEstimate(
            flops=flops, bytes_accessed=sum(v.size * v.dtype.itemsize for v in args[n_p:]), transcendentals=0
        ),
    )(where, kept, *args)


def normed_of(rows):
    width = rows.shape[-1]
    mean = jnp.sum(rows, axis=-1, keepdims=True) * (1.0 / width)
    centered = rows - mean
    spread = jnp.sum(centered * centered, axis=-1, keepdims=True) * (1.0 / width)
    factor = lax.rsqrt(spread + EPS)
    return centered * factor, factor


def norm_rows(rows, gain, shift):
    return normed_of(rows)[0] * gain + shift


def norm_back(dz, rows, gain):
    normed, factor = normed_of(rows)
    width = rows.shape[-1]
    prod = dz * normed
    dn = dz * gain
    m1 = jnp.sum(dn, axis=-1, keepdims=True) * (1.0 / width)
    m2 = jnp.sum(dn * normed, axis=-1, keepdims=True) * (1.0 / width)
    back = factor * (dn - m1 - normed * m2)
    return back, jnp.sum(prod, axis=0, keepdims=True), jnp.sum(dz, axis=0, keepdims=True)


def chunks(total, size):
    size = min(size, total)
    return [(k, size) for k in range(0, total, size)]


def qkv_body(kept, w, blocked, whole, outs):
    x = blocked[0][...]
    for k, n in chunks(outs[0].shape[1], 512):
        cols = pl.ds(k, n)
        outs[0][:, cols] = (dot(x, w[0][:, cols]) + whole[0][:, cols]).astype(BF)


def heads_of(ref):
    return ref[...].reshape(-1, ref.shape[-1])


def pairs_dot(x_ref, w_ref):
    depth = w_ref.shape[0]
    total = None
    for k in range(0, w_ref.shape[1], depth):
        term = dot(x_ref[:, k : k + depth], w_ref[:, k : k + depth])
        total = term if total is None else total + term
    return total


def attend(kept, proj_ref, probs_ref, att_ref):
    slots, third = proj_ref.shape[0], proj_ref.shape[1] // 3
    bound = BUFFER + kept[pl.program_id(0)]
    alive = lax.broadcasted_iota(jnp.int32, (slots, slots), 1) < bound
    outs = []
    for h in range(third // HEAD_DIM):
        lo = h * HEAD_DIM
        q = proj_ref[:, lo : lo + HEAD_DIM]
        k = proj_ref[:, third + lo : third + lo + HEAD_DIM]
        v = proj_ref[:, 2 * third + lo : 2 * third + lo + HEAD_DIM]
        s = jnp.where(alive, dot_t(q, k) * SCALE, -1e30)
        e = jnp.exp(s - jnp.max(s, axis=-1, keepdims=True))
        p = (e * (1.0 / jnp.sum(e, axis=-1, keepdims=True))).astype(BF)
        probs_ref[0, h] = p
        outs.append(dot(p, v).astype(BF))
        if h % 2:
            att_ref[:, lo - HEAD_DIM : lo + HEAD_DIM] = jnp.concatenate(outs, axis=1)
            outs = []


def attend_other(kept, w, blocked, whole, outs):
    attend(kept, blocked[0], outs[0], outs[1])
    outs[2][...] = dot(outs[1][...], heads_of(w[0]))


def attend_own(kept, w, blocked, whole, outs):
    attend(kept, blocked[0], outs[0], outs[1])
    middle = blocked[2][...] + (dot(outs[1][...], heads_of(w[0])) + blocked[1][...]) + whole[0][...]
    outs[2][...] = middle
    outs[3][...] = norm_rows(middle, whole[1][...], whole[2][...]).astype(BF)


def up_body(kept, w, blocked, whole, outs):
    x = blocked[0][...]
    for k, n in chunks(outs[0].shape[1], 256):
        cols = pl.ds(k, n)
        pre = dot(x, w[0][:, cols]) + whole[0][:, cols]
        phi = 0.5 + 0.5 * lax.erf(pre * (2.0**-0.5))
        dens = jnp.exp(-0.5 * (pre * pre)) * 0.3989422804014327
        outs[0][:, cols] = (pre * phi).astype(BF)
        outs[1][:, cols] = (phi + pre * dens).astype(BF)


def down_other(kept, w, blocked, whole, outs):
    outs[0][...] = pairs_dot(blocked[0], w[0])


def down_own(kept, w, blocked, whole, outs):
    state = blocked[2][...] + (pairs_dot(blocked[0], w[0]) + blocked[1][...]) + whole[0][...]
    outs[0][...] = state
    outs[1][...] = norm_rows(state, whole[1][...], whole[2][...]).astype(BF)


def down_last(kept, w, blocked, whole, outs):
    state = blocked[2][...] + (pairs_dot(blocked[0], w[0]) + blocked[1][...]) + whole[0][...]
    alive = lax.broadcasted_iota(jnp.int32, state.shape, 0) < BUFFER + kept[pl.program_id(0)]
    outs[0][...] = jnp.where(alive, state, 0.0).astype(BF)


def mlp_back(w, blocked, outs):
    low = blocked[0][...]
    depth = w[0].shape[0]
    for k, n in chunks(outs[0].shape[1], 512):
        cols = pl.ds(k, n)
        block = k // depth * depth
        t = dot_t(low, w[0][pl.ds(k - block, n), block : block + depth])
        outs[0][:, cols] = (t * blocked[1][:, cols].astype(F32)).astype(BF)
    return dot_t(outs[0][...], w[1][...])


def mlp_back_other(kept, w, blocked, whole, outs):
    outs[1][...] = mlp_back(w, blocked, outs)


def add_sums(ref, rows):
    sums = jnp.concatenate(rows + [jnp.zeros((8 - len(rows), rows[0].shape[1]), F32)], axis=0)

    @pl.when(pl.program_id(0) == 0)
    def _():
        ref[...] = sums

    @pl.when(pl.program_id(0) != 0)
    def _():
        ref[...] += sums


def mlp_back_own(kept, w, blocked, whole, outs):
    dz = mlp_back(w, blocked, outs) + blocked[2][...]
    back, gain, shift = norm_back(dz, blocked[3][...], whole[0][...])
    grad = blocked[4][...] + back
    low = grad.astype(BF)
    outs[1][...] = grad
    outs[2][...] = low
    add_sums(outs[3], [gain, shift, jnp.sum(low.astype(F32), axis=0, keepdims=True)])


def attend_back(w, blocked, outs):
    branch, proj_ref, probs_ref = blocked[0], blocked[1], blocked[2]
    third = proj_ref.shape[1] // 3
    datt = dot_t(branch[...], heads_of(w[0])).astype(BF)
    pairs = [[], [], []]
    for h in range(third // HEAD_DIM):
        lo = h * HEAD_DIM
        q = proj_ref[:, lo : lo + HEAD_DIM]
        k = proj_ref[:, third + lo : third + lo + HEAD_DIM]
        v = proj_ref[:, 2 * third + lo : 2 * third + lo + HEAD_DIM]
        da = datt[:, lo : lo + HEAD_DIM]
        p = probs_ref[0, h]
        dp = dot_t(da, v)
        pf = p.astype(F32)
        ds = (pf * (dp - jnp.sum(pf * dp, axis=-1, keepdims=True))).astype(BF)
        pairs[0].append((dot(ds, k) * SCALE).astype(BF))
        pairs[1].append((t_dot(ds, q) * SCALE).astype(BF))
        pairs[2].append(t_dot(p, da).astype(BF))
        if h % 2:
            for j in range(3):
                at = j * third + lo - HEAD_DIM
                outs[0][:, at : at + 2 * HEAD_DIM] = jnp.concatenate(pairs[j], axis=1)
            pairs = [[], [], []]
    return dot_t(outs[0][...], w[1][...])


def attend_back_other(kept, w, blocked, whole, outs):
    outs[1][...] = attend_back(w, blocked, outs)


def attend_back_own(kept, w, blocked, whole, outs):
    dz = attend_back(w, blocked, outs) + blocked[3][...]
    back, gain, shift = norm_back(dz, blocked[4][...], whole[0][...])
    grad = blocked[5][...] + back
    outs[1][...] = grad
    low = grad.astype(BF)
    outs[2][...] = low
    add_sums(outs[3], [gain, shift, jnp.sum(low.astype(F32), axis=0, keepdims=True)])


def weight_grad(plan, where, xs, ys, groups, first, sums):
    depth, n_x = xs[0].shape
    cols = ys[0].shape[1]
    ny, chips, bits = plan.ny, plan.chips, plan.bits
    half = cols // ny
    chunk = half if half <= 768 else 512
    steps = half // chunk
    rows = n_x // chips
    part = rows // groups
    dims = [ny] + [2] * bits
    dims[first] = 1
    block = [1] + dims[1:] + [rows, chunk]
    shape = dims + [rows, half]

    def kernel(where_ref, xo, xt, yo, yt, *rest):
        keep, send = rest[0], rest[1]
        flip, acc = rest[-2], rest[-1]
        step = pl.program_id(0)

        @pl.when(step == 0)
        def _():
            flip[:, :depth] = xo[...].T
            flip[:, depth:] = xt[...].T

        acc[...] = dot(flip[:, :depth], yo[...]) + dot(flip[:, depth:], yt[...])
        if sums:
            rest[2][...] = jnp.sum(yo[...].astype(F32), axis=0, keepdims=True) + jnp.sum(
                yt[...].astype(F32), axis=0, keepdims=True
            )

        def put(ref, r):
            at = [0]
            for k in range(1, bits + 1):
                at.append((r >> (bits - k)) & 1 if k != first else 0)
            chip = jnp.bitwise_xor(where_ref[1], r)
            for g in range(groups):
                start = pl.multiple_of(g * part * chips + chip * part, 16)
                ref[tuple(at) + (pl.ds(g * part, part),)] = acc[pl.ds(start, part)].astype(BF)

        if first:
            for r in range(chips):
                put(send if (r >> (bits - first)) & 1 else keep, r)
        else:

            @pl.when(step < steps)
            def _():
                for r in range(chips):
                    put(keep, r)

            @pl.when(step >= steps)
            def _():
                for r in range(chips):
                    put(send, r)

    def column(i, w):
        if ny == 1:
            return i
        return jnp.bitwise_xor(i // steps, w[2]) * steps + i % steps

    zeros = (0,) * (bits + 1)
    x_spec = pl.BlockSpec((depth, n_x), lambda i, w: (0, 0))
    y_spec = pl.BlockSpec((depth, chunk), lambda i, w: (0, column(i, w)))
    if first:
        specs = [pl.BlockSpec(block, lambda i, w: (i // steps,) + zeros + (i % steps,))] * 2
    else:
        specs = [
            pl.BlockSpec(block, lambda i, w: (0,) + zeros + (jnp.minimum(i, steps - 1),)),
            pl.BlockSpec(block, lambda i, w: (0,) + zeros + (jnp.maximum(i - steps, 0),)),
        ]
    out_shape = [jax.ShapeDtypeStruct(shape, BF)] * 2
    if sums:
        specs = specs + [pl.BlockSpec((1, chunk), lambda i, w: (0, column(i, w)))]
        out_shape = out_shape + [jax.ShapeDtypeStruct((1, cols), F32)]
    return pl.pallas_call(
        kernel,
        grid_spec=pltpu.PrefetchScalarGridSpec(
            num_scalar_prefetch=1,
            grid=(ny * steps,),
            in_specs=[x_spec, x_spec, y_spec, y_spec],
            out_specs=specs,
            scratch_shapes=[pltpu.VMEM((n_x, 2 * depth), BF), pltpu.VMEM((n_x, chunk), F32)],
        ),
        out_shape=out_shape,
        compiler_params=pltpu.CompilerParams(vmem_limit_bytes=LIMIT),
        cost_estimate=pl.CostEstimate(
            flops=4 * depth * n_x * cols, bytes_accessed=2 * (2 * depth * (n_x + cols) + n_x * cols), transcendentals=0
        ),
    )(where, *xs, *ys)


def sum_over(plan, keep, send, axes):
    for at, axis in enumerate(axes):
        got = plan.flip(send, axis)
        total = keep.astype(F32) + got.astype(F32)
        if at + 1 == len(axes):
            return total.reshape(total.shape[-2:])
        after = axes[at + 1]
        send = lax.slice_in_dim(total, 1, 2, axis=after).astype(BF)
        keep = lax.slice_in_dim(total, 0, 1, axis=after).astype(BF)


def pick(flag, a, b):
    return jnp.where(flag == 0, a, b)


def join_core(plan, v, c, groups):
    rows, cols = v.shape
    v = v.reshape(groups, 2, rows // groups // 2, cols)
    mine = pick(c, v[:, 0], v[:, 1]).astype(BF)
    got = plan.core(pick(c, v[:, 1], v[:, 0]).astype(BF))
    return jnp.stack([pick(c, mine, got), pick(c, got, mine)])


def join_rep(plan, v, y):
    if plan.ny == 1:
        return lax.psum(v, "rep").astype(F32)[..., None, :]
    got = plan.flip(v, 0)
    return jnp.stack([pick(y, v, got), pick(y, got, v)], axis=-2).astype(F32)


def per_device(
    plan,
    tokens,
    kept,
    attn_gain,
    attn_shift,
    qkv_weight,
    qv_bias,
    proj_weight,
    proj_bias,
    mlp_gain,
    mlp_shift,
    fc1_weight,
    fc1_bias,
    fc2_weight,
    fc2_bias,
    cotangent,
):
    images, slots, width = tokens.shape
    layers = attn_gain.shape[0]
    rows = images * slots
    n = plan.shards
    deep = qkv_weight.shape[1]
    shard = lax.axis_index("shard")
    c, chip, y = lax.rem(shard, 2), shard // 2, lax.axis_index("rep")
    where = jnp.stack([c, chip, y]).astype(jnp.int32)
    ff = fc2_weight.shape[1] * n
    quarters = fc2_weight.shape[1] // deep
    wide, half_width, half_ff = 3 * width // 2, width // 2, ff // 2
    half_heads = HEADS // 2

    small = jnp.concatenate(
        [attn_gain, attn_shift, qv_bias, proj_bias, mlp_gain, mlp_shift, fc1_bias, fc2_bias], axis=1
    )
    sizes = [v.shape[1] for v in (attn_gain, attn_shift, qv_bias, proj_bias, mlp_gain, mlp_shift, fc1_bias, fc2_bias)]
    lines = small.size // 128
    extra = jnp.pad(small.reshape(lines, 128), ((0, deep - lines), (0, 0)))

    def merged(layer):
        qkv = qkv_weight[layer].reshape(deep, 3 * half_heads, 2, HEAD_DIM).swapaxes(1, 2).reshape(deep, 3 * width)
        fc1 = fc1_weight[layer].reshape(deep, n, quarters, deep).swapaxes(1, 2).reshape(deep, ff)
        fc2 = [fc2_weight[layer, k * deep : (k + 1) * deep] for k in range(quarters)]
        return [qkv, proj_weight[layer], fc1] + fc2 + ([] if layer else [extra])

    gathered = [
        lax.all_gather(jnp.concatenate(merged(layer), axis=1), "shard", axis=0, tiled=True) for layer in range(layers)
    ]
    picks = {
        "qkv": columns(wide, 0),
        "proj": ("heads", width, 3),
        "fc1": columns(half_ff, 4 * width // half_ff),
        "fc2": columns(half_ff, (4 * width + ff) // half_ff),
    }

    every = gathered[0].reshape(n, deep, -1)[:, :lines, 4 * width + 2 * ff :]
    every = every.reshape(n, layers, small.shape[1]).astype(F32)
    vecs = []
    for layer in range(layers):
        at, d = 0, {}
        for name, size in zip(SMALL, sizes):
            d[name] = every[:, layer, at : at + size].reshape(1, n * size)
            at += size
        q = d["qvb"].reshape(2 * half_heads, 2, HEAD_DIM)
        q = pick(c, q[:, 0], q[:, 1]).reshape(2, half_width)
        d["qvb_c"] = jnp.stack([q[0], jnp.zeros_like(q[0]), q[1]]).reshape(1, wide)
        f = d["f1b"].reshape(n, quarters, deep).swapaxes(0, 1).reshape(2, half_ff)
        d["f1b_c"] = pick(c, f[0:1], f[1:2])
        vecs.append(d)

    kept_oth = plan.core(kept)
    state = tokens.astype(F32).reshape(rows, width)
    live = lax.broadcasted_iota(jnp.int32, (images, slots), 1) < BUFFER + kept[:, None]
    grad = jnp.where(live[:, :, None], cotangent.astype(F32), 0.0).reshape(rows, width)
    low_own = grad.astype(BF)
    low_oth = plan.core(low_own)
    first_own = norm_rows(state, vecs[0]["ag"], vecs[0]["as"]).astype(BF)

    qkv_flops = 2 * rows * width * wide
    att_flops = 4 * rows * slots * half_width + 2 * rows * half_width * width
    ff_flops = 2 * rows * width * half_ff
    f32_rows, low_rows = ("rows", (rows, width), F32), ("rows", (rows, width), BF)
    wide_rows, ff_rows = ("rows", (rows, wide), BF), ("rows", (rows, half_ff), BF)
    att_outs = [("image", (images, half_heads, slots, slots), BF), ("rows", (rows, half_width), BF)]
    full_sums = ("full", (8, width), F32)

    def call(body, layer, own, names, blocked, whole, outs, flops):
        chosen = [picks[name] for name in names]
        k = kept if own else kept_oth
        return row_call(body, where, k, gathered[layer], chosen, blocked, whole, outs, images, slots, flops)

    saved = []
    mixed = None
    for layer in range(layers):
        v = vecs[layer]
        first_oth = plan.core(first_own)
        proj_oth = call(qkv_body, layer, 0, ["qkv"], [first_oth], [v["qvb_c"]], [wide_rows], qkv_flops)[0]
        probs_oth, att_oth, part = call(attend_other, layer, 0, ["proj"], [proj_oth], [], att_outs + [f32_rows], att_flops)
        part = plan.core(part)
        proj_own = call(qkv_body, layer, 1, ["qkv"], [first_own], [v["qvb_c"]], [wide_rows], qkv_flops)[0]
        probs_own, att_own, middle, second_own = call(
            attend_own, layer, 1, ["proj"], [proj_own, part, state], [v["pb"], v["mg"], v["ms"]], att_outs + [f32_rows, low_rows], att_flops
        )
        second_oth = plan.core(second_own)
        hid_oth, slope_oth = call(up_body, layer, 0, ["fc1"], [second_oth], [v["f1b_c"]], [ff_rows] * 2, ff_flops)
        part = call(down_other, layer, 0, ["fc2"], [hid_oth], [], [f32_rows], ff_flops)[0]
        part = plan.core(part)
        hid_own, slope_own = call(up_body, layer, 1, ["fc1"], [second_own], [v["f1b_c"]], [ff_rows] * 2, ff_flops)
        saved.append(
            dict(
                state=state,
                first=(first_own, first_oth),
                proj=(proj_own, proj_oth),
                probs=(probs_own, probs_oth),
                att=(att_own, att_oth),
                middle=middle,
                second=(second_own, second_oth),
                hid=(hid_own, hid_oth),
                slope=(slope_own, slope_oth),
            )
        )
        if layer + 1 < layers:
            w = vecs[layer + 1]
            state, first_own = call(
                down_own, layer, 1, ["fc2"], [hid_own, part, middle], [v["f2b"], w["ag"], w["as"]], [f32_rows, low_rows], ff_flops
            )
        else:
            mixed = call(down_last, layer, 1, ["fc2"], [hid_own, part, middle], [v["f2b"]], [low_rows], ff_flops)[0]

    axes = list(range(plan.bits + 1)) if plan.ny == 2 else list(range(1, plan.bits + 1))
    x_axis = plan.bits
    z_axes = list(range(plan.bits - 1, 0, -1))
    y_axes = [0] if plan.ny == 2 else []
    order_y = y_axes + [x_axis] + z_axes
    order_x = [x_axis] + z_axes + y_axes
    order_z = z_axes[:1] + y_axes + [x_axis] + z_axes[1:]
    big = [None] * layers
    sums = [None] * layers
    f2b_sum = jnp.sum(low_own.astype(F32), axis=0, keepdims=True)
    mlp_flops = 4 * rows * width * half_ff
    back_flops = 12 * rows * slots * half_width + 2 * rows * width * (wide + half_width)
    for layer in reversed(range(layers)):
        v, s = vecs[layer], saved[layer]
        res2 = weight_grad(plan, where, s["hid"], (low_own, low_oth), 2, order_y[0], False)
        pre_oth, part = call(
            mlp_back_other, layer, 0, ["fc2", "fc1"], [low_oth, s["slope"][1]], [], [ff_rows, f32_rows], mlp_flops
        )
        part = plan.core(part)
        pre_own, mid_grad, branch_own, sum1 = call(
            mlp_back_own,
            layer,
            1,
            ["fc2", "fc1"],
            [low_own, s["slope"][0], part, s["middle"], grad],
            [v["mg"]],
            [ff_rows, f32_rows, low_rows, full_sums],
            mlp_flops,
        )
        branch_oth = plan.core(branch_own)
        res1 = weight_grad(plan, where, s["second"], (pre_own, pre_oth), 1, order_x[0], True)
        dproj_oth, part = call(
            attend_back_other,
            layer,
            0,
            ["proj", "qkv"],
            [branch_oth, s["proj"][1], s["probs"][1]],
            [],
            [wide_rows, f32_rows],
            back_flops,
        )
        part = plan.core(part)
        if n == HEADS:
            resp = weight_grad(plan, where, s["att"], (branch_own, branch_oth), 1, order_y[0], False)
            proj_part = sum_over(plan, *resp, order_y).astype(BF)
            proj_grad = join_rep(plan, proj_part, y).reshape(deep, width)
        else:
            term = t_dot(s["att"][0], branch_own) + t_dot(s["att"][1], branch_oth)
            term = term.astype(BF).reshape(half_heads, HEAD_DIM, width)
            none = jnp.zeros_like(term)
            term = jnp.stack([pick(c, term, none), pick(c, none, term)], axis=1).reshape(width, width)
            term = lax.psum_scatter(term, "shard", scatter_dimension=0, tiled=True)
            proj_grad = lax.psum(term, "rep").astype(F32)
        dproj_own, grad, low_own, sum2 = call(
            attend_back_own,
            layer,
            1,
            ["proj", "qkv"],
            [branch_own, s["proj"][0], s["probs"][0], part, s["state"], mid_grad],
            [v["ag"]],
            [wide_rows, f32_rows, low_rows, full_sums],
            back_flops,
        )
        if layer:
            low_oth = plan.core(low_own)
        resq = weight_grad(plan, where, s["first"], (dproj_own, dproj_oth), 1, order_z[0], True)

        fc2_part = join_rep(plan, join_core(plan, sum_over(plan, *res2, order_y), c, 2), y)
        fc2_grad = fc2_part.reshape(quarters * deep, width)
        fc1_part = join_rep(plan, join_core(plan, sum_over(plan, *res1[:2], order_x), c, 1), y)
        fc1_grad = fc1_part.reshape(2, deep, half_ff).swapaxes(0, 1)
        fc1_grad = fc1_grad.reshape(deep, quarters, n, deep).swapaxes(1, 2).reshape(deep, ff)
        qkv_part = join_rep(plan, join_core(plan, sum_over(plan, *resq[:2], order_z), c, 1), y)
        qkv_grad = qkv_part.reshape(2, deep, 3 * half_heads, HEAD_DIM).transpose(1, 2, 0, 3).reshape(deep, 3 * width)
        big[layer] = (qkv_grad, proj_grad, fc1_grad, fc2_grad)

        q = resq[2].reshape(3, half_heads, 1, HEAD_DIM)
        q = jnp.concatenate([q[:1], q[2:]])
        none = jnp.zeros_like(q)
        q = jnp.concatenate([pick(c, q, none), pick(c, none, q)], axis=2)
        f = res1[2]
        none = jnp.zeros_like(f)
        f = jnp.concatenate([pick(c, f, none), pick(c, none, f)], axis=0)
        f = f.reshape(quarters, n, deep).swapaxes(0, 1)
        full = {"ag": sum2[0], "as": sum2[1], "qvb": q, "pb": sum1[2], "mg": sum1[0], "ms": sum1[1], "f1b": f, "f2b": f2b_sum}
        f2b_sum = sum2[2]
        vec = jnp.concatenate([full[name].reshape(n, -1) for name in SMALL], axis=1)
        vec = vec + plan.core(vec)
        for axis in axes:
            vec = vec + plan.flip(vec, axis)
        if plan.ny == 1:
            vec = lax.psum(vec, "rep")
        sums[layer] = lax.dynamic_slice_in_dim(vec, shard, 1, axis=0)

    vec = jnp.concatenate(sums, axis=0)
    out, at = {}, 0
    for name, size in zip(SMALL, sizes):
        out[name] = vec[:, at : at + size]
        at += size
    qkv_g, proj_g, fc1_g, fc2_g = (jnp.stack([big[layer][k] for layer in range(layers)]) for k in range(4))
    return (
        mixed.reshape(images, slots, width),
        grad.reshape(images, slots, width),
        out["ag"],
        out["as"],
        qkv_g,
        out["qvb"],
        proj_g,
        out["pb"],
        out["mg"],
        out["ms"],
        fc1_g,
        out["f1b"],
        fc2_g,
        out["f2b"],
    )


def solution(mesh):
    rows = P(("shard", "rep"), None, None)
    vec = P(None, "shard")
    mat = P(None, "shard", None)
    return jax.shard_map(
        partial(per_device, Plan(mesh)),
        mesh=mesh,
        in_specs=(rows, P(("shard", "rep")), vec, vec, mat, vec, mat, vec, vec, vec, mat, vec, mat, vec, rows),
        out_specs=(rows, rows, vec, vec, mat, vec, mat, vec, vec, vec, mat, vec, mat, vec),
        check_vma=False,
    )
```

time: 1500 us -> 990 us (0.66)
  matrix products: 369 us -> 0 us
  Pallas kernels: 0 us -> 360 us
  waiting for transfers between devices: 666 us -> 412 us
  blocking collectives: 203 us -> 0 us
  local copies, waits for them, and re-layouts: 150 us -> 84.3 us
  starting transfers between devices: 0.69 us -> 64 us
  other arithmetic: 82.6 us -> 45.9 us
    reduce_scatter x8 -> x0, waiting for transfers between devices: 463 us -> none  [the longest x2 217 us: per_device(): lax.psum_scatter(grads[10].astype(jnp.bfloat16), 'shard', scatter_dimensi...]
    dot_general x36 -> x0, matrix products: 369 us -> none  [the longest x2 67.6 us: layer_forward(): jnp.dot(second_low, fc1_weight, preferred_element_type=jnp.float32)]
    pallas_call x0 -> x32, Pallas kernels: none -> 360 us  [the longest x24 272 us: row_call(): pl.pallas_call(kernel, grid_spec=pltpu.PrefetchScalarGridSpec(num_scalar_...]
    ppermute x0 -> x73, waiting for transfers between devices: none -> 242 us  [swap(): return lax.ppermute(v, AX, pairs)]
    unnamed x2 -> x0, blocking collectives: 125 us -> none
    psum x1 -> x0, waiting for transfers between devices: 72.9 us -> none  [per_device(): lax.psum(shares[2].astype(jnp.bfloat16), 'rep').astype(jnp.float32)]
    all_gather x4 -> x0, blocking collectives: 72.7 us -> none  [the longest x2 36.7 us: per_device(): lax.all_gather(fc1_bias[layer], 'shard', axis=0, tiled=True)]
    ppermute x0 -> x73, starting transfers between devices: none -> 63.9 us  [swap(): return lax.ppermute(v, AX, pairs)]
  transfers between devices with their start and end apart: 17 -> 75, of which waited for: 9 -> 32; matrix products, arithmetic and copies ran while one was open for 31% -> 10% of each run, Pallas kernels for 0% -> 32%
where the time goes in v1:
time: 990 us; the launch traced here: 982 us
  waiting for transfers between devices  412 us (42%)
  Pallas kernels  360 us (36%)
  local copies, waits for them, and re-layouts  84.3 us (9%)
  starting transfers between devices  64 us (6%)
  other arithmetic  45.9 us (5%)
  between operations  16 us (2%)
    pallas_call x24, Pallas kernels, row_call(): pl.pallas_call(kernel, grid_spec=pltpu.PrefetchScalarGridSpec(num_scalar_...  272 us
    ppermute x73, waiting for transfers between devices, swap(): return lax.ppermute(v, AX, pairs)  242 us
    all_gather x2, waiting for transfers between devices, per_device(): lax.all_gather(jnp.concatenate(merged(layer), axis=1), 'shard', axis=0, t...  169 us
    pallas_call x8, Pallas kernels, weight_grad(): pl.pallas_call(kernel, grid_spec=pltpu.PrefetchScalarGridSpec(num_scalar_...  88 us
    ppermute x73, starting transfers between devices, swap(): return lax.ppermute(v, AX, pairs)  63.9 us
    another operation x24, other arithmetic  22.7 us
    unnamed x100, local copies, waits for them, and re-layouts  21 us
  transfers between devices with their start and end apart: 75, of which 32 were waited for; matrix products, arithmetic and copies ran while one was open for 10% of the time, Pallas kernels for 32%

profile of v1, /device:TPU:0, one launch (start us, length us, event | category | flops | bytes accessed | tf_op | source)
XLA Modules:
  0.0 981.9 jit_solution(17900246790381460183)
XLA Ops:
  27.3 131.0 %all-gather.5.cloned.1.call-done.refs_0_.refs_1_ = bf16[1024,12416]{1,0:T(8,128)(2,1)} async-done(((bf16[64,12416]{1,0:T(8,128)(2,1)}), bf16[1024,12416]{1,0:T(8,128)(2,1)}) %all-gather.5.cloned.1.call-update) | async-done | bytes 25427984 | tf_op jit(solution)/shard_map/all_gather | solution.py:460
  192.4 13.4 %shard_map.257 = (bf16[2,8,320,320]{3,2,1,0:T(8,128)(2,1)}, bf16[640,512]{1,0:T(8,128)(2,1)}, f32[640,1024]{1,0:T(8,128)}, bf16[640,1024]{1,0:T(8,128)(2,1)}) custom-call(s32[3]{0:T(128)} %pad_add_fusion.where_ref, s32[2]{0:T(128)} %kept_ref.23, bf16[8,2,64,12416]{3,2,1,0:T(8,128)(2,1)} %bitcast.248, bf16[640,1536]{1,0:T(8,128)(2,1)} %shard_map.254.refs_1_.refs_3_, ...), custom_call_target="tpu_custom_call" | custom-call | flops 1090519040 | bytes 7221248 | tf_op jit(solution)/shard_map/pallas_call | solution.py:97
  250.7 38.4 %all-gather.3.cloned.1.call-done.refs_0_.refs_1_ = bf16[1024,12288]{1,0:T(8,128)(2,1)} async-done(((bf16[64,12288]{1,0:T(8,128)(2,1)}), bf16[1024,12288]{1,0:T(8,128)(2,1)}) %all-gather.3.cloned.1.call-update) | async-done | bytes 25165840 | tf_op jit(solution)/shard_map/all_gather | solution.py:460
  296.3 11.9 %shard_map.264 = (bf16[2,8,320,320]{3,2,1,0:T(8,128)(2,1)}, bf16[640,512]{1,0:T(8,128)(2,1)}, f32[640,1024]{1,0:T(8,128)}) custom-call(s32[3]{0:T(128)} %pad_add_fusion.where_ref, s32[2]{0:T(128)} %copy-done.24, bf16[8,2,64,12288]{3,2,1,0:T(8,128)(2,1)} %bitcast.251, bf16[640,1536]{1,0:T(8,128)(2,1)} %shard_map.263.refs_1_.refs_3_), custom_call_target="tpu_custom_call" | custom-call | flops 1090519040 | bytes 1966080 | tf_op jit(solution)/shard_map/pallas_call | solution.py:97
  317.2 13.6 %shard_map.265 = (bf16[2,8,320,320]{3,2,1,0:T(8,128)(2,1)}, bf16[640,512]{1,0:T(8,128)(2,1)}, f32[640,1024]{1,0:T(8,128)}, bf16[640,1024]{1,0:T(8,128)(2,1)}) custom-call(s32[3]{0:T(128)} %pad_add_fusion.where_ref, s32[2]{0:T(128)} %kept_ref.23, bf16[8,2,64,12288]{3,2,1,0:T(8,128)(2,1)} %bitcast.252, bf16[640,1536]{1,0:T(8,128)(2,1)} %shard_map.262.refs_1_.refs_3_, ...), custom_call_target="tpu_custom_call" | custom-call | flops 1090519040 | bytes 7221248 | tf_op jit(solution)/shard_map/pallas_call | solution.py:97
  365.3 14.6 %shard_map.285 = (bf16[1,2,2,2,256,512]{5,4,3,2,1,0:T(8,128)(2,1)}, bf16[1,2,2,2,256,512]{5,4,3,2,1,0:T(8,128)(2,1)}) custom-call(s32[3]{0:T(128)} %pad_add_fusion.where_ref, bf16[640,2048]{1,0:T(8,128)(2,1)} %get-tuple-element.90.refs_1_.xo, bf16[640,2048]{1,0:T(8,128)(2,1)} %get-tuple-element.91.refs_1_.xt, ...), custom_call_target="tpu_custom_call" | custom-call | flops 5368709120 | bytes 12058624 | tf_op jit(solution)/shard_map/pallas_call | solution.py:368
  388.9 39.1 %collective-permute-done.67 = bf16[1,2,2,2,256,512]{5,4,3,2,1,0:T(8,128)(2,1)S(1)} collective-permute-done((bf16[1,2,2,2,256,512]{5,4,3,2,1,0:T(8,128)(2,1)}, bf16[1,2,2,2,256,512]{5,4,3,2,1,0:T(8,128)(2,1)S(1)}, u32[]{:S(2)}, u32[]{:S(2)}) %collective-permute-start.67) | collective-permute-done | bytes 2097184 | tf_op jit(solution)/shard_map/ppermute | solution.py:35
  432.3 15.8 %shard_map.271 = (bf16[640,2048]{1,0:T(8,128)(2,1)}, f32[640,1024]{1,0:T(8,128)}, bf16[640,1024]{1,0:T(8,128)(2,1)}, f32[8,1024]{1,0:T(8,128)}) custom-call(s32[3]{0:T(128)} %pad_add_fusion.where_ref, s32[2]{0:T(128)} %kept_ref.23, bf16[1024,12288]{1,0:T(8,128)(2,1)} %all-gather.3.cloned.1.call-done.refs_0_.refs_1_, ...), custom_call_target="tpu_custom_call" | custom-call | flops 5368709120 | bytes 11800576 | tf_op jit(solution)/shard_map/pallas_call | solution.py:97
  448.2 12.6 %shard_map.281 = (bf16[2,2,2,1,128,1024]{5,4,3,2,1,0:T(8,128)(2,1)}, bf16[2,2,2,1,128,1024]{5,4,3,2,1,0:T(8,128)(2,1)}, f32[1,2048]{1,0:T(1,128)}) custom-call(s32[3]{0:T(128)} %pad_add_fusion.where_ref, bf16[640,1024]{1,0:T(8,128)(2,1)} %get-tuple-element.89.refs_1_.xo, bf16[640,1024]{1,0:T(8,128)(2,1)} %collective-permute-done.7.refs_1_.xt, ...), custom_call_target="tpu_custom_call" | custom-call | flops 5368709120 | bytes 12058624 | tf_op jit(solution)/shard_map/pallas_call | solution.py:368
  481.1 16.1 %shard_map.272 = (bf16[640,1536]{1,0:T(8,128)(2,1)}, f32[640,1024]{1,0:T(8,128)}) custom-call(s32[3]{0:T(128)} %pad_add_fusion.where_ref, s32[2]{0:T(128)} %copy-done.24, bf16[8,2,64,12288]{3,2,1,0:T(8,128)(2,1)} %bitcast.253, bf16[1024,12288]{1,0:T(8,128)(2,1)} %all-gather.3.cloned.1.call-done.refs_0_.refs_1_, bf16[640,1024]{1,0:T(8,128)(2,1)} %copy-done.18, ...), custom_call_target="tpu_custom_call" | custom-call | flops 3942645760 | bytes 6553600 | tf_op jit(solution)/shard_map/pallas_call | solution.py:97
  532.4 17.3 %collective-permute-done.46 = bf16[1,2,1,1,64,512]{5,4,3,2,1,0:T(8,128)(2,1)S(1)} collective-permute-done((bf16[1,2,1,1,64,512]{5,4,3,2,1,0:T(8,128)(2,1)S(1)}, bf16[1,2,1,1,64,512]{5,4,3,2,1,0:T(8,128)(2,1)S(1)}, u32[]{:S(2)}, u32[]{:S(2)}) %collective-permute-start.46) | collective-permute-done | bytes 131104 | tf_op jit(solution)/shard_map/ppermute | solution.py:35
  555.2 19.2 %shard_map.273 = (bf16[640,1536]{1,0:T(8,128)(2,1)}, f32[640,1024]{1,0:T(8,128)}, bf16[640,1024]{1,0:T(8,128)(2,1)}, f32[8,1024]{1,0:T(8,128)}) custom-call(s32[3]{0:T(128)} %pad_add_fusion.where_ref, s32[2]{0:T(128)} %kept_ref.23, bf16[8,2,64,12288]{3,2,1,0:T(8,128)(2,1)} %bitcast.254, bf16[1024,12288]{1,0:T(8,128)(2,1)} %all-gather.3.cloned.1.call-done.refs_0_.refs_1_, ...), custom_call_target="tpu_custom_call" | custom-call | flops 3942645760 | bytes 14422016 | tf_op jit(solution)/shard_map/pallas_call | solution.py:97
  597.4 22.3 %collective-permute-done.33 = bf16[2,2,1,2,128,768]{5,4,3,2,1,0:T(8,128)(2,1)S(1)} collective-permute-done((bf16[2,2,1,2,128,768]{5,4,3,2,1,0:T(8,128)(2,1)}, bf16[2,2,1,2,128,768]{5,4,3,2,1,0:T(8,128)(2,1)S(1)}, u32[]{:S(2)}, u32[]{:S(2)}) %collective-permute-start.33) | collective-permute-done | bytes 1572896 | tf_op jit(solution)/shard_map/ppermute | solution.py:35
  627.9 14.0 %collective-permute-done.23 = f32[16,768]{1,0:T(8,128)S(1)} collective-permute-done((f32[16,768]{1,0:T(8,128)S(1)}, f32[16,768]{1,0:T(8,128)S(1)}, u32[]{:S(2)}, u32[]{:S(2)}) %collective-permute-start.23) | collective-permute-done | bytes 49184 | tf_op jit(solution)/shard_map/ppermute | solution.py:35
  643.6 14.6 %shard_map.284 = (bf16[1,2,2,2,256,512]{5,4,3,2,1,0:T(8,128)(2,1)}, bf16[1,2,2,2,256,512]{5,4,3,2,1,0:T(8,128)(2,1)}) custom-call(s32[3]{0:T(128)} %pad_add_fusion.where_ref, bf16[640,2048]{1,0:T(8,128)(2,1)} %get-tuple-element.83.refs_1_.xo, bf16[640,2048]{1,0:T(8,128)(2,1)} %get-tuple-element.84.refs_1_.xt, ...), custom_call_target="tpu_custom_call" | custom-call | flops 5368709120 | bytes 12058624 | tf_op jit(solution)/shard_map/pallas_call | solution.py:368
  688.7 18.0 %collective-permute-done.61 = bf16[1,2,2,2,256,512]{5,4,3,2,1,0:T(8,128)(2,1)S(1)} collective-permute-done((bf16[1,2,2,2,256,512]{5,4,3,2,1,0:T(8,128)(2,1)}, bf16[1,2,2,2,256,512]{5,4,3,2,1,0:T(8,128)(2,1)S(1)}, u32[]{:S(2)}, u32[]{:S(2)}) %collective-permute-start.61) | collective-permute-done | bytes 2097184 | tf_op jit(solution)/shard_map/ppermute | solution.py:35
  731.5 15.0 %shard_map.275 = (bf16[640,2048]{1,0:T(8,128)(2,1)}, f32[640,1024]{1,0:T(8,128)}, bf16[640,1024]{1,0:T(8,128)(2,1)}, f32[8,1024]{1,0:T(8,128)}) custom-call(s32[3]{0:T(128)} %pad_add_fusion.where_ref, s32[2]{0:T(128)} %kept_ref.23, bf16[1024,12416]{1,0:T(8,128)(2,1)} %all-gather.5.cloned.1.call-done.refs_0_.refs_1_, ...), custom_call_target="tpu_custom_call" | custom-call | flops 5368709120 | bytes 11800576 | tf_op jit(solution)/shard_map/pallas_call | solution.py:97
  746.6 12.6 %shard_map.279 = (bf16[2,2,2,1,128,1024]{5,4,3,2,1,0:T(8,128)(2,1)}, bf16[2,2,2,1,128,1024]{5,4,3,2,1,0:T(8,128)(2,1)}, f32[1,2048]{1,0:T(1,128)}) custom-call(s32[3]{0:T(128)} %pad_add_fusion.where_ref, bf16[640,1024]{1,0:T(8,128)(2,1)} %get-tuple-element.82.refs_1_.xo, bf16[640,1024]{1,0:T(8,128)(2,1)} %copy-done.13, ...), custom_call_target="tpu_custom_call" | custom-call | flops 5368709120 | bytes 12058624 | tf_op jit(solution)/shard_map/pallas_call | solution.py:368
  762.6 12.0 %collective-permute-done.64 = bf16[1,1,1,1,256,512]{5,4,3,2,1,0:T(8,128)(2,1)S(1)} collective-permute-done((bf16[1,1,1,1,256,512]{5,4,3,2,1,0:T(8,128)(2,1)S(1)}, bf16[1,1,1,1,256,512]{5,4,3,2,1,0:T(8,128)(2,1)S(1)}, u32[]{:S(2)}, u32[]{:S(2)}) %collective-permute-start.64) | collective-permute-done | bytes 262176 | tf_op jit(solution)/shard_map/ppermute | solution.py:35
  776.0 16.3 %shard_map.276 = (bf16[640,1536]{1,0:T(8,128)(2,1)}, f32[640,1024]{1,0:T(8,128)}) custom-call(s32[3]{0:T(128)} %pad_add_fusion.where_ref, s32[2]{0:T(128)} %copy-done.24, bf16[8,2,64,12416]{3,2,1,0:T(8,128)(2,1)} %bitcast.249, bf16[1024,12416]{1,0:T(8,128)(2,1)} %all-gather.5.cloned.1.call-done.refs_0_.refs_1_, bf16[640,1024]{1,0:T(8,128)(2,1)} %copy-done.19, ...), custom_call_target="tpu_custom_call" | custom-call | flops 3942645760 | bytes 6553600 | tf_op jit(solution)/shard_map/pallas_call | solution.py:97
  801.3 12.2 %collective-permute-done.39 = bf16[1,2,2,2,64,512]{5,4,3,2,1,0:T(8,128)(2,1)S(1)} collective-permute-done((bf16[1,2,2,2,64,512]{5,4,3,2,1,0:T(8,128)(2,1)}, bf16[1,2,2,2,64,512]{5,4,3,2,1,0:T(8,128)(2,1)S(1)}, u32[]{:S(2)}, u32[]{:S(2)}) %collective-permute-start.39) | collective-permute-done | bytes 524320 | tf_op jit(solution)/shard_map/ppermute | solution.py:35
  834.9 17.6 %collective-permute-done.42 = bf16[1,1,1,1,64,512]{5,4,3,2,1,0:T(8,128)(2,1)S(1)} collective-permute-done((bf16[1,1,1,1,64,512]{5,4,3,2,1,0:T(8,128)(2,1)S(1)}, bf16[1,1,1,1,64,512]{5,4,3,2,1,0:T(8,128)(2,1)S(1)}, u32[]{:S(2)}, u32[]{:S(2)}) %collective-permute-start.42) | collective-permute-done | bytes 65568 | tf_op jit(solution)/shard_map/ppermute | solution.py:35
  862.3 19.3 %shard_map.277 = (bf16[640,1536]{1,0:T(8,128)(2,1)}, f32[640,1024]{1,0:T(8,128)}, bf16[640,1024]{1,0:T(8,128)(2,1)}, f32[8,1024]{1,0:T(8,128)}) custom-call(s32[3]{0:T(128)} %pad_add_fusion.where_ref, s32[2]{0:T(128)} %kept_ref.23, bf16[8,2,64,12416]{3,2,1,0:T(8,128)(2,1)} %bitcast.250, bf16[1024,12416]{1,0:T(8,128)(2,1)} %all-gather.5.cloned.1.call-done.refs_0_.refs_1_, ...), custom_call_target="tpu_custom_call" | custom-call | flops 3942645760 | bytes 14422016 | tf_op jit(solution)/shard_map/pallas_call | solution.py:97
  907.5 18.1 %collective-permute-done.27 = bf16[2,2,1,2,128,768]{5,4,3,2,1,0:T(8,128)(2,1)} collective-permute-done((bf16[2,2,1,2,128,768]{5,4,3,2,1,0:T(8,128)(2,1)}, bf16[2,2,1,2,128,768]{5,4,3,2,1,0:T(8,128)(2,1)}, u32[]{:S(2)}, u32[]{:S(2)}) %collective-permute-start.27) | collective-permute-done | bytes 1572896 | tf_op jit(solution)/shard_map/ppermute | solution.py:35
  (515 shorter events, 430.8 us)
Async XLA Ops:
  7.2 151.1 %all-gather.5.cloned.1.call-start = ((), (), s32[]{:S(2)}) async-start(), calls=%async_computation.1 | async-start | bytes 27017216 | tf_op jit(solution)/shard_map/all_gather | solution.py:460
  25.6 263.5 %all-gather.3.cloned.1.call-start = ((), (), s32[]{:S(2)}) async-start(), calls=%async_computation | async-start | bytes 26738688 | tf_op jit(solution)/shard_map/all_gather | solution.py:460
  250.0 39.1 %collective-permute-start.5 = (bf16[640,1024]{1,0:T(8,128)(2,1)}, bf16[640,1024]{1,0:T(8,128)(2,1)S(1)}, u32[]{:S(2)}, u32[]{:S(2)}) collective-permute-start(bf16[640,1024]{1,0:T(8,128)(2,1)} %get-tuple-element.86.refs_1_.xo), channel_id=1, source_target_pairs={{0,2},{1,3},{2,0},{3,1},{4,6},{5,7},{6,4},{7,5},{8,10},{9,11},{10,... | collective-permute-start | bytes 3932168 | tf_op jit(solution)/shard_map/ppermute | solution.py:35
  365.1 67.2 %collective-permute-start.10 = (f32[640,1024]{1,0:T(8,128)}, f32[640,1024]{1,0:T(8,128)}, u32[]{:S(2)}, u32[]{:S(2)}) collective-permute-start(f32[640,1024]{1,0:T(8,128)} %get-tuple-element.95), channel_id=1, source_target_pairs={{0,2},{1,3},{2,0},{3,1},{4,6},{5,7},{6,4},{7,5},{8,10},{9,11},{10,... | collective-permute-start | bytes 7864328 | tf_op jit(solution)/shard_map/ppermute | solution.py:35
  380.0 48.0 %collective-permute-start.67 = (bf16[1,2,2,2,256,512]{5,4,3,2,1,0:T(8,128)(2,1)}, bf16[1,2,2,2,256,512]{5,4,3,2,1,0:T(8,128)(2,1)S(1)}, u32[]{:S(2)}, u32[]{:S(2)}) collective-permute-start(bf16[1,2,2,2,256,512]{5,4,3,2,1,0:T(8,128)(2,1)} %get-tuple-element.147), channel_id=1, source_target_pairs={{0,1},{1,0},{2,3},{3,2},{4,5},{5,4},{6,7},{7,6},{8,9},{9,8},{10,11... | collective-permute-start | bytes 6291464 | tf_op jit(solution)/shard_map/ppermute | solution.py:35
  388.9 76.0 %collective-permute-start.8 = (f32[640,1024]{1,0:T(8,128)}, f32[640,1024]{1,0:T(8,128)}, u32[]{:S(2)}, u32[]{:S(2)}) collective-permute-start(f32[640,1024]{1,0:T(8,128)} %shard_map.268), channel_id=1, source_target_pairs={{0,2},{1,3},{2,0},{3,1},{4,6},{5,7},{6,4},{7,5},{8,10},{9,11},{10,... | collective-permute-start | bytes 7864328 | tf_op jit(solution)/shard_map/ppermute | solution.py:35
  429.7 32.0 %collective-permute-start.68 = (bf16[1,2,2,1,256,512]{5,4,3,2,1,0:T(8,128)(2,1)}, bf16[1,2,2,1,256,512]{5,4,3,2,1,0:T(8,128)(2,1)}, u32[]{:S(2)}, u32[]{:S(2)}) collective-permute-start(bf16[1,2,2,1,256,512]{5,4,3,2,1,0:T(8,128)(2,1)} %slice.688), channel_id=1, source_target_pairs={{0,4},{1,5},{2,6},{3,7},{4,0},{5,1},{6,2},{7,3},{8,12},{9,13},{10,... | collective-permute-start | bytes 3145736 | tf_op jit(solution)/shard_map/ppermute | solution.py:35
  448.1 31.9 %collective-permute-start.11 = (bf16[640,1024]{1,0:T(8,128)(2,1)}, bf16[640,1024]{1,0:T(8,128)(2,1)S(1)}, u32[]{:S(2)}, u32[]{:S(2)}) collective-permute-start(bf16[640,1024]{1,0:T(8,128)(2,1)} %get-tuple-element.96.refs_2_.yo), channel_id=1, source_target_pairs={{0,2},{1,3},{2,0},{3,1},{4,6},{5,7},{6,4},{7,5},{8,10},{9,11},{10,... | collective-permute-start | bytes 3932168 | tf_op jit(solution)/shard_map/ppermute | solution.py:35
  460.9 59.3 %collective-permute-start.55 = (bf16[2,2,2,1,128,1024]{5,4,3,2,1,0:T(8,128)(2,1)}, bf16[2,2,2,1,128,1024]{5,4,3,2,1,0:T(8,128)(2,1)S(1)}, u32[]{:S(2)}, u32[]{:S(2)}) collective-permute-start(bf16[2,2,2,1,128,1024]{5,4,3,2,1,0:T(8,128)(2,1)} %get-tuple-element.143), channel_id=1, source_target_pairs={{0,4},{1,5},{2,6},{3,7},{4,0},{5,1},{6,2},{7,3},{8,12},{9,13},{10,... | collective-permute-start | bytes 6291464 | tf_op jit(solution)/shard_map/ppermute | solution.py:35
  497.2 58.0 %collective-permute-start.12 = (f32[640,1024]{1,0:T(8,128)}, f32[640,1024]{1,0:T(8,128)}, u32[]{:S(2)}, u32[]{:S(2)}) collective-permute-start(f32[640,1024]{1,0:T(8,128)} %get-tuple-element.99), channel_id=1, source_target_pairs={{0,2},{1,3},{2,0},{3,1},{4,6},{5,7},{6,4},{7,5},{8,10},{9,11},{10,... | collective-permute-start | bytes 7864328 | tf_op jit(solution)/shard_map/ppermute | solution.py:35
  549.7 36.1 %collective-permute-start.47 = (bf16[1,1,1,1,64,512]{5,4,3,2,1,0:T(8,128)(2,1)S(1)}, bf16[1,1,1,1,64,512]{5,4,3,2,1,0:T(8,128)(2,1)S(1)}, u32[]{:S(2)}, u32[]{:S(2)}) collective-permute-start(bf16[1,1,1,1,64,512]{5,4,3,2,1,0:T(8,128)(2,1)S(1)} %slice.654), channel_id=1, source_target_pairs={{0,16},{1,17},{2,18},{3,19},{4,20},{5,21},{6,22},{7,23},{8,24},{9,... | collective-permute-start | bytes 196616 | tf_op jit(solution)/shard_map/ppermute | solution.py:35
  552.8 38.4 %collective-permute-start.57 = (bf16[2,1,1,1,128,1024]{5,4,3,2,1,0:T(8,128)(2,1)}, bf16[2,1,1,1,128,1024]{5,4,3,2,1,0:T(8,128)(2,1)}, u32[]{:S(2)}, u32[]{:S(2)}) collective-permute-start(bf16[2,1,1,1,128,1024]{5,4,3,2,1,0:T(8,128)(2,1)} %slice.672), channel_id=1, source_target_pairs={{0,16},{1,17},{2,18},{3,19},{4,20},{5,21},{6,22},{7,23},{8,24},{9,... | collective-permute-start | bytes 1572872 | tf_op jit(solution)/shard_map/ppermute | solution.py:35
  585.0 34.6 %collective-permute-start.33 = (bf16[2,2,1,2,128,768]{5,4,3,2,1,0:T(8,128)(2,1)}, bf16[2,2,1,2,128,768]{5,4,3,2,1,0:T(8,128)(2,1)S(1)}, u32[]{:S(2)}, u32[]{:S(2)}) collective-permute-start(bf16[2,2,1,2,128,768]{5,4,3,2,1,0:T(8,128)(2,1)} %get-tuple-element.131), channel_id=1, source_target_pairs={{0,8},{1,9},{2,10},{3,11},{4,12},{5,13},{6,14},{7,15},{8,0},{9,1},... | collective-permute-start | bytes 4718600 | tf_op jit(solution)/shard_map/ppermute | solution.py:35
  593.9 31.7 %collective-permute-start.58 = (bf16[1,1,1,1,128,1024]{5,4,3,2,1,0:T(8,128)(2,1)}, bf16[1,1,1,1,128,1024]{5,4,3,2,1,0:T(8,128)(2,1)}, u32[]{:S(2)}, u32[]{:S(2)}) collective-permute-start(bf16[1,1,1,1,128,1024]{5,4,3,2,1,0:T(8,128)(2,1)} %slice.674), channel_id=1, source_target_pairs={{0,1},{1,0},{2,3},{3,2},{4,5},{5,4},{6,7},{7,6},{8,9},{9,8},{10,11... | collective-permute-start | bytes 786440 | tf_op jit(solution)/shard_map/ppermute | solution.py:35
  595.4 47.2 %collective-permute-start.13 = (bf16[640,1024]{1,0:T(8,128)(2,1)}, bf16[640,1024]{1,0:T(8,128)(2,1)S(1)}, u32[]{:S(2)}, u32[]{:S(2)}) collective-permute-start(bf16[640,1024]{1,0:T(8,128)(2,1)} %get-tuple-element.101.refs_2_.yo), channel_id=1, source_target_pairs={{0,2},{1,3},{2,0},{3,1},{4,6},{5,7},{6,4},{7,5},{8,10},{9,11},{10,... | collective-permute-start | bytes 3932168 | tf_op jit(solution)/shard_map/ppermute | solution.py:35
  596.8 29.8 %collective-permute-start.22 = (f32[16,768]{1,0:T(8,128)S(1)}, f32[16,768]{1,0:T(8,128)S(1)}, u32[]{:S(2)}, u32[]{:S(2)}) collective-permute-start(f32[16,768]{1,0:T(8,128)S(1)} %concatenate.98), channel_id=1, source_target_pairs={{0,2},{1,3},{2,0},{3,1},{4,6},{5,7},{6,4},{7,5},{8,10},{9,11},{10,... | collective-permute-start | bytes 147464 | tf_op jit(solution)/shard_map/ppermute | solution.py:35
  624.1 35.6 %collective-permute-start.34 = (bf16[1,2,1,2,128,768]{5,4,3,2,1,0:T(8,128)(2,1)}, bf16[1,2,1,2,128,768]{5,4,3,2,1,0:T(8,128)(2,1)}, u32[]{:S(2)}, u32[]{:S(2)}) collective-permute-start(bf16[1,2,1,2,128,768]{5,4,3,2,1,0:T(8,128)(2,1)} %slice.634), channel_id=1, source_target_pairs={{0,1},{1,0},{2,3},{3,2},{4,5},{5,4},{6,7},{7,6},{8,9},{9,8},{10,11... | collective-permute-start | bytes 2359304 | tf_op jit(solution)/shard_map/ppermute | solution.py:35
  627.9 34.1 %collective-permute-start.59 = (bf16[1,64,1024]{2,1,0:T(8,128)(2,1)S(1)}, bf16[1,64,1024]{2,1,0:T(8,128)(2,1)S(1)}, u32[]{:S(2)}, u32[]{:S(2)}) collective-permute-start(bf16[1,64,1024]{2,1,0:T(8,128)(2,1)S(1)} %fusion.7), channel_id=1, source_target_pairs={{0,2},{1,3},{2,0},{3,1},{4,6},{5,7},{6,4},{7,5},{8,10},{9,11},{10,... | collective-permute-start | bytes 393224 | tf_op jit(solution)/shard_map/ppermute | solution.py:35
  658.2 48.5 %collective-permute-start.61 = (bf16[1,2,2,2,256,512]{5,4,3,2,1,0:T(8,128)(2,1)}, bf16[1,2,2,2,256,512]{5,4,3,2,1,0:T(8,128)(2,1)S(1)}, u32[]{:S(2)}, u32[]{:S(2)}) collective-permute-start(bf16[1,2,2,2,256,512]{5,4,3,2,1,0:T(8,128)(2,1)} %get-tuple-element.145), channel_id=1, source_target_pairs={{0,1},{1,0},{2,3},{3,2},{4,5},{5,4},{6,7},{7,6},{8,9},{9,8},{10,11... | collective-permute-start | bytes 6291464 | tf_op jit(solution)/shard_map/ppermute | solution.py:35
  683.2 48.2 %collective-permute-start.14 = (f32[640,1024]{1,0:T(8,128)}, f32[640,1024]{1,0:T(8,128)}, u32[]{:S(2)}, u32[]{:S(2)}) collective-permute-start(f32[640,1024]{1,0:T(8,128)} %get-tuple-element.104), channel_id=1, source_target_pairs={{0,2},{1,3},{2,0},{3,1},{4,6},{5,7},{6,4},{7,5},{8,10},{9,11},{10,... | collective-permute-start | bytes 7864328 | tf_op jit(solution)/shard_map/ppermute | solution.py:35
  762.5 61.0 %collective-permute-start.49 = (bf16[2,2,2,1,128,1024]{5,4,3,2,1,0:T(8,128)(2,1)}, bf16[2,2,2,1,128,1024]{5,4,3,2,1,0:T(8,128)(2,1)S(1)}, u32[]{:S(2)}, u32[]{:S(2)}) collective-permute-start(bf16[2,2,2,1,128,1024]{5,4,3,2,1,0:T(8,128)(2,1)} %get-tuple-element.141), channel_id=1, source_target_pairs={{0,4},{1,5},{2,6},{3,7},{4,0},{5,1},{6,2},{7,3},{8,12},{9,13},{10,... | collective-permute-start | bytes 6291464 | tf_op jit(solution)/shard_map/ppermute | solution.py:35
  792.2 70.0 %collective-permute-start.16 = (f32[640,1024]{1,0:T(8,128)}, f32[640,1024]{1,0:T(8,128)}, u32[]{:S(2)}, u32[]{:S(2)}) collective-permute-start(f32[640,1024]{1,0:T(8,128)} %get-tuple-element.109), channel_id=1, source_target_pairs={{0,2},{1,3},{2,0},{3,1},{4,6},{5,7},{6,4},{7,5},{8,10},{9,11},{10,... | collective-permute-start | bytes 7864328 | tf_op jit(solution)/shard_map/ppermute | solution.py:35
  858.8 34.7 %collective-permute-start.51 = (bf16[2,1,1,1,128,1024]{5,4,3,2,1,0:T(8,128)(2,1)S(1)}, bf16[2,1,1,1,128,1024]{5,4,3,2,1,0:T(8,128)(2,1)S(1)}, u32[]{:S(2)}, u32[]{:S(2)}) collective-permute-start(bf16[2,1,1,1,128,1024]{5,4,3,2,1,0:T(8,128)(2,1)S(1)} %slice.664), channel_id=1, source_target_pairs={{0,16},{1,17},{2,18},{3,19},{4,20},{5,21},{6,22},{7,23},{8,24},{9,... | collective-permute-start | bytes 1572872 | tf_op jit(solution)/shard_map/ppermute | solution.py:35
  892.6 33.0 %collective-permute-start.27 = (bf16[2,2,1,2,128,768]{5,4,3,2,1,0:T(8,128)(2,1)}, bf16[2,2,1,2,128,768]{5,4,3,2,1,0:T(8,128)(2,1)}, u32[]{:S(2)}, u32[]{:S(2)}) collective-permute-start(bf16[2,2,1,2,128,768]{5,4,3,2,1,0:T(8,128)(2,1)} %get-tuple-element.129), channel_id=1, source_target_pairs={{0,8},{1,9},{2,10},{3,11},{4,12},{5,13},{6,14},{7,15},{8,0},{9,1},... | collective-permute-start | bytes 4718600 | tf_op jit(solution)/shard_map/ppermute | solution.py:35
  (95 other events, 1107.5 us)
Sparse Core Ops, SparseCore 0:
  25.7 132.5 all-gather.4
  160.4 128.6 all-gather.2

commit v2 on v1

--- a/solution.py
+++ b/solution.py
@@ -15,7 +15,11 @@
 AX = ("shard", "rep")
 BF = jnp.bfloat16
 F32 = jnp.float32
-LIMIT = 56 * 2**20
+LIMIT = 32 * 2**20
+ONCE = pl.Buffered(1)
+ANY = pl.BlockSpec(memory_space=pl.ANY)
+FORWARD = pl.CostEstimate(flops=10**9 * 3, bytes_accessed=0, transcendentals=0)
+BACKWARD = pl.CostEstimate(flops=10**9 * 100, bytes_accessed=0, transcendentals=0)
 SMALL = ("ag", "as", "qvb", "pb", "mg", "ms", "f1b", "f2b")
 
 
@@ -55,20 +59,35 @@
     return lax.dot_general(x, w, (((0,), (0,)), ((), ())), preferred_element_type=F32)
 
 
-def columns(width, first):
-    return ("columns", width, first)
-
-
-def row_call(body, where, kept, gathered, picks, blocked, whole, outs, images, slots, flops=0):
+def columns(width, first, stride):
+    return ("columns", width, (first, stride))
+
+
+def row_call(body, where, kept, weights, blocked, whole, outs, images, slots, after=(), cost=FORWARD):
     in_specs, args = [], []
-    for kind, width, first in picks:
+    for v, pick_of in (part for w in weights for part in w):
+        if pick_of is None:
+            in_specs.append(pl.BlockSpec(v.shape, lambda i, w, k: (0, 0), pipeline_mode=ONCE))
+            args.append(v)
+            continue
+        kind, width, first = pick_of
         if kind == "columns":
-            depth = gathered.shape[0]
-            in_specs.append(pl.BlockSpec((depth, width), lambda i, w, k, f=first: (0, f + w[0])))
-            args.append(gathered)
+            spec = pl.BlockSpec((v.shape[0], width), lambda i, w, k, f=first: (0, f[0] + f[1] * w[0]), pipeline_mode=ONCE)
+            in_specs.append(spec)
+            args.append(v)
+        elif kind == "quarter":
+            at, stride, part = first
+            spec = pl.BlockSpec(
+                (v.shape[0], width),
+                lambda i, w, k, f=(at, stride, part): (0, f[0] + f[1] * w[0] + jnp.bitwise_xor(f[2], w[3])),
+                pipeline_mode=ONCE,
+            )
+            in_specs.append(spec)
+            args.append(v)
         else:
-            view = gathered.reshape(HEADS // 2, 2, HEAD_DIM, gathered.shape[1])
-            in_specs.append(pl.BlockSpec((HEADS // 2, None, HEAD_DIM, width), lambda i, w, k, f=first: (0, w[0], 0, f)))
+            view = v.reshape(HEADS // 2, 2, HEAD_DIM, v.shape[1])
+            spec = pl.BlockSpec((HEADS // 2, None, HEAD_DIM, width), lambda i, w, k, f=first: (0, w[0], 0, f), pipeline_mode=ONCE)
+            in_specs.append(spec)
             args.append(view)
     for v in blocked:
         if v.ndim == 2:
@@ -88,11 +107,17 @@
             out_specs.append(pl.BlockSpec((1,) + shape[1:], lambda i, *_, n=len(shape): (i,) + (0,) * (n - 1)))
         else:
             out_specs.append(pl.BlockSpec(shape, lambda i, *_, n=len(shape): (0,) * n))
-    n_p, n_b, n_in = len(picks), len(blocked), len(args)
+    n_p, n_b, n_in = sum(len(w) for w in weights), len(blocked), len(args)
+    in_specs += [ANY] * len(after)
+    args += list(after)
 
     def kernel(where_ref, kept_ref, *refs):
-        ins, res = refs[:n_in], refs[n_in:]
-        body(kept_ref, ins[:n_p], ins[n_p : n_p + n_b], ins[n_p + n_b :], res)
+        ins, res = refs[:n_in], refs[n_in + len(after) :]
+        held, at = [], 0
+        for w in weights:
+            held.append(ins[at : at + len(w)])
+            at += len(w)
+        body(kept_ref, held, ins[n_p : n_p + n_b], ins[n_p + n_b : n_in], res)
 
     return pl.pallas_call(
         kernel,
@@ -101,9 +126,7 @@
         ),
         out_shape=out_shape,
         compiler_params=pltpu.CompilerParams(vmem_limit_bytes=LIMIT),
-        cost_estimate=pl.CostEstimate(
-            flops=flops, bytes_accessed=sum(v.size * v.dtype.itemsize for v in args[n_p:]), transcendentals=0
-        ),
+        cost_estimate=cost,
     )(where, kept, *args)
 
 
@@ -140,19 +163,19 @@
     x = blocked[0][...]
     for k, n in chunks(outs[0].shape[1], 512):
         cols = pl.ds(k, n)
-        outs[0][:, cols] = (dot(x, w[0][:, cols]) + whole[0][:, cols]).astype(BF)
+        outs[0][:, cols] = (dot(x, w[0][0][:, cols]) + whole[0][:, cols]).astype(BF)
 
 
 def heads_of(ref):
     return ref[...].reshape(-1, ref.shape[-1])
 
 
-def pairs_dot(x_ref, w_ref):
-    depth = w_ref.shape[0]
-    total = None
-    for k in range(0, w_ref.shape[1], depth):
-        term = dot(x_ref[:, k : k + depth], w_ref[:, k : k + depth])
+def pairs_dot(x_ref, parts):
+    total, at = None, 0
+    for w_ref in parts:
+        term = dot(x_ref[:, at : at + w_ref.shape[0]], w_ref[...])
         total = term if total is None else total + term
+        at += w_ref.shape[0]
     return total
 
 
@@ -178,12 +201,12 @@
 
 def attend_other(kept, w, blocked, whole, outs):
     attend(kept, blocked[0], outs[0], outs[1])
-    outs[2][...] = dot(outs[1][...], heads_of(w[0]))
+    outs[2][...] = dot(outs[1][...], heads_of(w[0][0]))
 
 
 def attend_own(kept, w, blocked, whole, outs):
     attend(kept, blocked[0], outs[0], outs[1])
-    middle = blocked[2][...] + (dot(outs[1][...], heads_of(w[0])) + blocked[1][...]) + whole[0][...]
+    middle = blocked[2][...] + (dot(outs[1][...], heads_of(w[0][0])) + blocked[1][...]) + whole[0][...]
     outs[2][...] = middle
     outs[3][...] = norm_rows(middle, whole[1][...], whole[2][...]).astype(BF)
 
@@ -192,7 +215,8 @@
     x = blocked[0][...]
     for k, n in chunks(outs[0].shape[1], 256):
         cols = pl.ds(k, n)
-        pre = dot(x, w[0][:, cols]) + whole[0][:, cols]
+        held = w[0][k // w[0][0].shape[1]]
+        pre = dot(x, held[:, pl.ds(k % held.shape[1], n)]) + whole[0][:, cols]
         phi = 0.5 + 0.5 * lax.erf(pre * (2.0**-0.5))
         dens = jnp.exp(-0.5 * (pre * pre)) * 0.3989422804014327
         outs[0][:, cols] = (pre * phi).astype(BF)
@@ -217,13 +241,17 @@
 
 def mlp_back(w, blocked, outs):
     low = blocked[0][...]
-    depth = w[0].shape[0]
     for k, n in chunks(outs[0].shape[1], 512):
         cols = pl.ds(k, n)
-        block = k // depth * depth
-        t = dot_t(low, w[0][pl.ds(k - block, n), block : block + depth])
+        held = w[0][k // w[0][0].shape[0]]
+        t = dot_t(low, held[pl.ds(k % held.shape[0], n), :])
         outs[0][:, cols] = (t * blocked[1][:, cols].astype(F32)).astype(BF)
-    return dot_t(outs[0][...], w[1][...])
+    total, at = None, 0
+    for held in w[1]:
+        term = dot_t(outs[0][:, at : at + held.shape[1]], held[...])
+        total = term if total is None else total + term
+        at += held.shape[1]
+    return total
 
 
 def mlp_back_other(kept, w, blocked, whole, outs):
@@ -255,7 +283,7 @@
 def attend_back(w, blocked, outs):
     branch, proj_ref, probs_ref = blocked[0], blocked[1], blocked[2]
     third = proj_ref.shape[1] // 3
-    datt = dot_t(branch[...], heads_of(w[0])).astype(BF)
+    datt = dot_t(branch[...], heads_of(w[0][0])).astype(BF)
     pairs = [[], [], []]
     for h in range(third // HEAD_DIM):
         lo = h * HEAD_DIM
@@ -275,7 +303,7 @@
                 at = j * third + lo - HEAD_DIM
                 outs[0][:, at : at + 2 * HEAD_DIM] = jnp.concatenate(pairs[j], axis=1)
             pairs = [[], [], []]
-    return dot_t(outs[0][...], w[1][...])
+    return dot_t(outs[0][...], w[1][0][...])
 
 
 def attend_back_other(kept, w, blocked, whole, outs):
@@ -292,21 +320,24 @@
     add_sums(outs[3], [gain, shift, jnp.sum(low.astype(F32), axis=0, keepdims=True)])
 
 
-def weight_grad(plan, where, xs, ys, groups, first, sums):
+def weight_grad(plan, where, xs, ys, groups, first, sums=False, extra=0, relative=False, after=()):
     depth, n_x = xs[0].shape
     cols = ys[0].shape[1]
     ny, chips, bits = plan.ny, plan.chips, plan.bits
     half = cols // ny
-    chunk = half if half <= 768 else 512
-    steps = half // chunk
+    size = half
+    chunk = size if size <= 768 else 512
+    steps = size // chunk
     rows = n_x // chips
     part = rows // groups
     dims = [ny] + [2] * bits
     dims[first] = 1
     block = [1] + dims[1:] + [rows, chunk]
-    shape = dims + [rows, half]
+    shape = dims + [rows, size + extra]
+    n_after = len(after)
 
     def kernel(where_ref, xo, xt, yo, yt, *rest):
+        rest = rest[n_after:]
         keep, send = rest[0], rest[1]
         flip, acc = rest[-2], rest[-1]
         step = pl.program_id(0)
@@ -329,7 +360,11 @@
             chip = jnp.bitwise_xor(where_ref[1], r)
             for g in range(groups):
                 start = pl.multiple_of(g * part * chips + chip * part, 16)
-                ref[tuple(at) + (pl.ds(g * part, part),)] = acc[pl.ds(start, part)].astype(BF)
+                place = g
+                if groups == 2 and ny == 2:
+                    place = jnp.bitwise_xor(g, where_ref[2])
+                place = pl.multiple_of(place * part, 16)
+                ref[tuple(at) + (pl.ds(place, part),)] = acc[pl.ds(start, part)].astype(BF)
 
         if first:
             for r in range(chips):
@@ -346,13 +381,14 @@
                 for r in range(chips):
                     put(send, r)
 
+    per_rep = half // chunk
+
     def column(i, w):
-        if ny == 1:
-            return i
-        return jnp.bitwise_xor(i // steps, w[2]) * steps + i % steps
+        own = w[2] if ny == 2 and not relative else 0
+        return jnp.bitwise_xor(i // steps, own) * per_rep + i % steps
 
     zeros = (0,) * (bits + 1)
-    x_spec = pl.BlockSpec((depth, n_x), lambda i, w: (0, 0))
+    x_spec = pl.BlockSpec((depth, n_x), lambda i, w: (0, 0), pipeline_mode=ONCE)
     y_spec = pl.BlockSpec((depth, chunk), lambda i, w: (0, column(i, w)))
     if first:
         specs = [pl.BlockSpec(block, lambda i, w: (i // steps,) + zeros + (i % steps,))] * 2
@@ -370,46 +406,262 @@
         grid_spec=pltpu.PrefetchScalarGridSpec(
             num_scalar_prefetch=1,
             grid=(ny * steps,),
-            in_specs=[x_spec, x_spec, y_spec, y_spec],
+            in_specs=[x_spec, x_spec, y_spec, y_spec] + [ANY] * n_after,
             out_specs=specs,
             scratch_shapes=[pltpu.VMEM((n_x, 2 * depth), BF), pltpu.VMEM((n_x, chunk), F32)],
         ),
         out_shape=out_shape,
         compiler_params=pltpu.CompilerParams(vmem_limit_bytes=LIMIT),
-        cost_estimate=pl.CostEstimate(
-            flops=4 * depth * n_x * cols, bytes_accessed=2 * (2 * depth * (n_x + cols) + n_x * cols), transcendentals=0
+        cost_estimate=BACKWARD,
+    )(where, *xs, *ys, *after)
+
+
+def proj_grad_into(plan, where, xs, ys, first, keep, send):
+    depth, n_x = xs[0].shape
+    cols = ys[0].shape[1]
+    ny, chips, bits = plan.ny, plan.chips, plan.bits
+    half = cols // ny
+    part = n_x // chips
+    width = half * part // keep.shape[-2]
+    stacked = half // width
+    at_col = keep.shape[-1] // width - 1
+    block = [1] + list(keep.shape[1:-1]) + [width]
+
+    def kernel(where_ref, xo, xt, yo, yt, k_in, s_in, keep_ref, send_ref, acc):
+        acc[...] = t_dot(xo[...], yo[...]) + t_dot(xt[...], yt[...])
+        for r in range(chips):
+            at = [0]
+            for k in range(1, bits + 1):
+                at.append((r >> (bits - k)) & 1 if k != first else 0)
+            ref = send_ref if (r >> (bits - first)) & 1 else keep_ref
+            start = pl.multiple_of(jnp.bitwise_xor(where_ref[1], r) * part, 16)
+            for g in range(stacked):
+                piece = acc[pl.ds(start, part), g * width : (g + 1) * width]
+                ref[tuple(at) + (pl.ds(g * part, part),)] = piece.astype(BF)
+
+    zeros = (0,) * (bits + 1)
+    own = (lambda w: w[2]) if ny == 2 else (lambda w: 0)
+    x_spec = pl.BlockSpec((depth, n_x), lambda i, w: (0, 0), pipeline_mode=ONCE)
+    y_spec = pl.BlockSpec((depth, half), lambda i, w: (0, jnp.bitwise_xor(i, own(w))))
+    spec = pl.BlockSpec(block, lambda i, w: (i,) + zeros + (at_col,))
+    return pl.pallas_call(
+        kernel,
+        grid_spec=pltpu.PrefetchScalarGridSpec(
+            num_scalar_prefetch=1,
+            grid=(ny,),
+            in_specs=[x_spec, x_spec, y_spec, y_spec, ANY, ANY],
+            out_specs=[spec, spec],
+            scratch_shapes=[pltpu.VMEM((n_x, half), F32)],
         ),
-    )(where, *xs, *ys)
-
-
-def sum_over(plan, keep, send, axes):
-    for at, axis in enumerate(axes):
-        got = plan.flip(send, axis)
-        total = keep.astype(F32) + got.astype(F32)
-        if at + 1 == len(axes):
-            return total.reshape(total.shape[-2:])
-        after = axes[at + 1]
-        send = lax.slice_in_dim(total, 1, 2, axis=after).astype(BF)
-        keep = lax.slice_in_dim(total, 0, 1, axis=after).astype(BF)
+        out_shape=[jax.ShapeDtypeStruct(keep.shape, BF)] * 2,
+        input_output_aliases={5: 0, 6: 1},
+        compiler_params=pltpu.CompilerParams(vmem_limit_bytes=LIMIT),
+        cost_estimate=BACKWARD,
+    )(where, *xs, *ys, keep, send)
+
+
+class Term:
+    def __init__(self, plan, keep, send, order):
+        self.plan, self.keep, self.order = plan, keep, list(order)
+        self.got = plan.flip(send, self.order.pop(0))
+
+    def step(self, after):
+        axis = self.order.pop(0)
+        self.keep, send = combine(self.keep, self.got, axis, after)
+        self.got = self.plan.flip(send, axis)
+        return send
+
+
+def combine(keep, got, axis, after):
+    shape = keep.shape
+    rows, cols = shape[-2:]
+    cuts = 2
+    block = shape[:-2] + (rows // cuts, cols)
+    out = shape[:axis] + (1,) + shape[axis + 1 :]
+    out_block = out[:-2] + (rows // cuts, cols)
+    lead = len(shape) - 2
+
+    def kernel(k, g, *rest):
+        stay, go = rest[-2:]
+        for side, ref in ((0, stay), (1, go)):
+            at = tuple(pl.ds(side, 1) if d == axis else slice(None) for d in range(lead))
+            ref[...] = (k[at].astype(F32) + g[at].astype(F32)).astype(BF)
+
+    index = lambda i: (0,) * lead + (i, 0)
+    return pl.pallas_call(
+        kernel,
+        grid=(cuts,),
+        in_specs=[pl.BlockSpec(block, index)] * 2 + [ANY] * len(after),
+        out_specs=[pl.BlockSpec(out_block, index)] * 2,
+        out_shape=[jax.ShapeDtypeStruct(out, BF)] * 2,
+        compiler_params=pltpu.CompilerParams(vmem_limit_bytes=LIMIT),
+        cost_estimate=BACKWARD,
+    )(keep, got, *after)
+
+
+def last_combine(terms, axis, rows, after):
+    ins, specs, widths = [], [], []
+    for t in terms:
+        ins += [t.keep, t.got]
+        widths.append(t.keep.shape[-1] * (t.keep.shape[-2] // rows))
+    total = sum(widths)
+    n_in = len(ins)
+
+    def kernel(*refs):
+        stay, go = refs[-2:]
+        at = 0
+        for j, t in enumerate(terms):
+            k, g = refs[2 * j], refs[2 * j + 1]
+            lead = k.ndim - 2
+            cols = k.shape[-1]
+            for block in range(k.shape[-2] // rows):
+                for side, ref in ((0, stay), (1, go)):
+                    idx = tuple(side if d == axis else 0 for d in range(lead)) + (pl.ds(block * rows, rows),)
+                    ref[:, at : at + cols] = (k[idx].astype(F32) + g[idx].astype(F32)).astype(BF)
+                at += cols
+
+    whole = [pl.BlockSpec(v.shape, lambda n=v.ndim: (0,) * n) for v in ins]
+    return pl.pallas_call(
+        kernel,
+        in_specs=whole + [ANY] * len(after),
+        out_specs=[pl.BlockSpec((rows, total), lambda: (0, 0))] * 2,
+        out_shape=[jax.ShapeDtypeStruct((rows, total), BF)] * 2,
+        compiler_params=pltpu.CompilerParams(vmem_limit_bytes=LIMIT),
+        cost_estimate=BACKWARD,
+    )(*ins, *after)
 
 
 def pick(flag, a, b):
     return jnp.where(flag == 0, a, b)
 
 
-def join_core(plan, v, c, groups):
-    rows, cols = v.shape
-    v = v.reshape(groups, 2, rows // groups // 2, cols)
-    mine = pick(c, v[:, 0], v[:, 1]).astype(BF)
-    got = plan.core(pick(c, v[:, 1], v[:, 0]).astype(BF))
-    return jnp.stack([pick(c, mine, got), pick(c, got, mine)])
-
-
-def join_rep(plan, v, y):
-    if plan.ny == 1:
-        return lax.psum(v, "rep").astype(F32)[..., None, :]
-    got = plan.flip(v, 0)
-    return jnp.stack([pick(y, v, got), pick(y, got, v)], axis=-2).astype(F32)
+def small_call(kernel, where, ins, shapes, after, grid=None):
+    n = len(ins)
+
+    def body(where_ref, *refs):
+        kernel(where_ref, refs[:n], refs[n + len(after) :])
+
+    return pl.pallas_call(
+        body,
+        grid_spec=pltpu.PrefetchScalarGridSpec(
+            num_scalar_prefetch=1,
+            grid=(1,),
+            in_specs=[pl.BlockSpec(v.shape, lambda i, w, n=v.ndim: (0,) * n) for v in ins] + [ANY] * len(after),
+            out_specs=[pl.BlockSpec(s, lambda i, w, n=len(s): (0,) * n) for s, _ in shapes],
+        ),
+        out_shape=[jax.ShapeDtypeStruct(s, t) for s, t in shapes],
+        compiler_params=pltpu.CompilerParams(vmem_limit_bytes=LIMIT),
+        cost_estimate=BACKWARD,
+    )(where, *ins, *after)
+
+
+class Ending:
+    def __init__(self, plan, where, terms, axis, rows, tail, after):
+        self.plan, self.where, self.rows, self.tail = plan, where, rows, tail
+        self.keep, self.sent = last_combine(terms, axis, rows, after)
+        self.got = plan.flip(self.sent, axis)
+
+    def core(self, after):
+        rows, tail = self.rows // 2, self.tail
+        cols = self.cols = self.keep.shape[1] - tail
+
+        def kernel(where, ins, outs):
+            c = where[0]
+            for ref, row in ((outs[0], c), (outs[1], 1 - c)):
+                at = pl.ds(pl.multiple_of(row * rows, 16), rows)
+                ref[:, :cols] = (ins[0][at, :cols].astype(F32) + ins[1][at, :cols].astype(F32)).astype(BF)
+            if tail:
+                for g in range(2):
+                    at = pl.ds(g * rows, rows)
+                    piece = ins[0][at, cols:].astype(F32) + ins[1][at, cols:].astype(F32)
+                    outs[0][:, cols + g * tail : cols + (g + 1) * tail] = piece.astype(BF)
+
+        shapes = [((rows, cols + 2 * tail), BF), ((rows, cols), BF)]
+        self.mine, sent = small_call(kernel, self.where, [self.keep, self.got], shapes, after)
+        self.came = self.plan.core(sent)
+        return sent
+
+    def rep(self, after):
+        rows, cols, tail = self.rows // 2, self.cols, self.tail
+
+        def kernel(where, ins, outs):
+            outs[0][:, :cols] = ins[0][:, :cols]
+            outs[0][:, cols : 2 * cols] = ins[1][...]
+            if tail:
+                outs[0][:, 2 * cols :] = ins[0][:, cols:]
+
+        shapes = [((rows, 2 * cols + 2 * tail), BF)]
+        v = small_call(kernel, self.where, [self.mine, self.came], shapes, after)[0]
+        self.pair = [v, self.plan.flip(v, 0)] if self.plan.ny == 2 else [lax.psum(v, "rep")]
+        return v
+
+
+def place_grads(plan, where, layer, layers, end2, rest, sizes, before, after):
+    deep, width, ff, quarters = sizes
+    n, ny, halves = plan.shards, plan.ny, quarters // 2
+    wide, half_ff = 3 * width // 2, ff // 2
+    cols2, cols = end2.cols, rest.cols
+    fused = bool(rest.tail)
+    ins = end2.pair + rest.pair
+
+    def kernel(where_ref, *refs):
+        refs_in = refs[: 2 * ny]
+        outs = refs[-(4 if fused else 3) :]
+        c, y = where_ref[0], where_ref[2]
+
+        def source(group, p, q, at, size):
+            total = (cols2, cols)[group]
+            step = (at // 128) * 128
+            span = (at + size - step + 127) // 128 * 128
+            first = pl.multiple_of(jnp.where(p == c, 0, total) + step, 128)
+            v = refs_in[group * ny][:, pl.ds(first, span)]
+            if ny == 2:
+                v = jnp.where(y == q, v, refs_in[group * ny + 1][:, pl.ds(first, span)])
+            return v[:, at - step : at - step + size].astype(F32)
+
+        def core_columns(p, at, size, total, first):
+            part = total // ny
+            return source(1, p, at // part, first + at % part, size)
+
+        for k in range(3 * HEADS // 2):
+            pieces = [core_columns(p, k * HEAD_DIM, HEAD_DIM, wide, 0) for p in range(2)]
+            outs[0][0, :, k * 2 * HEAD_DIM : (k + 1) * 2 * HEAD_DIM] = jnp.concatenate(pieces, axis=1)
+        for k in range(n):
+            pieces = []
+            for p in range(2):
+                for h in range(halves):
+                    pieces.append(core_columns(p, (h * n + k) * deep, deep, half_ff, wide // ny))
+            outs[1][0, :, k * quarters * deep : (k + 1) * quarters * deep] = jnp.concatenate(pieces, axis=1)
+        part = width // ny
+        for p in range(2):
+            for h in range(halves):
+                for q in range(ny):
+                    at = pl.ds((p * halves + h) * deep, deep)
+                    outs[2][0, at, q * part : (q + 1) * part] = source(0, p, q, h * part, part)
+        if fused:
+            for q in range(ny):
+                v = refs_in[ny][:, 2 * cols :]
+                if ny == 2:
+                    v = jnp.where(y == q, v, refs_in[ny + 1][:, 2 * cols :])
+                outs[3][0, :, q * part : (q + 1) * part] = v.astype(F32)
+
+    shapes = [(deep, 3 * width), (deep, ff), (quarters * deep, width)] + ([(deep, width)] if fused else [])
+    in_specs = [pl.BlockSpec(v.shape, lambda i, w: (0, 0)) for v in ins]
+    args = list(ins) + list(before or []) + list(after)
+    n_before = len(before or [])
+    return pl.pallas_call(
+        kernel,
+        grid_spec=pltpu.PrefetchScalarGridSpec(
+            num_scalar_prefetch=1,
+            grid=(1,),
+            in_specs=in_specs + [ANY] * (n_before + len(after)),
+            out_specs=[pl.BlockSpec((1,) + s, lambda i, w: (layer, 0, 0)) for s in shapes],
+        ),
+        out_shape=[jax.ShapeDtypeStruct((layers,) + s, F32) for s in shapes],
+        input_output_aliases={1 + len(ins) + k: k for k in range(n_before)},
+        compiler_params=pltpu.CompilerParams(vmem_limit_bytes=LIMIT),
+        cost_estimate=BACKWARD,
+    )(where, *args)
 
 
 def per_device(
@@ -437,7 +689,7 @@
     deep = qkv_weight.shape[1]
     shard = lax.axis_index("shard")
     c, chip, y = lax.rem(shard, 2), shard // 2, lax.axis_index("rep")
-    where = jnp.stack([c, chip, y]).astype(jnp.int32)
+    where = jnp.stack([c, chip, y, y if plan.ny == 2 else 0 * y]).astype(jnp.int32)
     ff = fc2_weight.shape[1] * n
     quarters = fc2_weight.shape[1] // deep
     wide, half_width, half_ff = 3 * width // 2, width // 2, ff // 2
@@ -450,23 +702,41 @@
     lines = small.size // 128
     extra = jnp.pad(small.reshape(lines, 128), ((0, deep - lines), (0, 0)))
 
+    halves = quarters // 2
+    lead = 4 * width
+    block = n * deep
+    each = halves // plan.ny
+
     def merged(layer):
         qkv = qkv_weight[layer].reshape(deep, 3 * half_heads, 2, HEAD_DIM).swapaxes(1, 2).reshape(deep, 3 * width)
         fc1 = fc1_weight[layer].reshape(deep, n, quarters, deep).swapaxes(1, 2).reshape(deep, ff)
-        fc2 = [fc2_weight[layer, k * deep : (k + 1) * deep] for k in range(quarters)]
+        fc2 = fc2_weight[layer].reshape(2, halves, deep, width)
+        if plan.ny == 2:
+            fc2 = pick(y, fc2[:, :1], fc2[:, 1:])
+        fc2 = [fc2[p, k] for p in range(2) for k in range(each)]
         return [qkv, proj_weight[layer], fc1] + fc2 + ([] if layer else [extra])
 
-    gathered = [
-        lax.all_gather(jnp.concatenate(merged(layer), axis=1), "shard", axis=0, tiled=True) for layer in range(layers)
-    ]
-    picks = {
-        "qkv": columns(wide, 0),
-        "proj": ("heads", width, 3),
-        "fc1": columns(half_ff, 4 * width // half_ff),
-        "fc2": columns(half_ff, (4 * width + ff) // half_ff),
-    }
-
-    every = gathered[0].reshape(n, deep, -1)[:, :lines, 4 * width + 2 * ff :]
+    operands = lax.optimization_barrier([jnp.concatenate(merged(layer), axis=1) for layer in range(layers)])
+    gathered = [lax.all_gather(v, "shard", axis=0, tiled=True) for v in operands]
+    at_fc1, at_fc2 = lead // block, (lead + ff) // block
+    mlp_parts = []
+    for layer in range(layers):
+        found = {"fc1": [(gathered[layer], ("quarter", block, (at_fc1, halves, k))) for k in range(halves)]}
+        found["fc2"] = [(gathered[layer], columns(block, at_fc2 + k, each)) for k in range(each)]
+        if plan.ny == 2:
+            mine = lax.dynamic_slice_in_dim(gathered[layer], (at_fc2 + c) * block, block, axis=1)
+            found["fc2"].append((plan.flip(mine, 0), None))
+            found["sent"] = (mine,)
+        mlp_parts.append(found)
+
+    def weight_of(layer, name):
+        if name == "qkv":
+            return [(gathered[layer], columns(wide, 0, 1))]
+        if name == "proj":
+            return [(gathered[layer], ("heads", width, 3))]
+        return mlp_parts[layer][name]
+
+    every = gathered[0].reshape(n, deep, -1)[:, :lines, lead + ff + 2 * each * block :]
     every = every.reshape(n, layers, small.shape[1]).astype(F32)
     vecs = []
     for layer in range(layers):
@@ -477,8 +747,11 @@
         q = d["qvb"].reshape(2 * half_heads, 2, HEAD_DIM)
         q = pick(c, q[:, 0], q[:, 1]).reshape(2, half_width)
         d["qvb_c"] = jnp.stack([q[0], jnp.zeros_like(q[0]), q[1]]).reshape(1, wide)
-        f = d["f1b"].reshape(n, quarters, deep).swapaxes(0, 1).reshape(2, half_ff)
-        d["f1b_c"] = pick(c, f[0:1], f[1:2])
+        f = d["f1b"].reshape(n, 2, halves, deep).transpose(1, 2, 0, 3).reshape(2, halves, block)
+        f = pick(c, f[0], f[1])
+        if plan.ny == 2:
+            f = pick(y, f, f[::-1])
+        d["f1b_c"] = f.reshape(1, half_ff)
         vecs.append(d)
 
     kept_oth = plan.core(kept)
@@ -489,36 +762,33 @@
     low_oth = plan.core(low_own)
     first_own = norm_rows(state, vecs[0]["ag"], vecs[0]["as"]).astype(BF)
 
-    qkv_flops = 2 * rows * width * wide
-    att_flops = 4 * rows * slots * half_width + 2 * rows * half_width * width
-    ff_flops = 2 * rows * width * half_ff
     f32_rows, low_rows = ("rows", (rows, width), F32), ("rows", (rows, width), BF)
     wide_rows, ff_rows = ("rows", (rows, wide), BF), ("rows", (rows, half_ff), BF)
     att_outs = [("image", (images, half_heads, slots, slots), BF), ("rows", (rows, half_width), BF)]
     full_sums = ("full", (8, width), F32)
 
-    def call(body, layer, own, names, blocked, whole, outs, flops):
-        chosen = [picks[name] for name in names]
+    def call(body, layer, own, names, blocked, whole, outs, after=(), cost=None):
+        chosen = [weight_of(layer, name) for name in names]
         k = kept if own else kept_oth
-        return row_call(body, where, k, gathered[layer], chosen, blocked, whole, outs, images, slots, flops)
+        return row_call(body, where, k, chosen, blocked, whole, outs, images, slots, after, cost or (BACKWARD if after else FORWARD))
 
     saved = []
-    mixed = None
     for layer in range(layers):
         v = vecs[layer]
         first_oth = plan.core(first_own)
-        proj_oth = call(qkv_body, layer, 0, ["qkv"], [first_oth], [v["qvb_c"]], [wide_rows], qkv_flops)[0]
-        probs_oth, att_oth, part = call(attend_other, layer, 0, ["proj"], [proj_oth], [], att_outs + [f32_rows], att_flops)
+        sent = mlp_parts[layer].get("sent", ())
+        proj_oth = call(qkv_body, layer, 0, ["qkv"], [first_oth], [v["qvb_c"]], [wide_rows], sent, FORWARD)[0]
+        probs_oth, att_oth, part = call(attend_other, layer, 0, ["proj"], [proj_oth], [], att_outs + [f32_rows])
         part = plan.core(part)
-        proj_own = call(qkv_body, layer, 1, ["qkv"], [first_own], [v["qvb_c"]], [wide_rows], qkv_flops)[0]
+        proj_own = call(qkv_body, layer, 1, ["qkv"], [first_own], [v["qvb_c"]], [wide_rows])[0]
         probs_own, att_own, middle, second_own = call(
-            attend_own, layer, 1, ["proj"], [proj_own, part, state], [v["pb"], v["mg"], v["ms"]], att_outs + [f32_rows, low_rows], att_flops
-        )
+            attend_own, layer, 1, ["proj"], [proj_own, part, state], [v["pb"], v["mg"], v["ms"]], att_outs + [f32_rows, low_rows])
         second_oth = plan.core(second_own)
-        hid_oth, slope_oth = call(up_body, layer, 0, ["fc1"], [second_oth], [v["f1b_c"]], [ff_rows] * 2, ff_flops)
-        part = call(down_other, layer, 0, ["fc2"], [hid_oth], [], [f32_rows], ff_flops)[0]
-        part = plan.core(part)
-        hid_own, slope_own = call(up_body, layer, 1, ["fc1"], [second_own], [v["f1b_c"]], [ff_rows] * 2, ff_flops)
+        hid_oth, slope_oth = call(up_body, layer, 0, ["fc1"], [second_oth], [v["f1b_c"]], [ff_rows] * 2)
+        if layer + 1 < layers:
+            part = call(down_other, layer, 0, ["fc2"], [hid_oth], [], [f32_rows])[0]
+            part = plan.core(part)
+        hid_own, slope_own = call(up_body, layer, 1, ["fc1"], [second_own], [v["f1b_c"]], [ff_rows] * 2)
         saved.append(
             dict(
                 state=state,
@@ -535,30 +805,63 @@
         if layer + 1 < layers:
             w = vecs[layer + 1]
             state, first_own = call(
-                down_own, layer, 1, ["fc2"], [hid_own, part, middle], [v["f2b"], w["ag"], w["as"]], [f32_rows, low_rows], ff_flops
-            )
-        else:
-            mixed = call(down_last, layer, 1, ["fc2"], [hid_own, part, middle], [v["f2b"]], [low_rows], ff_flops)[0]
-
-    axes = list(range(plan.bits + 1)) if plan.ny == 2 else list(range(1, plan.bits + 1))
-    x_axis = plan.bits
-    z_axes = list(range(plan.bits - 1, 0, -1))
-    y_axes = [0] if plan.ny == 2 else []
-    order_y = y_axes + [x_axis] + z_axes
-    order_x = [x_axis] + z_axes + y_axes
-    order_z = z_axes[:1] + y_axes + [x_axis] + z_axes[1:]
-    big = [None] * layers
+                down_own, layer, 1, ["fc2"], [hid_own, part, middle], [v["f2b"], w["ag"], w["as"]], [f32_rows, low_rows])
+
+    axes = list(range(1 if plan.ny == 1 else 0, plan.bits + 1))
+    last_axis, z_axis, x_axis = 1, plan.bits - 1, plan.bits
+    y_axis = 0 if plan.ny == 2 else 2
+    order_f2 = [y_axis, x_axis, z_axis]
+    orders_f1 = [[x_axis, y_axis, z_axis]] + [[z_axis, x_axis, y_axis]] * (layers - 1)
+    orders_q = [[z_axis, x_axis, y_axis]] + [[x_axis, z_axis, y_axis]] * (layers - 1)
+    own_rows = 2 * deep
+    tail = width // plan.ny * HEAD_DIM // own_rows
+    fused = n == HEADS
+    tail = tail if fused else 0
+    big = [[None] * 4 for _ in range(layers)]
     sums = [None] * layers
     f2b_sum = jnp.sum(low_own.astype(F32), axis=0, keepdims=True)
-    mlp_flops = 4 * rows * width * half_ff
-    back_flops = 12 * rows * slots * half_width + 2 * rows * width * (wide + half_width)
+
+    def end_fc2(layer, prev):
+        ends["f2", layer] = Ending(plan, where, [terms["f2", layer]], last_axis, own_rows, 0, prev)
+        return (ends["f2", layer].sent,)
+
+    def end_rest(layer, prev):
+        group = [terms["q", layer], terms["f1", layer]]
+        ends["rest", layer] = Ending(plan, where, group, last_axis, own_rows, tail, prev)
+        return (ends["rest", layer].sent,)
+
+    def place(layer, before, prev):
+        return place_grads(
+            plan, where, layer, layers, ends["f2", layer], ends["rest", layer], (deep, width, ff, quarters), before, prev
+        )
+
+    ends = {}
+    prev = (hid_own,)
+    terms = {}
     for layer in reversed(range(layers)):
         v, s = vecs[layer], saved[layer]
-        res2 = weight_grad(plan, where, s["hid"], (low_own, low_oth), 2, order_y[0], False)
+        top = layer == layers - 1
+
+        def grad_fc2(prev):
+            r = weight_grad(plan, where, s["hid"], (low_own, low_oth), 2, order_f2[0], after=prev)
+            terms["f2", layer] = Term(plan, *r, order_f2)
+            return (r[1],)
+
+        if top:
+            prev = grad_fc2(prev)
         pre_oth, part = call(
-            mlp_back_other, layer, 0, ["fc2", "fc1"], [low_oth, s["slope"][1]], [], [ff_rows, f32_rows], mlp_flops
+            mlp_back_other, layer, 0, ["fc2", "fc1"], [low_oth, s["slope"][1]], [], [ff_rows, f32_rows], prev
         )
         part = plan.core(part)
+        prev = (pre_oth,)
+        if top:
+            last_part = call(down_other, layer, 0, ["fc2"], [s["hid"][1]], [], [f32_rows], prev)[0]
+            prev = (last_part,)
+            last_part = plan.core(last_part)
+        else:
+            prev = grad_fc2(prev)
+            prev += (terms["f1", layer + 1].step(prev[:1]),)
+            prev += end_fc2(layer + 1, prev[:1])
         pre_own, mid_grad, branch_own, sum1 = call(
             mlp_back_own,
             layer,
@@ -567,10 +870,32 @@
             [low_own, s["slope"][0], part, s["middle"], grad],
             [v["mg"]],
             [ff_rows, f32_rows, low_rows, full_sums],
-            mlp_flops,
+            prev,
         )
         branch_oth = plan.core(branch_own)
-        res1 = weight_grad(plan, where, s["second"], (pre_own, pre_oth), 1, order_x[0], True)
+        prev = (branch_own,)
+        if not top:
+            prev += (terms["q", layer + 1].step(prev),)
+        res1 = weight_grad(
+            plan, where, s["second"], (pre_own, pre_oth), 1, orders_f1[layer][0], sums=True, extra=tail, relative=True, after=prev
+        )
+        keep, send = res1[:2]
+        if fused:
+            keep, send = proj_grad_into(plan, where, s["att"], (branch_own, branch_oth), orders_f1[layer][0], keep, send)
+        else:
+            term = t_dot(s["att"][0], branch_own) + t_dot(s["att"][1], branch_oth)
+            term = term.astype(BF).reshape(half_heads, HEAD_DIM, width)
+            none = jnp.zeros_like(term)
+            term = jnp.stack([pick(c, term, none), pick(c, none, term)], axis=1).reshape(width, width)
+            term = lax.psum_scatter(term, "shard", scatter_dimension=0, tiled=True)
+            big[layer][1] = lax.psum(term, "rep").astype(F32)
+        terms["f1", layer] = Term(plan, keep, send, orders_f1[layer])
+        prev = (send,)
+        if top:
+            prev += (terms["f2", layer].step(prev),)
+        else:
+            prev += (terms["q", layer + 1].step(prev[:1]),)
+            prev += (ends["f2", layer + 1].core(prev[:1]),)
         dproj_oth, part = call(
             attend_back_other,
             layer,
@@ -579,20 +904,14 @@
             [branch_oth, s["proj"][1], s["probs"][1]],
             [],
             [wide_rows, f32_rows],
-            back_flops,
+            prev,
         )
         part = plan.core(part)
-        if n == HEADS:
-            resp = weight_grad(plan, where, s["att"], (branch_own, branch_oth), 1, order_y[0], False)
-            proj_part = sum_over(plan, *resp, order_y).astype(BF)
-            proj_grad = join_rep(plan, proj_part, y).reshape(deep, width)
-        else:
-            term = t_dot(s["att"][0], branch_own) + t_dot(s["att"][1], branch_oth)
-            term = term.astype(BF).reshape(half_heads, HEAD_DIM, width)
-            none = jnp.zeros_like(term)
-            term = jnp.stack([pick(c, term, none), pick(c, none, term)], axis=1).reshape(width, width)
-            term = lax.psum_scatter(term, "shard", scatter_dimension=0, tiled=True)
-            proj_grad = lax.psum(term, "rep").astype(F32)
+        prev = (dproj_oth,)
+        if not top:
+            prev += (terms["f2", layer].step(prev[:1]),)
+            prev += (terms["f1", layer + 1].step(prev[:1]),)
+            prev += (ends["f2", layer + 1].rep(prev[:1]),)
         dproj_own, grad, low_own, sum2 = call(
             attend_back_own,
             layer,
@@ -601,45 +920,73 @@
             [branch_own, s["proj"][0], s["probs"][0], part, s["state"], mid_grad],
             [v["ag"]],
             [wide_rows, f32_rows, low_rows, full_sums],
-            back_flops,
+            prev,
         )
+        prev = (dproj_own,)
         if layer:
             low_oth = plan.core(low_own)
-        resq = weight_grad(plan, where, s["first"], (dproj_own, dproj_oth), 1, order_z[0], True)
-
-        fc2_part = join_rep(plan, join_core(plan, sum_over(plan, *res2, order_y), c, 2), y)
-        fc2_grad = fc2_part.reshape(quarters * deep, width)
-        fc1_part = join_rep(plan, join_core(plan, sum_over(plan, *res1[:2], order_x), c, 1), y)
-        fc1_grad = fc1_part.reshape(2, deep, half_ff).swapaxes(0, 1)
-        fc1_grad = fc1_grad.reshape(deep, quarters, n, deep).swapaxes(1, 2).reshape(deep, ff)
-        qkv_part = join_rep(plan, join_core(plan, sum_over(plan, *resq[:2], order_z), c, 1), y)
-        qkv_grad = qkv_part.reshape(2, deep, 3 * half_heads, HEAD_DIM).transpose(1, 2, 0, 3).reshape(deep, 3 * width)
-        big[layer] = (qkv_grad, proj_grad, fc1_grad, fc2_grad)
-
+        if top:
+            prev += (terms["f2", layer].step(prev),)
+        resq = weight_grad(plan, where, s["first"], (dproj_own, dproj_oth), 1, orders_q[layer][0], sums=True, after=prev)
+        terms["q", layer] = Term(plan, *resq[:2], orders_q[layer])
+        prev = (resq[1],)
         q = resq[2].reshape(3, half_heads, 1, HEAD_DIM)
         q = jnp.concatenate([q[:1], q[2:]])
         none = jnp.zeros_like(q)
         q = jnp.concatenate([pick(c, q, none), pick(c, none, q)], axis=2)
-        f = res1[2]
+        f = res1[2].reshape(halves, block)
+        if plan.ny == 2:
+            f = pick(y, f, f[::-1])
         none = jnp.zeros_like(f)
         f = jnp.concatenate([pick(c, f, none), pick(c, none, f)], axis=0)
         f = f.reshape(quarters, n, deep).swapaxes(0, 1)
         full = {"ag": sum2[0], "as": sum2[1], "qvb": q, "pb": sum1[2], "mg": sum1[0], "ms": sum1[1], "f1b": f, "f2b": f2b_sum}
         f2b_sum = sum2[2]
         vec = jnp.concatenate([full[name].reshape(n, -1) for name in SMALL], axis=1)
-        vec = vec + plan.core(vec)
-        for axis in axes:
-            vec = vec + plan.flip(vec, axis)
-        if plan.ny == 1:
-            vec = lax.psum(vec, "rep")
-        sums[layer] = lax.dynamic_slice_in_dim(vec, shard, 1, axis=0)
-
-    vec = jnp.concatenate(sums, axis=0)
+        sums[layer] = vec
+
+    vec = jnp.concatenate(sums, axis=0).reshape(layers, n, -1)
+    got_vec = plan.core(vec)
+    vec_axes = list(axes)
+
+    def step_vec():
+        nonlocal vec, got_vec
+        vec = vec + got_vec
+        sent = vec
+        got_vec = plan.flip(vec, vec_axes.pop(0)) if vec_axes else None
+        return (sent,)
+
+    prev += (terms["f1", 0].step(prev[:1]),)
+    prev += end_rest(1, prev[:1])
+    w = layers - 1
+    mixed = call(
+        down_last, w, 1, ["fc2"], [saved[w]["hid"][0], last_part, saved[w]["middle"]], [vecs[w]["f2b"]], [low_rows], prev
+    )[0]
+    prev = (terms["f2", 0].step((mixed,)),) + step_vec()
+    prev = (ends["rest", 1].core(prev),) + step_vec()
+    prev = (terms["q", 0].step(prev),)
+    prev = (terms["f1", 0].step(prev),) + step_vec()
+    prev = (ends["rest", 1].rep(prev),)
+    prev = end_fc2(0, prev)
+    prev = (terms["q", 0].step(prev),) + step_vec()
+    prev = (ends["f2", 0].core(prev),)
+    while got_vec is not None:
+        prev += step_vec()
+    prev = end_rest(0, prev)
+    prev = (ends["f2", 0].rep(prev),)
+    placed = place(1, None, prev)
+    prev = (ends["rest", 0].core((placed[0],)),)
+    prev = (ends["rest", 0].rep(prev),)
+    placed = place(0, placed, prev)
+    if plan.ny == 1:
+        vec = lax.psum(vec, "rep")
+    vec = lax.dynamic_slice_in_dim(vec, shard, 1, axis=1)[:, 0]
     out, at = {}, 0
     for name, size in zip(SMALL, sizes):
         out[name] = vec[:, at : at + size]
         at += size
-    qkv_g, proj_g, fc1_g, fc2_g = (jnp.stack([big[layer][k] for layer in range(layers)]) for k in range(4))
+    qkv_g, fc1_g, fc2_g = placed[:3]
+    proj_g = placed[3] if fused else jnp.stack([big[layer][1] for layer in range(layers)])
     return (
         mixed.reshape(images, slots, width),
         grad.reshape(images, slots, width),

time: 990 us -> 812 us (0.82)
  waiting for transfers between devices: 412 us -> 271 us
  other arithmetic: 45.9 us -> 9.94 us
  starting transfers between devices: 64 us -> 41.3 us
  Pallas kernels: 360 us -> 372 us
    ppermute x73 -> x54, waiting for transfers between devices: 242 us -> 149 us  [swap(): return lax.ppermute(v, AX, pairs)]
    pallas_call x0 -> x28, Pallas kernels: none -> 62 us  [the longest x12 28.3 us: combine(): pl.pallas_call(kernel, grid=(cuts,), in_specs=[pl.BlockSpec(block, index)...]
    all_gather x2, waiting for transfers between devices: 169 us -> 121 us  [per_device(): lax.all_gather(v, 'shard', axis=0, tiled=True)]
    another operation x65 -> x1, other arithmetic: 35.3 us -> 0.08 us  [per_device(): jnp.stack([c, chip, y, y if plan.ny == 2 else 0 * y]).astype(jnp.int32)]
    unnamed x100 -> x278, local copies, waits for them, and re-layouts: 21 us -> 54.7 us
    pallas_call x24, Pallas kernels: 272 us -> 242 us  [row_call(): pl.pallas_call(kernel, grid_spec=pltpu.PrefetchScalarGridSpec(num_scalar_...]
    ppermute x73 -> x54, starting transfers between devices: 63.9 us -> 41.2 us  [swap(): return lax.ppermute(v, AX, pairs)]
    pallas_call x8 -> x6, Pallas kernels: 88 us -> 68 us  [weight_grad(): pl.pallas_call(kernel, grid_spec=pltpu.PrefetchScalarGridSpec(num_scalar_...]
  transfers between devices with their start and end apart: 75 -> 56, of which waited for: 32 -> 16; matrix products, arithmetic and copies ran while one was open for 10% -> 4% of each run, Pallas kernels for 32% -> 40%
where the time goes in v2:
time: 812 us; the launch traced here: 804 us
  Pallas kernels  372 us (46%)
  waiting for transfers between devices  271 us (33%)
  local copies, waits for them, and re-layouts  93.2 us (11%)
  starting transfers between devices  41.3 us (5%)
  between operations  16.1 us (2%)
  other arithmetic  9.94 us (1%)
    pallas_call x24, Pallas kernels, row_call(): pl.pallas_call(kernel, grid_spec=pltpu.PrefetchScalarGridSpec(num_scalar_...  242 us
    ppermute x54, waiting for transfers between devices, swap(): return lax.ppermute(v, AX, pairs)  149 us
    all_gather x2, waiting for transfers between devices, per_device(): lax.all_gather(v, 'shard', axis=0, tiled=True)  121 us
    pallas_call x6, Pallas kernels, weight_grad(): pl.pallas_call(kernel, grid_spec=pltpu.PrefetchScalarGridSpec(num_scalar_...  68 us
    unnamed x278, local copies, waits for them, and re-layouts  54.7 us
    ppermute x54, starting transfers between devices, swap(): return lax.ppermute(v, AX, pairs)  41.2 us
    pallas_call x12, Pallas kernels, combine(): pl.pallas_call(kernel, grid=(cuts,), in_specs=[pl.BlockSpec(block, index)...  28.3 us
  transfers between devices with their start and end apart: 56, of which 16 were waited for; matrix products, arithmetic and copies ran while one was open for 4% of the time, Pallas kernels for 40%

profile of v2, /device:TPU:0, one launch (start us, length us, event | category | flops | bytes accessed | tf_op | source)
XLA Modules:
  0.0 803.6 jit_solution(695342490734671326)
XLA Ops:
  31.5 111.2 %all-gather.5.cloned.1.call-done.refs_0_.refs_1_.refs_2_.refs_3_ = bf16[1024,10368]{1,0:T(8,128)(2,1)} async-done(((bf16[64,10368]{1,0:T(8,128)(2,1)}), bf16[1024,10368]{1,0:T(8,128)(2,1)}) %all-gather.5.cloned.1.call-update) | async-done | bytes 21233680 | tf_op jit(solution)/shard_map/all_gather | solution.py:720
  156.0 11.4 %shard_map.256 = (bf16[2,8,320,320]{3,2,1,0:T(8,128)(2,1)S(1)}, bf16[640,512]{1,0:T(8,128)(2,1)S(1)}, f32[640,1024]{1,0:T(8,128)}) custom-call(s32[4]{0:T(128)S(1)} %pad_add_fusion.where_ref, s32[2]{0:T(128)S(1)} %collective-permute-done.2.kept_ref, bf16[8,2,64,10368]{3,2,1,0:T(8,128)(2,1)} %bitcast.101, bf16[640,1536]{1,0:T(8,128)(2,1)S(1)} %shard_map.255.refs_1_.refs_3_), custom_call_target="tpu_custom_call" | custom-call | flops 3000000000 | tf_op jit(solution)/shard_map/pallas_call | solution.py:122
  176.3 12.0 %shard_map.257 = (bf16[2,8,320,320]{3,2,1,0:T(8,128)(2,1)S(1)}, bf16[640,512]{1,0:T(8,128)(2,1)S(1)}, f32[640,1024]{1,0:T(8,128)S(1)}, bf16[640,1024]{1,0:T(8,128)(2,1)}) custom-call(s32[4]{0:T(128)S(1)} %pad_add_fusion.where_ref, s32[2]{0:T(128)S(1)} %copy-done.32, bf16[8,2,64,10368]{3,2,1,0:T(8,128)(2,1)} %bitcast.102, ...), custom_call_target="tpu_custom_call" | custom-call | flops 3000000000 | tf_op jit(solution)/shard_map/pallas_call | solution.py:122
  205.6 10.6 %collective-permute-done.1.refs_1_ = bf16[1024,1024]{1,0:T(8,128)(2,1)} collective-permute-done((bf16[1024,1024]{1,0:T(8,128)(2,1)}, bf16[1024,1024]{1,0:T(8,128)(2,1)}, u32[]{:S(2)}, u32[]{:S(2)}) %collective-permute-start.1) | collective-permute-done | bytes 2097184 | tf_op jit(solution)/shard_map/ppermute | solution.py:39
  261.9 11.4 %shard_map.264 = (bf16[2,8,320,320]{3,2,1,0:T(8,128)(2,1)S(1)}, bf16[640,512]{1,0:T(8,128)(2,1)S(1)}, f32[640,1024]{1,0:T(8,128)}) custom-call(s32[4]{0:T(128)S(1)} %pad_add_fusion.where_ref, s32[2]{0:T(128)S(1)} %collective-permute-done.2.kept_ref, bf16[8,2,64,10240]{3,2,1,0:T(8,128)(2,1)} %bitcast.105, bf16[640,1536]{1,0:T(8,128)(2,1)S(1)} %shard_map.263.refs_1_.refs_3_), custom_call_target="tpu_custom_call" | custom-call | flops 3000000000 | tf_op jit(solution)/shard_map/pallas_call | solution.py:122
  283.0 12.7 %shard_map.265 = (bf16[2,8,320,320]{3,2,1,0:T(8,128)(2,1)S(1)}, bf16[640,512]{1,0:T(8,128)(2,1)S(1)}, f32[640,1024]{1,0:T(8,128)S(1)}, bf16[640,1024]{1,0:T(8,128)(2,1)}) custom-call(s32[4]{0:T(128)S(1)} %pad_add_fusion.where_ref, s32[2]{0:T(128)S(1)} %copy-done.32, bf16[8,2,64,10240]{3,2,1,0:T(8,128)(2,1)} %bitcast.106, ...), custom_call_target="tpu_custom_call" | custom-call | flops 3000000000 | tf_op jit(solution)/shard_map/pallas_call | solution.py:122
  318.8 12.3 %shard_map.268 = (bf16[1,2,2,2,256,512]{5,4,3,2,1,0:T(8,128)(2,1)S(1)}, bf16[1,2,2,2,256,512]{5,4,3,2,1,0:T(8,128)(2,1)}) custom-call(s32[4]{0:T(128)S(1)} %pad_add_fusion.where_ref, bf16[640,2048]{1,0:T(8,128)(2,1)S(1)} %get-tuple-element.142.xo.rest_0_.refs_2_, bf16[640,2048]{1,0:T(8,128)(2,1)S(1)} %get-tuple-element.143.xt.refs_2_, ...), custom_call_target="tpu_custom_call" | custom-call | flops 99999997952 | tf_op jit(solution)/shard_map/pallas_call | solution.py:404
  331.6 17.8 %collective-permute-done.refs_1_ = bf16[1024,1024]{1,0:T(8,128)(2,1)} collective-permute-done((bf16[1024,1024]{1,0:T(8,128)(2,1)}, bf16[1024,1024]{1,0:T(8,128)(2,1)}, u32[]{:S(2)}, u32[]{:S(2)}) %collective-permute-start) | collective-permute-done | bytes 2097184 | tf_op jit(solution)/shard_map/ppermute | solution.py:39
  349.4 10.1 %shard_map.269 = (bf16[640,2048]{1,0:T(8,128)(2,1)S(1)}, f32[640,1024]{1,0:T(8,128)S(1)}) custom-call(s32[4]{0:T(128)S(1)} %pad_add_fusion.where_ref, s32[2]{0:T(128)S(1)} %collective-permute-done.2.kept_ref, bf16[1024,10240]{1,0:T(8,128)(2,1)} %all-gather.3.cloned.1.call-done.refs_0_.refs_1_.refs_2_.refs_3_, ...), custom_call_target="tpu_custom_call" | custom-call | flops 99999997952 | tf_op jit(solution)/shard_map/pallas_call | solution.py:122
  366.8 11.6 %shard_map.271 = (bf16[640,2048]{1,0:T(8,128)(2,1)S(1)}, f32[640,1024]{1,0:T(8,128)S(1)}, bf16[640,1024]{1,0:T(8,128)(2,1)S(1)}, f32[8,1024]{1,0:T(8,128)S(1)}) custom-call(s32[4]{0:T(128)S(1)} %pad_add_fusion.where_ref, s32[2]{0:T(128)S(1)} %copy-done.32, bf16[1024,10240]{1,0:T(8,128)(2,1)} %all-gather.3.cloned.1.call-done.refs_0_.refs_1_.refs_2_.refs_3_, ...), custom_call_target="tpu_custom_call" | custom-call | flops 99999997952 | tf_op jit(solution)/shard_map/pallas_call | solution.py:122
  380.4 12.1 %shard_map.272 = (bf16[2,2,1,2,128,1280]{5,4,3,2,1,0:T(8,128)(2,1)S(1)}, bf16[2,2,1,2,128,1280]{5,4,3,2,1,0:T(8,128)(2,1)S(1)}, f32[1,2048]{1,0:T(1,128)S(1)}) custom-call(s32[4]{0:T(128)S(1)} %pad_add_fusion.where_ref, bf16[640,1024]{1,0:T(8,128)(2,1)} %get-tuple-element.141.refs_2_.xo, bf16[640,1024]{1,0:T(8,128)(2,1)} %collective-permute-done.9.refs_2_.xt, ...), custom_call_target="tpu_custom_call" | custom-call | flops 99999997952 | tf_op jit(solution)/shard_map/pallas_call | solution.py:404
  401.2 14.8 %shard_map.275 = (bf16[640,1536]{1,0:T(8,128)(2,1)S(1)}, f32[640,1024]{1,0:T(8,128)}) custom-call(s32[4]{0:T(128)S(1)} %pad_add_fusion.where_ref, s32[2]{0:T(128)S(1)} %collective-permute-done.2.kept_ref, bf16[8,2,64,10240]{3,2,1,0:T(8,128)(2,1)} %bitcast.107, bf16[1024,10240]{1,0:T(8,128)(2,1)} %all-gather.3.cloned.1.call-done.refs_0_.refs_1_.refs_2_.refs_3_, ...), custom_call_target="tpu_custom_call" | custom-call | flops 99999997952 | tf_op jit(solution)/shard_map/pallas_call | solution.py:122
  435.1 16.5 %shard_map.276 = (bf16[640,1536]{1,0:T(8,128)(2,1)S(1)}, f32[640,1024]{1,0:T(8,128)S(1)}, bf16[640,1024]{1,0:T(8,128)(2,1)}, f32[8,1024]{1,0:T(8,128)S(1)}) custom-call(s32[4]{0:T(128)S(1)} %pad_add_fusion.where_ref, s32[2]{0:T(128)S(1)} %copy-done.32, bf16[8,2,64,10240]{3,2,1,0:T(8,128)(2,1)} %bitcast.108, ...), custom_call_target="tpu_custom_call" | custom-call | flops 99999997952 | tf_op jit(solution)/shard_map/pallas_call | solution.py:122
  469.6 12.0 %shard_map.279 = (bf16[640,2048]{1,0:T(8,128)(2,1)S(1)}, f32[640,1024]{1,0:T(8,128)}) custom-call(s32[4]{0:T(128)S(1)} %pad_add_fusion.where_ref, s32[2]{0:T(128)S(1)} %collective-permute-done.2.kept_ref, bf16[1024,10368]{1,0:T(8,128)(2,1)} %all-gather.5.cloned.1.call-done.refs_0_.refs_1_.refs_2_.refs_3_, bf16[1024,1024]{1,0:T(8,128)(2,1)} %collective-permute-done.1.refs_1_, ...), custom_call_target="tpu_custom_call" | custom-call | flops 99999997952 | tf_op jit(solution)/shard_map/pallas_call | solution.py:122
  481.7 12.4 %shard_map.280 = (bf16[1,2,2,2,256,512]{5,4,3,2,1,0:T(8,128)(2,1)S(1)}, bf16[1,2,2,2,256,512]{5,4,3,2,1,0:T(8,128)(2,1)}) custom-call(s32[4]{0:T(128)S(1)} %pad_add_fusion.where_ref, bf16[640,2048]{1,0:T(8,128)(2,1)S(1)} %copy-done.22, bf16[640,2048]{1,0:T(8,128)(2,1)S(1)} %copy-done.20, bf16[640,1024]{1,0:T(8,128)(2,1)} %get-tuple-element.164.yo.refs_4_, ...), custom_call_target="tpu_custom_call" | custom-call | flops 99999997952 | tf_op jit(solution)/shard_map/pallas_call | solution.py:404
  506.2 13.2 %shard_map.283 = (bf16[640,2048]{1,0:T(8,128)(2,1)S(1)}, f32[640,1024]{1,0:T(8,128)S(1)}, bf16[640,1024]{1,0:T(8,128)(2,1)}, f32[8,1024]{1,0:T(8,128)S(1)}) custom-call(s32[4]{0:T(128)S(1)} %pad_add_fusion.where_ref, s32[2]{0:T(128)S(1)} %copy-done.32, bf16[1024,10368]{1,0:T(8,128)(2,1)} %all-gather.5.cloned.1.call-done.refs_0_.refs_1_.refs_2_.refs_3_, ...), custom_call_target="tpu_custom_call" | custom-call | flops 99999997952 | tf_op jit(solution)/shard_map/pallas_call | solution.py:122
  523.6 12.8 %shard_map.285 = (bf16[2,2,2,1,128,1280]{5,4,3,2,1,0:T(8,128)(2,1)S(1)}, bf16[2,2,2,1,128,1280]{5,4,3,2,1,0:T(8,128)(2,1)}, f32[1,2048]{1,0:T(1,128)S(1)}) custom-call(s32[4]{0:T(128)S(1)} %pad_add_fusion.where_ref, bf16[640,1024]{1,0:T(8,128)(2,1)} %get-tuple-element.134.refs_2_.xo, bf16[640,1024]{1,0:T(8,128)(2,1)} %collective-permute-done.5.refs_2_.xt, ...), custom_call_target="tpu_custom_call" | custom-call | flops 99999997952 | tf_op jit(solution)/shard_map/pallas_call | solution.py:404
  557.6 15.0 %shard_map.289 = (bf16[640,1536]{1,0:T(8,128)(2,1)S(1)}, f32[640,1024]{1,0:T(8,128)}) custom-call(s32[4]{0:T(128)S(1)} %pad_add_fusion.where_ref, s32[2]{0:T(128)S(1)} %collective-permute-done.2.kept_ref, bf16[8,2,64,10368]{3,2,1,0:T(8,128)(2,1)} %bitcast.103, bf16[1024,10368]{1,0:T(8,128)(2,1)} %all-gather.5.cloned.1.call-done.refs_0_.refs_1_.refs_2_.refs_3_, ...), custom_call_target="tpu_custom_call" | custom-call | flops 99999997952 | tf_op jit(solution)/shard_map/pallas_call | solution.py:122
  582.7 17.3 %shard_map.293 = (bf16[640,1536]{1,0:T(8,128)(2,1)S(1)}, f32[640,1024]{1,0:T(8,128)}, bf16[640,1024]{1,0:T(8,128)(2,1)}, f32[8,1024]{1,0:T(8,128)S(1)}) custom-call(s32[4]{0:T(128)S(1)} %pad_add_fusion.where_ref, s32[2]{0:T(128)S(1)} %copy-done.32, bf16[8,2,64,10368]{3,2,1,0:T(8,128)(2,1)} %bitcast.104, ...), custom_call_target="tpu_custom_call" | custom-call | flops 99999997952 | tf_op jit(solution)/shard_map/pallas_call | solution.py:122
  619.0 19.2 %collective-permute-done.33 = f32[2,16,768]{2,1,0:T(8,128)S(1)} collective-permute-done((f32[2,16,768]{2,1,0:T(8,128)S(1)}, f32[2,16,768]{2,1,0:T(8,128)S(1)}, u32[]{:S(2)}, u32[]{:S(2)}) %collective-permute-start.33) | collective-permute-done | bytes 98336 | tf_op jit(solution)/shard_map/ppermute | solution.py:39
  640.9 33.7 %collective-permute-done.34 = f32[2,16,768]{2,1,0:T(8,128)S(1)} collective-permute-done((f32[2,16,768]{2,1,0:T(8,128)S(1)}, f32[2,16,768]{2,1,0:T(8,128)S(1)}, u32[]{:S(2)}, u32[]{:S(2)}) %collective-permute-start.34) | collective-permute-done | bytes 98336 | tf_op jit(solution)/shard_map/ppermute | solution.py:39
  705.6 11.9 %collective-permute-done.41.g = bf16[1,2,2,1,128,1280]{5,4,3,2,1,0:T(8,128)(2,1)} collective-permute-done((bf16[1,2,2,1,128,1280]{5,4,3,2,1,0:T(8,128)(2,1)}, bf16[1,2,2,1,128,1280]{5,4,3,2,1,0:T(8,128)(2,1)}, u32[]{:S(2)}, u32[]{:S(2)}) %collective-permute-start.41) | collective-permute-done | bytes 1310752 | tf_op jit(solution)/shard_map/ppermute | solution.py:39
  749.9 18.7 %collective-permute-done.49.refs_1_ = bf16[128,2048]{1,0:T(8,128)(2,1)} collective-permute-done((bf16[128,2048]{1,0:T(8,128)(2,1)}, bf16[128,2048]{1,0:T(8,128)(2,1)}, u32[]{:S(2)}, u32[]{:S(2)}) %collective-permute-start.49) | collective-permute-done | bytes 524320 | tf_op jit(solution)/shard_map/ppermute | solution.py:39
  778.7 14.9 %collective-permute-done.48.refs_1_ = bf16[64,2048]{1,0:T(8,128)(2,1)S(1)} collective-permute-done((bf16[64,2048]{1,0:T(8,128)(2,1)S(1)}, bf16[64,2048]{1,0:T(8,128)(2,1)S(1)}, u32[]{:S(2)}, u32[]{:S(2)}) %collective-permute-start.48) | collective-permute-done | bytes 262176 | tf_op jit(solution)/shard_map/ppermute | solution.py:39
  (564 shorter events, 341.7 us)
Async XLA Ops:
  7.2 135.5 %all-gather.5.cloned.1.call-start = ((), (), s32[]{:S(2)}) async-start(), calls=%async_computation.1 | async-start | bytes 22560768 | tf_op jit(solution)/shard_map/all_gather | solution.py:720
  29.8 223.9 %all-gather.3.cloned.1.call-start = ((), (), s32[]{:S(2)}) async-start(), calls=%async_computation | async-start | bytes 22282240 | tf_op jit(solution)/shard_map/all_gather | solution.py:720
  168.2 48.0 %collective-permute-start.1 = (bf16[1024,1024]{1,0:T(8,128)(2,1)}, bf16[1024,1024]{1,0:T(8,128)(2,1)}, u32[]{:S(2)}, u32[]{:S(2)}) collective-permute-start(bf16[1024,1024]{1,0:T(8,128)(2,1)} %constant_dynamic-slice_fusion.1.refs_3_), channel_id=1, source_target_pairs={{0,1},{1,0},{2,3},{3,2},{4,5},{5,4},{6,7},{7,6},{8,9},{9,8},{10,11... | collective-permute-start | bytes 6291464 | tf_op jit(solution)/shard_map/ppermute | solution.py:39
  300.6 48.8 %collective-permute-start = (bf16[1024,1024]{1,0:T(8,128)(2,1)}, bf16[1024,1024]{1,0:T(8,128)(2,1)}, u32[]{:S(2)}, u32[]{:S(2)}) collective-permute-start(bf16[1024,1024]{1,0:T(8,128)(2,1)} %constant_dynamic-slice_fusion.2.refs_3_), channel_id=1, source_target_pairs={{0,1},{1,0},{2,3},{3,2},{4,5},{5,4},{6,7},{7,6},{8,9},{9,8},{10,11... | collective-permute-start | bytes 6291464 | tf_op jit(solution)/shard_map/ppermute | solution.py:39
  331.1 64.5 %collective-permute-start.14 = (bf16[1,2,2,2,256,512]{5,4,3,2,1,0:T(8,128)(2,1)}, bf16[1,2,2,2,256,512]{5,4,3,2,1,0:T(8,128)(2,1)}, u32[]{:S(2)}, u32[]{:S(2)}) collective-permute-start(bf16[1,2,2,2,256,512]{5,4,3,2,1,0:T(8,128)(2,1)} %get-tuple-element.145.refs_6_), channel_id=1, source_target_pairs={{0,1},{1,0},{2,3},{3,2},{4,5},{5,4},{6,7},{7,6},{8,9},{9,8},{10,11... | collective-permute-start | bytes 6291464 | tf_op jit(solution)/shard_map/ppermute | solution.py:39
  422.4 29.3 %collective-permute-start.17 = (bf16[1,2,2,1,256,512]{5,4,3,2,1,0:T(8,128)(2,1)}, bf16[1,2,2,1,256,512]{5,4,3,2,1,0:T(8,128)(2,1)S(1)}, u32[]{:S(2)}, u32[]{:S(2)}) collective-permute-start(bf16[1,2,2,1,256,512]{5,4,3,2,1,0:T(8,128)(2,1)} %copy-done.54), channel_id=1, source_target_pairs={{0,4},{1,5},{2,6},{3,7},{4,0},{5,1},{6,2},{7,3},{8,12},{9,13},{10,... | collective-permute-start | bytes 3145736 | tf_op jit(solution)/shard_map/ppermute | solution.py:39
  423.6 77.0 %collective-permute-start.19 = (bf16[2,2,1,2,128,1280]{5,4,3,2,1,0:T(8,128)(2,1)}, bf16[2,2,1,2,128,1280]{5,4,3,2,1,0:T(8,128)(2,1)}, u32[]{:S(2)}, u32[]{:S(2)}) collective-permute-start(bf16[2,2,1,2,128,1280]{5,4,3,2,1,0:T(8,128)(2,1)} %copy-done.50), channel_id=1, source_target_pairs={{0,8},{1,9},{2,10},{3,11},{4,12},{5,13},{6,14},{7,15},{8,0},{9,1},... | collective-permute-start | bytes 7864328 | tf_op jit(solution)/shard_map/ppermute | solution.py:39
  453.5 42.1 %collective-permute-start.20 = (bf16[1,2,1,1,256,512]{5,4,3,2,1,0:T(8,128)(2,1)}, bf16[1,2,1,1,256,512]{5,4,3,2,1,0:T(8,128)(2,1)}, u32[]{:S(2)}, u32[]{:S(2)}) collective-permute-start(bf16[1,2,1,1,256,512]{5,4,3,2,1,0:T(8,128)(2,1)} %get-tuple-element.169.rest_1_), channel_id=1, source_target_pairs={{0,8},{1,9},{2,10},{3,11},{4,12},{5,13},{6,14},{7,15},{8,0},{9,1},... | collective-permute-start | bytes 1572872 | tf_op jit(solution)/shard_map/ppermute | solution.py:39
  465.2 54.2 %collective-permute-start.22 = (bf16[2,2,2,1,128,768]{5,4,3,2,1,0:T(8,128)(2,1)}, bf16[2,2,2,1,128,768]{5,4,3,2,1,0:T(8,128)(2,1)}, u32[]{:S(2)}, u32[]{:S(2)}) collective-permute-start(bf16[2,2,2,1,128,768]{5,4,3,2,1,0:T(8,128)(2,1)} %get-tuple-element.170.refs_6_), channel_id=1, source_target_pairs={{0,4},{1,5},{2,6},{3,7},{4,0},{5,1},{6,2},{7,3},{8,12},{9,13},{10,... | collective-permute-start | bytes 4718600 | tf_op jit(solution)/shard_map/ppermute | solution.py:39
  494.1 81.6 %collective-permute-start.26 = (bf16[1,2,2,2,256,512]{5,4,3,2,1,0:T(8,128)(2,1)}, bf16[1,2,2,2,256,512]{5,4,3,2,1,0:T(8,128)(2,1)}, u32[]{:S(2)}, u32[]{:S(2)}) collective-permute-start(bf16[1,2,2,2,256,512]{5,4,3,2,1,0:T(8,128)(2,1)} %get-tuple-element.174.rest_0_.refs_2_.refs_10_), channel_id=1, source_target_pairs={{0,1},{1,0},{2,3},{3,2},{4,5},{5,4},{6,7},{7,6},{8,9},{9,8},{10,11... | collective-permute-start | bytes 6291464 | tf_op jit(solution)/shard_map/ppermute | solution.py:39
  498.2 54.0 %collective-permute-start.24 = (bf16[128,1024]{1,0:T(8,128)(2,1)}, bf16[128,1024]{1,0:T(8,128)(2,1)}, u32[]{:S(2)}, u32[]{:S(2)}) collective-permute-start(bf16[128,1024]{1,0:T(8,128)(2,1)} %get-tuple-element.178.refs_12_), channel_id=1, source_target_pairs={{0,16},{1,17},{2,18},{3,19},{4,20},{5,21},{6,22},{7,23},{8,24},{9,... | collective-permute-start | bytes 786440 | tf_op jit(solution)/shard_map/ppermute | solution.py:39
  505.0 68.2 %collective-permute-start.27 = (bf16[2,2,1,1,128,1280]{5,4,3,2,1,0:T(8,128)(2,1)}, bf16[2,2,1,1,128,1280]{5,4,3,2,1,0:T(8,128)(2,1)}, u32[]{:S(2)}, u32[]{:S(2)}) collective-permute-start(bf16[2,2,1,1,128,1280]{5,4,3,2,1,0:T(8,128)(2,1)} %get-tuple-element.176.refs_11_), channel_id=1, source_target_pairs={{0,4},{1,5},{2,6},{3,7},{4,0},{5,1},{6,2},{7,3},{8,12},{9,13},{10,... | collective-permute-start | bytes 3932168 | tf_op jit(solution)/shard_map/ppermute | solution.py:39
  522.9 31.6 %collective-permute-start.23 = (bf16[2,2,1,1,128,768]{5,4,3,2,1,0:T(8,128)(2,1)}, bf16[2,2,1,1,128,768]{5,4,3,2,1,0:T(8,128)(2,1)}, u32[]{:S(2)}, u32[]{:S(2)}) collective-permute-start(bf16[2,2,1,1,128,768]{5,4,3,2,1,0:T(8,128)(2,1)} %get-tuple-element.186.rest_1_), channel_id=1, source_target_pairs={{0,8},{1,9},{2,10},{3,11},{4,12},{5,13},{6,14},{7,15},{8,0},{9,1},... | collective-permute-start | bytes 2359304 | tf_op jit(solution)/shard_map/ppermute | solution.py:39
  550.8 62.7 %collective-permute-start.29 = (bf16[2,2,2,1,128,1280]{5,4,3,2,1,0:T(8,128)(2,1)}, bf16[2,2,2,1,128,1280]{5,4,3,2,1,0:T(8,128)(2,1)}, u32[]{:S(2)}, u32[]{:S(2)}) collective-permute-start(bf16[2,2,2,1,128,1280]{5,4,3,2,1,0:T(8,128)(2,1)} %get-tuple-element.189.rest_0_.refs_2_.refs_5_), channel_id=1, source_target_pairs={{0,4},{1,5},{2,6},{3,7},{4,0},{5,1},{6,2},{7,3},{8,12},{9,13},{10,... | collective-permute-start | bytes 7864328 | tf_op jit(solution)/shard_map/ppermute | solution.py:39
  610.4 67.7 %collective-permute-start.11 = (f32[640,1024]{1,0:T(8,128)}, f32[640,1024]{1,0:T(8,128)}, u32[]{:S(2)}, u32[]{:S(2)}) collective-permute-start(f32[640,1024]{1,0:T(8,128)} %shard_map.270.refs_10_), channel_id=1, source_target_pairs={{0,2},{1,3},{2,0},{3,1},{4,6},{5,7},{6,4},{7,5},{8,10},{9,11},{10,... | collective-permute-start | bytes 7864328 | tf_op jit(solution)/shard_map/ppermute | solution.py:39
  610.9 28.5 %collective-permute-start.31 = (bf16[1,2,1,1,128,1280]{5,4,3,2,1,0:T(8,128)(2,1)S(1)}, bf16[1,2,1,1,128,1280]{5,4,3,2,1,0:T(8,128)(2,1)S(1)}, u32[]{:S(2)}, u32[]{:S(2)}) collective-permute-start(bf16[1,2,1,1,128,1280]{5,4,3,2,1,0:T(8,128)(2,1)S(1)} %get-tuple-element.200.refs_11_), channel_id=1, source_target_pairs={{0,1},{1,0},{2,3},{3,2},{4,5},{5,4},{6,7},{7,6},{8,9},{9,8},{10,11... | collective-permute-start | bytes 1966088 | tf_op jit(solution)/shard_map/ppermute | solution.py:39
  611.5 27.3 %collective-permute-start.30 = (bf16[1,2,1,1,128,768]{5,4,3,2,1,0:T(8,128)(2,1)S(1)}, bf16[1,2,1,1,128,768]{5,4,3,2,1,0:T(8,128)(2,1)S(1)}, u32[]{:S(2)}, u32[]{:S(2)}) collective-permute-start(bf16[1,2,1,1,128,768]{5,4,3,2,1,0:T(8,128)(2,1)S(1)} %copy-done.62), channel_id=1, source_target_pairs={{0,1},{1,0},{2,3},{3,2},{4,5},{5,4},{6,7},{7,6},{8,9},{9,8},{10,11... | collective-permute-start | bytes 1179656 | tf_op jit(solution)/shard_map/ppermute | solution.py:39
  612.9 78.1 %collective-permute-start.37 = (bf16[1,2,2,1,256,512]{5,4,3,2,1,0:T(8,128)(2,1)}, bf16[1,2,2,1,256,512]{5,4,3,2,1,0:T(8,128)(2,1)}, u32[]{:S(2)}, u32[]{:S(2)}) collective-permute-start(bf16[1,2,2,1,256,512]{5,4,3,2,1,0:T(8,128)(2,1)} %copy-done.53), channel_id=1, source_target_pairs={{0,4},{1,5},{2,6},{3,7},{4,0},{5,1},{6,2},{7,3},{8,12},{9,13},{10,... | collective-permute-start | bytes 3145736 | tf_op jit(solution)/shard_map/ppermute | solution.py:39
  638.1 107.8 %collective-permute-start.50 = (bf16[64,2048]{1,0:T(8,128)(2,1)}, bf16[64,2048]{1,0:T(8,128)(2,1)}, u32[]{:S(2)}, u32[]{:S(2)}) collective-permute-start(bf16[64,2048]{1,0:T(8,128)(2,1)} %shard_map.292.refs_12_.refs_0_), channel_id=1, source_target_pairs={{0,1},{1,0},{2,3},{3,2},{4,5},{5,4},{6,7},{7,6},{8,9},{9,8},{10,11... | collective-permute-start | bytes 786440 | tf_op jit(solution)/shard_map/ppermute | solution.py:39
  638.8 63.1 %collective-permute-start.42 = (bf16[2,2,1,2,128,768]{5,4,3,2,1,0:T(8,128)(2,1)}, bf16[2,2,1,2,128,768]{5,4,3,2,1,0:T(8,128)(2,1)}, u32[]{:S(2)}, u32[]{:S(2)}) collective-permute-start(bf16[2,2,1,2,128,768]{5,4,3,2,1,0:T(8,128)(2,1)} %get-tuple-element.203.rest_0_.refs_4_.refs_6_), channel_id=1, source_target_pairs={{0,8},{1,9},{2,10},{3,11},{4,12},{5,13},{6,14},{7,15},{8,0},{9,1},... | collective-permute-start | bytes 4718600 | tf_op jit(solution)/shard_map/ppermute | solution.py:39
  639.4 35.2 %collective-permute-start.34 = (f32[2,16,768]{2,1,0:T(8,128)S(1)}, f32[2,16,768]{2,1,0:T(8,128)S(1)}, u32[]{:S(2)}, u32[]{:S(2)}) collective-permute-start(f32[2,16,768]{2,1,0:T(8,128)S(1)} %add.67.rest_1_), channel_id=1, source_target_pairs={{0,16},{1,17},{2,18},{3,19},{4,20},{5,21},{6,22},{7,23},{8,24},{9,... | collective-permute-start | bytes 294920 | tf_op jit(solution)/shard_map/ppermute | solution.py:39
  674.6 25.0 %collective-permute-start.39 = (bf16[128,2048]{1,0:T(8,128)(2,1)}, bf16[128,2048]{1,0:T(8,128)(2,1)}, u32[]{:S(2)}, u32[]{:S(2)}) collective-permute-start(bf16[128,2048]{1,0:T(8,128)(2,1)} %get-tuple-element.208.refs_8_), channel_id=1, source_target_pairs={{0,16},{1,17},{2,18},{3,19},{4,20},{5,21},{6,22},{7,23},{8,24},{9,... | collective-permute-start | bytes 1572872 | tf_op jit(solution)/shard_map/ppermute | solution.py:39
  689.6 27.9 %collective-permute-start.41 = (bf16[1,2,2,1,128,1280]{5,4,3,2,1,0:T(8,128)(2,1)}, bf16[1,2,2,1,128,1280]{5,4,3,2,1,0:T(8,128)(2,1)}, u32[]{:S(2)}, u32[]{:S(2)}) collective-permute-start(bf16[1,2,2,1,128,1280]{5,4,3,2,1,0:T(8,128)(2,1)} %get-tuple-element.205.refs_7_), channel_id=1, source_target_pairs={{0,1},{1,0},{2,3},{3,2},{4,5},{5,4},{6,7},{7,6},{8,9},{9,8},{10,11... | collective-permute-start | bytes 3932168 | tf_op jit(solution)/shard_map/ppermute | solution.py:39
  695.8 30.3 %collective-permute-start.38 = (bf16[1,2,1,1,256,512]{5,4,3,2,1,0:T(8,128)(2,1)}, bf16[1,2,1,1,256,512]{5,4,3,2,1,0:T(8,128)(2,1)}, u32[]{:S(2)}, u32[]{:S(2)}) collective-permute-start(bf16[1,2,1,1,256,512]{5,4,3,2,1,0:T(8,128)(2,1)} %get-tuple-element.220.refs_2_), channel_id=1, source_target_pairs={{0,8},{1,9},{2,10},{3,11},{4,12},{5,13},{6,14},{7,15},{8,0},{9,1},... | collective-permute-start | bytes 1572872 | tf_op jit(solution)/shard_map/ppermute | solution.py:39
  (164 other events, 1572.9 us)
Sparse Core Ops, SparseCore 0:
  29.9 112.7 all-gather.4
  144.9 108.8 all-gather.2

commit v3 on v2

--- a/solution.py
+++ b/solution.py
@@ -18,8 +18,8 @@
 LIMIT = 32 * 2**20
 ONCE = pl.Buffered(1)
 ANY = pl.BlockSpec(memory_space=pl.ANY)
-FORWARD = pl.CostEstimate(flops=10**9 * 3, bytes_accessed=0, transcendentals=0)
-BACKWARD = pl.CostEstimate(flops=10**9 * 100, bytes_accessed=0, transcendentals=0)
+FORWARD = pl.CostEstimate(flops=10**9, bytes_accessed=0, transcendentals=0)
+BACKWARD = pl.CostEstimate(flops=10**9 * 30, bytes_accessed=0, transcendentals=0)
 SMALL = ("ag", "as", "qvb", "pb", "mg", "ms", "f1b", "f2b")
 
 
@@ -320,12 +320,12 @@
     add_sums(outs[3], [gain, shift, jnp.sum(low.astype(F32), axis=0, keepdims=True)])
 
 
-def weight_grad(plan, where, xs, ys, groups, first, sums=False, extra=0, relative=False, after=()):
+def weight_grad(plan, where, xs, ys, groups, first, sums=False, extra=0, relative=False, window=(0, 1), after=()):
     depth, n_x = xs[0].shape
     cols = ys[0].shape[1]
     ny, chips, bits = plan.ny, plan.chips, plan.bits
     half = cols // ny
-    size = half
+    size = half // window[1]
     chunk = size if size <= 768 else 512
     steps = size // chunk
     rows = n_x // chips
@@ -385,7 +385,7 @@
 
     def column(i, w):
         own = w[2] if ny == 2 and not relative else 0
-        return jnp.bitwise_xor(i // steps, own) * per_rep + i % steps
+        return jnp.bitwise_xor(i // steps, own) * per_rep + window[0] * steps + i % steps
 
     zeros = (0,) * (bits + 1)
     x_spec = pl.BlockSpec((depth, n_x), lambda i, w: (0, 0), pipeline_mode=ONCE)
@@ -399,8 +399,11 @@
         ]
     out_shape = [jax.ShapeDtypeStruct(shape, BF)] * 2
     if sums:
-        specs = specs + [pl.BlockSpec((1, chunk), lambda i, w: (0, column(i, w)))]
-        out_shape = out_shape + [jax.ShapeDtypeStruct((1, cols), F32)]
+        own = (lambda w: w[2]) if ny == 2 and not relative else (lambda w: 0)
+        specs = specs + [
+            pl.BlockSpec((1, chunk), lambda i, w: (0, jnp.bitwise_xor(i // steps, own(w)) * steps + i % steps))
+        ]
+        out_shape = out_shape + [jax.ShapeDtypeStruct((1, size * ny), F32)]
     return pl.pallas_call(
         kernel,
         grid_spec=pltpu.PrefetchScalarGridSpec(
@@ -416,7 +419,49 @@
     )(where, *xs, *ys, *after)
 
 
-def proj_grad_into(plan, where, xs, ys, first, keep, send):
+def chip_grad(plan, where, xs, ys, groups, after=()):
+    depth, n_x = xs[0].shape
+    cols = ys[0].shape[1]
+    chips = plan.chips
+    chunk = min(cols, 512)
+    rows = n_x // chips
+    part = rows // groups
+    n_after = len(after)
+
+    def kernel(where_ref, xo, xt, yo, yt, *rest):
+        out, flip, acc = rest[n_after:]
+
+        @pl.when(pl.program_id(0) == 0)
+        def _():
+            flip[:, :depth] = xo[...].T
+            flip[:, depth:] = xt[...].T
+
+        acc[...] = dot(flip[:, :depth], yo[...]) + dot(flip[:, depth:], yt[...])
+        for g in range(groups):
+            place = jnp.bitwise_xor(g, where_ref[3]) * part
+            for chip in range(chips):
+                at = pl.ds(pl.multiple_of(place + chip * rows, 16), part)
+                first = (g * chips + chip) * part
+                out[at, :] = acc[first : first + part].astype(BF)
+
+    x_spec = pl.BlockSpec((depth, n_x), lambda i, w: (0, 0), pipeline_mode=ONCE)
+    y_spec = pl.BlockSpec((depth, chunk), lambda i, w: (0, i))
+    return pl.pallas_call(
+        kernel,
+        grid_spec=pltpu.PrefetchScalarGridSpec(
+            num_scalar_prefetch=1,
+            grid=(cols // chunk,),
+            in_specs=[x_spec, x_spec, y_spec, y_spec] + [ANY] * n_after,
+            out_specs=pl.BlockSpec((n_x, chunk), lambda i, w: (0, i)),
+            scratch_shapes=[pltpu.VMEM((n_x, 2 * depth), BF), pltpu.VMEM((n_x, chunk), F32)],
+        ),
+        out_shape=jax.ShapeDtypeStruct((n_x, cols), BF),
+        compiler_params=pltpu.CompilerParams(vmem_limit_bytes=LIMIT),
+        cost_estimate=BACKWARD,
+    )(where, *xs, *ys, *after)
+
+
+def proj_grad_into(plan, where, xs, ys, first, keep, send, after=()):
     depth, n_x = xs[0].shape
     cols = ys[0].shape[1]
     ny, chips, bits = plan.ny, plan.chips, plan.bits
@@ -427,29 +472,47 @@
     at_col = keep.shape[-1] // width - 1
     block = [1] + list(keep.shape[1:-1]) + [width]
 
-    def kernel(where_ref, xo, xt, yo, yt, k_in, s_in, keep_ref, send_ref, acc):
+    n_after = len(after)
+
+    def kernel(where_ref, xo, xt, yo, yt, k_in, s_in, *rest):
+        keep_ref, send_ref, acc = rest[n_after:]
         acc[...] = t_dot(xo[...], yo[...]) + t_dot(xt[...], yt[...])
-        for r in range(chips):
+
+        def put(ref, r):
             at = [0]
             for k in range(1, bits + 1):
                 at.append((r >> (bits - k)) & 1 if k != first else 0)
-            ref = send_ref if (r >> (bits - first)) & 1 else keep_ref
             start = pl.multiple_of(jnp.bitwise_xor(where_ref[1], r) * part, 16)
             for g in range(stacked):
                 piece = acc[pl.ds(start, part), g * width : (g + 1) * width]
                 ref[tuple(at) + (pl.ds(g * part, part),)] = piece.astype(BF)
 
+        if first:
+            for r in range(chips):
+                put(send_ref if (r >> (bits - first)) & 1 else keep_ref, r)
+        else:
+
+            @pl.when(pl.program_id(0) == 0)
+            def _():
+                for r in range(chips):
+                    put(keep_ref, r)
+
+            @pl.when(pl.program_id(0) != 0)
+            def _():
+                for r in range(chips):
+                    put(send_ref, r)
+
     zeros = (0,) * (bits + 1)
     own = (lambda w: w[2]) if ny == 2 else (lambda w: 0)
     x_spec = pl.BlockSpec((depth, n_x), lambda i, w: (0, 0), pipeline_mode=ONCE)
     y_spec = pl.BlockSpec((depth, half), lambda i, w: (0, jnp.bitwise_xor(i, own(w))))
-    spec = pl.BlockSpec(block, lambda i, w: (i,) + zeros + (at_col,))
+    spec = pl.BlockSpec(block, lambda i, w: (i if first else 0,) + zeros + (at_col,))
     return pl.pallas_call(
         kernel,
         grid_spec=pltpu.PrefetchScalarGridSpec(
             num_scalar_prefetch=1,
             grid=(ny,),
-            in_specs=[x_spec, x_spec, y_spec, y_spec, ANY, ANY],
+            in_specs=[x_spec, x_spec, y_spec, y_spec, ANY, ANY] + [ANY] * n_after,
             out_specs=[spec, spec],
             scratch_shapes=[pltpu.VMEM((n_x, half), F32)],
         ),
@@ -457,7 +520,7 @@
         input_output_aliases={5: 0, 6: 1},
         compiler_params=pltpu.CompilerParams(vmem_limit_bytes=LIMIT),
         cost_estimate=BACKWARD,
-    )(where, *xs, *ys, keep, send)
+    )(where, *xs, *ys, keep, send, *after)
 
 
 class Term:
@@ -596,11 +659,45 @@
         return v
 
 
+class ChipEnding:
+    def __init__(self, plan, where, term):
+        self.plan, self.where = plan, where
+        groups = [[2 * chip + c for chip in range(plan.chips)] for c in range(2)]
+        self.term = lax.psum_scatter(term, "shard", scatter_dimension=0, axis_index_groups=groups, tiled=True)
+
+    def core(self, after):
+        rows, cols = self.term.shape
+        part = rows // 4
+
+        def kernel(where, ins, outs):
+            c = where[0]
+            for ref, row in ((outs[0], c), (outs[1], 1 - c)):
+                for k in range(2):
+                    at = pl.ds(pl.multiple_of((2 * k + row) * part, 16), part)
+                    ref[k * part : (k + 1) * part] = ins[0][at]
+
+        shapes = [((rows // 2, cols), BF)] * 2
+        self.mine, sent = small_call(kernel, self.where, [self.term], shapes, after)
+        self.came = self.plan.core(sent)
+        return sent
+
+    def rep(self, after):
+        rows, cols = self.mine.shape
+
+        def kernel(where, ins, outs):
+            outs[0][:rows] = ins[0][...]
+            outs[0][rows:] = ins[1][...]
+
+        v = small_call(kernel, self.where, [self.mine, self.came], [((2 * rows, cols), BF)], after)[0]
+        self.pair = [v, self.plan.flip(v, 0)] if self.plan.ny == 2 else [lax.psum(v, "rep")]
+        return v
+
+
 def place_grads(plan, where, layer, layers, end2, rest, sizes, before, after):
     deep, width, ff, quarters = sizes
     n, ny, halves = plan.shards, plan.ny, quarters // 2
     wide, half_ff = 3 * width // 2, ff // 2
-    cols2, cols = end2.cols, rest.cols
+    cols = rest.cols
     fused = bool(rest.tail)
     ins = end2.pair + rest.pair
 
@@ -609,19 +706,18 @@
         outs = refs[-(4 if fused else 3) :]
         c, y = where_ref[0], where_ref[2]
 
-        def source(group, p, q, at, size):
-            total = (cols2, cols)[group]
+        def source(p, q, at, size):
             step = (at // 128) * 128
             span = (at + size - step + 127) // 128 * 128
-            first = pl.multiple_of(jnp.where(p == c, 0, total) + step, 128)
-            v = refs_in[group * ny][:, pl.ds(first, span)]
+            first = pl.multiple_of(jnp.where(p == c, 0, cols) + step, 128)
+            v = refs_in[ny][:, pl.ds(first, span)]
             if ny == 2:
-                v = jnp.where(y == q, v, refs_in[group * ny + 1][:, pl.ds(first, span)])
+                v = jnp.where(y == q, v, refs_in[ny + 1][:, pl.ds(first, span)])
             return v[:, at - step : at - step + size].astype(F32)
 
         def core_columns(p, at, size, total, first):
             part = total // ny
-            return source(1, p, at // part, first + at % part, size)
+            return source(p, at // part, first + at % part, size)
 
         for k in range(3 * HEADS // 2):
             pieces = [core_columns(p, k * HEAD_DIM, HEAD_DIM, wide, 0) for p in range(2)]
@@ -634,10 +730,11 @@
             outs[1][0, :, k * quarters * deep : (k + 1) * quarters * deep] = jnp.concatenate(pieces, axis=1)
         part = width // ny
         for p in range(2):
-            for h in range(halves):
-                for q in range(ny):
-                    at = pl.ds((p * halves + h) * deep, deep)
-                    outs[2][0, at, q * part : (q + 1) * part] = source(0, p, q, h * part, part)
+            at = pl.ds(pl.multiple_of(jnp.where(p == c, 0, halves * deep), 16), halves * deep)
+            v = refs_in[0][at].astype(F32)
+            if ny == 2:
+                v = v + refs_in[1][at].astype(F32)
+            outs[2][0, p * halves * deep : (p + 1) * halves * deep] = v
         if fused:
             for q in range(ny):
                 v = refs_in[ny][:, 2 * cols :]
@@ -716,7 +813,7 @@
         fc2 = [fc2[p, k] for p in range(2) for k in range(each)]
         return [qkv, proj_weight[layer], fc1] + fc2 + ([] if layer else [extra])
 
-    operands = lax.optimization_barrier([jnp.concatenate(merged(layer), axis=1) for layer in range(layers)])
+    operands = [jnp.concatenate(merged(layer), axis=1) for layer in range(layers)]
     gathered = [lax.all_gather(v, "shard", axis=0, tiled=True) for v in operands]
     at_fc1, at_fc2 = lead // block, (lead + ff) // block
     mlp_parts = []
@@ -726,7 +823,7 @@
         if plan.ny == 2:
             mine = lax.dynamic_slice_in_dim(gathered[layer], (at_fc2 + c) * block, block, axis=1)
             found["fc2"].append((plan.flip(mine, 0), None))
-            found["sent"] = (mine,)
+            found["sent"], found["came"] = (mine,), (found["fc2"][-1][0],)
         mlp_parts.append(found)
 
     def weight_of(layer, name):
@@ -784,7 +881,8 @@
         probs_own, att_own, middle, second_own = call(
             attend_own, layer, 1, ["proj"], [proj_own, part, state], [v["pb"], v["mg"], v["ms"]], att_outs + [f32_rows, low_rows])
         second_oth = plan.core(second_own)
-        hid_oth, slope_oth = call(up_body, layer, 0, ["fc1"], [second_oth], [v["f1b_c"]], [ff_rows] * 2)
+        came = mlp_parts[layer].get("came", ())
+        hid_oth, slope_oth = call(up_body, layer, 0, ["fc1"], [second_oth], [v["f1b_c"]], [ff_rows] * 2, came, FORWARD)
         if layer + 1 < layers:
             part = call(down_other, layer, 0, ["fc2"], [hid_oth], [], [f32_rows])[0]
             part = plan.core(part)
@@ -810,9 +908,8 @@
     axes = list(range(1 if plan.ny == 1 else 0, plan.bits + 1))
     last_axis, z_axis, x_axis = 1, plan.bits - 1, plan.bits
     y_axis = 0 if plan.ny == 2 else 2
-    order_f2 = [y_axis, x_axis, z_axis]
-    orders_f1 = [[x_axis, y_axis, z_axis]] + [[z_axis, x_axis, y_axis]] * (layers - 1)
-    orders_q = [[z_axis, x_axis, y_axis]] + [[x_axis, z_axis, y_axis]] * (layers - 1)
+    orders_f1 = [[y_axis, x_axis, z_axis]] * layers
+    orders_q = [[[z_axis, x_axis, y_axis], [y_axis, z_axis, x_axis]]] + [[[x_axis, z_axis, y_axis]]] * (layers - 1)
     own_rows = 2 * deep
     tail = width // plan.ny * HEAD_DIM // own_rows
     fused = n == HEADS
@@ -821,12 +918,8 @@
     sums = [None] * layers
     f2b_sum = jnp.sum(low_own.astype(F32), axis=0, keepdims=True)
 
-    def end_fc2(layer, prev):
-        ends["f2", layer] = Ending(plan, where, [terms["f2", layer]], last_axis, own_rows, 0, prev)
-        return (ends["f2", layer].sent,)
-
     def end_rest(layer, prev):
-        group = [terms["q", layer], terms["f1", layer]]
+        group = terms["q", layer] + [terms["f1", layer]]
         ends["rest", layer] = Ending(plan, where, group, last_axis, own_rows, tail, prev)
         return (ends["rest", layer].sent,)
 
@@ -843,9 +936,9 @@
         top = layer == layers - 1
 
         def grad_fc2(prev):
-            r = weight_grad(plan, where, s["hid"], (low_own, low_oth), 2, order_f2[0], after=prev)
-            terms["f2", layer] = Term(plan, *r, order_f2)
-            return (r[1],)
+            term = chip_grad(plan, where, s["hid"], (low_own, low_oth), 2, prev)
+            ends["f2", layer] = ChipEnding(plan, where, term)
+            return (term,)
 
         if top:
             prev = grad_fc2(prev)
@@ -859,9 +952,8 @@
             prev = (last_part,)
             last_part = plan.core(last_part)
         else:
+            prev += (terms["f1", layer + 1].step(prev[:1]),)
             prev = grad_fc2(prev)
-            prev += (terms["f1", layer + 1].step(prev[:1]),)
-            prev += end_fc2(layer + 1, prev[:1])
         pre_own, mid_grad, branch_own, sum1 = call(
             mlp_back_own,
             layer,
@@ -875,26 +967,13 @@
         branch_oth = plan.core(branch_own)
         prev = (branch_own,)
         if not top:
-            prev += (terms["q", layer + 1].step(prev),)
+            prev += (terms["q", layer + 1][0].step(prev),)
         res1 = weight_grad(
             plan, where, s["second"], (pre_own, pre_oth), 1, orders_f1[layer][0], sums=True, extra=tail, relative=True, after=prev
         )
-        keep, send = res1[:2]
-        if fused:
-            keep, send = proj_grad_into(plan, where, s["att"], (branch_own, branch_oth), orders_f1[layer][0], keep, send)
-        else:
-            term = t_dot(s["att"][0], branch_own) + t_dot(s["att"][1], branch_oth)
-            term = term.astype(BF).reshape(half_heads, HEAD_DIM, width)
-            none = jnp.zeros_like(term)
-            term = jnp.stack([pick(c, term, none), pick(c, none, term)], axis=1).reshape(width, width)
-            term = lax.psum_scatter(term, "shard", scatter_dimension=0, tiled=True)
-            big[layer][1] = lax.psum(term, "rep").astype(F32)
-        terms["f1", layer] = Term(plan, keep, send, orders_f1[layer])
-        prev = (send,)
-        if top:
-            prev += (terms["f2", layer].step(prev),)
-        else:
-            prev += (terms["q", layer + 1].step(prev[:1]),)
+        prev = tuple(res1[:1])
+        if not top:
+            prev += (terms["f1", layer + 1].step(prev[:1]),)
             prev += (ends["f2", layer + 1].core(prev[:1]),)
         dproj_oth, part = call(
             attend_back_other,
@@ -908,9 +987,22 @@
         )
         part = plan.core(part)
         prev = (dproj_oth,)
+        keep, send = res1[:2]
+        if fused:
+            keep, send = proj_grad_into(
+                plan, where, s["att"], (branch_own, branch_oth), orders_f1[layer][0], keep, send, prev
+            )
+        else:
+            term = t_dot(s["att"][0], branch_own) + t_dot(s["att"][1], branch_oth)
+            term = term.astype(BF).reshape(half_heads, HEAD_DIM, width)
+            none = jnp.zeros_like(term)
+            term = jnp.stack([pick(c, term, none), pick(c, none, term)], axis=1).reshape(width, width)
+            term = lax.psum_scatter(term, "shard", scatter_dimension=0, tiled=True)
+            big[layer][1] = lax.psum(term, "rep").astype(F32)
+        terms["f1", layer] = Term(plan, keep, send, orders_f1[layer])
+        prev = (send,)
         if not top:
-            prev += (terms["f2", layer].step(prev[:1]),)
-            prev += (terms["f1", layer + 1].step(prev[:1]),)
+            prev += (terms["q", layer + 1][0].step(prev[:1]),)
             prev += (ends["f2", layer + 1].rep(prev[:1]),)
         dproj_own, grad, low_own, sum2 = call(
             attend_back_own,
@@ -925,12 +1017,19 @@
         prev = (dproj_own,)
         if layer:
             low_oth = plan.core(low_own)
-        if top:
-            prev += (terms["f2", layer].step(prev),)
-        resq = weight_grad(plan, where, s["first"], (dproj_own, dproj_oth), 1, orders_q[layer][0], sums=True, after=prev)
-        terms["q", layer] = Term(plan, *resq[:2], orders_q[layer])
-        prev = (resq[1],)
-        q = resq[2].reshape(3, half_heads, 1, HEAD_DIM)
+        if not top:
+            prev += end_rest(layer + 1, prev[:1])
+            prev += (ends["f2", layer].core(prev[:1]),)
+        terms["q", layer], q_sums = [], []
+        of = len(orders_q[layer])
+        for k, order in enumerate(orders_q[layer]):
+            resq = weight_grad(
+                plan, where, s["first"], (dproj_own, dproj_oth), 1, order[0], sums=True, window=(k, of), after=prev
+            )
+            terms["q", layer].append(Term(plan, *resq[:2], order))
+            q_sums.append(resq[2].reshape(plan.ny, -1))
+            prev = (resq[1],)
+        q = jnp.concatenate(q_sums, axis=1).reshape(3, half_heads, 1, HEAD_DIM)
         q = jnp.concatenate([q[:1], q[2:]])
         none = jnp.zeros_like(q)
         q = jnp.concatenate([pick(c, q, none), pick(c, none, q)], axis=2)
@@ -957,25 +1056,25 @@
         return (sent,)
 
     prev += (terms["f1", 0].step(prev[:1]),)
-    prev += end_rest(1, prev[:1])
+    prev += (ends["rest", 1].core(prev[:1]),)
     w = layers - 1
     mixed = call(
         down_last, w, 1, ["fc2"], [saved[w]["hid"][0], last_part, saved[w]["middle"]], [vecs[w]["f2b"]], [low_rows], prev
     )[0]
-    prev = (terms["f2", 0].step((mixed,)),) + step_vec()
-    prev = (ends["rest", 1].core(prev),) + step_vec()
-    prev = (terms["q", 0].step(prev),)
-    prev = (terms["f1", 0].step(prev),) + step_vec()
-    prev = (ends["rest", 1].rep(prev),)
-    prev = end_fc2(0, prev)
-    prev = (terms["q", 0].step(prev),) + step_vec()
-    prev = (ends["f2", 0].core(prev),)
+    qa, qb = terms["q", 0]
+    prev = (qa.step((mixed,)),) + step_vec()
+    prev = (qb.step(prev),)
+    prev = (ends["rest", 1].rep(prev),) + step_vec()
+    prev = (qa.step(prev),)
+    prev = (terms["f1", 0].step(prev),)
+    prev = (qb.step(prev),) + step_vec()
+    prev = end_rest(0, prev) + step_vec()
+    prev = (ends["f2", 0].rep(prev),)
+    placed = place(1, None, prev)
+    prev = (placed[0],)
     while got_vec is not None:
         prev += step_vec()
-    prev = end_rest(0, prev)
-    prev = (ends["f2", 0].rep(prev),)
-    placed = place(1, None, prev)
-    prev = (ends["rest", 0].core((placed[0],)),)
+    prev = (ends["rest", 0].core(prev),)
     prev = (ends["rest", 0].rep(prev),)
     placed = place(0, placed, prev)
     if plan.ny == 1:

time: 812 us -> 827 us (1.018)
  local copies, waits for them, and re-layouts: 93.2 us -> 122 us
  Pallas kernels: 372 us -> 351 us
  waiting for transfers between devices: 271 us -> 283 us
    unnamed x278 -> x299, local copies, waits for them, and re-layouts: 54.7 us -> 84.2 us
    ppermute x54 -> x49, waiting for transfers between devices: 149 us -> 173 us  [swap(): return lax.ppermute(v, AX, pairs)]
    pallas_call x6 -> x5, Pallas kernels: 68 us -> 45.5 us  [weight_grad(): pl.pallas_call(kernel, grid_spec=pltpu.PrefetchScalarGridSpec(num_scalar_...]
    pallas_call x0 -> x2, Pallas kernels: none -> 21 us  [chip_grad(): pl.pallas_call(kernel, grid_spec=pltpu.PrefetchScalarGridSpec(num_scalar_...]
    all_gather x2, waiting for transfers between devices: 121 us -> 109 us  [per_device(): lax.all_gather(v, 'shard', axis=0, tiled=True)]
    pallas_call x12 -> x10, Pallas kernels: 28.3 us -> 17.5 us  [combine(): pl.pallas_call(kernel, grid=(cuts,), in_specs=[pl.BlockSpec(block, index)...]
    ppermute x54 -> x49, starting transfers between devices: 41.2 us -> 33 us  [swap(): return lax.ppermute(v, AX, pairs)]
  transfers between devices with their start and end apart: 56 -> 53, of which waited for: 16 -> 16; matrix products, arithmetic and copies ran while one was open for 4% -> 4% of each run, Pallas kernels for 40% -> 39%
where the time goes in v3:
time: 827 us; the launch traced here: 817 us
  Pallas kernels  351 us (42%)
  waiting for transfers between devices  283 us (34%)
  local copies, waits for them, and re-layouts  122 us (15%)
  starting transfers between devices  33.2 us (4%)
  between operations  15.7 us (2%)
  other arithmetic  12.3 us (1%)
    pallas_call x24, Pallas kernels, row_call(): pl.pallas_call(kernel, grid_spec=pltpu.PrefetchScalarGridSpec(num_scalar_...  240 us
    ppermute x49, waiting for transfers between devices, swap(): return lax.ppermute(v, AX, pairs)  173 us
    all_gather x2, waiting for transfers between devices, per_device(): lax.all_gather(v, 'shard', axis=0, tiled=True)  109 us
    unnamed x299, local copies, waits for them, and re-layouts  84.2 us
    pallas_call x5, Pallas kernels, weight_grad(): pl.pallas_call(kernel, grid_spec=pltpu.PrefetchScalarGridSpec(num_scalar_...  45.5 us
    ppermute x49, starting transfers between devices, swap(): return lax.ppermute(v, AX, pairs)  33 us
    pallas_call x2, Pallas kernels, chip_grad(): pl.pallas_call(kernel, grid_spec=pltpu.PrefetchScalarGridSpec(num_scalar_...  21 us
    pallas_call x10, Pallas kernels, combine(): pl.pallas_call(kernel, grid=(cuts,), in_specs=[pl.BlockSpec(block, index)...  17.5 us
  transfers between devices with their start and end apart: 53, of which 16 were waited for; matrix products, arithmetic and copies ran while one was open for 4% of the time, Pallas kernels for 39%

profile of v3, /device:TPU:0, one launch (start us, length us, event | category | flops | bytes accessed | tf_op | source)
XLA Modules:
  0.0 817.3 jit_solution(4849650783009005585)
XLA Ops:
  31.4 109.5 %all-gather.5.cloned.1.call-done.refs_0_.refs_1_.refs_2_.refs_3_ = bf16[1024,10368]{1,0:T(8,128)(2,1)} async-done(((bf16[64,10368]{1,0:T(8,128)(2,1)}), bf16[1024,10368]{1,0:T(8,128)(2,1)}) %all-gather.5.cloned.1.call-update) | async-done | bytes 21233680 | tf_op jit(solution)/shard_map/all_gather | solution.py:817
  156.5 11.5 %shard_map.256 = (bf16[2,8,320,320]{3,2,1,0:T(8,128)(2,1)S(1)}, bf16[640,512]{1,0:T(8,128)(2,1)S(1)}, f32[640,1024]{1,0:T(8,128)}) custom-call(s32[4]{0:T(128)S(1)} %pad_add_fusion.where_ref, s32[2]{0:T(128)S(1)} %collective-permute-done.2.kept_ref, bf16[8,2,64,10368]{3,2,1,0:T(8,128)(2,1)} %bitcast.102, bf16[640,1536]{1,0:T(8,128)(2,1)S(1)} %shard_map.255.refs_1_.refs_3_), custom_call_target="tpu_custom_call" | custom-call | flops 1000000000 | tf_op jit(solution)/shard_map/pallas_call | solution.py:122
  178.7 12.0 %shard_map.257 = (bf16[2,8,320,320]{3,2,1,0:T(8,128)(2,1)S(1)}, bf16[640,512]{1,0:T(8,128)(2,1)S(1)}, f32[640,1024]{1,0:T(8,128)S(1)}, bf16[640,1024]{1,0:T(8,128)(2,1)}) custom-call(s32[4]{0:T(128)S(1)} %pad_add_fusion.where_ref, s32[2]{0:T(128)S(1)} %copy-done.29, bf16[8,2,64,10368]{3,2,1,0:T(8,128)(2,1)} %bitcast.103, ...), custom_call_target="tpu_custom_call" | custom-call | flops 1000000000 | tf_op jit(solution)/shard_map/pallas_call | solution.py:122
  196.8 20.3 %collective-permute-done.1.refs_4_.refs_1_ = bf16[1024,1024]{1,0:T(8,128)(2,1)S(1)} collective-permute-done((bf16[1024,1024]{1,0:T(8,128)(2,1)}, bf16[1024,1024]{1,0:T(8,128)(2,1)S(1)}, u32[]{:S(2)}, u32[]{:S(2)}) %collective-permute-start.1) | collective-permute-done | bytes 2097184 | tf_op jit(solution)/shard_map/ppermute | solution.py:39
  260.9 11.4 %shard_map.264 = (bf16[2,8,320,320]{3,2,1,0:T(8,128)(2,1)S(1)}, bf16[640,512]{1,0:T(8,128)(2,1)S(1)}, f32[640,1024]{1,0:T(8,128)}) custom-call(s32[4]{0:T(128)S(1)} %pad_add_fusion.where_ref, s32[2]{0:T(128)S(1)} %collective-permute-done.2.kept_ref, bf16[8,2,64,10240]{3,2,1,0:T(8,128)(2,1)} %bitcast.106, bf16[640,1536]{1,0:T(8,128)(2,1)S(1)} %shard_map.263.refs_1_.refs_3_), custom_call_target="tpu_custom_call" | custom-call | flops 1000000000 | tf_op jit(solution)/shard_map/pallas_call | solution.py:122
  282.6 12.8 %shard_map.265 = (bf16[2,8,320,320]{3,2,1,0:T(8,128)(2,1)S(1)}, bf16[640,512]{1,0:T(8,128)(2,1)S(1)}, f32[640,1024]{1,0:T(8,128)S(1)}, bf16[640,1024]{1,0:T(8,128)(2,1)}) custom-call(s32[4]{0:T(128)S(1)} %pad_add_fusion.where_ref, s32[2]{0:T(128)S(1)} %copy-done.29, bf16[8,2,64,10240]{3,2,1,0:T(8,128)(2,1)} %bitcast.107, ...), custom_call_target="tpu_custom_call" | custom-call | flops 1000000000 | tf_op jit(solution)/shard_map/pallas_call | solution.py:122
  309.2 12.4 %collective-permute-done.refs_4_.refs_1_ = bf16[1024,1024]{1,0:T(8,128)(2,1)} collective-permute-done((bf16[1024,1024]{1,0:T(8,128)(2,1)}, bf16[1024,1024]{1,0:T(8,128)(2,1)}, u32[]{:S(2)}, u32[]{:S(2)}) %collective-permute-start) | collective-permute-done | bytes 2097184 | tf_op jit(solution)/shard_map/ppermute | solution.py:39
  331.1 10.5 %shard_map.268.refs_6_ = bf16[2048,1024]{1,0:T(8,128)(2,1)S(1)} custom-call(s32[4]{0:T(128)S(1)} %pad_add_fusion.where_ref, bf16[640,2048]{1,0:T(8,128)(2,1)S(1)} %get-tuple-element.129.xo.rest_0_.refs_2_, bf16[640,2048]{1,0:T(8,128)(2,1)S(1)} %get-tuple-element.130.xt.refs_2_, bf16[640,1024]{1,0:T(8,128)(2,1)} %bitcast_convert_fusion.yo.refs_4_, ...), custom_call_target="tpu_custom_call" | custom-call | flops 30000001024 | tf_op jit(solution)/shard_map/pallas_call | solution.py:449
  349.1 10.7 %shard_map.269 = (bf16[640,2048]{1,0:T(8,128)(2,1)S(1)}, f32[640,1024]{1,0:T(8,128)S(1)}) custom-call(s32[4]{0:T(128)S(1)} %pad_add_fusion.where_ref, s32[2]{0:T(128)S(1)} %collective-permute-done.2.kept_ref, bf16[1024,10240]{1,0:T(8,128)(2,1)} %all-gather.3.cloned.1.call-done.refs_0_.refs_1_.refs_2_.refs_3_, ...), custom_call_target="tpu_custom_call" | custom-call | flops 30000001024 | tf_op jit(solution)/shard_map/pallas_call | solution.py:122
  367.8 12.9 %shard_map.271 = (bf16[640,2048]{1,0:T(8,128)(2,1)S(1)}, f32[640,1024]{1,0:T(8,128)S(1)}, bf16[640,1024]{1,0:T(8,128)(2,1)}, f32[8,1024]{1,0:T(8,128)S(1)}) custom-call(s32[4]{0:T(128)S(1)} %pad_add_fusion.where_ref, s32[2]{0:T(128)S(1)} %copy-done.29, bf16[1024,10240]{1,0:T(8,128)(2,1)} %all-gather.3.cloned.1.call-done.refs_0_.refs_1_.refs_2_.refs_3_, ...), custom_call_target="tpu_custom_call" | custom-call | flops 30000001024 | tf_op jit(solution)/shard_map/pallas_call | solution.py:122
  382.2 12.5 %shard_map.272 = (bf16[1,2,2,2,128,1280]{5,4,3,2,1,0:T(8,128)(2,1)S(1)}, bf16[1,2,2,2,128,1280]{5,4,3,2,1,0:T(8,128)(2,1)}, f32[1,2048]{1,0:T(1,128)S(1)}) custom-call(s32[4]{0:T(128)S(1)} %pad_add_fusion.where_ref, bf16[640,1024]{1,0:T(8,128)(2,1)} %get-tuple-element.128.refs_2_.xo, bf16[640,1024]{1,0:T(8,128)(2,1)} %collective-permute-done.9.refs_2_.xt, ...), custom_call_target="tpu_custom_call" | custom-call | flops 30000001024 | tf_op jit(solution)/shard_map/pallas_call | solution.py:407
  403.6 14.7 %shard_map.273 = (bf16[640,1536]{1,0:T(8,128)(2,1)S(1)}, f32[640,1024]{1,0:T(8,128)S(1)}) custom-call(s32[4]{0:T(128)S(1)} %pad_add_fusion.where_ref, s32[2]{0:T(128)S(1)} %collective-permute-done.2.kept_ref, bf16[8,2,64,10240]{3,2,1,0:T(8,128)(2,1)} %bitcast.108, bf16[1024,10240]{1,0:T(8,128)(2,1)} %all-gather.3.cloned.1.call-done.refs_0_.refs_1_.refs_2_.refs_3_, ...), custom_call_target="tpu_custom_call" | custom-call | flops 30000001024 | tf_op jit(solution)/shard_map/pallas_call | solution.py:122
  425.5 16.9 %shard_map.275 = (bf16[640,1536]{1,0:T(8,128)(2,1)S(1)}, f32[640,1024]{1,0:T(8,128)S(1)}, bf16[640,1024]{1,0:T(8,128)(2,1)}, f32[8,1024]{1,0:T(8,128)S(1)}) custom-call(s32[4]{0:T(128)S(1)} %pad_add_fusion.where_ref, s32[2]{0:T(128)S(1)} %copy-done.29, bf16[8,2,64,10240]{3,2,1,0:T(8,128)(2,1)} %bitcast.109, ...), custom_call_target="tpu_custom_call" | custom-call | flops 30000001024 | tf_op jit(solution)/shard_map/pallas_call | solution.py:122
  460.4 10.8 %shard_map.277 = (bf16[640,2048]{1,0:T(8,128)(2,1)S(1)}, f32[640,1024]{1,0:T(8,128)}) custom-call(s32[4]{0:T(128)S(1)} %pad_add_fusion.where_ref, s32[2]{0:T(128)S(1)} %collective-permute-done.2.kept_ref, bf16[1024,10368]{1,0:T(8,128)(2,1)} %all-gather.5.cloned.1.call-done.refs_0_.refs_1_.refs_2_.refs_3_, ...), custom_call_target="tpu_custom_call" | custom-call | flops 30000001024 | tf_op jit(solution)/shard_map/pallas_call | solution.py:122
  471.2 11.9 %collective-permute-done.17.g = bf16[1,2,2,2,128,1280]{5,4,3,2,1,0:T(8,128)(2,1)} collective-permute-done((bf16[1,2,2,2,128,1280]{5,4,3,2,1,0:T(8,128)(2,1)}, bf16[1,2,2,2,128,1280]{5,4,3,2,1,0:T(8,128)(2,1)}, u32[]{:S(2)}, u32[]{:S(2)}) %collective-permute-start.17) | collective-permute-done | bytes 2621472 | tf_op jit(solution)/shard_map/ppermute | solution.py:39
  488.6 10.5 %shard_map.279.refs_10_ = bf16[2048,1024]{1,0:T(8,128)(2,1)S(1)} custom-call(s32[4]{0:T(128)S(1)} %pad_add_fusion.where_ref, bf16[640,2048]{1,0:T(8,128)(2,1)S(1)} %copy-done.24, bf16[640,2048]{1,0:T(8,128)(2,1)S(1)} %copy-done.22, bf16[640,1024]{1,0:T(8,128)(2,1)} %get-tuple-element.148.yo.refs_4_, bf16[640,1024]{1,0:T(8,128)(2,1)} %collective-permute-done.15.refs_4_.yt, ...), custom_call_target="tpu_custom_call" | custom-call | flops 30000001024 | tf_op jit(solution)/shard_map/pallas_call | solution.py:449
  506.3 13.0 %shard_map.280 = (bf16[640,2048]{1,0:T(8,128)(2,1)S(1)}, f32[640,1024]{1,0:T(8,128)S(1)}, bf16[640,1024]{1,0:T(8,128)(2,1)}, f32[8,1024]{1,0:T(8,128)S(1)}) custom-call(s32[4]{0:T(128)S(1)} %pad_add_fusion.where_ref, s32[2]{0:T(128)S(1)} %copy-done.29, bf16[1024,10368]{1,0:T(8,128)(2,1)} %all-gather.5.cloned.1.call-done.refs_0_.refs_1_.refs_2_.refs_3_, ...), custom_call_target="tpu_custom_call" | custom-call | flops 30000001024 | tf_op jit(solution)/shard_map/pallas_call | solution.py:122
  524.9 12.6 %shard_map.282 = (bf16[1,2,2,2,128,1280]{5,4,3,2,1,0:T(8,128)(2,1)S(1)}, bf16[1,2,2,2,128,1280]{5,4,3,2,1,0:T(8,128)(2,1)}, f32[1,2048]{1,0:T(1,128)S(1)}) custom-call(s32[4]{0:T(128)S(1)} %pad_add_fusion.where_ref, bf16[640,1024]{1,0:T(8,128)(2,1)} %get-tuple-element.121.refs_2_.xo, bf16[640,1024]{1,0:T(8,128)(2,1)} %collective-permute-done.5.refs_2_.xt, ...), custom_call_target="tpu_custom_call" | custom-call | flops 30000001024 | tf_op jit(solution)/shard_map/pallas_call | solution.py:407
  554.6 14.1 %shard_map.285 = (bf16[640,1536]{1,0:T(8,128)(2,1)S(1)}, f32[640,1024]{1,0:T(8,128)S(1)}) custom-call(s32[4]{0:T(128)S(1)} %pad_add_fusion.where_ref, s32[2]{0:T(128)S(1)} %collective-permute-done.2.kept_ref, bf16[8,2,64,10368]{3,2,1,0:T(8,128)(2,1)} %bitcast.104, bf16[1024,10368]{1,0:T(8,128)(2,1)} %all-gather.5.cloned.1.call-done.refs_0_.refs_1_.refs_2_.refs_3_, ...), custom_call_target="tpu_custom_call" | custom-call | flops 30000001024 | tf_op jit(solution)/shard_map/pallas_call | solution.py:122
  584.1 16.7 %shard_map.289 = (bf16[640,1536]{1,0:T(8,128)(2,1)S(1)}, f32[640,1024]{1,0:T(8,128)}, bf16[640,1024]{1,0:T(8,128)(2,1)}, f32[8,1024]{1,0:T(8,128)S(1)}) custom-call(s32[4]{0:T(128)S(1)} %pad_add_fusion.where_ref, s32[2]{0:T(128)S(1)} %copy-done.29, bf16[8,2,64,10368]{3,2,1,0:T(8,128)(2,1)} %bitcast.105, ...), custom_call_target="tpu_custom_call" | custom-call | flops 30000001024 | tf_op jit(solution)/shard_map/pallas_call | solution.py:122
  602.2 39.6 %collective-permute-done.24.refs_1_ = bf16[1,2,1,1,128,768]{5,4,3,2,1,0:T(8,128)(2,1)} collective-permute-done((bf16[1,2,1,1,128,768]{5,4,3,2,1,0:T(8,128)(2,1)}, bf16[1,2,1,1,128,768]{5,4,3,2,1,0:T(8,128)(2,1)}, u32[]{:S(2)}, u32[]{:S(2)}) %collective-permute-start.24) | collective-permute-done | bytes 393248 | tf_op jit(solution)/shard_map/ppermute | solution.py:39
  684.7 12.5 %collective-permute-done.29 = f32[2,16,768]{2,1,0:T(8,128)S(1)} collective-permute-done((f32[2,16,768]{2,1,0:T(8,128)S(1)}, f32[2,16,768]{2,1,0:T(8,128)S(1)}, u32[]{:S(2)}, u32[]{:S(2)}) %collective-permute-start.29) | collective-permute-done | bytes 98336 | tf_op jit(solution)/shard_map/ppermute | solution.py:39
  714.0 22.2 %collective-permute-done.35.g = bf16[2,2,1,1,128,384]{5,4,3,2,1,0:T(8,128)(2,1)S(1)} collective-permute-done((bf16[2,2,1,1,128,384]{5,4,3,2,1,0:T(8,128)(2,1)S(1)}, bf16[2,2,1,1,128,384]{5,4,3,2,1,0:T(8,128)(2,1)S(1)}, u32[]{:S(2)}, u32[]{:S(2)}) %collective-permute-start.35) | collective-permute-done | bytes 393248 | tf_op jit(solution)/shard_map/ppermute | solution.py:39
  795.7 10.8 %collective-permute-done.48.refs_3_ = bf16[64,4096]{1,0:T(8,128)(2,1)S(1)} collective-permute-done((bf16[64,4096]{1,0:T(8,128)(2,1)S(1)}, bf16[64,4096]{1,0:T(8,128)(2,1)S(1)}, u32[]{:S(2)}, u32[]{:S(2)}) %collective-permute-start.48) | collective-permute-done | bytes 524320 | tf_op jit(solution)/shard_map/ppermute | solution.py:39
  (582 shorter events, 359.0 us)
Async XLA Ops:
  7.2 133.6 %all-gather.5.cloned.1.call-start = ((), (), s32[]{:S(2)}) async-start(), calls=%async_computation.3 | async-start | bytes 22560768 | tf_op jit(solution)/shard_map/all_gather | solution.py:817
  27.9 224.8 %all-gather.3.cloned.1.call-start = ((), (), s32[]{:S(2)}) async-start(), calls=%async_computation.2 | async-start | bytes 22282240 | tf_op jit(solution)/shard_map/all_gather | solution.py:817
  30.4 508.6 %reduce-scatter.3.cloned.1.call-start = ((), (), s32[]{:S(2)}) async-start(), calls=%async_computation.4 | async-start | bytes 4718592 | tf_op jit(solution)/shard_map/reduce_scatter | solution.py:666
  169.1 48.0 %collective-permute-start.1 = (bf16[1024,1024]{1,0:T(8,128)(2,1)}, bf16[1024,1024]{1,0:T(8,128)(2,1)S(1)}, u32[]{:S(2)}, u32[]{:S(2)}) collective-permute-start(bf16[1024,1024]{1,0:T(8,128)(2,1)} %constant_dynamic-slice_fusion.1.refs_3_), channel_id=1, source_target_pairs={{0,1},{1,0},{2,3},{3,2},{4,5},{5,4},{6,7},{7,6},{8,9},{9,8},{10,11... | collective-permute-start | bytes 6291464 | tf_op jit(solution)/shard_map/ppermute | solution.py:39
  273.5 48.1 %collective-permute-start = (bf16[1024,1024]{1,0:T(8,128)(2,1)}, bf16[1024,1024]{1,0:T(8,128)(2,1)}, u32[]{:S(2)}, u32[]{:S(2)}) collective-permute-start(bf16[1024,1024]{1,0:T(8,128)(2,1)} %constant_dynamic-slice_fusion.2.refs_3_), channel_id=1, source_target_pairs={{0,1},{1,0},{2,3},{3,2},{4,5},{5,4},{6,7},{7,6},{8,9},{9,8},{10,11... | collective-permute-start | bytes 6291464 | tf_op jit(solution)/shard_map/ppermute | solution.py:39
  300.0 31.1 %collective-permute-start.10 = (bf16[640,1024]{1,0:T(8,128)(2,1)}, bf16[640,1024]{1,0:T(8,128)(2,1)}, u32[]{:S(2)}, u32[]{:S(2)}) collective-permute-start(bf16[640,1024]{1,0:T(8,128)(2,1)} %bitcast_convert_fusion.yo.refs_4_), channel_id=1, source_target_pairs={{0,2},{1,3},{2,0},{3,1},{4,6},{5,7},{6,4},{7,5},{8,10},{9,11},{10,... | collective-permute-start | bytes 3932168 | tf_op jit(solution)/shard_map/ppermute | solution.py:39
  345.1 305.1 %reduce-scatter.5.cloned.1.call-start = ((), (), s32[]{:S(2)}) async-start(), calls=%async_computation.5 | async-start | bytes 4718592 | tf_op jit(solution)/shard_map/reduce_scatter | solution.py:666
  367.3 331.0 %collective-permute-start.11 = (f32[640,1024]{1,0:T(8,128)}, f32[640,1024]{1,0:T(8,128)}, u32[]{:S(2)}, u32[]{:S(2)}) collective-permute-start(f32[640,1024]{1,0:T(8,128)} %shard_map.270.refs_10_), channel_id=1, source_target_pairs={{0,2},{1,3},{2,0},{3,1},{4,6},{5,7},{6,4},{7,5},{8,10},{9,11},{10,... | collective-permute-start | bytes 7864328 | tf_op jit(solution)/shard_map/ppermute | solution.py:39
  423.9 59.2 %collective-permute-start.17 = (bf16[1,2,2,2,128,1280]{5,4,3,2,1,0:T(8,128)(2,1)}, bf16[1,2,2,2,128,1280]{5,4,3,2,1,0:T(8,128)(2,1)}, u32[]{:S(2)}, u32[]{:S(2)}) collective-permute-start(bf16[1,2,2,2,128,1280]{5,4,3,2,1,0:T(8,128)(2,1)} %get-tuple-element.147.refs_9_), channel_id=1, source_target_pairs={{0,1},{1,0},{2,3},{3,2},{4,5},{5,4},{6,7},{7,6},{8,9},{9,8},{10,11... | collective-permute-start | bytes 7864328 | tf_op jit(solution)/shard_map/ppermute | solution.py:39
  455.7 64.2 %collective-permute-start.19 = (bf16[2,2,2,1,128,768]{5,4,3,2,1,0:T(8,128)(2,1)}, bf16[2,2,2,1,128,768]{5,4,3,2,1,0:T(8,128)(2,1)}, u32[]{:S(2)}, u32[]{:S(2)}) collective-permute-start(bf16[2,2,2,1,128,768]{5,4,3,2,1,0:T(8,128)(2,1)} %copy-done.52), channel_id=1, source_target_pairs={{0,4},{1,5},{2,6},{3,7},{4,0},{5,1},{6,2},{7,3},{8,12},{9,13},{10,... | collective-permute-start | bytes 4718600 | tf_op jit(solution)/shard_map/ppermute | solution.py:39
  487.4 59.7 %collective-permute-start.20 = (bf16[1,2,2,1,128,1280]{5,4,3,2,1,0:T(8,128)(2,1)}, bf16[1,2,2,1,128,1280]{5,4,3,2,1,0:T(8,128)(2,1)}, u32[]{:S(2)}, u32[]{:S(2)}) collective-permute-start(bf16[1,2,2,1,128,1280]{5,4,3,2,1,0:T(8,128)(2,1)} %get-tuple-element.157.rest_1_), channel_id=1, source_target_pairs={{0,4},{1,5},{2,6},{3,7},{4,0},{5,1},{6,2},{7,3},{8,12},{9,13},{10,... | collective-permute-start | bytes 3932168 | tf_op jit(solution)/shard_map/ppermute | solution.py:39
  519.3 33.9 %collective-permute-start.18 = (bf16[640,1024]{1,0:T(8,128)(2,1)}, bf16[640,1024]{1,0:T(8,128)(2,1)}, u32[]{:S(2)}, u32[]{:S(2)}) collective-permute-start(bf16[640,1024]{1,0:T(8,128)(2,1)} %get-tuple-element.158.rest_0_.yo.refs_2_), channel_id=1, source_target_pairs={{0,2},{1,3},{2,0},{3,1},{4,6},{5,7},{6,4},{7,5},{8,10},{9,11},{10,... | collective-permute-start | bytes 3932168 | tf_op jit(solution)/shard_map/ppermute | solution.py:39
  523.6 51.9 %collective-permute-start.22 = (bf16[2,2,1,1,128,768]{5,4,3,2,1,0:T(8,128)(2,1)}, bf16[2,2,1,1,128,768]{5,4,3,2,1,0:T(8,128)(2,1)}, u32[]{:S(2)}, u32[]{:S(2)}) collective-permute-start(bf16[2,2,1,1,128,768]{5,4,3,2,1,0:T(8,128)(2,1)} %get-tuple-element.163.rest_1_), channel_id=1, source_target_pairs={{0,8},{1,9},{2,10},{3,11},{4,12},{5,13},{6,14},{7,15},{8,0},{9,1},... | collective-permute-start | bytes 2359304 | tf_op jit(solution)/shard_map/ppermute | solution.py:39
  546.9 32.3 %collective-permute-start.23 = (bf16[128,1024]{1,0:T(8,128)(2,1)}, bf16[128,1024]{1,0:T(8,128)(2,1)S(1)}, u32[]{:S(2)}, u32[]{:S(2)}) collective-permute-start(bf16[128,1024]{1,0:T(8,128)(2,1)} %get-tuple-element.167.refs_7_), channel_id=1, source_target_pairs={{0,2},{1,3},{2,0},{3,1},{4,6},{5,7},{6,4},{7,5},{8,10},{9,11},{10,... | collective-permute-start | bytes 786440 | tf_op jit(solution)/shard_map/ppermute | solution.py:39
  552.6 49.6 %collective-permute-start.25 = (bf16[1,2,1,1,128,1280]{5,4,3,2,1,0:T(8,128)(2,1)}, bf16[1,2,1,1,128,1280]{5,4,3,2,1,0:T(8,128)(2,1)}, u32[]{:S(2)}, u32[]{:S(2)}) collective-permute-start(bf16[1,2,1,1,128,1280]{5,4,3,2,1,0:T(8,128)(2,1)} %get-tuple-element.166.refs_6_), channel_id=1, source_target_pairs={{0,8},{1,9},{2,10},{3,11},{4,12},{5,13},{6,14},{7,15},{8,0},{9,1},... | collective-permute-start | bytes 1966088 | tf_op jit(solution)/shard_map/ppermute | solution.py:39
  574.0 106.9 %collective-permute-start.26 = (bf16[1,2,2,2,128,1280]{5,4,3,2,1,0:T(8,128)(2,1)}, bf16[1,2,2,2,128,1280]{5,4,3,2,1,0:T(8,128)(2,1)}, u32[]{:S(2)}, u32[]{:S(2)}) collective-permute-start(bf16[1,2,2,2,128,1280]{5,4,3,2,1,0:T(8,128)(2,1)} %get-tuple-element.174.rest_0_.refs_2_.refs_9_), channel_id=1, source_target_pairs={{0,1},{1,0},{2,3},{3,2},{4,5},{5,4},{6,7},{7,6},{8,9},{9,8},{10,11... | collective-permute-start | bytes 7864328 | tf_op jit(solution)/shard_map/ppermute | solution.py:39
  578.2 63.6 %collective-permute-start.24 = (bf16[1,2,1,1,128,768]{5,4,3,2,1,0:T(8,128)(2,1)}, bf16[1,2,1,1,128,768]{5,4,3,2,1,0:T(8,128)(2,1)}, u32[]{:S(2)}, u32[]{:S(2)}) collective-permute-start(bf16[1,2,1,1,128,768]{5,4,3,2,1,0:T(8,128)(2,1)} %get-tuple-element.176.refs_10_), channel_id=1, source_target_pairs={{0,1},{1,0},{2,3},{3,2},{4,5},{5,4},{6,7},{7,6},{8,9},{9,8},{10,11... | collective-permute-start | bytes 1179656 | tf_op jit(solution)/shard_map/ppermute | solution.py:39
  648.4 26.5 %collective-permute-start.27 = (bf16[128,2048]{1,0:T(8,128)(2,1)}, bf16[128,2048]{1,0:T(8,128)(2,1)}, u32[]{:S(2)}, u32[]{:S(2)}) collective-permute-start(bf16[128,2048]{1,0:T(8,128)(2,1)} %get-tuple-element.181.rest_1_), channel_id=1, source_target_pairs={{0,16},{1,17},{2,18},{3,19},{4,20},{5,21},{6,22},{7,23},{8,24},{9,... | collective-permute-start | bytes 1572872 | tf_op jit(solution)/shard_map/ppermute | solution.py:39
  662.1 46.3 %collective-permute-start.34 = (bf16[2,2,1,2,128,384]{5,4,3,2,1,0:T(8,128)(2,1)}, bf16[2,2,1,2,128,384]{5,4,3,2,1,0:T(8,128)(2,1)}, u32[]{:S(2)}, u32[]{:S(2)}) collective-permute-start(bf16[2,2,1,2,128,384]{5,4,3,2,1,0:T(8,128)(2,1)} %copy-done.57), channel_id=1, source_target_pairs={{0,8},{1,9},{2,10},{3,11},{4,12},{5,13},{6,14},{7,15},{8,0},{9,1},... | collective-permute-start | bytes 2359304 | tf_op jit(solution)/shard_map/ppermute | solution.py:39
  674.9 37.3 %collective-permute-start.37 = (bf16[1,2,2,2,128,384]{5,4,3,2,1,0:T(8,128)(2,1)}, bf16[1,2,2,2,128,384]{5,4,3,2,1,0:T(8,128)(2,1)S(1)}, u32[]{:S(2)}, u32[]{:S(2)}) collective-permute-start(bf16[1,2,2,2,128,384]{5,4,3,2,1,0:T(8,128)(2,1)} %copy-done.54), channel_id=1, source_target_pairs={{0,1},{1,0},{2,3},{3,2},{4,5},{5,4},{6,7},{7,6},{8,9},{9,8},{10,11... | collective-permute-start | bytes 2359304 | tf_op jit(solution)/shard_map/ppermute | solution.py:39
  680.7 32.7 %collective-permute-start.36 = (bf16[64,1792]{1,0:T(8,128)(2,1)S(1)}, bf16[64,1792]{1,0:T(8,128)(2,1)S(1)}, u32[]{:S(2)}, u32[]{:S(2)}) collective-permute-start(bf16[64,1792]{1,0:T(8,128)(2,1)S(1)} %get-tuple-element.188.refs_8_), channel_id=1, source_target_pairs={{0,2},{1,3},{2,0},{3,1},{4,6},{5,7},{6,4},{7,5},{8,10},{9,11},{10,... | collective-permute-start | bytes 688136 | tf_op jit(solution)/shard_map/ppermute | solution.py:39
  697.2 40.8 %collective-permute-start.40 = (bf16[1,2,2,1,128,1280]{5,4,3,2,1,0:T(8,128)(2,1)}, bf16[1,2,2,1,128,1280]{5,4,3,2,1,0:T(8,128)(2,1)}, u32[]{:S(2)}, u32[]{:S(2)}) collective-permute-start(bf16[1,2,2,1,128,1280]{5,4,3,2,1,0:T(8,128)(2,1)} %get-tuple-element.186.refs_7_), channel_id=1, source_target_pairs={{0,4},{1,5},{2,6},{3,7},{4,0},{5,1},{6,2},{7,3},{8,12},{9,13},{10,... | collective-permute-start | bytes 3932168 | tf_op jit(solution)/shard_map/ppermute | solution.py:39
  706.9 35.6 %collective-permute-start.31 = (f32[2,16,768]{2,1,0:T(8,128)}, f32[2,16,768]{2,1,0:T(8,128)}, u32[]{:S(2)}, u32[]{:S(2)}) collective-permute-start(f32[2,16,768]{2,1,0:T(8,128)} %add.72.refs_7_), channel_id=1, source_target_pairs={{0,8},{1,9},{2,10},{3,11},{4,12},{5,13},{6,14},{7,15},{8,0},{9,1},... | collective-permute-start | bytes 294920 | tf_op jit(solution)/shard_map/ppermute | solution.py:39
  712.7 27.9 %collective-permute-start.39 = (bf16[1,2,1,2,128,384]{5,4,3,2,1,0:T(8,128)(2,1)S(1)}, bf16[1,2,1,2,128,384]{5,4,3,2,1,0:T(8,128)(2,1)S(1)}, u32[]{:S(2)}, u32[]{:S(2)}) collective-permute-start(bf16[1,2,1,2,128,384]{5,4,3,2,1,0:T(8,128)(2,1)S(1)} %get-tuple-element.205.refs_2_), channel_id=1, source_target_pairs={{0,8},{1,9},{2,10},{3,11},{4,12},{5,13},{6,14},{7,15},{8,0},{9,1},... | collective-permute-start | bytes 1179656 | tf_op jit(solution)/shard_map/ppermute | solution.py:39
  (172 other events, 1248.7 us)
Sparse Core Ops, SparseCore 0:
  28.0 112.7 all-gather.4
  143.0 108.8 all-gather.2
  345.2 88.3 reduce-scatter.2
  501.2 113.0 reduce-scatter.4

commit v4 on v3

--- a/solution.py
+++ b/solution.py
@@ -15,10 +15,11 @@
 AX = ("shard", "rep")
 BF = jnp.bfloat16
 F32 = jnp.float32
-LIMIT = 32 * 2**20
+LIMIT = 60 * 2**20
+SMALL_LIMIT = 16 * 2**20
 ONCE = pl.Buffered(1)
 ANY = pl.BlockSpec(memory_space=pl.ANY)
-FORWARD = pl.CostEstimate(flops=10**9, bytes_accessed=0, transcendentals=0)
+FORWARD = pl.CostEstimate(flops=10**7, bytes_accessed=0, transcendentals=0)
 BACKWARD = pl.CostEstimate(flops=10**9 * 30, bytes_accessed=0, transcendentals=0)
 SMALL = ("ag", "as", "qvb", "pb", "mg", "ms", "f1b", "f2b")
 
@@ -243,8 +244,12 @@
     low = blocked[0][...]
     for k, n in chunks(outs[0].shape[1], 512):
         cols = pl.ds(k, n)
-        held = w[0][k // w[0][0].shape[0]]
-        t = dot_t(low, held[pl.ds(k % held.shape[0], n), :])
+        held, first = w[0][0], 0
+        for part in w[0][1:]:
+            if k >= first + held.shape[0]:
+                first += held.shape[0]
+                held = part
+        t = dot_t(low, held[pl.ds(k - first, n), :])
         outs[0][:, cols] = (t * blocked[1][:, cols].astype(F32)).astype(BF)
     total, at = None, 0
     for held in w[1]:
@@ -557,7 +562,7 @@
         in_specs=[pl.BlockSpec(block, index)] * 2 + [ANY] * len(after),
         out_specs=[pl.BlockSpec(out_block, index)] * 2,
         out_shape=[jax.ShapeDtypeStruct(out, BF)] * 2,
-        compiler_params=pltpu.CompilerParams(vmem_limit_bytes=LIMIT),
+        compiler_params=pltpu.CompilerParams(vmem_limit_bytes=SMALL_LIMIT),
         cost_estimate=BACKWARD,
     )(keep, got, *after)
 
@@ -589,7 +594,7 @@
         in_specs=whole + [ANY] * len(after),
         out_specs=[pl.BlockSpec((rows, total), lambda: (0, 0))] * 2,
         out_shape=[jax.ShapeDtypeStruct((rows, total), BF)] * 2,
-        compiler_params=pltpu.CompilerParams(vmem_limit_bytes=LIMIT),
+        compiler_params=pltpu.CompilerParams(vmem_limit_bytes=SMALL_LIMIT),
         cost_estimate=BACKWARD,
     )(*ins, *after)
 
@@ -613,7 +618,7 @@
             out_specs=[pl.BlockSpec(s, lambda i, w, n=len(s): (0,) * n) for s, _ in shapes],
         ),
         out_shape=[jax.ShapeDtypeStruct(s, t) for s, t in shapes],
-        compiler_params=pltpu.CompilerParams(vmem_limit_bytes=LIMIT),
+        compiler_params=pltpu.CompilerParams(vmem_limit_bytes=SMALL_LIMIT),
         cost_estimate=BACKWARD,
     )(where, *ins, *after)
 
@@ -821,9 +826,14 @@
         found = {"fc1": [(gathered[layer], ("quarter", block, (at_fc1, halves, k))) for k in range(halves)]}
         found["fc2"] = [(gathered[layer], columns(block, at_fc2 + k, each)) for k in range(each)]
         if plan.ny == 2:
-            mine = lax.dynamic_slice_in_dim(gathered[layer], (at_fc2 + c) * block, block, axis=1)
-            found["fc2"].append((plan.flip(mine, 0), None))
-            found["sent"], found["came"] = (mine,), (found["fc2"][-1][0],)
+            found["sent"], found["came"] = (), ()
+            for k in range(1):
+                mine = lax.dynamic_slice(
+                    gathered[layer], (0, (at_fc2 + c) * block), (block, block)
+                )
+                found["sent"] += (mine,)
+                found["came"] += (plan.flip(mine, 0),)
+                found["fc2"].append((found["came"][k], None))
         mlp_parts.append(found)
 
     def weight_of(layer, name):
@@ -873,7 +883,7 @@
     for layer in range(layers):
         v = vecs[layer]
         first_oth = plan.core(first_own)
-        sent = mlp_parts[layer].get("sent", ())
+        sent, came = mlp_parts[layer].get("sent", ()), mlp_parts[layer].get("came", ())
         proj_oth = call(qkv_body, layer, 0, ["qkv"], [first_oth], [v["qvb_c"]], [wide_rows], sent, FORWARD)[0]
         probs_oth, att_oth, part = call(attend_other, layer, 0, ["proj"], [proj_oth], [], att_outs + [f32_rows])
         part = plan.core(part)
@@ -881,8 +891,7 @@
         probs_own, att_own, middle, second_own = call(
             attend_own, layer, 1, ["proj"], [proj_own, part, state], [v["pb"], v["mg"], v["ms"]], att_outs + [f32_rows, low_rows])
         second_oth = plan.core(second_own)
-        came = mlp_parts[layer].get("came", ())
-        hid_oth, slope_oth = call(up_body, layer, 0, ["fc1"], [second_oth], [v["f1b_c"]], [ff_rows] * 2, came, FORWARD)
+        hid_oth, slope_oth = call(up_body, layer, 0, ["fc1"], [second_oth], [v["f1b_c"]], [ff_rows] * 2)
         if layer + 1 < layers:
             part = call(down_other, layer, 0, ["fc2"], [hid_oth], [], [f32_rows])[0]
             part = plan.core(part)
@@ -909,7 +918,7 @@
     last_axis, z_axis, x_axis = 1, plan.bits - 1, plan.bits
     y_axis = 0 if plan.ny == 2 else 2
     orders_f1 = [[y_axis, x_axis, z_axis]] * layers
-    orders_q = [[[z_axis, x_axis, y_axis], [y_axis, z_axis, x_axis]]] + [[[x_axis, z_axis, y_axis]]] * (layers - 1)
+    orders_q = [[[z_axis, y_axis, x_axis], [y_axis, z_axis, x_axis]]] + [[[x_axis, z_axis, y_axis]]] * (layers - 1)
     own_rows = 2 * deep
     tail = width // plan.ny * HEAD_DIM // own_rows
     fused = n == HEADS
@@ -929,7 +938,7 @@
         )
 
     ends = {}
-    prev = (hid_own,)
+    prev = (hid_own,) + mlp_parts[layers - 1].get("came", ())
     terms = {}
     for layer in reversed(range(layers)):
         v, s = vecs[layer], saved[layer]
@@ -952,8 +961,8 @@
             prev = (last_part,)
             last_part = plan.core(last_part)
         else:
+            prev = grad_fc2(prev)
             prev += (terms["f1", layer + 1].step(prev[:1]),)
-            prev = grad_fc2(prev)
         pre_own, mid_grad, branch_own, sum1 = call(
             mlp_back_own,
             layer,
@@ -973,6 +982,7 @@
         )
         prev = tuple(res1[:1])
         if not top:
+            prev += (terms["q", layer + 1][0].step(prev[:1]),)
             prev += (terms["f1", layer + 1].step(prev[:1]),)
             prev += (ends["f2", layer + 1].core(prev[:1]),)
         dproj_oth, part = call(
@@ -1002,7 +1012,6 @@
         terms["f1", layer] = Term(plan, keep, send, orders_f1[layer])
         prev = (send,)
         if not top:
-            prev += (terms["q", layer + 1][0].step(prev[:1]),)
             prev += (ends["f2", layer + 1].rep(prev[:1]),)
         dproj_own, grad, low_own, sum2 = call(
             attend_back_own,

time: 827 us -> 762 us (0.921)
  waiting for transfers between devices: 283 us -> 205 us
  Pallas kernels: 351 us -> 392 us
  local copies, waits for them, and re-layouts: 122 us -> 93 us
    ppermute x49, waiting for transfers between devices: 173 us -> 89.2 us  [swap(): return lax.ppermute(v, AX, pairs)]
    unnamed x299 -> x181, local copies, waits for them, and re-layouts: 84.2 us -> 48.5 us
    pallas_call x24, Pallas kernels: 240 us -> 274 us  [row_call(): pl.pallas_call(kernel, grid_spec=pltpu.PrefetchScalarGridSpec(num_scalar_...]
    pallas_call x5, Pallas kernels: 45.5 us -> 54 us  [weight_grad(): pl.pallas_call(kernel, grid_spec=pltpu.PrefetchScalarGridSpec(num_scalar_...]
  transfers between devices with their start and end apart: 53 -> 53, of which waited for: 16 -> 18; matrix products, arithmetic and copies ran while one was open for 4% -> 6% of each run, Pallas kernels for 39% -> 47%
where the time goes in v4:
time: 762 us; the launch traced here: 753 us
  Pallas kernels  392 us (51%)
  waiting for transfers between devices  205 us (27%)
  local copies, waits for them, and re-layouts  93 us (12%)
  starting transfers between devices  33.7 us (4%)
  between operations  15.4 us (2%)
  other arithmetic  13 us (2%)
    pallas_call x24, Pallas kernels, row_call(): pl.pallas_call(kernel, grid_spec=pltpu.PrefetchScalarGridSpec(num_scalar_...  274 us
    all_gather x2, waiting for transfers between devices, per_device(): lax.all_gather(v, 'shard', axis=0, tiled=True)  116 us
    ppermute x49, waiting for transfers between devices, swap(): return lax.ppermute(v, AX, pairs)  89.2 us
    pallas_call x5, Pallas kernels, weight_grad(): pl.pallas_call(kernel, grid_spec=pltpu.PrefetchScalarGridSpec(num_scalar_...  54 us
    unnamed x181, local copies, waits for them, and re-layouts  48.5 us
    ppermute x49, starting transfers between devices, swap(): return lax.ppermute(v, AX, pairs)  33.6 us
    pallas_call x2, Pallas kernels, chip_grad(): pl.pallas_call(kernel, grid_spec=pltpu.PrefetchScalarGridSpec(num_scalar_...  26.6 us
  transfers between devices with their start and end apart: 53, of which 18 were waited for; matrix products, arithmetic and copies ran while one was open for 6% of the time, Pallas kernels for 47%

profile of v4, /device:TPU:0, one launch (start us, length us, event | category | flops | bytes accessed | tf_op | source)
XLA Modules:
  0.0 752.7 jit_solution(4892087296737884701)
XLA Ops:
  28.6 110.5 %all-gather.5.cloned.1.call-done.refs_0_.refs_1_.refs_2_.refs_3_ = bf16[1024,10368]{1,0:T(8,128)(2,1)} async-done(((bf16[64,10368]{1,0:T(8,128)(2,1)}), bf16[1024,10368]{1,0:T(8,128)(2,1)}) %all-gather.5.cloned.1.call-update) | async-done | bytes 21233680 | tf_op jit(solution)/shard_map/all_gather | solution.py:822
  154.2 12.0 %shard_map.256 = (bf16[2,8,320,320]{3,2,1,0:T(8,128)(2,1)}, bf16[640,512]{1,0:T(8,128)(2,1)}, f32[640,1024]{1,0:T(8,128)}) custom-call(s32[4]{0:T(128)} %pad_add_fusion.where_ref, s32[2]{0:T(128)} %copy-done.72, bf16[8,2,64,10368]{3,2,1,0:T(8,128)(2,1)} %bitcast.93, bf16[640,1536]{1,0:T(8,128)(2,1)} %shard_map.255.refs_1_.refs_3_), custom_call_target="tpu_custom_call" | custom-call | flops 10000000 | tf_op jit(solution)/shard_map/pallas_call | solution.py:123
  178.0 13.6 %shard_map.257 = (bf16[2,8,320,320]{3,2,1,0:T(8,128)(2,1)}, bf16[640,512]{1,0:T(8,128)(2,1)}, f32[640,1024]{1,0:T(8,128)}, bf16[640,1024]{1,0:T(8,128)(2,1)}) custom-call(s32[4]{0:T(128)} %pad_add_fusion.where_ref, s32[2]{0:T(128)} %kept_ref.23, bf16[8,2,64,10368]{3,2,1,0:T(8,128)(2,1)} %bitcast.94, bf16[640,1536]{1,0:T(8,128)(2,1)} %shard_map.254.refs_1_.refs_3_, ...), custom_call_target="tpu_custom_call" | custom-call | flops 10000000 | tf_op jit(solution)/shard_map/pallas_call | solution.py:123
  195.9 9.7 %shard_map.259 = (bf16[640,2048]{1,0:T(8,128)(2,1)}, bf16[640,2048]{1,0:T(8,128)(2,1)}) custom-call(s32[4]{0:T(128)} %pad_add_fusion.where_ref, s32[2]{0:T(128)} %copy-done.72, bf16[1024,10368]{1,0:T(8,128)(2,1)} %all-gather.5.cloned.1.call-done.refs_0_.refs_1_.refs_2_.refs_3_, ...), custom_call_target="tpu_custom_call" | custom-call | flops 10000000 | tf_op jit(solution)/shard_map/pallas_call | solution.py:123
  224.1 9.7 %shard_map.258 = (bf16[640,2048]{1,0:T(8,128)(2,1)}, bf16[640,2048]{1,0:T(8,128)(2,1)}) custom-call(s32[4]{0:T(128)} %pad_add_fusion.where_ref, s32[2]{0:T(128)} %kept_ref.23, bf16[1024,10368]{1,0:T(8,128)(2,1)} %all-gather.5.cloned.1.call-done.refs_0_.refs_1_.refs_2_.refs_3_, ...), custom_call_target="tpu_custom_call" | custom-call | flops 10000000 | tf_op jit(solution)/shard_map/pallas_call | solution.py:123
  261.0 11.9 %shard_map.264 = (bf16[2,8,320,320]{3,2,1,0:T(8,128)(2,1)}, bf16[640,512]{1,0:T(8,128)(2,1)}, f32[640,1024]{1,0:T(8,128)}) custom-call(s32[4]{0:T(128)} %pad_add_fusion.where_ref, s32[2]{0:T(128)} %copy-done.72, bf16[8,2,64,10240]{3,2,1,0:T(8,128)(2,1)} %bitcast.97, bf16[640,1536]{1,0:T(8,128)(2,1)} %shard_map.263.refs_1_.refs_3_), custom_call_target="tpu_custom_call" | custom-call | flops 10000000 | tf_op jit(solution)/shard_map/pallas_call | solution.py:123
  284.8 13.8 %shard_map.265 = (bf16[2,8,320,320]{3,2,1,0:T(8,128)(2,1)}, bf16[640,512]{1,0:T(8,128)(2,1)}, f32[640,1024]{1,0:T(8,128)}, bf16[640,1024]{1,0:T(8,128)(2,1)}) custom-call(s32[4]{0:T(128)} %pad_add_fusion.where_ref, s32[2]{0:T(128)} %kept_ref.23, bf16[8,2,64,10240]{3,2,1,0:T(8,128)(2,1)} %bitcast.98, bf16[640,1536]{1,0:T(8,128)(2,1)} %shard_map.262.refs_1_.refs_3_, ...), custom_call_target="tpu_custom_call" | custom-call | flops 10000000 | tf_op jit(solution)/shard_map/pallas_call | solution.py:123
  313.1 9.6 %shard_map.267 = (bf16[640,2048]{1,0:T(8,128)(2,1)}, bf16[640,2048]{1,0:T(8,128)(2,1)}) custom-call(s32[4]{0:T(128)} %pad_add_fusion.where_ref, s32[2]{0:T(128)} %copy-done.72, bf16[1024,10240]{1,0:T(8,128)(2,1)} %all-gather.3.cloned.1.call-done.refs_0_.refs_1_.refs_2_.refs_3_, ...), custom_call_target="tpu_custom_call" | custom-call | flops 10000000 | tf_op jit(solution)/shard_map/pallas_call | solution.py:123
  323.8 13.3 %shard_map.268.refs_6_ = bf16[2048,1024]{1,0:T(8,128)(2,1)} custom-call(s32[4]{0:T(128)} %pad_add_fusion.where_ref, bf16[640,2048]{1,0:T(8,128)(2,1)} %get-tuple-element.129.xo.rest_0_.refs_2_, bf16[640,2048]{1,0:T(8,128)(2,1)} %get-tuple-element.130.xt.refs_2_, bf16[640,1024]{1,0:T(8,128)(2,1)} %bitcast_convert_fusion.yo.refs_4_, ...), custom_call_target="tpu_custom_call" | custom-call | flops 30000001024 | tf_op jit(solution)/shard_map/pallas_call | solution.py:454
  337.2 11.9 %shard_map.269 = (bf16[640,2048]{1,0:T(8,128)(2,1)}, f32[640,1024]{1,0:T(8,128)}) custom-call(s32[4]{0:T(128)} %pad_add_fusion.where_ref, s32[2]{0:T(128)} %copy-done.72, bf16[1024,10240]{1,0:T(8,128)(2,1)} %all-gather.3.cloned.1.call-done.refs_0_.refs_1_.refs_2_.refs_3_, bf16[1024,1024]{1,0:T(8,128)(2,1)} %collective-permute-done.rest_1_.refs_1_, ...), custom_call_target="tpu_custom_call" | custom-call | flops 30000001024 | tf_op jit(solution)/shard_map/pallas_call | solution.py:123
  358.6 16.3 %shard_map.271 = (bf16[640,2048]{1,0:T(8,128)(2,1)}, f32[640,1024]{1,0:T(8,128)}, bf16[640,1024]{1,0:T(8,128)(2,1)}, f32[8,1024]{1,0:T(8,128)}) custom-call(s32[4]{0:T(128)} %pad_add_fusion.where_ref, s32[2]{0:T(128)} %kept_ref.23, bf16[1024,10240]{1,0:T(8,128)(2,1)} %all-gather.3.cloned.1.call-done.refs_0_.refs_1_.refs_2_.refs_3_, ...), custom_call_target="tpu_custom_call" | custom-call | flops 30000001024 | tf_op jit(solution)/shard_map/pallas_call | solution.py:123
  374.9 13.2 %shard_map.272 = (bf16[1,2,2,2,128,1280]{5,4,3,2,1,0:T(8,128)(2,1)}, bf16[1,2,2,2,128,1280]{5,4,3,2,1,0:T(8,128)(2,1)}, f32[1,2048]{1,0:T(1,128)}) custom-call(s32[4]{0:T(128)} %pad_add_fusion.where_ref, bf16[640,1024]{1,0:T(8,128)(2,1)} %get-tuple-element.128.refs_2_.xo, bf16[640,1024]{1,0:T(8,128)(2,1)} %collective-permute-done.9.refs_2_.xt, ...), custom_call_target="tpu_custom_call" | custom-call | flops 30000001024 | tf_op jit(solution)/shard_map/pallas_call | solution.py:412
  392.6 16.5 %shard_map.273 = (bf16[640,1536]{1,0:T(8,128)(2,1)}, f32[640,1024]{1,0:T(8,128)}) custom-call(s32[4]{0:T(128)} %pad_add_fusion.where_ref, s32[2]{0:T(128)} %copy-done.72, bf16[8,2,64,10240]{3,2,1,0:T(8,128)(2,1)} %bitcast.99, bf16[1024,10240]{1,0:T(8,128)(2,1)} %all-gather.3.cloned.1.call-done.refs_0_.refs_1_.refs_2_.refs_3_, bf16[640,1024]{1,0:T(8,128)(2,1)} %copy-done.78, ...), custom_call_target="tpu_custom_call" | custom-call | flops 30000001024 | tf_op jit(solution)/shard_map/pallas_call | solution.py:123
  415.5 19.2 %shard_map.275 = (bf16[640,1536]{1,0:T(8,128)(2,1)}, f32[640,1024]{1,0:T(8,128)}, bf16[640,1024]{1,0:T(8,128)(2,1)}, f32[8,1024]{1,0:T(8,128)}) custom-call(s32[4]{0:T(128)} %pad_add_fusion.where_ref, s32[2]{0:T(128)} %kept_ref.23, bf16[8,2,64,10240]{3,2,1,0:T(8,128)(2,1)} %bitcast.100, ...), custom_call_target="tpu_custom_call" | custom-call | flops 30000001024 | tf_op jit(solution)/shard_map/pallas_call | solution.py:123
  434.8 11.1 %shard_map.276 = (bf16[2,2,2,1,128,768]{5,4,3,2,1,0:T(8,128)(2,1)}, bf16[2,2,2,1,128,768]{5,4,3,2,1,0:T(8,128)(2,1)}, f32[1,1536]{1,0:T(1,128)}) custom-call(s32[4]{0:T(128)} %pad_add_fusion.where_ref, bf16[640,1024]{1,0:T(8,128)(2,1)} %get-tuple-element.125.refs_1_.xo, bf16[640,1024]{1,0:T(8,128)(2,1)} %copy-done.56, ...), custom_call_target="tpu_custom_call" | custom-call | flops 30000001024 | tf_op jit(solution)/shard_map/pallas_call | solution.py:412
  450.5 11.7 %shard_map.277 = (bf16[640,2048]{1,0:T(8,128)(2,1)}, f32[640,1024]{1,0:T(8,128)}) custom-call(s32[4]{0:T(128)} %pad_add_fusion.where_ref, s32[2]{0:T(128)} %copy-done.72, bf16[1024,10368]{1,0:T(8,128)(2,1)} %all-gather.5.cloned.1.call-done.refs_0_.refs_1_.refs_2_.refs_3_, bf16[1024,1024]{1,0:T(8,128)(2,1)} %collective-permute-done.1.refs_1_, ...), custom_call_target="tpu_custom_call" | custom-call | flops 30000001024 | tf_op jit(solution)/shard_map/pallas_call | solution.py:123
  462.5 13.3 %shard_map.278.rest_0_.refs_10_ = bf16[2048,1024]{1,0:T(8,128)(2,1)} custom-call(s32[4]{0:T(128)} %pad_add_fusion.where_ref, bf16[640,2048]{1,0:T(8,128)(2,1)} %get-tuple-element.122.refs_2_.xo, bf16[640,2048]{1,0:T(8,128)(2,1)} %get-tuple-element.123.refs_2_.xt, bf16[640,1024]{1,0:T(8,128)(2,1)} %get-tuple-element.148.yo.refs_4_, ...), custom_call_target="tpu_custom_call" | custom-call | flops 30000001024 | tf_op jit(solution)/shard_map/pallas_call | solution.py:454
  483.5 15.1 %shard_map.280 = (bf16[640,2048]{1,0:T(8,128)(2,1)}, f32[640,1024]{1,0:T(8,128)}, bf16[640,1024]{1,0:T(8,128)(2,1)}, f32[8,1024]{1,0:T(8,128)}) custom-call(s32[4]{0:T(128)} %pad_add_fusion.where_ref, s32[2]{0:T(128)} %kept_ref.23, bf16[1024,10368]{1,0:T(8,128)(2,1)} %all-gather.5.cloned.1.call-done.refs_0_.refs_1_.refs_2_.refs_3_, ...), custom_call_target="tpu_custom_call" | custom-call | flops 30000001024 | tf_op jit(solution)/shard_map/pallas_call | solution.py:123
  505.7 13.3 %shard_map.282 = (bf16[1,2,2,2,128,1280]{5,4,3,2,1,0:T(8,128)(2,1)}, bf16[1,2,2,2,128,1280]{5,4,3,2,1,0:T(8,128)(2,1)}, f32[1,2048]{1,0:T(1,128)}) custom-call(s32[4]{0:T(128)} %pad_add_fusion.where_ref, bf16[640,1024]{1,0:T(8,128)(2,1)} %get-tuple-element.121.refs_2_.xo, bf16[640,1024]{1,0:T(8,128)(2,1)} %copy-done.57, ...), custom_call_target="tpu_custom_call" | custom-call | flops 30000001024 | tf_op jit(solution)/shard_map/pallas_call | solution.py:412
  542.6 16.2 %shard_map.286 = (bf16[640,1536]{1,0:T(8,128)(2,1)}, f32[640,1024]{1,0:T(8,128)}) custom-call(s32[4]{0:T(128)} %pad_add_fusion.where_ref, s32[2]{0:T(128)} %copy-done.72, bf16[8,2,64,10368]{3,2,1,0:T(8,128)(2,1)} %bitcast.95, bf16[1024,10368]{1,0:T(8,128)(2,1)} %all-gather.5.cloned.1.call-done.refs_0_.refs_1_.refs_2_.refs_3_, ...), custom_call_target="tpu_custom_call" | custom-call | flops 30000001024 | tf_op jit(solution)/shard_map/pallas_call | solution.py:123
  572.0 19.3 %shard_map.289 = (bf16[640,1536]{1,0:T(8,128)(2,1)}, f32[640,1024]{1,0:T(8,128)}, bf16[640,1024]{1,0:T(8,128)(2,1)}, f32[8,1024]{1,0:T(8,128)}) custom-call(s32[4]{0:T(128)} %pad_add_fusion.where_ref, s32[2]{0:T(128)} %kept_ref.23, bf16[8,2,64,10368]{3,2,1,0:T(8,128)(2,1)} %bitcast.96, ...), custom_call_target="tpu_custom_call" | custom-call | flops 30000001024 | tf_op jit(solution)/shard_map/pallas_call | solution.py:123
  630.1 12.9 %collective-permute-done.29 = f32[2,16,768]{2,1,0:T(8,128)S(1)} collective-permute-done((f32[2,16,768]{2,1,0:T(8,128)S(1)}, f32[2,16,768]{2,1,0:T(8,128)S(1)}, u32[]{:S(2)}, u32[]{:S(2)}) %collective-permute-start.29) | collective-permute-done | bytes 98336 | tf_op jit(solution)/shard_map/ppermute | solution.py:40
  719.8 10.2 %collective-permute-done.43.refs_1_ = bf16[256,1024]{1,0:T(8,128)(2,1)S(1)} collective-permute-done((bf16[256,1024]{1,0:T(8,128)(2,1)S(1)}, bf16[256,1024]{1,0:T(8,128)(2,1)S(1)}, u32[]{:S(2)}, u32[]{:S(2)}) %collective-permute-start.43) | collective-permute-done | bytes 524320 | tf_op jit(solution)/shard_map/ppermute | solution.py:40
  730.0 10.5 %collective-permute-done.48.refs_3_ = bf16[64,4096]{1,0:T(8,128)(2,1)S(1)} collective-permute-done((bf16[64,4096]{1,0:T(8,128)(2,1)S(1)}, bf16[64,4096]{1,0:T(8,128)(2,1)S(1)}, u32[]{:S(2)}, u32[]{:S(2)}) %collective-permute-start.48) | collective-permute-done | bytes 524320 | tf_op jit(solution)/shard_map/ppermute | solution.py:40
  (464 shorter events, 322.5 us)
Async XLA Ops:
  7.2 131.9 %all-gather.5.cloned.1.call-start = ((), (), s32[]{:S(2)}) async-start(), calls=%async_computation.3 | async-start | bytes 22560768 | tf_op jit(solution)/shard_map/all_gather | solution.py:822
  26.2 223.9 %all-gather.3.cloned.1.call-start = ((), (), s32[]{:S(2)}) async-start(), calls=%async_computation.2 | async-start | bytes 22282240 | tf_op jit(solution)/shard_map/all_gather | solution.py:822
  27.6 491.3 %reduce-scatter.3.cloned.1.call-start = ((), (), s32[]{:S(2)}) async-start(), calls=%async_computation.4 | async-start | bytes 4718592 | tf_op jit(solution)/shard_map/reduce_scatter | solution.py:671
  166.4 47.9 %collective-permute-start.1 = (bf16[1024,1024]{1,0:T(8,128)(2,1)S(1)}, bf16[1024,1024]{1,0:T(8,128)(2,1)}, u32[]{:S(2)}, u32[]{:S(2)}) collective-permute-start(bf16[1024,1024]{1,0:T(8,128)(2,1)S(1)} %copy-done.51), channel_id=1, source_target_pairs={{0,1},{1,0},{2,3},{3,2},{4,5},{5,4},{6,7},{7,6},{8,9},{9,8},{10,11... | collective-permute-start | bytes 6291464 | tf_op jit(solution)/shard_map/ppermute | solution.py:40
  273.3 49.4 %collective-permute-start = (bf16[1024,1024]{1,0:T(8,128)(2,1)}, bf16[1024,1024]{1,0:T(8,128)(2,1)}, u32[]{:S(2)}, u32[]{:S(2)}) collective-permute-start(bf16[1024,1024]{1,0:T(8,128)(2,1)} %constant_dynamic-slice_fusion.2.refs_3_), channel_id=1, source_target_pairs={{0,1},{1,0},{2,3},{3,2},{4,5},{5,4},{6,7},{7,6},{8,9},{9,8},{10,11... | collective-permute-start | bytes 6291464 | tf_op jit(solution)/shard_map/ppermute | solution.py:40
  300.0 22.7 %collective-permute-start.10 = (bf16[640,1024]{1,0:T(8,128)(2,1)}, bf16[640,1024]{1,0:T(8,128)(2,1)S(1)}, u32[]{:S(2)}, u32[]{:S(2)}) collective-permute-start(bf16[640,1024]{1,0:T(8,128)(2,1)} %bitcast_convert_fusion.yo.refs_4_), channel_id=1, source_target_pairs={{0,2},{1,3},{2,0},{3,1},{4,6},{5,7},{6,4},{7,5},{8,10},{9,11},{10,... | collective-permute-start | bytes 3932168 | tf_op jit(solution)/shard_map/ppermute | solution.py:40
  337.1 260.2 %reduce-scatter.5.cloned.1.call-start = ((), (), s32[]{:S(2)}) async-start(), calls=%async_computation.5 | async-start | bytes 4718592 | tf_op jit(solution)/shard_map/reduce_scatter | solution.py:671
  356.6 286.8 %collective-permute-start.11 = (f32[640,1024]{1,0:T(8,128)}, f32[640,1024]{1,0:T(8,128)}, u32[]{:S(2)}, u32[]{:S(2)}) collective-permute-start(f32[640,1024]{1,0:T(8,128)} %shard_map.270.refs_10_), channel_id=1, source_target_pairs={{0,2},{1,3},{2,0},{3,1},{4,6},{5,7},{6,4},{7,5},{8,10},{9,11},{10,... | collective-permute-start | bytes 7864328 | tf_op jit(solution)/shard_map/ppermute | solution.py:40
  415.1 60.8 %collective-permute-start.17 = (bf16[1,2,2,2,128,1280]{5,4,3,2,1,0:T(8,128)(2,1)}, bf16[1,2,2,2,128,1280]{5,4,3,2,1,0:T(8,128)(2,1)S(1)}, u32[]{:S(2)}, u32[]{:S(2)}) collective-permute-start(bf16[1,2,2,2,128,1280]{5,4,3,2,1,0:T(8,128)(2,1)} %get-tuple-element.147.refs_9_), channel_id=1, source_target_pairs={{0,1},{1,0},{2,3},{3,2},{4,5},{5,4},{6,7},{7,6},{8,9},{9,8},{10,11... | collective-permute-start | bytes 7864328 | tf_op jit(solution)/shard_map/ppermute | solution.py:40
  448.6 50.2 %collective-permute-start.19 = (bf16[2,2,2,1,128,768]{5,4,3,2,1,0:T(8,128)(2,1)}, bf16[2,2,2,1,128,768]{5,4,3,2,1,0:T(8,128)(2,1)}, u32[]{:S(2)}, u32[]{:S(2)}) collective-permute-start(bf16[2,2,2,1,128,768]{5,4,3,2,1,0:T(8,128)(2,1)} %get-tuple-element.152.refs_6_), channel_id=1, source_target_pairs={{0,4},{1,5},{2,6},{3,7},{4,0},{5,1},{6,2},{7,3},{8,12},{9,13},{10,... | collective-permute-start | bytes 4718600 | tf_op jit(solution)/shard_map/ppermute | solution.py:40
  482.7 44.6 %collective-permute-start.21 = (bf16[1,2,2,1,128,1280]{5,4,3,2,1,0:T(8,128)(2,1)}, bf16[1,2,2,1,128,1280]{5,4,3,2,1,0:T(8,128)(2,1)S(1)}, u32[]{:S(2)}, u32[]{:S(2)}) collective-permute-start(bf16[1,2,2,1,128,1280]{5,4,3,2,1,0:T(8,128)(2,1)} %get-tuple-element.157.refs_11_), channel_id=1, source_target_pairs={{0,4},{1,5},{2,6},{3,7},{4,0},{5,1},{6,2},{7,3},{8,12},{9,13},{10,... | collective-permute-start | bytes 3932168 | tf_op jit(solution)/shard_map/ppermute | solution.py:40
  498.7 44.0 %collective-permute-start.18 = (bf16[640,1024]{1,0:T(8,128)(2,1)}, bf16[640,1024]{1,0:T(8,128)(2,1)}, u32[]{:S(2)}, u32[]{:S(2)}) collective-permute-start(bf16[640,1024]{1,0:T(8,128)(2,1)} %get-tuple-element.158.rest_0_.yo.refs_2_), channel_id=1, source_target_pairs={{0,2},{1,3},{2,0},{3,1},{4,6},{5,7},{6,4},{7,5},{8,10},{9,11},{10,... | collective-permute-start | bytes 3932168 | tf_op jit(solution)/shard_map/ppermute | solution.py:40
  504.1 36.5 %collective-permute-start.20 = (bf16[2,2,1,1,128,768]{5,4,3,2,1,0:T(8,128)(2,1)S(1)}, bf16[2,2,1,1,128,768]{5,4,3,2,1,0:T(8,128)(2,1)S(1)}, u32[]{:S(2)}, u32[]{:S(2)}) collective-permute-start(bf16[2,2,1,1,128,768]{5,4,3,2,1,0:T(8,128)(2,1)S(1)} %get-tuple-element.163.rest_1_), channel_id=1, source_target_pairs={{0,8},{1,9},{2,10},{3,11},{4,12},{5,13},{6,14},{7,15},{8,0},{9,1},... | collective-permute-start | bytes 2359304 | tf_op jit(solution)/shard_map/ppermute | solution.py:40
  527.2 38.3 %collective-permute-start.23 = (bf16[128,1024]{1,0:T(8,128)(2,1)S(1)}, bf16[128,1024]{1,0:T(8,128)(2,1)S(1)}, u32[]{:S(2)}, u32[]{:S(2)}) collective-permute-start(bf16[128,1024]{1,0:T(8,128)(2,1)S(1)} %get-tuple-element.169.refs_8_), channel_id=1, source_target_pairs={{0,2},{1,3},{2,0},{3,1},{4,6},{5,7},{6,4},{7,5},{8,10},{9,11},{10,... | collective-permute-start | bytes 786440 | tf_op jit(solution)/shard_map/ppermute | solution.py:40
  532.6 59.8 %collective-permute-start.25 = (bf16[1,2,1,1,128,1280]{5,4,3,2,1,0:T(8,128)(2,1)}, bf16[1,2,1,1,128,1280]{5,4,3,2,1,0:T(8,128)(2,1)}, u32[]{:S(2)}, u32[]{:S(2)}) collective-permute-start(bf16[1,2,1,1,128,1280]{5,4,3,2,1,0:T(8,128)(2,1)} %get-tuple-element.168.refs_7_), channel_id=1, source_target_pairs={{0,8},{1,9},{2,10},{3,11},{4,12},{5,13},{6,14},{7,15},{8,0},{9,1},... | collective-permute-start | bytes 1966088 | tf_op jit(solution)/shard_map/ppermute | solution.py:40
  541.1 51.3 %collective-permute-start.24 = (bf16[1,2,1,1,128,768]{5,4,3,2,1,0:T(8,128)(2,1)S(1)}, bf16[1,2,1,1,128,768]{5,4,3,2,1,0:T(8,128)(2,1)S(1)}, u32[]{:S(2)}, u32[]{:S(2)}) collective-permute-start(bf16[1,2,1,1,128,768]{5,4,3,2,1,0:T(8,128)(2,1)S(1)} %get-tuple-element.166.refs_6_), channel_id=1, source_target_pairs={{0,1},{1,0},{2,3},{3,2},{4,5},{5,4},{6,7},{7,6},{8,9},{9,8},{10,11... | collective-permute-start | bytes 1179656 | tf_op jit(solution)/shard_map/ppermute | solution.py:40
  564.7 60.0 %collective-permute-start.26 = (bf16[1,2,2,2,128,1280]{5,4,3,2,1,0:T(8,128)(2,1)}, bf16[1,2,2,2,128,1280]{5,4,3,2,1,0:T(8,128)(2,1)}, u32[]{:S(2)}, u32[]{:S(2)}) collective-permute-start(bf16[1,2,2,2,128,1280]{5,4,3,2,1,0:T(8,128)(2,1)} %get-tuple-element.176.refs_2_.refs_9_), channel_id=1, source_target_pairs={{0,1},{1,0},{2,3},{3,2},{4,5},{5,4},{6,7},{7,6},{8,9},{9,8},{10,11... | collective-permute-start | bytes 7864328 | tf_op jit(solution)/shard_map/ppermute | solution.py:40
  595.2 26.1 %collective-permute-start.27 = (bf16[128,2048]{1,0:T(8,128)(2,1)S(1)}, bf16[128,2048]{1,0:T(8,128)(2,1)S(1)}, u32[]{:S(2)}, u32[]{:S(2)}) collective-permute-start(bf16[128,2048]{1,0:T(8,128)(2,1)S(1)} %get-tuple-element.181.rest_1_), channel_id=1, source_target_pairs={{0,16},{1,17},{2,18},{3,19},{4,20},{5,21},{6,22},{7,23},{8,24},{9,... | collective-permute-start | bytes 1572872 | tf_op jit(solution)/shard_map/ppermute | solution.py:40
  610.0 44.9 %collective-permute-start.34 = (bf16[2,2,1,2,128,384]{5,4,3,2,1,0:T(8,128)(2,1)}, bf16[2,2,1,2,128,384]{5,4,3,2,1,0:T(8,128)(2,1)S(1)}, u32[]{:S(2)}, u32[]{:S(2)}) collective-permute-start(bf16[2,2,1,2,128,384]{5,4,3,2,1,0:T(8,128)(2,1)} %get-tuple-element.183.rest_0_), channel_id=1, source_target_pairs={{0,8},{1,9},{2,10},{3,11},{4,12},{5,13},{6,14},{7,15},{8,0},{9,1},... | collective-permute-start | bytes 2359304 | tf_op jit(solution)/shard_map/ppermute | solution.py:40
  621.3 36.7 %collective-permute-start.37 = (bf16[1,2,2,2,128,384]{5,4,3,2,1,0:T(8,128)(2,1)}, bf16[1,2,2,2,128,384]{5,4,3,2,1,0:T(8,128)(2,1)S(1)}, u32[]{:S(2)}, u32[]{:S(2)}) collective-permute-start(bf16[1,2,2,2,128,384]{5,4,3,2,1,0:T(8,128)(2,1)} %get-tuple-element.184.rest_0_.refs_2_.refs_6_), channel_id=1, source_target_pairs={{0,1},{1,0},{2,3},{3,2},{4,5},{5,4},{6,7},{7,6},{8,9},{9,8},{10,11... | collective-permute-start | bytes 2359304 | tf_op jit(solution)/shard_map/ppermute | solution.py:40
  624.6 35.0 %collective-permute-start.36 = (bf16[64,1792]{1,0:T(8,128)(2,1)S(1)}, bf16[64,1792]{1,0:T(8,128)(2,1)S(1)}, u32[]{:S(2)}, u32[]{:S(2)}) collective-permute-start(bf16[64,1792]{1,0:T(8,128)(2,1)S(1)} %get-tuple-element.188.refs_8_), channel_id=1, source_target_pairs={{0,2},{1,3},{2,0},{3,1},{4,6},{5,7},{6,4},{7,5},{8,10},{9,11},{10,... | collective-permute-start | bytes 688136 | tf_op jit(solution)/shard_map/ppermute | solution.py:40
  643.0 32.0 %collective-permute-start.40 = (bf16[1,2,2,1,128,1280]{5,4,3,2,1,0:T(8,128)(2,1)}, bf16[1,2,2,1,128,1280]{5,4,3,2,1,0:T(8,128)(2,1)}, u32[]{:S(2)}, u32[]{:S(2)}) collective-permute-start(bf16[1,2,2,1,128,1280]{5,4,3,2,1,0:T(8,128)(2,1)} %get-tuple-element.186.refs_7_), channel_id=1, source_target_pairs={{0,4},{1,5},{2,6},{3,7},{4,0},{5,1},{6,2},{7,3},{8,12},{9,13},{10,... | collective-permute-start | bytes 3932168 | tf_op jit(solution)/shard_map/ppermute | solution.py:40
  654.2 24.5 %collective-permute-start.31 = (f32[2,16,768]{2,1,0:T(8,128)}, f32[2,16,768]{2,1,0:T(8,128)}, u32[]{:S(2)}, u32[]{:S(2)}) collective-permute-start(f32[2,16,768]{2,1,0:T(8,128)} %add.72.refs_7_), channel_id=1, source_target_pairs={{0,8},{1,9},{2,10},{3,11},{4,12},{5,13},{6,14},{7,15},{8,0},{9,1},... | collective-permute-start | bytes 294920 | tf_op jit(solution)/shard_map/ppermute | solution.py:40
  717.0 23.5 %collective-permute-start.48 = (bf16[64,4096]{1,0:T(8,128)(2,1)S(1)}, bf16[64,4096]{1,0:T(8,128)(2,1)S(1)}, u32[]{:S(2)}, u32[]{:S(2)}) collective-permute-start(bf16[64,4096]{1,0:T(8,128)(2,1)S(1)} %shard_map.307.refs_2_.refs_8_), channel_id=1, source_target_pairs={{0,1},{1,0},{2,3},{3,2},{4,5},{5,4},{6,7},{7,6},{8,9},{9,8},{10,11... | collective-permute-start | bytes 1572872 | tf_op jit(solution)/shard_map/ppermute | solution.py:40
  (113 other events, 890.0 us)
Sparse Core Ops, SparseCore 0:
  26.3 112.7 all-gather.4
  141.3 108.8 all-gather.2
  337.2 86.9 reduce-scatter.2
  476.0 106.5 reduce-scatter.4

commit v5 on v4

--- a/solution.py
+++ b/solution.py
@@ -766,6 +766,58 @@
     )(where, *args)
 
 
+def pack(plan, where, layer, qkv, proj, fc1, fc2, extra, after):
+    deep, width = proj.shape[1:]
+    ff, n = fc1.shape[2], plan.shards
+    quarters = fc2.shape[1] // deep
+    halves = quarters // 2
+    each = halves // plan.ny
+    ins = [qkv, proj, fc1, fc2] + ([extra] if extra is not None else [])
+    total = 4 * width + ff + 2 * each * width + (extra.shape[1] if extra is not None else 0)
+
+    def kernel(where_ref, *refs):
+        out = refs[-1]
+
+        def lay(at, pieces):
+            held, wide = [], 0
+            for p in pieces:
+                held.append(p)
+                wide += p.shape[1]
+                if wide % 128 == 0:
+                    out[:, at : at + wide] = held[0] if len(held) == 1 else jnp.concatenate(held, axis=1)
+                    at, held, wide = at + wide, [], 0
+
+        for p in range(2):
+            cols = [k * 2 * HEAD_DIM + p * HEAD_DIM for k in range(3 * HEADS // 2)]
+            lay(p * (3 * width // 2), [refs[0][0, :, k : k + HEAD_DIM] for k in cols])
+        out[:, 3 * width : 4 * width] = refs[1][0]
+        cols = [s * quarters * deep + k * deep for k in range(quarters) for s in range(n)]
+        lay(4 * width, [refs[2][0, :, k : k + deep] for k in cols])
+        at = 4 * width + ff
+        for p in range(2):
+            for k in range(each):
+                row = (p * halves + k) * deep + where_ref[3] * deep
+                out[:, at : at + width] = refs[3][0, pl.ds(pl.multiple_of(row, 16), deep)]
+                at += width
+        if extra is not None:
+            out[:, at:] = refs[4][...]
+
+    specs = [pl.BlockSpec((1,) + v.shape[1:], lambda i, w: (layer, 0, 0)) for v in ins[:4]]
+    specs += [pl.BlockSpec(v.shape, lambda i, w: (0, 0)) for v in ins[4:]]
+    return pl.pallas_call(
+        kernel,
+        grid_spec=pltpu.PrefetchScalarGridSpec(
+            num_scalar_prefetch=1,
+            grid=(1,),
+            in_specs=specs + [ANY] * len(after),
+            out_specs=pl.BlockSpec((deep, total), lambda i, w: (0, 0)),
+        ),
+        out_shape=jax.ShapeDtypeStruct((deep, total), BF),
+        compiler_params=pltpu.CompilerParams(vmem_limit_bytes=SMALL_LIMIT),
+        cost_estimate=FORWARD,
+    )(where, *ins, *after)
+
+
 def per_device(
     plan,
     tokens,
@@ -809,17 +861,11 @@
     block = n * deep
     each = halves // plan.ny
 
-    def merged(layer):
-        qkv = qkv_weight[layer].reshape(deep, 3 * half_heads, 2, HEAD_DIM).swapaxes(1, 2).reshape(deep, 3 * width)
-        fc1 = fc1_weight[layer].reshape(deep, n, quarters, deep).swapaxes(1, 2).reshape(deep, ff)
-        fc2 = fc2_weight[layer].reshape(2, halves, deep, width)
-        if plan.ny == 2:
-            fc2 = pick(y, fc2[:, :1], fc2[:, 1:])
-        fc2 = [fc2[p, k] for p in range(2) for k in range(each)]
-        return [qkv, proj_weight[layer], fc1] + fc2 + ([] if layer else [extra])
-
-    operands = [jnp.concatenate(merged(layer), axis=1) for layer in range(layers)]
-    gathered = [lax.all_gather(v, "shard", axis=0, tiled=True) for v in operands]
+    gathered, done = [], ()
+    for layer in range(layers):
+        shards = (qkv_weight, proj_weight, fc1_weight, fc2_weight)
+        done = (pack(plan, where, layer, *shards, None if layer else extra, done),)
+        gathered.append(lax.all_gather(done[0], "shard", axis=0, tiled=True))
     at_fc1, at_fc2 = lead // block, (lead + ff) // block
     mlp_parts = []
     for layer in range(layers):
@@ -1057,12 +1103,15 @@
     got_vec = plan.core(vec)
     vec_axes = list(axes)
 
-    def step_vec():
+    def step_vec(prev):
         nonlocal vec, got_vec
-        vec = vec + got_vec
-        sent = vec
+
+        def kernel(where, ins, outs):
+            outs[0][...] = ins[0][...] + ins[1][...]
+
+        vec = small_call(kernel, where, [vec, got_vec], [(vec.shape, F32)], prev)[0]
         got_vec = plan.flip(vec, vec_axes.pop(0)) if vec_axes else None
-        return (sent,)
+        return (vec,)
 
     prev += (terms["f1", 0].step(prev[:1]),)
     prev += (ends["rest", 1].core(prev[:1]),)
@@ -1071,19 +1120,22 @@
         down_last, w, 1, ["fc2"], [saved[w]["hid"][0], last_part, saved[w]["middle"]], [vecs[w]["f2b"]], [low_rows], prev
     )[0]
     qa, qb = terms["q", 0]
-    prev = (qa.step((mixed,)),) + step_vec()
+    prev = (ends["f2", 0].rep(step_vec((mixed,))),)
+    prev = (qa.step(prev),)
     prev = (qb.step(prev),)
-    prev = (ends["rest", 1].rep(prev),) + step_vec()
+    prev = (ends["rest", 1].rep(prev),)
+    prev = step_vec(prev)
     prev = (qa.step(prev),)
     prev = (terms["f1", 0].step(prev),)
-    prev = (qb.step(prev),) + step_vec()
-    prev = end_rest(0, prev) + step_vec()
-    prev = (ends["f2", 0].rep(prev),)
+    prev = (qb.step(prev),)
+    prev = step_vec(prev)
+    prev = end_rest(0, prev)
+    prev = step_vec(prev)
     placed = place(1, None, prev)
     prev = (placed[0],)
     while got_vec is not None:
-        prev += step_vec()
-    prev = (ends["rest", 0].core(prev),)
+        prev = step_vec(prev)
+    prev = (ends["rest", 0].core(prev + tuple(ends["f2", 0].pair[1:])),)
     prev = (ends["rest", 0].rep(prev),)
     placed = place(0, placed, prev)
     if plan.ny == 1:

time: 762 us -> 754 us (0.990)
  local copies, waits for them, and re-layouts: 93 us -> 78.4 us
  Pallas kernels: 392 us -> 405 us
    unnamed x181 -> x176, local copies, waits for them, and re-layouts: 48.5 us -> 46.8 us
  transfers between devices with their start and end apart: 53 -> 53, of which waited for: 18 -> 17; matrix products, arithmetic and copies ran while one was open for 6% -> 6% of each run, Pallas kernels for 47% -> 49%
where the time goes in v5:
time: 754 us; the launch traced here: 749 us
  Pallas kernels  405 us (54%)
  waiting for transfers between devices  206 us (27%)
  local copies, waits for them, and re-layouts  78.4 us (10%)
  starting transfers between devices  32.6 us (4%)
  between operations  15.1 us (2%)
  other arithmetic  12.2 us (2%)
    pallas_call x24, Pallas kernels, row_call(): pl.pallas_call(kernel, grid_spec=pltpu.PrefetchScalarGridSpec(num_scalar_...  274 us
    all_gather x2, waiting for transfers between devices, per_device(): gathered.append(lax.all_gather(done[0], 'shard', axis=0, tiled=True))  114 us
    ppermute x49, waiting for transfers between devices, swap(): return lax.ppermute(v, AX, pairs)  91.4 us
    pallas_call x5, Pallas kernels, weight_grad(): pl.pallas_call(kernel, grid_spec=pltpu.PrefetchScalarGridSpec(num_scalar_...  53.7 us
    unnamed x176, local copies, waits for them, and re-layouts  46.8 us
    ppermute x49, starting transfers between devices, swap(): return lax.ppermute(v, AX, pairs)  32.4 us
    pallas_call x2, Pallas kernels, chip_grad(): pl.pallas_call(kernel, grid_spec=pltpu.PrefetchScalarGridSpec(num_scalar_...  26.6 us
  transfers between devices with their start and end apart: 53, of which 17 were waited for; matrix products, arithmetic and copies ran while one was open for 6% of the time, Pallas kernels for 49%

profile of v5, /device:TPU:0, one launch (start us, length us, event | category | flops | bytes accessed | tf_op | source)
XLA Modules:
  0.0 749.1 jit_solution(2189254189540224476)
XLA Ops:
  19.2 108.5 %all-gather.5.cloned.1.call-done.refs_0_.refs_1_.refs_2_.refs_3_ = bf16[1024,10368]{1,0:T(8,128)(2,1)} async-done(((bf16[64,10368]{1,0:T(8,128)(2,1)}), bf16[1024,10368]{1,0:T(8,128)(2,1)}) %all-gather.5.cloned.1.call-update) | async-done | bytes 21233680 | tf_op jit(solution)/shard_map/all_gather | solution.py:868
  142.3 12.0 %shard_map.258 = (bf16[2,8,320,320]{3,2,1,0:T(8,128)(2,1)}, bf16[640,512]{1,0:T(8,128)(2,1)}, f32[640,1024]{1,0:T(8,128)}) custom-call(s32[4]{0:T(128)} %copy-done.9, s32[2]{0:T(128)} %copy-done.74, bf16[8,2,64,10368]{3,2,1,0:T(8,128)(2,1)} %bitcast.53, bf16[640,1536]{1,0:T(8,128)(2,1)} %shard_map.257.refs_1_.refs_3_), custom_call_target="tpu_custom_call" | custom-call | flops 10000000 | tf_op jit(solution)/shard_map/pallas_call | solution.py:123
  166.2 13.6 %shard_map.259 = (bf16[2,8,320,320]{3,2,1,0:T(8,128)(2,1)}, bf16[640,512]{1,0:T(8,128)(2,1)}, f32[640,1024]{1,0:T(8,128)}, bf16[640,1024]{1,0:T(8,128)(2,1)}) custom-call(s32[4]{0:T(128)} %copy-done.9, s32[2]{0:T(128)} %kept_ref.23, bf16[8,2,64,10368]{3,2,1,0:T(8,128)(2,1)} %bitcast.54, bf16[640,1536]{1,0:T(8,128)(2,1)} %shard_map.256.refs_1_.refs_3_, ...), custom_call_target="tpu_custom_call" | custom-call | flops 10000000 | tf_op jit(solution)/shard_map/pallas_call | solution.py:123
  184.1 9.8 %shard_map.261 = (bf16[640,2048]{1,0:T(8,128)(2,1)}, bf16[640,2048]{1,0:T(8,128)(2,1)}) custom-call(s32[4]{0:T(128)} %copy-done.9, s32[2]{0:T(128)} %copy-done.74, bf16[1024,10368]{1,0:T(8,128)(2,1)} %all-gather.5.cloned.1.call-done.refs_0_.refs_1_.refs_2_.refs_3_, bf16[1024,10368]{1,0:T(8,128)(2,1)} %all-gather.5.cloned.1.call-done.refs_0_.refs_1_.refs_2_.refs_3_, ...), custom_call_target="tpu_custom_call" | custom-call | flops 10000000 | tf_op jit(solution)/shard_map/pallas_call | solution.py:123
  249.6 11.9 %shard_map.266 = (bf16[2,8,320,320]{3,2,1,0:T(8,128)(2,1)}, bf16[640,512]{1,0:T(8,128)(2,1)}, f32[640,1024]{1,0:T(8,128)}) custom-call(s32[4]{0:T(128)} %copy-done.9, s32[2]{0:T(128)} %copy-done.74, bf16[8,2,64,10240]{3,2,1,0:T(8,128)(2,1)} %bitcast.57, bf16[640,1536]{1,0:T(8,128)(2,1)} %shard_map.265.refs_1_.refs_3_), custom_call_target="tpu_custom_call" | custom-call | flops 10000000 | tf_op jit(solution)/shard_map/pallas_call | solution.py:123
  273.4 13.6 %shard_map.267 = (bf16[2,8,320,320]{3,2,1,0:T(8,128)(2,1)}, bf16[640,512]{1,0:T(8,128)(2,1)}, f32[640,1024]{1,0:T(8,128)}, bf16[640,1024]{1,0:T(8,128)(2,1)}) custom-call(s32[4]{0:T(128)} %copy-done.9, s32[2]{0:T(128)} %kept_ref.23, bf16[8,2,64,10240]{3,2,1,0:T(8,128)(2,1)} %bitcast.58, bf16[640,1536]{1,0:T(8,128)(2,1)} %shard_map.264.refs_1_.refs_3_, ...), custom_call_target="tpu_custom_call" | custom-call | flops 10000000 | tf_op jit(solution)/shard_map/pallas_call | solution.py:123
  301.4 9.7 %shard_map.269 = (bf16[640,2048]{1,0:T(8,128)(2,1)}, bf16[640,2048]{1,0:T(8,128)(2,1)}) custom-call(s32[4]{0:T(128)} %copy-done.9, s32[2]{0:T(128)} %copy-done.74, bf16[1024,10240]{1,0:T(8,128)(2,1)} %all-gather.3.cloned.1.call-done.refs_0_.refs_1_.refs_2_.refs_3_, bf16[1024,10240]{1,0:T(8,128)(2,1)} %all-gather.3.cloned.1.call-done.refs_0_.refs_1_.refs_2_.refs_3_, ...), custom_call_target="tpu_custom_call" | custom-call | flops 10000000 | tf_op jit(solution)/shard_map/pallas_call | solution.py:123
  312.1 13.3 %shard_map.270.refs_6_ = bf16[2048,1024]{1,0:T(8,128)(2,1)} custom-call(s32[4]{0:T(128)} %copy-done.9, bf16[640,2048]{1,0:T(8,128)(2,1)} %get-tuple-element.129.xo.rest_0_.refs_2_, bf16[640,2048]{1,0:T(8,128)(2,1)} %get-tuple-element.130.xt.refs_2_, bf16[640,1024]{1,0:T(8,128)(2,1)} %bitcast_convert_fusion.yo.refs_4_, bf16[640,1024]{1,0:T(8,128)(2,1)} %copy-done.81, ...), custom_call_target="tpu_custom_call" | custom-call | flops 30000001024 | tf_op jit(solution)/shard_map/pallas_call | solution.py:454
  325.5 11.9 %shard_map.271 = (bf16[640,2048]{1,0:T(8,128)(2,1)}, f32[640,1024]{1,0:T(8,128)}) custom-call(s32[4]{0:T(128)} %copy-done.9, s32[2]{0:T(128)} %copy-done.74, bf16[1024,10240]{1,0:T(8,128)(2,1)} %all-gather.3.cloned.1.call-done.refs_0_.refs_1_.refs_2_.refs_3_, bf16[1024,1024]{1,0:T(8,128)(2,1)} %collective-permute-done.rest_1_.refs_1_, ...), custom_call_target="tpu_custom_call" | custom-call | flops 30000001024 | tf_op jit(solution)/shard_map/pallas_call | solution.py:123
  347.0 16.2 %shard_map.273 = (bf16[640,2048]{1,0:T(8,128)(2,1)}, f32[640,1024]{1,0:T(8,128)}, bf16[640,1024]{1,0:T(8,128)(2,1)}, f32[8,1024]{1,0:T(8,128)}) custom-call(s32[4]{0:T(128)} %copy-done.9, s32[2]{0:T(128)} %kept_ref.23, bf16[1024,10240]{1,0:T(8,128)(2,1)} %all-gather.3.cloned.1.call-done.refs_0_.refs_1_.refs_2_.refs_3_, ...), custom_call_target="tpu_custom_call" | custom-call | flops 30000001024 | tf_op jit(solution)/shard_map/pallas_call | solution.py:123
  363.3 13.2 %shard_map.274 = (bf16[1,2,2,2,128,1280]{5,4,3,2,1,0:T(8,128)(2,1)}, bf16[1,2,2,2,128,1280]{5,4,3,2,1,0:T(8,128)(2,1)}, f32[1,2048]{1,0:T(1,128)}) custom-call(s32[4]{0:T(128)} %copy-done.9, bf16[640,1024]{1,0:T(8,128)(2,1)} %get-tuple-element.128.refs_2_.xo, bf16[640,1024]{1,0:T(8,128)(2,1)} %collective-permute-done.9.refs_2_.xt, ...), custom_call_target="tpu_custom_call" | custom-call | flops 30000001024 | tf_op jit(solution)/shard_map/pallas_call | solution.py:412
  381.0 16.6 %shard_map.275 = (bf16[640,1536]{1,0:T(8,128)(2,1)}, f32[640,1024]{1,0:T(8,128)}) custom-call(s32[4]{0:T(128)} %copy-done.9, s32[2]{0:T(128)} %copy-done.74, bf16[8,2,64,10240]{3,2,1,0:T(8,128)(2,1)} %bitcast.59, bf16[1024,10240]{1,0:T(8,128)(2,1)} %all-gather.3.cloned.1.call-done.refs_0_.refs_1_.refs_2_.refs_3_, bf16[640,1024]{1,0:T(8,128)(2,1)} %copy-done.80, ...), custom_call_target="tpu_custom_call" | custom-call | flops 30000001024 | tf_op jit(solution)/shard_map/pallas_call | solution.py:123
  404.1 19.2 %shard_map.277 = (bf16[640,1536]{1,0:T(8,128)(2,1)}, f32[640,1024]{1,0:T(8,128)}, bf16[640,1024]{1,0:T(8,128)(2,1)}, f32[8,1024]{1,0:T(8,128)}) custom-call(s32[4]{0:T(128)} %copy-done.9, s32[2]{0:T(128)} %kept_ref.23, bf16[8,2,64,10240]{3,2,1,0:T(8,128)(2,1)} %bitcast.60, bf16[1024,10240]{1,0:T(8,128)(2,1)} %all-gather.3.cloned.1.call-done.refs_0_.refs_1_.refs_2_.refs_3_, ...), custom_call_target="tpu_custom_call" | custom-call | flops 30000001024 | tf_op jit(solution)/shard_map/pallas_call | solution.py:123
  423.4 10.8 %shard_map.278 = (bf16[2,2,2,1,128,768]{5,4,3,2,1,0:T(8,128)(2,1)}, bf16[2,2,2,1,128,768]{5,4,3,2,1,0:T(8,128)(2,1)}, f32[1,1536]{1,0:T(1,128)}) custom-call(s32[4]{0:T(128)} %copy-done.9, bf16[640,1024]{1,0:T(8,128)(2,1)} %get-tuple-element.125.refs_1_.xo, bf16[640,1024]{1,0:T(8,128)(2,1)} %copy-done.56, bf16[640,1536]{1,0:T(8,128)(2,1)} %get-tuple-element.151.yo.rest_0_, ...), custom_call_target="tpu_custom_call" | custom-call | flops 30000001024 | tf_op jit(solution)/shard_map/pallas_call | solution.py:412
  438.8 11.7 %shard_map.279 = (bf16[640,2048]{1,0:T(8,128)(2,1)}, f32[640,1024]{1,0:T(8,128)}) custom-call(s32[4]{0:T(128)} %copy-done.9, s32[2]{0:T(128)} %copy-done.74, bf16[1024,10368]{1,0:T(8,128)(2,1)} %all-gather.5.cloned.1.call-done.refs_0_.refs_1_.refs_2_.refs_3_, bf16[1024,1024]{1,0:T(8,128)(2,1)} %collective-permute-done.1.refs_1_, ...), custom_call_target="tpu_custom_call" | custom-call | flops 30000001024 | tf_op jit(solution)/shard_map/pallas_call | solution.py:123
  450.8 13.3 %shard_map.280.rest_0_.refs_10_ = bf16[2048,1024]{1,0:T(8,128)(2,1)} custom-call(s32[4]{0:T(128)} %copy-done.9, bf16[640,2048]{1,0:T(8,128)(2,1)} %get-tuple-element.122.refs_2_.xo, bf16[640,2048]{1,0:T(8,128)(2,1)} %get-tuple-element.123.refs_2_.xt, bf16[640,1024]{1,0:T(8,128)(2,1)} %get-tuple-element.148.yo.refs_4_, ...), custom_call_target="tpu_custom_call" | custom-call | flops 30000001024 | tf_op jit(solution)/shard_map/pallas_call | solution.py:454
  471.8 15.3 %shard_map.282 = (bf16[640,2048]{1,0:T(8,128)(2,1)}, f32[640,1024]{1,0:T(8,128)}, bf16[640,1024]{1,0:T(8,128)(2,1)}, f32[8,1024]{1,0:T(8,128)}) custom-call(s32[4]{0:T(128)} %copy-done.9, s32[2]{0:T(128)} %kept_ref.23, bf16[1024,10368]{1,0:T(8,128)(2,1)} %all-gather.5.cloned.1.call-done.refs_0_.refs_1_.refs_2_.refs_3_, ...), custom_call_target="tpu_custom_call" | custom-call | flops 30000001024 | tf_op jit(solution)/shard_map/pallas_call | solution.py:123
  494.1 13.3 %shard_map.284 = (bf16[1,2,2,2,128,1280]{5,4,3,2,1,0:T(8,128)(2,1)}, bf16[1,2,2,2,128,1280]{5,4,3,2,1,0:T(8,128)(2,1)}, f32[1,2048]{1,0:T(1,128)}) custom-call(s32[4]{0:T(128)} %copy-done.9, bf16[640,1024]{1,0:T(8,128)(2,1)} %get-tuple-element.121.refs_2_.xo, bf16[640,1024]{1,0:T(8,128)(2,1)} %copy-done.57, bf16[640,2048]{1,0:T(8,128)(2,1)} %get-tuple-element.161.yo, ...), custom_call_target="tpu_custom_call" | custom-call | flops 30000001024 | tf_op jit(solution)/shard_map/pallas_call | solution.py:412
  530.8 16.2 %shard_map.288 = (bf16[640,1536]{1,0:T(8,128)(2,1)}, f32[640,1024]{1,0:T(8,128)}) custom-call(s32[4]{0:T(128)} %copy-done.9, s32[2]{0:T(128)} %copy-done.74, bf16[8,2,64,10368]{3,2,1,0:T(8,128)(2,1)} %bitcast.55, bf16[1024,10368]{1,0:T(8,128)(2,1)} %all-gather.5.cloned.1.call-done.refs_0_.refs_1_.refs_2_.refs_3_, ...), custom_call_target="tpu_custom_call" | custom-call | flops 30000001024 | tf_op jit(solution)/shard_map/pallas_call | solution.py:123
  560.3 19.3 %shard_map.291 = (bf16[640,1536]{1,0:T(8,128)(2,1)}, f32[640,1024]{1,0:T(8,128)}, bf16[640,1024]{1,0:T(8,128)(2,1)}, f32[8,1024]{1,0:T(8,128)}) custom-call(s32[4]{0:T(128)} %copy-done.9, s32[2]{0:T(128)} %kept_ref.23, bf16[8,2,64,10368]{3,2,1,0:T(8,128)(2,1)} %bitcast.56, bf16[1024,10368]{1,0:T(8,128)(2,1)} %all-gather.5.cloned.1.call-done.refs_0_.refs_1_.refs_2_.refs_3_, ...), custom_call_target="tpu_custom_call" | custom-call | flops 30000001024 | tf_op jit(solution)/shard_map/pallas_call | solution.py:123
  636.9 14.4 %collective-permute-done.32.g = bf16[2,2,1,2,128,384]{5,4,3,2,1,0:T(8,128)(2,1)S(1)} collective-permute-done((bf16[2,2,1,2,128,384]{5,4,3,2,1,0:T(8,128)(2,1)S(1)}, bf16[2,2,1,2,128,384]{5,4,3,2,1,0:T(8,128)(2,1)S(1)}, u32[]{:S(2)}, u32[]{:S(2)}) %collective-permute-start.32) | collective-permute-done | bytes 786464 | tf_op jit(solution)/shard_map/ppermute | solution.py:40
  659.4 16.2 %collective-permute-done.37.g = bf16[1,2,1,2,128,384]{5,4,3,2,1,0:T(8,128)(2,1)S(1)} collective-permute-done((bf16[1,2,1,2,128,384]{5,4,3,2,1,0:T(8,128)(2,1)S(1)}, bf16[1,2,1,2,128,384]{5,4,3,2,1,0:T(8,128)(2,1)S(1)}, u32[]{:S(2)}, u32[]{:S(2)}) %collective-permute-start.37) | collective-permute-done | bytes 393248 | tf_op jit(solution)/shard_map/ppermute | solution.py:40
  708.6 11.7 %collective-permute-done.46.refs_1_ = bf16[128,2048]{1,0:T(8,128)(2,1)S(1)} collective-permute-done((bf16[128,2048]{1,0:T(8,128)(2,1)S(1)}, bf16[128,2048]{1,0:T(8,128)(2,1)S(1)}, u32[]{:S(2)}, u32[]{:S(2)}) %collective-permute-start.46) | collective-permute-done | bytes 524320 | tf_op jit(solution)/shard_map/ppermute | solution.py:40
  725.7 11.4 %collective-permute-done.48.refs_3_ = bf16[64,4096]{1,0:T(8,128)(2,1)S(1)} collective-permute-done((bf16[64,4096]{1,0:T(8,128)(2,1)S(1)}, bf16[64,4096]{1,0:T(8,128)(2,1)S(1)}, u32[]{:S(2)}, u32[]{:S(2)}) %collective-permute-start.48) | collective-permute-done | bytes 524320 | tf_op jit(solution)/shard_map/ppermute | solution.py:40
  (442 shorter events, 311.0 us)
Async XLA Ops:
  7.2 120.5 %all-gather.5.cloned.1.call-start = ((), (), s32[]{:S(2)}) async-start(), calls=%async_computation.3 | async-start | bytes 22560768 | tf_op jit(solution)/shard_map/all_gather | solution.py:868
  14.7 223.9 %all-gather.3.cloned.1.call-start = ((), (), s32[]{:S(2)}) async-start(), calls=%async_computation.2 | async-start | bytes 22282240 | tf_op jit(solution)/shard_map/all_gather | solution.py:868
  16.8 490.6 %reduce-scatter.3.cloned.1.call-start = ((), (), s32[]{:S(2)}) async-start(), calls=%async_computation.4 | async-start | bytes 4718592 | tf_op jit(solution)/shard_map/reduce_scatter | solution.py:671
  154.5 47.9 %collective-permute-start.1 = (bf16[1024,1024]{1,0:T(8,128)(2,1)S(1)}, bf16[1024,1024]{1,0:T(8,128)(2,1)}, u32[]{:S(2)}, u32[]{:S(2)}) collective-permute-start(bf16[1024,1024]{1,0:T(8,128)(2,1)S(1)} %copy-done.53), channel_id=1, source_target_pairs={{0,1},{1,0},{2,3},{3,2},{4,5},{5,4},{6,7},{7,6},{8,9},{9,8},{10,11... | collective-permute-start | bytes 6291464 | tf_op jit(solution)/shard_map/ppermute | solution.py:40
  261.9 49.2 %collective-permute-start = (bf16[1024,1024]{1,0:T(8,128)(2,1)}, bf16[1024,1024]{1,0:T(8,128)(2,1)}, u32[]{:S(2)}, u32[]{:S(2)}) collective-permute-start(bf16[1024,1024]{1,0:T(8,128)(2,1)} %constant_dynamic-slice_fusion.2.refs_3_), channel_id=1, source_target_pairs={{0,1},{1,0},{2,3},{3,2},{4,5},{5,4},{6,7},{7,6},{8,9},{9,8},{10,11... | collective-permute-start | bytes 6291464 | tf_op jit(solution)/shard_map/ppermute | solution.py:40
  325.5 262.2 %reduce-scatter.5.cloned.1.call-start = ((), (), s32[]{:S(2)}) async-start(), calls=%async_computation.5 | async-start | bytes 4718592 | tf_op jit(solution)/shard_map/reduce_scatter | solution.py:671
  345.0 277.6 %collective-permute-start.11 = (f32[640,1024]{1,0:T(8,128)}, f32[640,1024]{1,0:T(8,128)}, u32[]{:S(2)}, u32[]{:S(2)}) collective-permute-start(f32[640,1024]{1,0:T(8,128)} %shard_map.272.refs_10_), channel_id=1, source_target_pairs={{0,2},{1,3},{2,0},{3,1},{4,6},{5,7},{6,4},{7,5},{8,10},{9,11},{10,... | collective-permute-start | bytes 7864328 | tf_op jit(solution)/shard_map/ppermute | solution.py:40
  403.7 60.5 %collective-permute-start.17 = (bf16[1,2,2,2,128,1280]{5,4,3,2,1,0:T(8,128)(2,1)}, bf16[1,2,2,2,128,1280]{5,4,3,2,1,0:T(8,128)(2,1)S(1)}, u32[]{:S(2)}, u32[]{:S(2)}) collective-permute-start(bf16[1,2,2,2,128,1280]{5,4,3,2,1,0:T(8,128)(2,1)} %get-tuple-element.147.refs_9_), channel_id=1, source_target_pairs={{0,1},{1,0},{2,3},{3,2},{4,5},{5,4},{6,7},{7,6},{8,9},{9,8},{10,11... | collective-permute-start | bytes 7864328 | tf_op jit(solution)/shard_map/ppermute | solution.py:40
  436.8 50.3 %collective-permute-start.19 = (bf16[2,2,2,1,128,768]{5,4,3,2,1,0:T(8,128)(2,1)}, bf16[2,2,2,1,128,768]{5,4,3,2,1,0:T(8,128)(2,1)}, u32[]{:S(2)}, u32[]{:S(2)}) collective-permute-start(bf16[2,2,2,1,128,768]{5,4,3,2,1,0:T(8,128)(2,1)} %get-tuple-element.152.refs_6_), channel_id=1, source_target_pairs={{0,4},{1,5},{2,6},{3,7},{4,0},{5,1},{6,2},{7,3},{8,12},{9,13},{10,... | collective-permute-start | bytes 4718600 | tf_op jit(solution)/shard_map/ppermute | solution.py:40
  471.0 44.9 %collective-permute-start.21 = (bf16[1,2,2,1,128,1280]{5,4,3,2,1,0:T(8,128)(2,1)}, bf16[1,2,2,1,128,1280]{5,4,3,2,1,0:T(8,128)(2,1)S(1)}, u32[]{:S(2)}, u32[]{:S(2)}) collective-permute-start(bf16[1,2,2,1,128,1280]{5,4,3,2,1,0:T(8,128)(2,1)} %get-tuple-element.157.refs_11_), channel_id=1, source_target_pairs={{0,4},{1,5},{2,6},{3,7},{4,0},{5,1},{6,2},{7,3},{8,12},{9,13},{10,... | collective-permute-start | bytes 3932168 | tf_op jit(solution)/shard_map/ppermute | solution.py:40
  487.0 43.8 %collective-permute-start.18 = (bf16[640,1024]{1,0:T(8,128)(2,1)}, bf16[640,1024]{1,0:T(8,128)(2,1)}, u32[]{:S(2)}, u32[]{:S(2)}) collective-permute-start(bf16[640,1024]{1,0:T(8,128)(2,1)} %get-tuple-element.158.rest_0_.yo.refs_2_), channel_id=1, source_target_pairs={{0,2},{1,3},{2,0},{3,1},{4,6},{5,7},{6,4},{7,5},{8,10},{9,11},{10,... | collective-permute-start | bytes 3932168 | tf_op jit(solution)/shard_map/ppermute | solution.py:40
  492.5 36.4 %collective-permute-start.20 = (bf16[2,2,1,1,128,768]{5,4,3,2,1,0:T(8,128)(2,1)S(1)}, bf16[2,2,1,1,128,768]{5,4,3,2,1,0:T(8,128)(2,1)S(1)}, u32[]{:S(2)}, u32[]{:S(2)}) collective-permute-start(bf16[2,2,1,1,128,768]{5,4,3,2,1,0:T(8,128)(2,1)S(1)} %get-tuple-element.163.rest_1_), channel_id=1, source_target_pairs={{0,8},{1,9},{2,10},{3,11},{4,12},{5,13},{6,14},{7,15},{8,0},{9,1},... | collective-permute-start | bytes 2359304 | tf_op jit(solution)/shard_map/ppermute | solution.py:40
  515.6 38.2 %collective-permute-start.23 = (bf16[128,1024]{1,0:T(8,128)(2,1)S(1)}, bf16[128,1024]{1,0:T(8,128)(2,1)S(1)}, u32[]{:S(2)}, u32[]{:S(2)}) collective-permute-start(bf16[128,1024]{1,0:T(8,128)(2,1)S(1)} %get-tuple-element.169.refs_8_), channel_id=1, source_target_pairs={{0,2},{1,3},{2,0},{3,1},{4,6},{5,7},{6,4},{7,5},{8,10},{9,11},{10,... | collective-permute-start | bytes 786440 | tf_op jit(solution)/shard_map/ppermute | solution.py:40
  521.1 60.7 %collective-permute-start.25 = (bf16[1,2,1,1,128,1280]{5,4,3,2,1,0:T(8,128)(2,1)}, bf16[1,2,1,1,128,1280]{5,4,3,2,1,0:T(8,128)(2,1)}, u32[]{:S(2)}, u32[]{:S(2)}) collective-permute-start(bf16[1,2,1,1,128,1280]{5,4,3,2,1,0:T(8,128)(2,1)} %get-tuple-element.168.refs_7_), channel_id=1, source_target_pairs={{0,8},{1,9},{2,10},{3,11},{4,12},{5,13},{6,14},{7,15},{8,0},{9,1},... | collective-permute-start | bytes 1966088 | tf_op jit(solution)/shard_map/ppermute | solution.py:40
  529.2 52.6 %collective-permute-start.24 = (bf16[1,2,1,1,128,768]{5,4,3,2,1,0:T(8,128)(2,1)S(1)}, bf16[1,2,1,1,128,768]{5,4,3,2,1,0:T(8,128)(2,1)S(1)}, u32[]{:S(2)}, u32[]{:S(2)}) collective-permute-start(bf16[1,2,1,1,128,768]{5,4,3,2,1,0:T(8,128)(2,1)S(1)} %get-tuple-element.166.refs_6_), channel_id=1, source_target_pairs={{0,1},{1,0},{2,3},{3,2},{4,5},{5,4},{6,7},{7,6},{8,9},{9,8},{10,11... | collective-permute-start | bytes 1179656 | tf_op jit(solution)/shard_map/ppermute | solution.py:40
  553.1 60.1 %collective-permute-start.26 = (bf16[1,2,2,2,128,1280]{5,4,3,2,1,0:T(8,128)(2,1)}, bf16[1,2,2,2,128,1280]{5,4,3,2,1,0:T(8,128)(2,1)}, u32[]{:S(2)}, u32[]{:S(2)}) collective-permute-start(bf16[1,2,2,2,128,1280]{5,4,3,2,1,0:T(8,128)(2,1)} %get-tuple-element.176.refs_2_.refs_9_), channel_id=1, source_target_pairs={{0,1},{1,0},{2,3},{3,2},{4,5},{5,4},{6,7},{7,6},{8,9},{9,8},{10,11... | collective-permute-start | bytes 7864328 | tf_op jit(solution)/shard_map/ppermute | solution.py:40
  558.9 141.6 %collective-permute-start.43 = (bf16[256,1024]{1,0:T(8,128)(2,1)}, bf16[256,1024]{1,0:T(8,128)(2,1)}, u32[]{:S(2)}, u32[]{:S(2)}) collective-permute-start(bf16[256,1024]{1,0:T(8,128)(2,1)} %shard_map.290.refs_10_.refs_0_), channel_id=1, source_target_pairs={{0,1},{1,0},{2,3},{3,2},{4,5},{5,4},{6,7},{7,6},{8,9},{9,8},{10,11... | collective-permute-start | bytes 1572872 | tf_op jit(solution)/shard_map/ppermute | solution.py:40
  585.5 34.7 %collective-permute-start.27 = (bf16[128,2048]{1,0:T(8,128)(2,1)S(1)}, bf16[128,2048]{1,0:T(8,128)(2,1)S(1)}, u32[]{:S(2)}, u32[]{:S(2)}) collective-permute-start(bf16[128,2048]{1,0:T(8,128)(2,1)S(1)} %get-tuple-element.181.rest_1_), channel_id=1, source_target_pairs={{0,16},{1,17},{2,18},{3,19},{4,20},{5,21},{6,22},{7,23},{8,24},{9,... | collective-permute-start | bytes 1572872 | tf_op jit(solution)/shard_map/ppermute | solution.py:40
  592.3 41.9 %collective-permute-start.33 = (bf16[128,1024]{1,0:T(8,128)(2,1)}, bf16[128,1024]{1,0:T(8,128)(2,1)}, u32[]{:S(2)}, u32[]{:S(2)}) collective-permute-start(bf16[128,1024]{1,0:T(8,128)(2,1)} %get-tuple-element.182.rest_2_), channel_id=1, source_target_pairs={{0,2},{1,3},{2,0},{3,1},{4,6},{5,7},{6,4},{7,5},{8,10},{9,11},{10,... | collective-permute-start | bytes 786440 | tf_op jit(solution)/shard_map/ppermute | solution.py:40
  613.2 40.0 %collective-permute-start.31 = (bf16[1,2,2,2,128,384]{5,4,3,2,1,0:T(8,128)(2,1)}, bf16[1,2,2,2,128,384]{5,4,3,2,1,0:T(8,128)(2,1)}, u32[]{:S(2)}, u32[]{:S(2)}) collective-permute-start(bf16[1,2,2,2,128,384]{5,4,3,2,1,0:T(8,128)(2,1)} %get-tuple-element.184.rest_0_.refs_2_.refs_6_), channel_id=1, source_target_pairs={{0,1},{1,0},{2,3},{3,2},{4,5},{5,4},{6,7},{7,6},{8,9},{9,8},{10,11... | collective-permute-start | bytes 2359304 | tf_op jit(solution)/shard_map/ppermute | solution.py:40
  622.6 32.6 %collective-permute-start.30 = (bf16[64,1792]{1,0:T(8,128)(2,1)}, bf16[64,1792]{1,0:T(8,128)(2,1)}, u32[]{:S(2)}, u32[]{:S(2)}) collective-permute-start(bf16[64,1792]{1,0:T(8,128)(2,1)} %get-tuple-element.188.refs_8_), channel_id=1, source_target_pairs={{0,2},{1,3},{2,0},{3,1},{4,6},{5,7},{6,4},{7,5},{8,10},{9,11},{10,... | collective-permute-start | bytes 688136 | tf_op jit(solution)/shard_map/ppermute | solution.py:40
  634.2 43.8 %collective-permute-start.36 = (bf16[1,2,2,1,128,1280]{5,4,3,2,1,0:T(8,128)(2,1)}, bf16[1,2,2,1,128,1280]{5,4,3,2,1,0:T(8,128)(2,1)}, u32[]{:S(2)}, u32[]{:S(2)}) collective-permute-start(bf16[1,2,2,1,128,1280]{5,4,3,2,1,0:T(8,128)(2,1)} %get-tuple-element.186.refs_7_), channel_id=1, source_target_pairs={{0,4},{1,5},{2,6},{3,7},{4,0},{5,1},{6,2},{7,3},{8,12},{9,13},{10,... | collective-permute-start | bytes 3932168 | tf_op jit(solution)/shard_map/ppermute | solution.py:40
  653.2 55.4 %collective-permute-start.45 = (bf16[256,1024]{1,0:T(8,128)(2,1)}, bf16[256,1024]{1,0:T(8,128)(2,1)}, u32[]{:S(2)}, u32[]{:S(2)}) collective-permute-start(bf16[256,1024]{1,0:T(8,128)(2,1)} %shard_map.300.rest_0_.refs_0_), channel_id=1, source_target_pairs={{0,1},{1,0},{2,3},{3,2},{4,5},{5,4},{6,7},{7,6},{8,9},{9,8},{10,11... | collective-permute-start | bytes 1572872 | tf_op jit(solution)/shard_map/ppermute | solution.py:40
  655.2 25.0 %collective-permute-start.35 = (bf16[1,2,1,2,128,384]{5,4,3,2,1,0:T(8,128)(2,1)S(1)}, bf16[1,2,1,2,128,384]{5,4,3,2,1,0:T(8,128)(2,1)S(1)}, u32[]{:S(2)}, u32[]{:S(2)}) collective-permute-start(bf16[1,2,1,2,128,384]{5,4,3,2,1,0:T(8,128)(2,1)S(1)} %get-tuple-element.204.refs_2_), channel_id=1, source_target_pairs={{0,8},{1,9},{2,10},{3,11},{4,12},{5,13},{6,14},{7,15},{8,0},{9,1},... | collective-permute-start | bytes 1179656 | tf_op jit(solution)/shard_map/ppermute | solution.py:40
  (114 other events, 824.0 us)
Sparse Core Ops, SparseCore 0:
  14.9 112.7 all-gather.4
  129.8 108.8 all-gather.2
  325.6 86.9 reduce-scatter.2
  464.2 106.3 reduce-scatter.4

commit v6 on v5

--- a/solution.py
+++ b/solution.py
@@ -813,7 +813,7 @@
             out_specs=pl.BlockSpec((deep, total), lambda i, w: (0, 0)),
         ),
         out_shape=jax.ShapeDtypeStruct((deep, total), BF),
-        compiler_params=pltpu.CompilerParams(vmem_limit_bytes=SMALL_LIMIT),
+        compiler_params=pltpu.CompilerParams(vmem_limit_bytes=LIMIT),
         cost_estimate=FORWARD,
     )(where, *ins, *after)
 
@@ -1026,7 +1026,7 @@
         res1 = weight_grad(
             plan, where, s["second"], (pre_own, pre_oth), 1, orders_f1[layer][0], sums=True, extra=tail, relative=True, after=prev
         )
-        prev = tuple(res1[:1])
+        prev = tuple(res1[:1]) + ((last_part,) if top else ())
         if not top:
             prev += (terms["q", layer + 1][0].step(prev[:1]),)
             prev += (terms["f1", layer + 1].step(prev[:1]),)
@@ -1083,7 +1083,7 @@
             )
             terms["q", layer].append(Term(plan, *resq[:2], order))
             q_sums.append(resq[2].reshape(plan.ny, -1))
-            prev = (resq[1],)
+            prev = (resq[1],) + (() if top else (ends["f2", layer].came,))
         q = jnp.concatenate(q_sums, axis=1).reshape(3, half_heads, 1, HEAD_DIM)
         q = jnp.concatenate([q[:1], q[2:]])
         none = jnp.zeros_like(q)
@@ -1120,23 +1120,24 @@
         down_last, w, 1, ["fc2"], [saved[w]["hid"][0], last_part, saved[w]["middle"]], [vecs[w]["f2b"]], [low_rows], prev
     )[0]
     qa, qb = terms["q", 0]
-    prev = (ends["f2", 0].rep(step_vec((mixed,))),)
-    prev = (qa.step(prev),)
+    prev = (qa.step((mixed, ends["rest", 1].came)),)
     prev = (qb.step(prev),)
-    prev = (ends["rest", 1].rep(prev),)
     prev = step_vec(prev)
     prev = (qa.step(prev),)
     prev = (terms["f1", 0].step(prev),)
     prev = (qb.step(prev),)
     prev = step_vec(prev)
     prev = end_rest(0, prev)
+    prev = (ends["rest", 1].rep(prev),)
+    prev = (ends["f2", 0].rep(prev),)
     prev = step_vec(prev)
     placed = place(1, None, prev)
     prev = (placed[0],)
+    prev = (ends["rest", 0].core(prev + tuple(ends["f2", 0].pair[1:])),)
+    prev = step_vec(prev)
+    prev = (ends["rest", 0].rep(prev),)
     while got_vec is not None:
         prev = step_vec(prev)
-    prev = (ends["rest", 0].core(prev + tuple(ends["f2", 0].pair[1:])),)
-    prev = (ends["rest", 0].rep(prev),)
     placed = place(0, placed, prev)
     if plan.ny == 1:
         vec = lax.psum(vec, "rep")

time: 754 us -> 727 us (0.964)
  waiting for transfers between devices: 206 us -> 182 us
    ppermute x49, waiting for transfers between devices: 91.4 us -> 68.6 us  [swap(): return lax.ppermute(v, AX, pairs)]
  transfers between devices with their start and end apart: 53 -> 53, of which waited for: 17 -> 16; matrix products, arithmetic and copies ran while one was open for 6% -> 6% of each run, Pallas kernels for 49% -> 50%
where the time goes in v6:
time: 727 us; the launch traced here: 722 us
  Pallas kernels  403 us (55%)
  waiting for transfers between devices  182 us (25%)
  local copies, waits for them, and re-layouts  75.9 us (10%)
  starting transfers between devices  34.6 us (5%)
  between operations  15.1 us (2%)
  other arithmetic  10.7 us (1%)
    pallas_call x24, Pallas kernels, row_call(): pl.pallas_call(kernel, grid_spec=pltpu.PrefetchScalarGridSpec(num_scalar_...  274 us
    all_gather x2, waiting for transfers between devices, per_device(): gathered.append(lax.all_gather(done[0], 'shard', axis=0, tiled=True))  114 us
    ppermute x49, waiting for transfers between devices, swap(): return lax.ppermute(v, AX, pairs)  68.6 us
    pallas_call x5, Pallas kernels, weight_grad(): pl.pallas_call(kernel, grid_spec=pltpu.PrefetchScalarGridSpec(num_scalar_...  53.6 us
    unnamed x176, local copies, waits for them, and re-layouts  43.7 us
    ppermute x49, starting transfers between devices, swap(): return lax.ppermute(v, AX, pairs)  34.5 us
    pallas_call x2, Pallas kernels, chip_grad(): pl.pallas_call(kernel, grid_spec=pltpu.PrefetchScalarGridSpec(num_scalar_...  26.6 us
  transfers between devices with their start and end apart: 53, of which 16 were waited for; matrix products, arithmetic and copies ran while one was open for 6% of the time, Pallas kernels for 50%

profile of v6, /device:TPU:0, one launch (start us, length us, event | category | flops | bytes accessed | tf_op | source)
XLA Modules:
  0.0 721.8 jit_solution(8289372361091996752)
XLA Ops:
  17.5 108.3 %all-gather.5.cloned.1.call-done.refs_0_.refs_1_.refs_2_.refs_3_ = bf16[1024,10368]{1,0:T(8,128)(2,1)} async-done(((bf16[64,10368]{1,0:T(8,128)(2,1)}), bf16[1024,10368]{1,0:T(8,128)(2,1)}) %all-gather.5.cloned.1.call-update) | async-done | bytes 21233680 | tf_op jit(solution)/shard_map/all_gather | solution.py:868
  140.4 12.0 %shard_map.258 = (bf16[2,8,320,320]{3,2,1,0:T(8,128)(2,1)}, bf16[640,512]{1,0:T(8,128)(2,1)}, f32[640,1024]{1,0:T(8,128)}) custom-call(s32[4]{0:T(128)} %pad_add_fusion.where_ref, s32[2]{0:T(128)} %copy-done.74, bf16[8,2,64,10368]{3,2,1,0:T(8,128)(2,1)} %bitcast.53, bf16[640,1536]{1,0:T(8,128)(2,1)} %shard_map.257.refs_1_.refs_3_), custom_call_target="tpu_custom_call" | custom-call | flops 10000000 | tf_op jit(solution)/shard_map/pallas_call | solution.py:123
  164.3 13.6 %shard_map.259 = (bf16[2,8,320,320]{3,2,1,0:T(8,128)(2,1)}, bf16[640,512]{1,0:T(8,128)(2,1)}, f32[640,1024]{1,0:T(8,128)}, bf16[640,1024]{1,0:T(8,128)(2,1)}) custom-call(s32[4]{0:T(128)} %pad_add_fusion.where_ref, s32[2]{0:T(128)} %kept_ref.23, bf16[8,2,64,10368]{3,2,1,0:T(8,128)(2,1)} %bitcast.54, bf16[640,1536]{1,0:T(8,128)(2,1)} %shard_map.256.refs_1_.refs_3_, ...), custom_call_target="tpu_custom_call" | custom-call | flops 10000000 | tf_op jit(solution)/shard_map/pallas_call | solution.py:123
  182.2 9.7 %shard_map.261 = (bf16[640,2048]{1,0:T(8,128)(2,1)}, bf16[640,2048]{1,0:T(8,128)(2,1)}) custom-call(s32[4]{0:T(128)} %pad_add_fusion.where_ref, s32[2]{0:T(128)} %copy-done.74, bf16[1024,10368]{1,0:T(8,128)(2,1)} %all-gather.5.cloned.1.call-done.refs_0_.refs_1_.refs_2_.refs_3_, ...), custom_call_target="tpu_custom_call" | custom-call | flops 10000000 | tf_op jit(solution)/shard_map/pallas_call | solution.py:123
  210.7 9.7 %shard_map.260 = (bf16[640,2048]{1,0:T(8,128)(2,1)}, bf16[640,2048]{1,0:T(8,128)(2,1)}) custom-call(s32[4]{0:T(128)} %pad_add_fusion.where_ref, s32[2]{0:T(128)} %kept_ref.23, bf16[1024,10368]{1,0:T(8,128)(2,1)} %all-gather.5.cloned.1.call-done.refs_0_.refs_1_.refs_2_.refs_3_, ...), custom_call_target="tpu_custom_call" | custom-call | flops 10000000 | tf_op jit(solution)/shard_map/pallas_call | solution.py:123
  247.7 11.9 %shard_map.266 = (bf16[2,8,320,320]{3,2,1,0:T(8,128)(2,1)}, bf16[640,512]{1,0:T(8,128)(2,1)}, f32[640,1024]{1,0:T(8,128)}) custom-call(s32[4]{0:T(128)} %pad_add_fusion.where_ref, s32[2]{0:T(128)} %copy-done.74, bf16[8,2,64,10240]{3,2,1,0:T(8,128)(2,1)} %bitcast.57, bf16[640,1536]{1,0:T(8,128)(2,1)} %shard_map.265.refs_1_.refs_3_), custom_call_target="tpu_custom_call" | custom-call | flops 10000000 | tf_op jit(solution)/shard_map/pallas_call | solution.py:123
  271.5 13.6 %shard_map.267 = (bf16[2,8,320,320]{3,2,1,0:T(8,128)(2,1)}, bf16[640,512]{1,0:T(8,128)(2,1)}, f32[640,1024]{1,0:T(8,128)}, bf16[640,1024]{1,0:T(8,128)(2,1)}) custom-call(s32[4]{0:T(128)} %pad_add_fusion.where_ref, s32[2]{0:T(128)} %kept_ref.23, bf16[8,2,64,10240]{3,2,1,0:T(8,128)(2,1)} %bitcast.58, bf16[640,1536]{1,0:T(8,128)(2,1)} %shard_map.264.refs_1_.refs_3_, ...), custom_call_target="tpu_custom_call" | custom-call | flops 10000000 | tf_op jit(solution)/shard_map/pallas_call | solution.py:123
  290.0 9.6 %shard_map.268 = (bf16[640,2048]{1,0:T(8,128)(2,1)}, bf16[640,2048]{1,0:T(8,128)(2,1)}) custom-call(s32[4]{0:T(128)} %pad_add_fusion.where_ref, s32[2]{0:T(128)} %kept_ref.23, bf16[1024,10240]{1,0:T(8,128)(2,1)} %all-gather.3.cloned.1.call-done.refs_0_.refs_1_.refs_2_.refs_3_, ...), custom_call_target="tpu_custom_call" | custom-call | flops 10000000 | tf_op jit(solution)/shard_map/pallas_call | solution.py:123
  310.2 13.3 %shard_map.270.refs_6_ = bf16[2048,1024]{1,0:T(8,128)(2,1)} custom-call(s32[4]{0:T(128)} %pad_add_fusion.where_ref, bf16[640,2048]{1,0:T(8,128)(2,1)} %get-tuple-element.129.xo.rest_0_.refs_2_, bf16[640,2048]{1,0:T(8,128)(2,1)} %get-tuple-element.130.xt.refs_2_, bf16[640,1024]{1,0:T(8,128)(2,1)} %bitcast_convert_fusion.yo.refs_4_, ...), custom_call_target="tpu_custom_call" | custom-call | flops 30000001024 | tf_op jit(solution)/shard_map/pallas_call | solution.py:454
  323.5 11.9 %shard_map.271 = (bf16[640,2048]{1,0:T(8,128)(2,1)}, f32[640,1024]{1,0:T(8,128)}) custom-call(s32[4]{0:T(128)} %pad_add_fusion.where_ref, s32[2]{0:T(128)} %copy-done.74, bf16[1024,10240]{1,0:T(8,128)(2,1)} %all-gather.3.cloned.1.call-done.refs_0_.refs_1_.refs_2_.refs_3_, bf16[1024,1024]{1,0:T(8,128)(2,1)} %collective-permute-done.rest_1_.refs_1_, ...), custom_call_target="tpu_custom_call" | custom-call | flops 30000001024 | tf_op jit(solution)/shard_map/pallas_call | solution.py:123
  344.9 16.3 %shard_map.273 = (bf16[640,2048]{1,0:T(8,128)(2,1)}, f32[640,1024]{1,0:T(8,128)}, bf16[640,1024]{1,0:T(8,128)(2,1)}, f32[8,1024]{1,0:T(8,128)}) custom-call(s32[4]{0:T(128)} %pad_add_fusion.where_ref, s32[2]{0:T(128)} %kept_ref.23, bf16[1024,10240]{1,0:T(8,128)(2,1)} %all-gather.3.cloned.1.call-done.refs_0_.refs_1_.refs_2_.refs_3_, ...), custom_call_target="tpu_custom_call" | custom-call | flops 30000001024 | tf_op jit(solution)/shard_map/pallas_call | solution.py:123
  361.2 13.1 %shard_map.274 = (bf16[1,2,2,2,128,1280]{5,4,3,2,1,0:T(8,128)(2,1)}, bf16[1,2,2,2,128,1280]{5,4,3,2,1,0:T(8,128)(2,1)}, f32[1,2048]{1,0:T(1,128)}) custom-call(s32[4]{0:T(128)} %pad_add_fusion.where_ref, bf16[640,1024]{1,0:T(8,128)(2,1)} %get-tuple-element.128.refs_2_.xo, bf16[640,1024]{1,0:T(8,128)(2,1)} %collective-permute-done.9.refs_2_.xt, ...), custom_call_target="tpu_custom_call" | custom-call | flops 30000001024 | tf_op jit(solution)/shard_map/pallas_call | solution.py:412
  378.9 16.6 %shard_map.275 = (bf16[640,1536]{1,0:T(8,128)(2,1)}, f32[640,1024]{1,0:T(8,128)}) custom-call(s32[4]{0:T(128)} %pad_add_fusion.where_ref, s32[2]{0:T(128)} %copy-done.74, bf16[8,2,64,10240]{3,2,1,0:T(8,128)(2,1)} %bitcast.59, bf16[1024,10240]{1,0:T(8,128)(2,1)} %all-gather.3.cloned.1.call-done.refs_0_.refs_1_.refs_2_.refs_3_, bf16[640,1024]{1,0:T(8,128)(2,1)} %copy-done.81, ...), custom_call_target="tpu_custom_call" | custom-call | flops 30000001024 | tf_op jit(solution)/shard_map/pallas_call | solution.py:123
  402.0 19.2 %shard_map.277 = (bf16[640,1536]{1,0:T(8,128)(2,1)}, f32[640,1024]{1,0:T(8,128)}, bf16[640,1024]{1,0:T(8,128)(2,1)}, f32[8,1024]{1,0:T(8,128)}) custom-call(s32[4]{0:T(128)} %pad_add_fusion.where_ref, s32[2]{0:T(128)} %kept_ref.23, bf16[8,2,64,10240]{3,2,1,0:T(8,128)(2,1)} %bitcast.60, ...), custom_call_target="tpu_custom_call" | custom-call | flops 30000001024 | tf_op jit(solution)/shard_map/pallas_call | solution.py:123
  421.3 10.8 %shard_map.278 = (bf16[2,2,2,1,128,768]{5,4,3,2,1,0:T(8,128)(2,1)}, bf16[2,2,2,1,128,768]{5,4,3,2,1,0:T(8,128)(2,1)}, f32[1,1536]{1,0:T(1,128)}) custom-call(s32[4]{0:T(128)} %pad_add_fusion.where_ref, bf16[640,1024]{1,0:T(8,128)(2,1)} %get-tuple-element.125.refs_1_.xo, bf16[640,1024]{1,0:T(8,128)(2,1)} %copy-done.56, ...), custom_call_target="tpu_custom_call" | custom-call | flops 30000001024 | tf_op jit(solution)/shard_map/pallas_call | solution.py:412
  436.7 11.7 %shard_map.279 = (bf16[640,2048]{1,0:T(8,128)(2,1)}, f32[640,1024]{1,0:T(8,128)}) custom-call(s32[4]{0:T(128)} %pad_add_fusion.where_ref, s32[2]{0:T(128)} %copy-done.74, bf16[1024,10368]{1,0:T(8,128)(2,1)} %all-gather.5.cloned.1.call-done.refs_0_.refs_1_.refs_2_.refs_3_, bf16[1024,1024]{1,0:T(8,128)(2,1)} %collective-permute-done.1.refs_1_, ...), custom_call_target="tpu_custom_call" | custom-call | flops 30000001024 | tf_op jit(solution)/shard_map/pallas_call | solution.py:123
  448.7 13.3 %shard_map.280.rest_0_.refs_10_ = bf16[2048,1024]{1,0:T(8,128)(2,1)} custom-call(s32[4]{0:T(128)} %pad_add_fusion.where_ref, bf16[640,2048]{1,0:T(8,128)(2,1)} %get-tuple-element.122.refs_2_.xo, bf16[640,2048]{1,0:T(8,128)(2,1)} %get-tuple-element.123.refs_2_.xt, bf16[640,1024]{1,0:T(8,128)(2,1)} %get-tuple-element.148.yo.refs_4_, ...), custom_call_target="tpu_custom_call" | custom-call | flops 30000001024 | tf_op jit(solution)/shard_map/pallas_call | solution.py:454
  469.7 15.2 %shard_map.282 = (bf16[640,2048]{1,0:T(8,128)(2,1)}, f32[640,1024]{1,0:T(8,128)}, bf16[640,1024]{1,0:T(8,128)(2,1)}, f32[8,1024]{1,0:T(8,128)}) custom-call(s32[4]{0:T(128)} %pad_add_fusion.where_ref, s32[2]{0:T(128)} %kept_ref.23, bf16[1024,10368]{1,0:T(8,128)(2,1)} %all-gather.5.cloned.1.call-done.refs_0_.refs_1_.refs_2_.refs_3_, ...), custom_call_target="tpu_custom_call" | custom-call | flops 30000001024 | tf_op jit(solution)/shard_map/pallas_call | solution.py:123
  491.9 13.3 %shard_map.284 = (bf16[1,2,2,2,128,1280]{5,4,3,2,1,0:T(8,128)(2,1)}, bf16[1,2,2,2,128,1280]{5,4,3,2,1,0:T(8,128)(2,1)}, f32[1,2048]{1,0:T(1,128)}) custom-call(s32[4]{0:T(128)} %pad_add_fusion.where_ref, bf16[640,1024]{1,0:T(8,128)(2,1)} %get-tuple-element.121.refs_2_.xo, bf16[640,1024]{1,0:T(8,128)(2,1)} %copy-done.57, ...), custom_call_target="tpu_custom_call" | custom-call | flops 30000001024 | tf_op jit(solution)/shard_map/pallas_call | solution.py:412
  528.8 16.2 %shard_map.288 = (bf16[640,1536]{1,0:T(8,128)(2,1)}, f32[640,1024]{1,0:T(8,128)}) custom-call(s32[4]{0:T(128)} %pad_add_fusion.where_ref, s32[2]{0:T(128)} %copy-done.74, bf16[8,2,64,10368]{3,2,1,0:T(8,128)(2,1)} %bitcast.55, bf16[1024,10368]{1,0:T(8,128)(2,1)} %all-gather.5.cloned.1.call-done.refs_0_.refs_1_.refs_2_.refs_3_, ...), custom_call_target="tpu_custom_call" | custom-call | flops 30000001024 | tf_op jit(solution)/shard_map/pallas_call | solution.py:123
  558.3 19.3 %shard_map.291 = (bf16[640,1536]{1,0:T(8,128)(2,1)}, f32[640,1024]{1,0:T(8,128)}, bf16[640,1024]{1,0:T(8,128)(2,1)}, f32[8,1024]{1,0:T(8,128)}) custom-call(s32[4]{0:T(128)} %pad_add_fusion.where_ref, s32[2]{0:T(128)} %kept_ref.23, bf16[8,2,64,10368]{3,2,1,0:T(8,128)(2,1)} %bitcast.56, ...), custom_call_target="tpu_custom_call" | custom-call | flops 30000001024 | tf_op jit(solution)/shard_map/pallas_call | solution.py:123
  629.5 9.7 %collective-permute-done.30.g = bf16[1,2,2,2,128,384]{5,4,3,2,1,0:T(8,128)(2,1)S(1)} collective-permute-done((bf16[1,2,2,2,128,384]{5,4,3,2,1,0:T(8,128)(2,1)}, bf16[1,2,2,2,128,384]{5,4,3,2,1,0:T(8,128)(2,1)S(1)}, u32[]{:S(2)}, u32[]{:S(2)}) %collective-permute-start.30) | collective-permute-done | bytes 786464 | tf_op jit(solution)/shard_map/ppermute | solution.py:40
  657.5 9.9 %collective-permute-done.40.refs_5_ = bf16[1,2,1,1,128,1280]{5,4,3,2,1,0:T(8,128)(2,1)S(1)} collective-permute-done((bf16[1,2,1,1,128,1280]{5,4,3,2,1,0:T(8,128)(2,1)S(1)}, bf16[1,2,1,1,128,1280]{5,4,3,2,1,0:T(8,128)(2,1)S(1)}, u32[]{:S(2)}, u32[]{:S(2)}) %collective-permute-start.40) | collective-permute-done | bytes 655392 | tf_op jit(solution)/shard_map/ppermute | solution.py:40
  674.2 9.6 %collective-permute-done.44.refs_3_ = bf16[64,4096]{1,0:T(8,128)(2,1)S(1)} collective-permute-done((bf16[64,4096]{1,0:T(8,128)(2,1)S(1)}, bf16[64,4096]{1,0:T(8,128)(2,1)S(1)}, u32[]{:S(2)}, u32[]{:S(2)}) %collective-permute-start.44) | collective-permute-done | bytes 524320 | tf_op jit(solution)/shard_map/ppermute | solution.py:40
  (442 shorter events, 299.0 us)
Async XLA Ops:
  7.2 118.6 %all-gather.5.cloned.1.call-start = ((), (), s32[]{:S(2)}) async-start(), calls=%async_computation.3 | async-start | bytes 22560768 | tf_op jit(solution)/shard_map/all_gather | solution.py:868
  12.9 223.9 %all-gather.3.cloned.1.call-start = ((), (), s32[]{:S(2)}) async-start(), calls=%async_computation.2 | async-start | bytes 22282240 | tf_op jit(solution)/shard_map/all_gather | solution.py:868
  16.5 488.6 %reduce-scatter.3.cloned.1.call-start = ((), (), s32[]{:S(2)}) async-start(), calls=%async_computation.4 | async-start | bytes 4718592 | tf_op jit(solution)/shard_map/reduce_scatter | solution.py:671
  152.7 47.9 %collective-permute-start.1 = (bf16[1024,1024]{1,0:T(8,128)(2,1)S(1)}, bf16[1024,1024]{1,0:T(8,128)(2,1)}, u32[]{:S(2)}, u32[]{:S(2)}) collective-permute-start(bf16[1024,1024]{1,0:T(8,128)(2,1)S(1)} %copy-done.53), channel_id=1, source_target_pairs={{0,1},{1,0},{2,3},{3,2},{4,5},{5,4},{6,7},{7,6},{8,9},{9,8},{10,11... | collective-permute-start | bytes 6291464 | tf_op jit(solution)/shard_map/ppermute | solution.py:40
  260.0 49.1 %collective-permute-start = (bf16[1024,1024]{1,0:T(8,128)(2,1)}, bf16[1024,1024]{1,0:T(8,128)(2,1)}, u32[]{:S(2)}, u32[]{:S(2)}) collective-permute-start(bf16[1024,1024]{1,0:T(8,128)(2,1)} %constant_dynamic-slice_fusion.2.refs_3_), channel_id=1, source_target_pairs={{0,1},{1,0},{2,3},{3,2},{4,5},{5,4},{6,7},{7,6},{8,9},{9,8},{10,11... | collective-permute-start | bytes 6291464 | tf_op jit(solution)/shard_map/ppermute | solution.py:40
  286.5 22.6 %collective-permute-start.10 = (bf16[640,1024]{1,0:T(8,128)(2,1)}, bf16[640,1024]{1,0:T(8,128)(2,1)S(1)}, u32[]{:S(2)}, u32[]{:S(2)}) collective-permute-start(bf16[640,1024]{1,0:T(8,128)(2,1)} %bitcast_convert_fusion.yo.refs_4_), channel_id=1, source_target_pairs={{0,2},{1,3},{2,0},{3,1},{4,6},{5,7},{6,4},{7,5},{8,10},{9,11},{10,... | collective-permute-start | bytes 3932168 | tf_op jit(solution)/shard_map/ppermute | solution.py:40
  323.5 262.1 %reduce-scatter.5.cloned.1.call-start = ((), (), s32[]{:S(2)}) async-start(), calls=%async_computation.5 | async-start | bytes 4718592 | tf_op jit(solution)/shard_map/reduce_scatter | solution.py:671
  342.9 34.9 %collective-permute-start.11 = (f32[640,1024]{1,0:T(8,128)}, f32[640,1024]{1,0:T(8,128)}, u32[]{:S(2)}, u32[]{:S(2)}) collective-permute-start(f32[640,1024]{1,0:T(8,128)} %shard_map.272.refs_10_), channel_id=1, source_target_pairs={{0,2},{1,3},{2,0},{3,1},{4,6},{5,7},{6,4},{7,5},{8,10},{9,11},{10,... | collective-permute-start | bytes 7864328 | tf_op jit(solution)/shard_map/ppermute | solution.py:40
  401.5 60.5 %collective-permute-start.17 = (bf16[1,2,2,2,128,1280]{5,4,3,2,1,0:T(8,128)(2,1)}, bf16[1,2,2,2,128,1280]{5,4,3,2,1,0:T(8,128)(2,1)S(1)}, u32[]{:S(2)}, u32[]{:S(2)}) collective-permute-start(bf16[1,2,2,2,128,1280]{5,4,3,2,1,0:T(8,128)(2,1)} %get-tuple-element.147.refs_9_), channel_id=1, source_target_pairs={{0,1},{1,0},{2,3},{3,2},{4,5},{5,4},{6,7},{7,6},{8,9},{9,8},{10,11... | collective-permute-start | bytes 7864328 | tf_op jit(solution)/shard_map/ppermute | solution.py:40
  434.7 50.2 %collective-permute-start.19 = (bf16[2,2,2,1,128,768]{5,4,3,2,1,0:T(8,128)(2,1)}, bf16[2,2,2,1,128,768]{5,4,3,2,1,0:T(8,128)(2,1)}, u32[]{:S(2)}, u32[]{:S(2)}) collective-permute-start(bf16[2,2,2,1,128,768]{5,4,3,2,1,0:T(8,128)(2,1)} %get-tuple-element.152.refs_6_), channel_id=1, source_target_pairs={{0,4},{1,5},{2,6},{3,7},{4,0},{5,1},{6,2},{7,3},{8,12},{9,13},{10,... | collective-permute-start | bytes 4718600 | tf_op jit(solution)/shard_map/ppermute | solution.py:40
  468.9 44.8 %collective-permute-start.21 = (bf16[1,2,2,1,128,1280]{5,4,3,2,1,0:T(8,128)(2,1)}, bf16[1,2,2,1,128,1280]{5,4,3,2,1,0:T(8,128)(2,1)S(1)}, u32[]{:S(2)}, u32[]{:S(2)}) collective-permute-start(bf16[1,2,2,1,128,1280]{5,4,3,2,1,0:T(8,128)(2,1)} %get-tuple-element.157.refs_11_), channel_id=1, source_target_pairs={{0,4},{1,5},{2,6},{3,7},{4,0},{5,1},{6,2},{7,3},{8,12},{9,13},{10,... | collective-permute-start | bytes 3932168 | tf_op jit(solution)/shard_map/ppermute | solution.py:40
  484.9 43.9 %collective-permute-start.18 = (bf16[640,1024]{1,0:T(8,128)(2,1)}, bf16[640,1024]{1,0:T(8,128)(2,1)}, u32[]{:S(2)}, u32[]{:S(2)}) collective-permute-start(bf16[640,1024]{1,0:T(8,128)(2,1)} %get-tuple-element.158.rest_0_.yo.refs_2_), channel_id=1, source_target_pairs={{0,2},{1,3},{2,0},{3,1},{4,6},{5,7},{6,4},{7,5},{8,10},{9,11},{10,... | collective-permute-start | bytes 3932168 | tf_op jit(solution)/shard_map/ppermute | solution.py:40
  490.3 36.4 %collective-permute-start.20 = (bf16[2,2,1,1,128,768]{5,4,3,2,1,0:T(8,128)(2,1)S(1)}, bf16[2,2,1,1,128,768]{5,4,3,2,1,0:T(8,128)(2,1)S(1)}, u32[]{:S(2)}, u32[]{:S(2)}) collective-permute-start(bf16[2,2,1,1,128,768]{5,4,3,2,1,0:T(8,128)(2,1)S(1)} %get-tuple-element.163.rest_1_), channel_id=1, source_target_pairs={{0,8},{1,9},{2,10},{3,11},{4,12},{5,13},{6,14},{7,15},{8,0},{9,1},... | collective-permute-start | bytes 2359304 | tf_op jit(solution)/shard_map/ppermute | solution.py:40
  513.4 38.4 %collective-permute-start.23 = (bf16[128,1024]{1,0:T(8,128)(2,1)S(1)}, bf16[128,1024]{1,0:T(8,128)(2,1)S(1)}, u32[]{:S(2)}, u32[]{:S(2)}) collective-permute-start(bf16[128,1024]{1,0:T(8,128)(2,1)S(1)} %get-tuple-element.169.refs_8_), channel_id=1, source_target_pairs={{0,2},{1,3},{2,0},{3,1},{4,6},{5,7},{6,4},{7,5},{8,10},{9,11},{10,... | collective-permute-start | bytes 786440 | tf_op jit(solution)/shard_map/ppermute | solution.py:40
  518.8 61.0 %collective-permute-start.25 = (bf16[1,2,1,1,128,1280]{5,4,3,2,1,0:T(8,128)(2,1)}, bf16[1,2,1,1,128,1280]{5,4,3,2,1,0:T(8,128)(2,1)}, u32[]{:S(2)}, u32[]{:S(2)}) collective-permute-start(bf16[1,2,1,1,128,1280]{5,4,3,2,1,0:T(8,128)(2,1)} %get-tuple-element.168.refs_7_), channel_id=1, source_target_pairs={{0,8},{1,9},{2,10},{3,11},{4,12},{5,13},{6,14},{7,15},{8,0},{9,1},... | collective-permute-start | bytes 1966088 | tf_op jit(solution)/shard_map/ppermute | solution.py:40
  527.1 52.7 %collective-permute-start.24 = (bf16[1,2,1,1,128,768]{5,4,3,2,1,0:T(8,128)(2,1)S(1)}, bf16[1,2,1,1,128,768]{5,4,3,2,1,0:T(8,128)(2,1)S(1)}, u32[]{:S(2)}, u32[]{:S(2)}) collective-permute-start(bf16[1,2,1,1,128,768]{5,4,3,2,1,0:T(8,128)(2,1)S(1)} %get-tuple-element.166.refs_6_), channel_id=1, source_target_pairs={{0,1},{1,0},{2,3},{3,2},{4,5},{5,4},{6,7},{7,6},{8,9},{9,8},{10,11... | collective-permute-start | bytes 1179656 | tf_op jit(solution)/shard_map/ppermute | solution.py:40
  551.1 60.3 %collective-permute-start.27 = (bf16[1,2,2,2,128,1280]{5,4,3,2,1,0:T(8,128)(2,1)}, bf16[1,2,2,2,128,1280]{5,4,3,2,1,0:T(8,128)(2,1)}, u32[]{:S(2)}, u32[]{:S(2)}) collective-permute-start(bf16[1,2,2,2,128,1280]{5,4,3,2,1,0:T(8,128)(2,1)} %get-tuple-element.176.refs_2_.refs_9_), channel_id=1, source_target_pairs={{0,1},{1,0},{2,3},{3,2},{4,5},{5,4},{6,7},{7,6},{8,9},{9,8},{10,11... | collective-permute-start | bytes 7864328 | tf_op jit(solution)/shard_map/ppermute | solution.py:40
  554.9 119.3 %collective-permute-start.43 = (bf16[256,1024]{1,0:T(8,128)(2,1)}, bf16[256,1024]{1,0:T(8,128)(2,1)}, u32[]{:S(2)}, u32[]{:S(2)}) collective-permute-start(bf16[256,1024]{1,0:T(8,128)(2,1)} %shard_map.290.refs_10_.refs_0_), channel_id=1, source_target_pairs={{0,1},{1,0},{2,3},{3,2},{4,5},{5,4},{6,7},{7,6},{8,9},{9,8},{10,11... | collective-permute-start | bytes 1572872 | tf_op jit(solution)/shard_map/ppermute | solution.py:40
  583.5 25.9 %collective-permute-start.28 = (bf16[128,2048]{1,0:T(8,128)(2,1)S(1)}, bf16[128,2048]{1,0:T(8,128)(2,1)S(1)}, u32[]{:S(2)}, u32[]{:S(2)}) collective-permute-start(bf16[128,2048]{1,0:T(8,128)(2,1)S(1)} %get-tuple-element.181.rest_1_), channel_id=1, source_target_pairs={{0,16},{1,17},{2,18},{3,19},{4,20},{5,21},{6,22},{7,23},{8,24},{9,... | collective-permute-start | bytes 1572872 | tf_op jit(solution)/shard_map/ppermute | solution.py:40
  598.1 28.1 %collective-permute-start.31 = (bf16[2,2,1,2,128,384]{5,4,3,2,1,0:T(8,128)(2,1)}, bf16[2,2,1,2,128,384]{5,4,3,2,1,0:T(8,128)(2,1)S(1)}, u32[]{:S(2)}, u32[]{:S(2)}) collective-permute-start(bf16[2,2,1,2,128,384]{5,4,3,2,1,0:T(8,128)(2,1)} %get-tuple-element.183.rest_0_), channel_id=1, source_target_pairs={{0,8},{1,9},{2,10},{3,11},{4,12},{5,13},{6,14},{7,15},{8,0},{9,1},... | collective-permute-start | bytes 2359304 | tf_op jit(solution)/shard_map/ppermute | solution.py:40
  607.9 31.2 %collective-permute-start.30 = (bf16[1,2,2,2,128,384]{5,4,3,2,1,0:T(8,128)(2,1)}, bf16[1,2,2,2,128,384]{5,4,3,2,1,0:T(8,128)(2,1)S(1)}, u32[]{:S(2)}, u32[]{:S(2)}) collective-permute-start(bf16[1,2,2,2,128,384]{5,4,3,2,1,0:T(8,128)(2,1)} %get-tuple-element.184.rest_0_.refs_2_.refs_6_), channel_id=1, source_target_pairs={{0,1},{1,0},{2,3},{3,2},{4,5},{5,4},{6,7},{7,6},{8,9},{9,8},{10,11... | collective-permute-start | bytes 2359304 | tf_op jit(solution)/shard_map/ppermute | solution.py:40
  616.8 31.4 %collective-permute-start.35 = (bf16[1,2,2,1,128,1280]{5,4,3,2,1,0:T(8,128)(2,1)}, bf16[1,2,2,1,128,1280]{5,4,3,2,1,0:T(8,128)(2,1)}, u32[]{:S(2)}, u32[]{:S(2)}) collective-permute-start(bf16[1,2,2,1,128,1280]{5,4,3,2,1,0:T(8,128)(2,1)} %get-tuple-element.186.refs_8_), channel_id=1, source_target_pairs={{0,4},{1,5},{2,6},{3,7},{4,0},{5,1},{6,2},{7,3},{8,12},{9,13},{10,... | collective-permute-start | bytes 3932168 | tf_op jit(solution)/shard_map/ppermute | solution.py:40
  667.6 23.8 %collective-permute-start.42 = (bf16[128,2048]{1,0:T(8,128)(2,1)S(1)}, bf16[128,2048]{1,0:T(8,128)(2,1)S(1)}, u32[]{:S(2)}, u32[]{:S(2)}) collective-permute-start(bf16[128,2048]{1,0:T(8,128)(2,1)S(1)} %get-tuple-element.214.refs_2_), channel_id=1, source_target_pairs={{0,16},{1,17},{2,18},{3,19},{4,20},{5,21},{6,22},{7,23},{8,24},{9,... | collective-permute-start | bytes 1572872 | tf_op jit(solution)/shard_map/ppermute | solution.py:40
  672.2 21.5 %collective-permute-start.41 = (f32[2,16,768]{2,1,0:T(8,128)S(1)}, f32[2,16,768]{2,1,0:T(8,128)S(1)}, u32[]{:S(2)}, u32[]{:S(2)}) collective-permute-start(f32[2,16,768]{2,1,0:T(8,128)S(1)} %shard_map.309.refs_4_.refs_0_), channel_id=1, source_target_pairs={{0,8},{1,9},{2,10},{3,11},{4,12},{5,13},{6,14},{7,15},{8,0},{9,1},... | collective-permute-start | bytes 294920 | tf_op jit(solution)/shard_map/ppermute | solution.py:40
  (114 other events, 877.2 us)
Sparse Core Ops, SparseCore 0:
  13.0 112.7 all-gather.4
  128.0 108.8 all-gather.2
  323.6 86.9 reduce-scatter.2
  462.1 106.4 reduce-scatter.4

commit v7 on v6

--- a/solution.py
+++ b/solution.py
@@ -64,32 +64,47 @@
     return ("columns", width, (first, stride))
 
 
+class Held:
+    def __init__(self, ref, copy):
+        self.ref, self.copy, self.shape, self.waited = ref, copy, ref.shape, False
+
+    def ready(self):
+        if not self.waited:
+            self.waited = True
+
+            @pl.when(pl.program_id(0) == 0)
+            def _():
+                self.copy.wait()
+
+        return self.ref
+
+
 def row_call(body, where, kept, weights, blocked, whole, outs, images, slots, after=(), cost=FORWARD):
-    in_specs, args = [], []
+    in_specs, args, held_shapes, sources = [], [], [], []
     for v, pick_of in (part for w in weights for part in w):
+        in_specs.append(ANY)
         if pick_of is None:
-            in_specs.append(pl.BlockSpec(v.shape, lambda i, w, k: (0, 0), pipeline_mode=ONCE))
             args.append(v)
+            held_shapes.append(v.shape)
+            sources.append(lambda ref, w: ref)
             continue
         kind, width, first = pick_of
-        if kind == "columns":
-            spec = pl.BlockSpec((v.shape[0], width), lambda i, w, k, f=first: (0, f[0] + f[1] * w[0]), pipeline_mode=ONCE)
-            in_specs.append(spec)
-            args.append(v)
-        elif kind == "quarter":
-            at, stride, part = first
-            spec = pl.BlockSpec(
-                (v.shape[0], width),
-                lambda i, w, k, f=(at, stride, part): (0, f[0] + f[1] * w[0] + jnp.bitwise_xor(f[2], w[3])),
-                pipeline_mode=ONCE,
-            )
-            in_specs.append(spec)
-            args.append(v)
-        else:
-            view = v.reshape(HEADS // 2, 2, HEAD_DIM, v.shape[1])
-            spec = pl.BlockSpec((HEADS // 2, None, HEAD_DIM, width), lambda i, w, k, f=first: (0, w[0], 0, f), pipeline_mode=ONCE)
-            in_specs.append(spec)
-            args.append(view)
+        if kind == "heads":
+            args.append(v.reshape(HEADS // 2, 2, HEAD_DIM, v.shape[1]))
+            held_shapes.append((HEADS // 2, HEAD_DIM, width))
+            sources.append(lambda ref, w, f=first * width, n=width: ref.at[:, w[0], :, pl.ds(f, n)])
+            continue
+        args.append(v)
+        held_shapes.append((v.shape[0], width))
+        at, stride, part = first if kind == "quarter" else first + (None,)
+
+        def source(ref, w, at=at, stride=stride, part=part, width=width):
+            column = at + stride * w[0]
+            if part is not None:
+                column = column + jnp.bitwise_xor(part, w[3])
+            return ref.at[:, pl.ds(pl.multiple_of(column * width, 128), width)]
+
+        sources.append(source)
     for v in blocked:
         if v.ndim == 2:
             in_specs.append(pl.BlockSpec((slots, v.shape[1]), lambda i, *_: (i, 0)))
@@ -111,19 +126,36 @@
     n_p, n_b, n_in = sum(len(w) for w in weights), len(blocked), len(args)
     in_specs += [ANY] * len(after)
     args += list(after)
+    n_out = len(outs)
 
     def kernel(where_ref, kept_ref, *refs):
-        ins, res = refs[:n_in], refs[n_in + len(after) :]
+        ins, rest = refs[:n_in], refs[n_in + len(after) :]
+        res, parts, sems = rest[:n_out], rest[n_out:-1], rest[-1]
+        copies = [
+            pltpu.make_async_copy(sources[k](ins[k], where_ref), parts[k], sems.at[k]) for k in range(n_p)
+        ]
+
+        @pl.when(pl.program_id(0) == 0)
+        def _():
+            for c in copies:
+                c.start()
+
         held, at = [], 0
         for w in weights:
-            held.append(ins[at : at + len(w)])
+            held.append([Held(parts[k], copies[k]) for k in range(at, at + len(w))])
             at += len(w)
         body(kept_ref, held, ins[n_p : n_p + n_b], ins[n_p + n_b : n_in], res)
+        for h in (h for w in held for h in w):
+            h.ready()
 
     return pl.pallas_call(
         kernel,
         grid_spec=pltpu.PrefetchScalarGridSpec(
-            num_scalar_prefetch=2, grid=(images,), in_specs=in_specs, out_specs=out_specs
+            num_scalar_prefetch=2,
+            grid=(images,),
+            in_specs=in_specs,
+            out_specs=out_specs,
+            scratch_shapes=[pltpu.VMEM(shape, BF) for shape in held_shapes] + [pltpu.SemaphoreType.DMA((n_p,))],
         ),
         out_shape=out_shape,
         compiler_params=pltpu.CompilerParams(vmem_limit_bytes=LIMIT),
@@ -164,17 +196,17 @@
     x = blocked[0][...]
     for k, n in chunks(outs[0].shape[1], 512):
         cols = pl.ds(k, n)
-        outs[0][:, cols] = (dot(x, w[0][0][:, cols]) + whole[0][:, cols]).astype(BF)
+        outs[0][:, cols] = (dot(x, w[0][0].ready()[:, cols]) + whole[0][:, cols]).astype(BF)
 
 
 def heads_of(ref):
-    return ref[...].reshape(-1, ref.shape[-1])
+    return ref.ready()[...].reshape(-1, ref.shape[-1])
 
 
 def pairs_dot(x_ref, parts):
     total, at = None, 0
     for w_ref in parts:
-        term = dot(x_ref[:, at : at + w_ref.shape[0]], w_ref[...])
+        term = dot(x_ref[:, at : at + w_ref.shape[0]], w_ref.ready()[...])
         total = term if total is None else total + term
         at += w_ref.shape[0]
     return total
@@ -217,7 +249,7 @@
     for k, n in chunks(outs[0].shape[1], 256):
         cols = pl.ds(k, n)
         held = w[0][k // w[0][0].shape[1]]
-        pre = dot(x, held[:, pl.ds(k % held.shape[1], n)]) + whole[0][:, cols]
+        pre = dot(x, held.ready()[:, pl.ds(k % held.shape[1], n)]) + whole[0][:, cols]
         phi = 0.5 + 0.5 * lax.erf(pre * (2.0**-0.5))
         dens = jnp.exp(-0.5 * (pre * pre)) * 0.3989422804014327
         outs[0][:, cols] = (pre * phi).astype(BF)
@@ -249,11 +281,11 @@
             if k >= first + held.shape[0]:
                 first += held.shape[0]
                 held = part
-        t = dot_t(low, held[pl.ds(k - first, n), :])
+        t = dot_t(low, held.ready()[pl.ds(k - first, n), :])
         outs[0][:, cols] = (t * blocked[1][:, cols].astype(F32)).astype(BF)
     total, at = None, 0
     for held in w[1]:
-        term = dot_t(outs[0][:, at : at + held.shape[1]], held[...])
+        term = dot_t(outs[0][:, at : at + held.shape[1]], held.ready()[...])
         total = term if total is None else total + term
         at += held.shape[1]
     return total
@@ -308,7 +340,7 @@
                 at = j * third + lo - HEAD_DIM
                 outs[0][:, at : at + 2 * HEAD_DIM] = jnp.concatenate(pairs[j], axis=1)
             pairs = [[], [], []]
-    return dot_t(outs[0][...], w[1][0][...])
+    return dot_t(outs[0][...], w[1][0].ready()[...])
 
 
 def attend_back_other(kept, w, blocked, whole, outs):
@@ -562,7 +594,7 @@
         in_specs=[pl.BlockSpec(block, index)] * 2 + [ANY] * len(after),
         out_specs=[pl.BlockSpec(out_block, index)] * 2,
         out_shape=[jax.ShapeDtypeStruct(out, BF)] * 2,
-        compiler_params=pltpu.CompilerParams(vmem_limit_bytes=SMALL_LIMIT),
+        compiler_params=pltpu.CompilerParams(vmem_limit_bytes=LIMIT),
         cost_estimate=BACKWARD,
     )(keep, got, *after)
 

time: 727 us -> 745 us (1.025)
  Pallas kernels: 403 us -> 442 us
  waiting for transfers between devices: 182 us -> 169 us
  local copies, waits for them, and re-layouts: 75.9 us -> 67.3 us
    pallas_call x24, Pallas kernels: 274 us -> 295 us  [row_call(): pl.pallas_call(kernel, grid_spec=pltpu.PrefetchScalarGridSpec(num_scalar_...]
    pallas_call x10, Pallas kernels: 11.3 us -> 26.7 us  [combine(): pl.pallas_call(kernel, grid=(cuts,), in_specs=[pl.BlockSpec(block, index)...]
    unnamed x176 -> x168, local copies, waits for them, and re-layouts: 43.7 us -> 35.1 us
    ppermute x49, waiting for transfers between devices: 68.6 us -> 60.3 us  [swap(): return lax.ppermute(v, AX, pairs)]
  transfers between devices with their start and end apart: 53 -> 53, of which waited for: 16 -> 15; matrix products, arithmetic and copies ran while one was open for 6% -> 6% of each run, Pallas kernels for 50% -> 54%
where the time goes in v7:
time: 745 us; the launch traced here: 739 us
  Pallas kernels  442 us (59%)
  waiting for transfers between devices  169 us (23%)
  local copies, waits for them, and re-layouts  67.3 us (9%)
  starting transfers between devices  35.2 us (5%)
  between operations  15.4 us (2%)
  other arithmetic  10.5 us (1%)
    pallas_call x24, Pallas kernels, row_call(): pl.pallas_call(kernel, grid_spec=pltpu.PrefetchScalarGridSpec(num_scalar_...  295 us
    all_gather x2, waiting for transfers between devices, per_device(): gathered.append(lax.all_gather(done[0], 'shard', axis=0, tiled=True))  109 us
    ppermute x49, waiting for transfers between devices, swap(): return lax.ppermute(v, AX, pairs)  60.3 us
    pallas_call x5, Pallas kernels, weight_grad(): pl.pallas_call(kernel, grid_spec=pltpu.PrefetchScalarGridSpec(num_scalar_...  53.8 us
    unnamed x168, local copies, waits for them, and re-layouts  35.1 us
    ppermute x49, starting transfers between devices, swap(): return lax.ppermute(v, AX, pairs)  35 us
    pallas_call x10, Pallas kernels, combine(): pl.pallas_call(kernel, grid=(cuts,), in_specs=[pl.BlockSpec(block, index)...  26.7 us
    pallas_call x2, Pallas kernels, chip_grad(): pl.pallas_call(kernel, grid_spec=pltpu.PrefetchScalarGridSpec(num_scalar_...  26.7 us
  transfers between devices with their start and end apart: 53, of which 15 were waited for; matrix products, arithmetic and copies ran while one was open for 6% of the time, Pallas kernels for 54%

profile of v7, /device:TPU:0, one launch (start us, length us, event | category | flops | bytes accessed | tf_op | source)
XLA Modules:
  0.0 739.2 jit_solution(2962749998629568119)
XLA Ops:
  17.4 108.3 %all-gather.5.cloned.1.call-done.refs_0_.refs_1_.refs_2_.refs_3_ = bf16[1024,10368]{1,0:T(8,128)(2,1)} async-done(((bf16[64,10368]{1,0:T(8,128)(2,1)}), bf16[1024,10368]{1,0:T(8,128)(2,1)}) %all-gather.5.cloned.1.call-update) | async-done | bytes 21233680 | tf_op jit(solution)/shard_map/all_gather | solution.py:900
  141.5 11.7 %shard_map.258 = (bf16[2,8,320,320]{3,2,1,0:T(8,128)(2,1)}, bf16[640,512]{1,0:T(8,128)(2,1)}, f32[640,1024]{1,0:T(8,128)}) custom-call(s32[4]{0:T(128)} %pad_add_fusion.where_ref, s32[2]{0:T(128)} %copy-done.63, bf16[8,2,64,10368]{3,2,1,0:T(8,128)(2,1)} %bitcast.52, bf16[640,1536]{1,0:T(8,128)(2,1)} %shard_map.257.refs_1_.refs_3_), custom_call_target="tpu_custom_call" | custom-call | flops 10000000 | tf_op jit(solution)/shard_map/pallas_call | solution.py:151
  166.1 13.3 %shard_map.259 = (bf16[2,8,320,320]{3,2,1,0:T(8,128)(2,1)}, bf16[640,512]{1,0:T(8,128)(2,1)}, f32[640,1024]{1,0:T(8,128)}, bf16[640,1024]{1,0:T(8,128)(2,1)}) custom-call(s32[4]{0:T(128)} %pad_add_fusion.where_ref, s32[2]{0:T(128)} %kept_ref.23, bf16[8,2,64,10368]{3,2,1,0:T(8,128)(2,1)} %bitcast.53, bf16[640,1536]{1,0:T(8,128)(2,1)} %shard_map.256.refs_1_.refs_3_, ...), custom_call_target="tpu_custom_call" | custom-call | flops 10000000 | tf_op jit(solution)/shard_map/pallas_call | solution.py:151
  183.8 10.2 %shard_map.261 = (bf16[640,2048]{1,0:T(8,128)(2,1)}, bf16[640,2048]{1,0:T(8,128)(2,1)}) custom-call(s32[4]{0:T(128)} %pad_add_fusion.where_ref, s32[2]{0:T(128)} %copy-done.63, bf16[1024,10368]{1,0:T(8,128)(2,1)} %all-gather.5.cloned.1.call-done.refs_0_.refs_1_.refs_2_.refs_3_, ...), custom_call_target="tpu_custom_call" | custom-call | flops 10000000 | tf_op jit(solution)/shard_map/pallas_call | solution.py:151
  212.8 10.3 %shard_map.260 = (bf16[640,2048]{1,0:T(8,128)(2,1)}, bf16[640,2048]{1,0:T(8,128)(2,1)}) custom-call(s32[4]{0:T(128)} %pad_add_fusion.where_ref, s32[2]{0:T(128)} %kept_ref.23, bf16[1024,10368]{1,0:T(8,128)(2,1)} %all-gather.5.cloned.1.call-done.refs_0_.refs_1_.refs_2_.refs_3_, ...), custom_call_target="tpu_custom_call" | custom-call | flops 10000000 | tf_op jit(solution)/shard_map/pallas_call | solution.py:151
  224.6 10.8 %shard_map.263 = (f32[640,1024]{1,0:T(8,128)}, bf16[640,1024]{1,0:T(8,128)(2,1)}) custom-call(s32[4]{0:T(128)} %pad_add_fusion.where_ref, s32[2]{0:T(128)} %kept_ref.23, bf16[1024,10368]{1,0:T(8,128)(2,1)} %all-gather.5.cloned.1.call-done.refs_0_.refs_1_.refs_2_.refs_3_, bf16[1024,1024]{1,0:T(8,128)(2,1)} %collective-permute-done.1.refs_1_, ...), custom_call_target="tpu_custom_call" | custom-call | flops 10000000 | tf_op jit(solution)/shard_map/pallas_call | solution.py:151
  248.6 11.8 %shard_map.266 = (bf16[2,8,320,320]{3,2,1,0:T(8,128)(2,1)}, bf16[640,512]{1,0:T(8,128)(2,1)}, f32[640,1024]{1,0:T(8,128)}) custom-call(s32[4]{0:T(128)} %pad_add_fusion.where_ref, s32[2]{0:T(128)} %copy-done.63, bf16[8,2,64,10240]{3,2,1,0:T(8,128)(2,1)} %bitcast.56, bf16[640,1536]{1,0:T(8,128)(2,1)} %shard_map.265.refs_1_.refs_3_), custom_call_target="tpu_custom_call" | custom-call | flops 10000000 | tf_op jit(solution)/shard_map/pallas_call | solution.py:151
  273.2 13.4 %shard_map.267 = (bf16[2,8,320,320]{3,2,1,0:T(8,128)(2,1)}, bf16[640,512]{1,0:T(8,128)(2,1)}, f32[640,1024]{1,0:T(8,128)}, bf16[640,1024]{1,0:T(8,128)(2,1)}) custom-call(s32[4]{0:T(128)} %pad_add_fusion.where_ref, s32[2]{0:T(128)} %kept_ref.23, bf16[8,2,64,10240]{3,2,1,0:T(8,128)(2,1)} %bitcast.57, bf16[640,1536]{1,0:T(8,128)(2,1)} %shard_map.264.refs_1_.refs_3_, ...), custom_call_target="tpu_custom_call" | custom-call | flops 10000000 | tf_op jit(solution)/shard_map/pallas_call | solution.py:151
  291.4 10.2 %shard_map.268 = (bf16[640,2048]{1,0:T(8,128)(2,1)}, bf16[640,2048]{1,0:T(8,128)(2,1)}) custom-call(s32[4]{0:T(128)} %pad_add_fusion.where_ref, s32[2]{0:T(128)} %kept_ref.23, bf16[1024,10240]{1,0:T(8,128)(2,1)} %all-gather.3.cloned.1.call-done.refs_0_.refs_1_.refs_2_.refs_3_, ...), custom_call_target="tpu_custom_call" | custom-call | flops 10000000 | tf_op jit(solution)/shard_map/pallas_call | solution.py:151
  301.6 10.2 %shard_map.269 = (bf16[640,2048]{1,0:T(8,128)(2,1)}, bf16[640,2048]{1,0:T(8,128)(2,1)}) custom-call(s32[4]{0:T(128)} %pad_add_fusion.where_ref, s32[2]{0:T(128)} %copy-done.63, bf16[1024,10240]{1,0:T(8,128)(2,1)} %all-gather.3.cloned.1.call-done.refs_0_.refs_1_.refs_2_.refs_3_, ...), custom_call_target="tpu_custom_call" | custom-call | flops 10000000 | tf_op jit(solution)/shard_map/pallas_call | solution.py:151
  312.8 13.3 %shard_map.270.refs_6_ = bf16[2048,1024]{1,0:T(8,128)(2,1)} custom-call(s32[4]{0:T(128)} %pad_add_fusion.where_ref, bf16[640,2048]{1,0:T(8,128)(2,1)} %get-tuple-element.129.xo.rest_0_.refs_2_, bf16[640,2048]{1,0:T(8,128)(2,1)} %get-tuple-element.130.xt.refs_2_, bf16[640,1024]{1,0:T(8,128)(2,1)} %bitcast_convert_fusion.yo.refs_4_, ...), custom_call_target="tpu_custom_call" | custom-call | flops 30000001024 | tf_op jit(solution)/shard_map/pallas_call | solution.py:486
  326.2 12.6 %shard_map.271 = (bf16[640,2048]{1,0:T(8,128)(2,1)}, f32[640,1024]{1,0:T(8,128)}) custom-call(s32[4]{0:T(128)} %pad_add_fusion.where_ref, s32[2]{0:T(128)} %copy-done.63, bf16[1024,10240]{1,0:T(8,128)(2,1)} %all-gather.3.cloned.1.call-done.refs_0_.refs_1_.refs_2_.refs_3_, bf16[1024,1024]{1,0:T(8,128)(2,1)} %collective-permute-done.rest_1_.refs_1_, ...), custom_call_target="tpu_custom_call" | custom-call | flops 30000001024 | tf_op jit(solution)/shard_map/pallas_call | solution.py:151
  348.2 16.7 %shard_map.273 = (bf16[640,2048]{1,0:T(8,128)(2,1)}, f32[640,1024]{1,0:T(8,128)}, bf16[640,1024]{1,0:T(8,128)(2,1)}, f32[8,1024]{1,0:T(8,128)}) custom-call(s32[4]{0:T(128)} %pad_add_fusion.where_ref, s32[2]{0:T(128)} %kept_ref.23, bf16[1024,10240]{1,0:T(8,128)(2,1)} %all-gather.3.cloned.1.call-done.refs_0_.refs_1_.refs_2_.refs_3_, ...), custom_call_target="tpu_custom_call" | custom-call | flops 30000001024 | tf_op jit(solution)/shard_map/pallas_call | solution.py:151
  365.0 13.2 %shard_map.274 = (bf16[1,2,2,2,128,1280]{5,4,3,2,1,0:T(8,128)(2,1)}, bf16[1,2,2,2,128,1280]{5,4,3,2,1,0:T(8,128)(2,1)}, f32[1,2048]{1,0:T(1,128)}) custom-call(s32[4]{0:T(128)} %pad_add_fusion.where_ref, bf16[640,1024]{1,0:T(8,128)(2,1)} %get-tuple-element.128.refs_2_.xo, bf16[640,1024]{1,0:T(8,128)(2,1)} %collective-permute-done.9.refs_2_.xt, ...), custom_call_target="tpu_custom_call" | custom-call | flops 30000001024 | tf_op jit(solution)/shard_map/pallas_call | solution.py:444
  383.2 17.5 %shard_map.275 = (bf16[640,1536]{1,0:T(8,128)(2,1)}, f32[640,1024]{1,0:T(8,128)}) custom-call(s32[4]{0:T(128)} %pad_add_fusion.where_ref, s32[2]{0:T(128)} %copy-done.63, bf16[8,2,64,10240]{3,2,1,0:T(8,128)(2,1)} %bitcast.58, bf16[1024,10240]{1,0:T(8,128)(2,1)} %all-gather.3.cloned.1.call-done.refs_0_.refs_1_.refs_2_.refs_3_, ...), custom_call_target="tpu_custom_call" | custom-call | flops 30000001024 | tf_op jit(solution)/shard_map/pallas_call | solution.py:151
  407.4 21.5 %shard_map.277 = (bf16[640,1536]{1,0:T(8,128)(2,1)}, f32[640,1024]{1,0:T(8,128)}, bf16[640,1024]{1,0:T(8,128)(2,1)}, f32[8,1024]{1,0:T(8,128)}) custom-call(s32[4]{0:T(128)} %pad_add_fusion.where_ref, s32[2]{0:T(128)} %kept_ref.23, bf16[8,2,64,10240]{3,2,1,0:T(8,128)(2,1)} %bitcast.59, ...), custom_call_target="tpu_custom_call" | custom-call | flops 30000001024 | tf_op jit(solution)/shard_map/pallas_call | solution.py:151
  429.0 10.9 %shard_map.278 = (bf16[2,2,2,1,128,768]{5,4,3,2,1,0:T(8,128)(2,1)}, bf16[2,2,2,1,128,768]{5,4,3,2,1,0:T(8,128)(2,1)}, f32[1,1536]{1,0:T(1,128)}) custom-call(s32[4]{0:T(128)} %pad_add_fusion.where_ref, bf16[640,1024]{1,0:T(8,128)(2,1)} %get-tuple-element.125.refs_1_.xo, bf16[640,1024]{1,0:T(8,128)(2,1)} %copy-done.45, ...), custom_call_target="tpu_custom_call" | custom-call | flops 30000001024 | tf_op jit(solution)/shard_map/pallas_call | solution.py:444
  444.5 12.2 %shard_map.279 = (bf16[640,2048]{1,0:T(8,128)(2,1)}, f32[640,1024]{1,0:T(8,128)}) custom-call(s32[4]{0:T(128)} %pad_add_fusion.where_ref, s32[2]{0:T(128)} %copy-done.63, bf16[1024,10368]{1,0:T(8,128)(2,1)} %all-gather.5.cloned.1.call-done.refs_0_.refs_1_.refs_2_.refs_3_, bf16[1024,1024]{1,0:T(8,128)(2,1)} %collective-permute-done.1.refs_1_, ...), custom_call_target="tpu_custom_call" | custom-call | flops 30000001024 | tf_op jit(solution)/shard_map/pallas_call | solution.py:151
  457.0 13.3 %shard_map.280.rest_0_.refs_10_ = bf16[2048,1024]{1,0:T(8,128)(2,1)} custom-call(s32[4]{0:T(128)} %pad_add_fusion.where_ref, bf16[640,2048]{1,0:T(8,128)(2,1)} %get-tuple-element.122.refs_2_.xo, bf16[640,2048]{1,0:T(8,128)(2,1)} %get-tuple-element.123.refs_2_.xt, bf16[640,1024]{1,0:T(8,128)(2,1)} %get-tuple-element.148.yo.refs_4_, ...), custom_call_target="tpu_custom_call" | custom-call | flops 30000001024 | tf_op jit(solution)/shard_map/pallas_call | solution.py:486
  476.6 16.8 %shard_map.282 = (bf16[640,2048]{1,0:T(8,128)(2,1)}, f32[640,1024]{1,0:T(8,128)}, bf16[640,1024]{1,0:T(8,128)(2,1)}, f32[8,1024]{1,0:T(8,128)}) custom-call(s32[4]{0:T(128)} %pad_add_fusion.where_ref, s32[2]{0:T(128)} %kept_ref.23, bf16[1024,10368]{1,0:T(8,128)(2,1)} %all-gather.5.cloned.1.call-done.refs_0_.refs_1_.refs_2_.refs_3_, ...), custom_call_target="tpu_custom_call" | custom-call | flops 30000001024 | tf_op jit(solution)/shard_map/pallas_call | solution.py:151
  498.2 13.3 %shard_map.284 = (bf16[1,2,2,2,128,1280]{5,4,3,2,1,0:T(8,128)(2,1)}, bf16[1,2,2,2,128,1280]{5,4,3,2,1,0:T(8,128)(2,1)}, f32[1,2048]{1,0:T(1,128)}) custom-call(s32[4]{0:T(128)} %pad_add_fusion.where_ref, bf16[640,1024]{1,0:T(8,128)(2,1)} %get-tuple-element.121.refs_2_.xo, bf16[640,1024]{1,0:T(8,128)(2,1)} %copy-done.46, ...), custom_call_target="tpu_custom_call" | custom-call | flops 30000001024 | tf_op jit(solution)/shard_map/pallas_call | solution.py:444
  524.2 11.1 %collective-permute-done.20.g = bf16[2,2,1,1,128,768]{5,4,3,2,1,0:T(8,128)(2,1)S(1)} collective-permute-done((bf16[2,2,1,1,128,768]{5,4,3,2,1,0:T(8,128)(2,1)}, bf16[2,2,1,1,128,768]{5,4,3,2,1,0:T(8,128)(2,1)S(1)}, u32[]{:S(2)}, u32[]{:S(2)}) %collective-permute-start.20) | collective-permute-done | bytes 786464 | tf_op jit(solution)/shard_map/ppermute | solution.py:40
  539.8 17.4 %shard_map.288 = (bf16[640,1536]{1,0:T(8,128)(2,1)}, f32[640,1024]{1,0:T(8,128)}) custom-call(s32[4]{0:T(128)} %pad_add_fusion.where_ref, s32[2]{0:T(128)} %copy-done.63, bf16[8,2,64,10368]{3,2,1,0:T(8,128)(2,1)} %bitcast.54, bf16[1024,10368]{1,0:T(8,128)(2,1)} %all-gather.5.cloned.1.call-done.refs_0_.refs_1_.refs_2_.refs_3_, ...), custom_call_target="tpu_custom_call" | custom-call | flops 30000001024 | tf_op jit(solution)/shard_map/pallas_call | solution.py:151
  570.2 21.7 %shard_map.291 = (bf16[640,1536]{1,0:T(8,128)(2,1)}, f32[640,1024]{1,0:T(8,128)}, bf16[640,1024]{1,0:T(8,128)(2,1)}, f32[8,1024]{1,0:T(8,128)}) custom-call(s32[4]{0:T(128)} %pad_add_fusion.where_ref, s32[2]{0:T(128)} %kept_ref.23, bf16[8,2,64,10368]{3,2,1,0:T(8,128)(2,1)} %bitcast.55, ...), custom_call_target="tpu_custom_call" | custom-call | flops 30000001024 | tf_op jit(solution)/shard_map/pallas_call | solution.py:151
  (434 shorter events, 302.3 us)
Async XLA Ops:
  7.2 118.5 %all-gather.5.cloned.1.call-start = ((), (), s32[]{:S(2)}) async-start(), calls=%async_computation.3 | async-start | bytes 22560768 | tf_op jit(solution)/shard_map/all_gather | solution.py:900
  12.8 223.9 %all-gather.3.cloned.1.call-start = ((), (), s32[]{:S(2)}) async-start(), calls=%async_computation.2 | async-start | bytes 22282240 | tf_op jit(solution)/shard_map/all_gather | solution.py:900
  16.4 495.0 %reduce-scatter.3.cloned.1.call-start = ((), (), s32[]{:S(2)}) async-start(), calls=%async_computation.4 | async-start | bytes 4718592 | tf_op jit(solution)/shard_map/reduce_scatter | solution.py:703
  153.5 47.9 %collective-permute-start.1 = (bf16[1024,1024]{1,0:T(8,128)(2,1)S(1)}, bf16[1024,1024]{1,0:T(8,128)(2,1)}, u32[]{:S(2)}, u32[]{:S(2)}) collective-permute-start(bf16[1024,1024]{1,0:T(8,128)(2,1)S(1)} %copy-done.42), channel_id=1, source_target_pairs={{0,1},{1,0},{2,3},{3,2},{4,5},{5,4},{6,7},{7,6},{8,9},{9,8},{10,11... | collective-permute-start | bytes 6291464 | tf_op jit(solution)/shard_map/ppermute | solution.py:40
  260.7 51.0 %collective-permute-start = (bf16[1024,1024]{1,0:T(8,128)(2,1)}, bf16[1024,1024]{1,0:T(8,128)(2,1)}, u32[]{:S(2)}, u32[]{:S(2)}) collective-permute-start(bf16[1024,1024]{1,0:T(8,128)(2,1)} %constant_dynamic-slice_fusion.2.refs_3_), channel_id=1, source_target_pairs={{0,1},{1,0},{2,3},{3,2},{4,5},{5,4},{6,7},{7,6},{8,9},{9,8},{10,11... | collective-permute-start | bytes 6291464 | tf_op jit(solution)/shard_map/ppermute | solution.py:40
  287.9 23.8 %collective-permute-start.10 = (bf16[640,1024]{1,0:T(8,128)(2,1)}, bf16[640,1024]{1,0:T(8,128)(2,1)S(1)}, u32[]{:S(2)}, u32[]{:S(2)}) collective-permute-start(bf16[640,1024]{1,0:T(8,128)(2,1)} %bitcast_convert_fusion.yo.refs_4_), channel_id=1, source_target_pairs={{0,2},{1,3},{2,0},{3,1},{4,6},{5,7},{6,4},{7,5},{8,10},{9,11},{10,... | collective-permute-start | bytes 3932168 | tf_op jit(solution)/shard_map/ppermute | solution.py:40
  326.2 274.0 %reduce-scatter.5.cloned.1.call-start = ((), (), s32[]{:S(2)}) async-start(), calls=%async_computation.5 | async-start | bytes 4718592 | tf_op jit(solution)/shard_map/reduce_scatter | solution.py:703
  347.6 34.1 %collective-permute-start.11 = (f32[640,1024]{1,0:T(8,128)}, f32[640,1024]{1,0:T(8,128)S(1)}, u32[]{:S(2)}, u32[]{:S(2)}) collective-permute-start(f32[640,1024]{1,0:T(8,128)} %shard_map.272.refs_10_), channel_id=1, source_target_pairs={{0,2},{1,3},{2,0},{3,1},{4,6},{5,7},{6,4},{7,5},{8,10},{9,11},{10,... | collective-permute-start | bytes 7864328 | tf_op jit(solution)/shard_map/ppermute | solution.py:40
  406.8 63.6 %collective-permute-start.17 = (bf16[1,2,2,2,128,1280]{5,4,3,2,1,0:T(8,128)(2,1)}, bf16[1,2,2,2,128,1280]{5,4,3,2,1,0:T(8,128)(2,1)S(1)}, u32[]{:S(2)}, u32[]{:S(2)}) collective-permute-start(bf16[1,2,2,2,128,1280]{5,4,3,2,1,0:T(8,128)(2,1)} %get-tuple-element.147.refs_9_), channel_id=1, source_target_pairs={{0,1},{1,0},{2,3},{3,2},{4,5},{5,4},{6,7},{7,6},{8,9},{9,8},{10,11... | collective-permute-start | bytes 7864328 | tf_op jit(solution)/shard_map/ppermute | solution.py:40
  442.5 51.0 %collective-permute-start.19 = (bf16[2,2,2,1,128,768]{5,4,3,2,1,0:T(8,128)(2,1)}, bf16[2,2,2,1,128,768]{5,4,3,2,1,0:T(8,128)(2,1)}, u32[]{:S(2)}, u32[]{:S(2)}) collective-permute-start(bf16[2,2,2,1,128,768]{5,4,3,2,1,0:T(8,128)(2,1)} %get-tuple-element.152.refs_6_), channel_id=1, source_target_pairs={{0,4},{1,5},{2,6},{3,7},{4,0},{5,1},{6,2},{7,3},{8,12},{9,13},{10,... | collective-permute-start | bytes 4718600 | tf_op jit(solution)/shard_map/ppermute | solution.py:40
  475.8 44.0 %collective-permute-start.21 = (bf16[1,2,2,1,128,1280]{5,4,3,2,1,0:T(8,128)(2,1)}, bf16[1,2,2,1,128,1280]{5,4,3,2,1,0:T(8,128)(2,1)S(1)}, u32[]{:S(2)}, u32[]{:S(2)}) collective-permute-start(bf16[1,2,2,1,128,1280]{5,4,3,2,1,0:T(8,128)(2,1)} %get-tuple-element.157.refs_11_), channel_id=1, source_target_pairs={{0,4},{1,5},{2,6},{3,7},{4,0},{5,1},{6,2},{7,3},{8,12},{9,13},{10,... | collective-permute-start | bytes 3932168 | tf_op jit(solution)/shard_map/ppermute | solution.py:40
  493.4 46.4 %collective-permute-start.18 = (bf16[640,1024]{1,0:T(8,128)(2,1)}, bf16[640,1024]{1,0:T(8,128)(2,1)}, u32[]{:S(2)}, u32[]{:S(2)}) collective-permute-start(bf16[640,1024]{1,0:T(8,128)(2,1)} %get-tuple-element.158.rest_0_.yo.refs_2_), channel_id=1, source_target_pairs={{0,2},{1,3},{2,0},{3,1},{4,6},{5,7},{6,4},{7,5},{8,10},{9,11},{10,... | collective-permute-start | bytes 3932168 | tf_op jit(solution)/shard_map/ppermute | solution.py:40
  496.6 38.7 %collective-permute-start.20 = (bf16[2,2,1,1,128,768]{5,4,3,2,1,0:T(8,128)(2,1)}, bf16[2,2,1,1,128,768]{5,4,3,2,1,0:T(8,128)(2,1)S(1)}, u32[]{:S(2)}, u32[]{:S(2)}) collective-permute-start(bf16[2,2,1,1,128,768]{5,4,3,2,1,0:T(8,128)(2,1)} %get-tuple-element.163.rest_1_), channel_id=1, source_target_pairs={{0,8},{1,9},{2,10},{3,11},{4,12},{5,13},{6,14},{7,15},{8,0},{9,1},... | collective-permute-start | bytes 2359304 | tf_op jit(solution)/shard_map/ppermute | solution.py:40
  519.6 44.2 %collective-permute-start.23 = (bf16[128,1024]{1,0:T(8,128)(2,1)S(1)}, bf16[128,1024]{1,0:T(8,128)(2,1)S(1)}, u32[]{:S(2)}, u32[]{:S(2)}) collective-permute-start(bf16[128,1024]{1,0:T(8,128)(2,1)S(1)} %get-tuple-element.169.refs_8_), channel_id=1, source_target_pairs={{0,2},{1,3},{2,0},{3,1},{4,6},{5,7},{6,4},{7,5},{8,10},{9,11},{10,... | collective-permute-start | bytes 786440 | tf_op jit(solution)/shard_map/ppermute | solution.py:40
  523.5 70.5 %collective-permute-start.25 = (bf16[1,2,1,1,128,1280]{5,4,3,2,1,0:T(8,128)(2,1)}, bf16[1,2,1,1,128,1280]{5,4,3,2,1,0:T(8,128)(2,1)}, u32[]{:S(2)}, u32[]{:S(2)}) collective-permute-start(bf16[1,2,1,1,128,1280]{5,4,3,2,1,0:T(8,128)(2,1)} %get-tuple-element.168.refs_7_), channel_id=1, source_target_pairs={{0,8},{1,9},{2,10},{3,11},{4,12},{5,13},{6,14},{7,15},{8,0},{9,1},... | collective-permute-start | bytes 1966088 | tf_op jit(solution)/shard_map/ppermute | solution.py:40
  538.4 55.7 %collective-permute-start.24 = (bf16[1,2,1,1,128,768]{5,4,3,2,1,0:T(8,128)(2,1)}, bf16[1,2,1,1,128,768]{5,4,3,2,1,0:T(8,128)(2,1)S(1)}, u32[]{:S(2)}, u32[]{:S(2)}) collective-permute-start(bf16[1,2,1,1,128,768]{5,4,3,2,1,0:T(8,128)(2,1)} %get-tuple-element.166.refs_6_), channel_id=1, source_target_pairs={{0,1},{1,0},{2,3},{3,2},{4,5},{5,4},{6,7},{7,6},{8,9},{9,8},{10,11... | collective-permute-start | bytes 1179656 | tf_op jit(solution)/shard_map/ppermute | solution.py:40
  563.4 63.1 %collective-permute-start.27 = (bf16[1,2,2,2,128,1280]{5,4,3,2,1,0:T(8,128)(2,1)}, bf16[1,2,2,2,128,1280]{5,4,3,2,1,0:T(8,128)(2,1)}, u32[]{:S(2)}, u32[]{:S(2)}) collective-permute-start(bf16[1,2,2,2,128,1280]{5,4,3,2,1,0:T(8,128)(2,1)} %get-tuple-element.176.refs_2_.refs_9_), channel_id=1, source_target_pairs={{0,1},{1,0},{2,3},{3,2},{4,5},{5,4},{6,7},{7,6},{8,9},{9,8},{10,11... | collective-permute-start | bytes 7864328 | tf_op jit(solution)/shard_map/ppermute | solution.py:40
  567.0 123.9 %collective-permute-start.43 = (bf16[256,1024]{1,0:T(8,128)(2,1)}, bf16[256,1024]{1,0:T(8,128)(2,1)}, u32[]{:S(2)}, u32[]{:S(2)}) collective-permute-start(bf16[256,1024]{1,0:T(8,128)(2,1)} %shard_map.290.refs_10_.refs_0_), channel_id=1, source_target_pairs={{0,1},{1,0},{2,3},{3,2},{4,5},{5,4},{6,7},{7,6},{8,9},{9,8},{10,11... | collective-permute-start | bytes 1572872 | tf_op jit(solution)/shard_map/ppermute | solution.py:40
  598.9 25.7 %collective-permute-start.28 = (bf16[128,2048]{1,0:T(8,128)(2,1)S(1)}, bf16[128,2048]{1,0:T(8,128)(2,1)S(1)}, u32[]{:S(2)}, u32[]{:S(2)}) collective-permute-start(bf16[128,2048]{1,0:T(8,128)(2,1)S(1)} %get-tuple-element.181.rest_1_), channel_id=1, source_target_pairs={{0,16},{1,17},{2,18},{3,19},{4,20},{5,21},{6,22},{7,23},{8,24},{9,... | collective-permute-start | bytes 1572872 | tf_op jit(solution)/shard_map/ppermute | solution.py:40
  611.9 30.2 %collective-permute-start.31 = (bf16[2,2,1,2,128,384]{5,4,3,2,1,0:T(8,128)(2,1)}, bf16[2,2,1,2,128,384]{5,4,3,2,1,0:T(8,128)(2,1)S(1)}, u32[]{:S(2)}, u32[]{:S(2)}) collective-permute-start(bf16[2,2,1,2,128,384]{5,4,3,2,1,0:T(8,128)(2,1)} %get-tuple-element.183.rest_0_), channel_id=1, source_target_pairs={{0,8},{1,9},{2,10},{3,11},{4,12},{5,13},{6,14},{7,15},{8,0},{9,1},... | collective-permute-start | bytes 2359304 | tf_op jit(solution)/shard_map/ppermute | solution.py:40
  622.6 28.9 %collective-permute-start.30 = (bf16[1,2,2,2,128,384]{5,4,3,2,1,0:T(8,128)(2,1)}, bf16[1,2,2,2,128,384]{5,4,3,2,1,0:T(8,128)(2,1)S(1)}, u32[]{:S(2)}, u32[]{:S(2)}) collective-permute-start(bf16[1,2,2,2,128,384]{5,4,3,2,1,0:T(8,128)(2,1)} %get-tuple-element.184.rest_0_.refs_2_.refs_6_), channel_id=1, source_target_pairs={{0,1},{1,0},{2,3},{3,2},{4,5},{5,4},{6,7},{7,6},{8,9},{9,8},{10,11... | collective-permute-start | bytes 2359304 | tf_op jit(solution)/shard_map/ppermute | solution.py:40
  630.4 32.0 %collective-permute-start.35 = (bf16[1,2,2,1,128,1280]{5,4,3,2,1,0:T(8,128)(2,1)}, bf16[1,2,2,1,128,1280]{5,4,3,2,1,0:T(8,128)(2,1)}, u32[]{:S(2)}, u32[]{:S(2)}) collective-permute-start(bf16[1,2,2,1,128,1280]{5,4,3,2,1,0:T(8,128)(2,1)} %get-tuple-element.186.refs_8_), channel_id=1, source_target_pairs={{0,4},{1,5},{2,6},{3,7},{4,0},{5,1},{6,2},{7,3},{8,12},{9,13},{10,... | collective-permute-start | bytes 3932168 | tf_op jit(solution)/shard_map/ppermute | solution.py:40
  683.6 25.1 %collective-permute-start.42 = (bf16[128,2048]{1,0:T(8,128)(2,1)S(1)}, bf16[128,2048]{1,0:T(8,128)(2,1)S(1)}, u32[]{:S(2)}, u32[]{:S(2)}) collective-permute-start(bf16[128,2048]{1,0:T(8,128)(2,1)S(1)} %get-tuple-element.214.refs_2_), channel_id=1, source_target_pairs={{0,16},{1,17},{2,18},{3,19},{4,20},{5,21},{6,22},{7,23},{8,24},{9,... | collective-permute-start | bytes 1572872 | tf_op jit(solution)/shard_map/ppermute | solution.py:40
  688.4 22.7 %collective-permute-start.41 = (f32[2,16,768]{2,1,0:T(8,128)S(1)}, f32[2,16,768]{2,1,0:T(8,128)S(1)}, u32[]{:S(2)}, u32[]{:S(2)}) collective-permute-start(f32[2,16,768]{2,1,0:T(8,128)S(1)} %shard_map.309.refs_4_.refs_0_), channel_id=1, source_target_pairs={{0,8},{1,9},{2,10},{3,11},{4,12},{5,13},{6,14},{7,15},{8,0},{9,1},... | collective-permute-start | bytes 294920 | tf_op jit(solution)/shard_map/ppermute | solution.py:40
  (110 other events, 898.0 us)
Sparse Core Ops, SparseCore 0:
  12.9 112.7 all-gather.4
  127.9 108.8 all-gather.2
  326.3 86.9 reduce-scatter.2
  470.5 108.4 reduce-scatter.4

commit v8 on v6

--- a/solution.py
+++ b/solution.py
@@ -325,12 +325,12 @@
     add_sums(outs[3], [gain, shift, jnp.sum(low.astype(F32), axis=0, keepdims=True)])
 
 
-def weight_grad(plan, where, xs, ys, groups, first, sums=False, extra=0, relative=False, window=(0, 1), after=()):
+def weight_grad(plan, where, xs, ys, groups, first, sums=False, extra=0, relative=False, after=()):
     depth, n_x = xs[0].shape
     cols = ys[0].shape[1]
     ny, chips, bits = plan.ny, plan.chips, plan.bits
     half = cols // ny
-    size = half // window[1]
+    size = half
     chunk = size if size <= 768 else 512
     steps = size // chunk
     rows = n_x // chips
@@ -390,7 +390,7 @@
 
     def column(i, w):
         own = w[2] if ny == 2 and not relative else 0
-        return jnp.bitwise_xor(i // steps, own) * per_rep + window[0] * steps + i % steps
+        return jnp.bitwise_xor(i // steps, own) * per_rep + i % steps
 
     zeros = (0,) * (bits + 1)
     x_spec = pl.BlockSpec((depth, n_x), lambda i, w: (0, 0), pipeline_mode=ONCE)
@@ -424,6 +424,86 @@
     )(where, *xs, *ys, *after)
 
 
+def parted_grad(plan, where, xs, ys, firsts, after=()):
+    depth, n_x = xs[0].shape
+    cols = ys[0].shape[1]
+    ny, chips, bits = plan.ny, plan.chips, plan.bits
+    parts = len(firsts)
+    chunk = cols // ny // parts
+    rows = n_x // chips
+    n_after = len(after)
+
+    def kernel(where_ref, xo, xt, yo, yt, *rest):
+        outs, sums, flip, acc = rest[n_after:-3], rest[-3], rest[-2], rest[-1]
+        step = pl.program_id(0)
+
+        @pl.when(step == 0)
+        def _():
+            flip[:, :depth] = xo[...].T
+            flip[:, depth:] = xt[...].T
+
+        acc[...] = dot(flip[:, :depth], yo[...]) + dot(flip[:, depth:], yt[...])
+        total = jnp.sum(yo[...].astype(F32), axis=0, keepdims=True)
+        sums[...] = total + jnp.sum(yt[...].astype(F32), axis=0, keepdims=True)
+
+        def put(ref, r, first):
+            at = [0]
+            for k in range(1, bits + 1):
+                at.append((r >> (bits - k)) & 1 if k != first else 0)
+            start = pl.multiple_of(jnp.bitwise_xor(where_ref[1], r) * rows, 16)
+            ref[tuple(at)] = acc[pl.ds(start, rows)].astype(BF)
+
+        for p, first in enumerate(firsts):
+            keep, send = outs[2 * p], outs[2 * p + 1]
+            if first:
+
+                @pl.when(step % parts == p)
+                def _(keep=keep, send=send, first=first):
+                    for r in range(chips):
+                        put(send if (r >> (bits - first)) & 1 else keep, r, first)
+            else:
+
+                @pl.when(step == p)
+                def _(keep=keep, first=first):
+                    for r in range(chips):
+                        put(keep, r, first)
+
+                @pl.when(step == parts + p)
+                def _(send=send, first=first):
+                    for r in range(chips):
+                        put(send, r, first)
+
+    def column(i, w):
+        own = w[2] if ny == 2 else 0
+        return jnp.bitwise_xor(i // parts, own) * parts + i % parts
+
+    zeros = (0,) * (bits + 2)
+    x_spec = pl.BlockSpec((depth, n_x), lambda i, w: (0, 0), pipeline_mode=ONCE)
+    y_spec = pl.BlockSpec((depth, chunk), lambda i, w: (0, column(i, w)))
+    specs, shapes = [], []
+    for first in firsts:
+        dims = [ny] + [2] * bits
+        dims[first] = 1
+        block = [1] + dims[1:] + [rows, chunk]
+        index = (lambda i, w: (i // parts,) + zeros) if first else (lambda i, w: (0,) + zeros)
+        specs += [pl.BlockSpec(block, index)] * 2
+        shapes += [jax.ShapeDtypeStruct(dims + [rows, chunk], BF)] * 2
+    res = pl.pallas_call(
+        kernel,
+        grid_spec=pltpu.PrefetchScalarGridSpec(
+            num_scalar_prefetch=1,
+            grid=(ny * parts,),
+            in_specs=[x_spec, x_spec, y_spec, y_spec] + [ANY] * n_after,
+            out_specs=specs + [pl.BlockSpec((1, chunk), lambda i, w: (0, column(i, w)))],
+            scratch_shapes=[pltpu.VMEM((n_x, 2 * depth), BF), pltpu.VMEM((n_x, chunk), F32)],
+        ),
+        out_shape=shapes + [jax.ShapeDtypeStruct((1, cols), F32)],
+        compiler_params=pltpu.CompilerParams(vmem_limit_bytes=LIMIT),
+        cost_estimate=BACKWARD,
+    )(where, *xs, *ys, *after)
+    return [res[2 * p : 2 * p + 2] for p in range(parts)], res[-1]
+
+
 def chip_grad(plan, where, xs, ys, groups, after=()):
     depth, n_x = xs[0].shape
     cols = ys[0].shape[1]
@@ -562,7 +642,7 @@
         in_specs=[pl.BlockSpec(block, index)] * 2 + [ANY] * len(after),
         out_specs=[pl.BlockSpec(out_block, index)] * 2,
         out_shape=[jax.ShapeDtypeStruct(out, BF)] * 2,
-        compiler_params=pltpu.CompilerParams(vmem_limit_bytes=SMALL_LIMIT),
+        compiler_params=pltpu.CompilerParams(vmem_limit_bytes=LIMIT),
         cost_estimate=BACKWARD,
     )(keep, got, *after)
 
@@ -1074,17 +1154,12 @@
             low_oth = plan.core(low_own)
         if not top:
             prev += end_rest(layer + 1, prev[:1])
-            prev += (ends["f2", layer].core(prev[:1]),)
-        terms["q", layer], q_sums = [], []
-        of = len(orders_q[layer])
-        for k, order in enumerate(orders_q[layer]):
-            resq = weight_grad(
-                plan, where, s["first"], (dproj_own, dproj_oth), 1, order[0], sums=True, window=(k, of), after=prev
-            )
-            terms["q", layer].append(Term(plan, *resq[:2], order))
-            q_sums.append(resq[2].reshape(plan.ny, -1))
-            prev = (resq[1],) + (() if top else (ends["f2", layer].came,))
-        q = jnp.concatenate(q_sums, axis=1).reshape(3, half_heads, 1, HEAD_DIM)
+        pairs, q_sums = parted_grad(
+            plan, where, s["first"], (dproj_own, dproj_oth), [order[0] for order in orders_q[layer]], prev
+        )
+        terms["q", layer] = [Term(plan, *pair, order) for pair, order in zip(pairs, orders_q[layer])]
+        prev = (pairs[0][1],)
+        q = q_sums.reshape(3, half_heads, 1, HEAD_DIM)
         q = jnp.concatenate([q[:1], q[2:]])
         none = jnp.zeros_like(q)
         q = jnp.concatenate([pick(c, q, none), pick(c, none, q)], axis=2)
@@ -1113,18 +1188,19 @@
         got_vec = plan.flip(vec, vec_axes.pop(0)) if vec_axes else None
         return (vec,)
 
-    prev += (terms["f1", 0].step(prev[:1]),)
-    prev += (ends["rest", 1].core(prev[:1]),)
+    prev += (terms["f1", 0].step(prev),)
     w = layers - 1
     mixed = call(
         down_last, w, 1, ["fc2"], [saved[w]["hid"][0], last_part, saved[w]["middle"]], [vecs[w]["f2b"]], [low_rows], prev
     )[0]
     qa, qb = terms["q", 0]
-    prev = (qa.step((mixed, ends["rest", 1].came)),)
-    prev = (qb.step(prev),)
+    prev = (ends["rest", 1].core((mixed,)),)
+    prev = (qa.step(prev),)
+    prev = (qb.step(prev + (ends["rest", 1].came,)),)
     prev = step_vec(prev)
     prev = (qa.step(prev),)
     prev = (terms["f1", 0].step(prev),)
+    prev = (ends["f2", 0].core(prev),)
     prev = (qb.step(prev),)
     prev = step_vec(prev)
     prev = end_rest(0, prev)

time: 727 us -> 735 us (1.011)
  Pallas kernels: 403 us -> 416 us
  local copies, waits for them, and re-layouts: 75.9 us -> 63.8 us
  waiting for transfers between devices: 182 us -> 192 us
    pallas_call x5 -> x2, Pallas kernels: 53.6 us -> 26.3 us  [weight_grad(): pl.pallas_call(kernel, grid_spec=pltpu.PrefetchScalarGridSpec(num_scalar_...]
    pallas_call x0 -> x2, Pallas kernels: none -> 23.2 us  [parted_grad(): pl.pallas_call(kernel, grid_spec=pltpu.PrefetchScalarGridSpec(num_scalar_...]
    pallas_call x10, Pallas kernels: 11.3 us -> 26.8 us  [combine(): pl.pallas_call(kernel, grid=(cuts,), in_specs=[pl.BlockSpec(block, index)...]
    unnamed x176 -> x149, local copies, waits for them, and re-layouts: 43.7 us -> 32 us
    ppermute x49, waiting for transfers between devices: 68.6 us -> 77.9 us  [swap(): return lax.ppermute(v, AX, pairs)]
  transfers between devices with their start and end apart: 53 -> 53, of which waited for: 16 -> 18; matrix products, arithmetic and copies ran while one was open for 6% -> 6% of each run, Pallas kernels for 50% -> 52%
where the time goes in v8:
time: 735 us; the launch traced here: 730 us
  Pallas kernels  416 us (57%)
  waiting for transfers between devices  192 us (26%)
  local copies, waits for them, and re-layouts  63.8 us (9%)
  starting transfers between devices  32.9 us (4%)
  between operations  15 us (2%)
  other arithmetic  10.5 us (1%)
    pallas_call x24, Pallas kernels, row_call(): pl.pallas_call(kernel, grid_spec=pltpu.PrefetchScalarGridSpec(num_scalar_...  275 us
    all_gather x2, waiting for transfers between devices, per_device(): gathered.append(lax.all_gather(done[0], 'shard', axis=0, tiled=True))  114 us
    ppermute x49, waiting for transfers between devices, swap(): return lax.ppermute(v, AX, pairs)  77.9 us
    ppermute x49, starting transfers between devices, swap(): return lax.ppermute(v, AX, pairs)  32.8 us
    unnamed x149, local copies, waits for them, and re-layouts  32 us
    pallas_call x10, Pallas kernels, combine(): pl.pallas_call(kernel, grid=(cuts,), in_specs=[pl.BlockSpec(block, index)...  26.8 us
    pallas_call x2, Pallas kernels, chip_grad(): pl.pallas_call(kernel, grid_spec=pltpu.PrefetchScalarGridSpec(num_scalar_...  26.6 us
    pallas_call x2, Pallas kernels, weight_grad(): pl.pallas_call(kernel, grid_spec=pltpu.PrefetchScalarGridSpec(num_scalar_...  26.3 us
  transfers between devices with their start and end apart: 53, of which 18 were waited for; matrix products, arithmetic and copies ran while one was open for 6% of the time, Pallas kernels for 52%

profile of v8, /device:TPU:0, one launch (start us, length us, event | category | flops | bytes accessed | tf_op | source)
XLA Modules:
  0.0 729.9 jit_solution(15944889477291766079)
XLA Ops:
  17.5 108.3 %all-gather.5.cloned.1.call-done.refs_0_.refs_1_.refs_2_.refs_3_ = bf16[1024,10368]{1,0:T(8,128)(2,1)} async-done(((bf16[64,10368]{1,0:T(8,128)(2,1)}), bf16[1024,10368]{1,0:T(8,128)(2,1)}) %all-gather.5.cloned.1.call-update) | async-done | bytes 21233680 | tf_op jit(solution)/shard_map/all_gather | solution.py:948
  140.4 12.0 %shard_map.258 = (bf16[2,8,320,320]{3,2,1,0:T(8,128)(2,1)}, bf16[640,512]{1,0:T(8,128)(2,1)}, f32[640,1024]{1,0:T(8,128)}) custom-call(s32[4]{0:T(128)} %pad_add_fusion.where_ref, s32[2]{0:T(128)} %copy-done.55, bf16[8,2,64,10368]{3,2,1,0:T(8,128)(2,1)} %bitcast.50, bf16[640,1536]{1,0:T(8,128)(2,1)} %shard_map.257.refs_1_.refs_3_), custom_call_target="tpu_custom_call" | custom-call | flops 10000000 | tf_op jit(solution)/shard_map/pallas_call | solution.py:123
  164.2 13.6 %shard_map.259 = (bf16[2,8,320,320]{3,2,1,0:T(8,128)(2,1)}, bf16[640,512]{1,0:T(8,128)(2,1)}, f32[640,1024]{1,0:T(8,128)}, bf16[640,1024]{1,0:T(8,128)(2,1)}) custom-call(s32[4]{0:T(128)} %pad_add_fusion.where_ref, s32[2]{0:T(128)} %kept_ref.23, bf16[8,2,64,10368]{3,2,1,0:T(8,128)(2,1)} %bitcast.51, bf16[640,1536]{1,0:T(8,128)(2,1)} %shard_map.256.refs_1_.refs_3_, ...), custom_call_target="tpu_custom_call" | custom-call | flops 10000000 | tf_op jit(solution)/shard_map/pallas_call | solution.py:123
  210.6 9.7 %shard_map.260 = (bf16[640,2048]{1,0:T(8,128)(2,1)}, bf16[640,2048]{1,0:T(8,128)(2,1)}) custom-call(s32[4]{0:T(128)} %pad_add_fusion.where_ref, s32[2]{0:T(128)} %kept_ref.23, bf16[1024,10368]{1,0:T(8,128)(2,1)} %all-gather.5.cloned.1.call-done.refs_0_.refs_1_.refs_2_.refs_3_, ...), custom_call_target="tpu_custom_call" | custom-call | flops 10000000 | tf_op jit(solution)/shard_map/pallas_call | solution.py:123
  247.7 11.9 %shard_map.266 = (bf16[2,8,320,320]{3,2,1,0:T(8,128)(2,1)}, bf16[640,512]{1,0:T(8,128)(2,1)}, f32[640,1024]{1,0:T(8,128)}) custom-call(s32[4]{0:T(128)} %pad_add_fusion.where_ref, s32[2]{0:T(128)} %copy-done.55, bf16[8,2,64,10240]{3,2,1,0:T(8,128)(2,1)} %bitcast.54, bf16[640,1536]{1,0:T(8,128)(2,1)} %shard_map.265.refs_1_.refs_3_), custom_call_target="tpu_custom_call" | custom-call | flops 10000000 | tf_op jit(solution)/shard_map/pallas_call | solution.py:123
  271.5 13.6 %shard_map.267 = (bf16[2,8,320,320]{3,2,1,0:T(8,128)(2,1)}, bf16[640,512]{1,0:T(8,128)(2,1)}, f32[640,1024]{1,0:T(8,128)}, bf16[640,1024]{1,0:T(8,128)(2,1)}) custom-call(s32[4]{0:T(128)} %pad_add_fusion.where_ref, s32[2]{0:T(128)} %kept_ref.23, bf16[8,2,64,10240]{3,2,1,0:T(8,128)(2,1)} %bitcast.55, bf16[640,1536]{1,0:T(8,128)(2,1)} %shard_map.264.refs_1_.refs_3_, ...), custom_call_target="tpu_custom_call" | custom-call | flops 10000000 | tf_op jit(solution)/shard_map/pallas_call | solution.py:123
  310.3 13.3 %shard_map.270.refs_6_ = bf16[2048,1024]{1,0:T(8,128)(2,1)} custom-call(s32[4]{0:T(128)} %pad_add_fusion.where_ref, bf16[640,2048]{1,0:T(8,128)(2,1)} %get-tuple-element.128.xo.rest_0_.refs_2_, bf16[640,2048]{1,0:T(8,128)(2,1)} %get-tuple-element.129.xt.refs_2_, bf16[640,1024]{1,0:T(8,128)(2,1)} %bitcast_convert_fusion.yo.refs_4_, ...), custom_call_target="tpu_custom_call" | custom-call | flops 30000001024 | tf_op jit(solution)/shard_map/pallas_call | solution.py:534
  323.7 11.9 %shard_map.271 = (bf16[640,2048]{1,0:T(8,128)(2,1)}, f32[640,1024]{1,0:T(8,128)}) custom-call(s32[4]{0:T(128)} %pad_add_fusion.where_ref, s32[2]{0:T(128)} %copy-done.55, bf16[1024,10240]{1,0:T(8,128)(2,1)} %all-gather.3.cloned.1.call-done.refs_0_.refs_1_.refs_2_.refs_3_, bf16[1024,1024]{1,0:T(8,128)(2,1)} %collective-permute-done.rest_1_.refs_1_, ...), custom_call_target="tpu_custom_call" | custom-call | flops 30000001024 | tf_op jit(solution)/shard_map/pallas_call | solution.py:123
  343.7 16.1 %shard_map.273 = (bf16[640,2048]{1,0:T(8,128)(2,1)}, f32[640,1024]{1,0:T(8,128)}, bf16[640,1024]{1,0:T(8,128)(2,1)}, f32[8,1024]{1,0:T(8,128)}) custom-call(s32[4]{0:T(128)} %pad_add_fusion.where_ref, s32[2]{0:T(128)} %kept_ref.23, bf16[1024,10240]{1,0:T(8,128)(2,1)} %all-gather.3.cloned.1.call-done.refs_0_.refs_1_.refs_2_.refs_3_, ...), custom_call_target="tpu_custom_call" | custom-call | flops 30000001024 | tf_op jit(solution)/shard_map/pallas_call | solution.py:123
  359.9 13.1 %shard_map.274 = (bf16[1,2,2,2,128,1280]{5,4,3,2,1,0:T(8,128)(2,1)}, bf16[1,2,2,2,128,1280]{5,4,3,2,1,0:T(8,128)(2,1)}, f32[1,2048]{1,0:T(1,128)}) custom-call(s32[4]{0:T(128)} %pad_add_fusion.where_ref, bf16[640,1024]{1,0:T(8,128)(2,1)} %get-tuple-element.127.refs_2_.xo, bf16[640,1024]{1,0:T(8,128)(2,1)} %collective-permute-done.9.refs_2_.xt, ...), custom_call_target="tpu_custom_call" | custom-call | flops 30000001024 | tf_op jit(solution)/shard_map/pallas_call | solution.py:412
  378.0 16.5 %shard_map.275 = (bf16[640,1536]{1,0:T(8,128)(2,1)}, f32[640,1024]{1,0:T(8,128)}) custom-call(s32[4]{0:T(128)} %pad_add_fusion.where_ref, s32[2]{0:T(128)} %copy-done.55, bf16[8,2,64,10240]{3,2,1,0:T(8,128)(2,1)} %bitcast.56, bf16[1024,10240]{1,0:T(8,128)(2,1)} %all-gather.3.cloned.1.call-done.refs_0_.refs_1_.refs_2_.refs_3_, ...), custom_call_target="tpu_custom_call" | custom-call | flops 30000001024 | tf_op jit(solution)/shard_map/pallas_call | solution.py:123
  401.0 19.2 %shard_map.277 = (bf16[640,1536]{1,0:T(8,128)(2,1)}, f32[640,1024]{1,0:T(8,128)}, bf16[640,1024]{1,0:T(8,128)(2,1)}, f32[8,1024]{1,0:T(8,128)}) custom-call(s32[4]{0:T(128)} %pad_add_fusion.where_ref, s32[2]{0:T(128)} %kept_ref.23, bf16[8,2,64,10240]{3,2,1,0:T(8,128)(2,1)} %bitcast.57, ...), custom_call_target="tpu_custom_call" | custom-call | flops 30000001024 | tf_op jit(solution)/shard_map/pallas_call | solution.py:123
  420.3 10.8 %shard_map.278 = (bf16[2,2,2,1,128,768]{5,4,3,2,1,0:T(8,128)(2,1)}, bf16[2,2,2,1,128,768]{5,4,3,2,1,0:T(8,128)(2,1)}, f32[1,1536]{1,0:T(1,128)}) custom-call(s32[4]{0:T(128)} %pad_add_fusion.where_ref, bf16[640,1024]{1,0:T(8,128)(2,1)} %get-tuple-element.124.refs_1_.xo, bf16[640,1024]{1,0:T(8,128)(2,1)} %copy-done.39, ...), custom_call_target="tpu_custom_call" | custom-call | flops 30000001024 | tf_op jit(solution)/shard_map/pallas_call | solution.py:491
  435.8 11.9 %shard_map.279 = (bf16[640,2048]{1,0:T(8,128)(2,1)}, f32[640,1024]{1,0:T(8,128)}) custom-call(s32[4]{0:T(128)} %pad_add_fusion.where_ref, s32[2]{0:T(128)} %copy-done.55, bf16[1024,10368]{1,0:T(8,128)(2,1)} %all-gather.5.cloned.1.call-done.refs_0_.refs_1_.refs_2_.refs_3_, bf16[1024,1024]{1,0:T(8,128)(2,1)} %collective-permute-done.1.refs_1_, ...), custom_call_target="tpu_custom_call" | custom-call | flops 30000001024 | tf_op jit(solution)/shard_map/pallas_call | solution.py:123
  447.9 13.3 %shard_map.280.rest_0_.refs_10_ = bf16[2048,1024]{1,0:T(8,128)(2,1)} custom-call(s32[4]{0:T(128)} %pad_add_fusion.where_ref, bf16[640,2048]{1,0:T(8,128)(2,1)} %get-tuple-element.121.refs_2_.xo, bf16[640,2048]{1,0:T(8,128)(2,1)} %get-tuple-element.122.refs_2_.xt, bf16[640,1024]{1,0:T(8,128)(2,1)} %get-tuple-element.147.yo.refs_4_, ...), custom_call_target="tpu_custom_call" | custom-call | flops 30000001024 | tf_op jit(solution)/shard_map/pallas_call | solution.py:534
  467.3 15.4 %shard_map.282 = (bf16[640,2048]{1,0:T(8,128)(2,1)}, f32[640,1024]{1,0:T(8,128)}, bf16[640,1024]{1,0:T(8,128)(2,1)}, f32[8,1024]{1,0:T(8,128)}) custom-call(s32[4]{0:T(128)} %pad_add_fusion.where_ref, s32[2]{0:T(128)} %kept_ref.23, bf16[1024,10368]{1,0:T(8,128)(2,1)} %all-gather.5.cloned.1.call-done.refs_0_.refs_1_.refs_2_.refs_3_, ...), custom_call_target="tpu_custom_call" | custom-call | flops 30000001024 | tf_op jit(solution)/shard_map/pallas_call | solution.py:123
  487.5 13.2 %shard_map.284 = (bf16[1,2,2,2,128,1280]{5,4,3,2,1,0:T(8,128)(2,1)}, bf16[1,2,2,2,128,1280]{5,4,3,2,1,0:T(8,128)(2,1)}, f32[1,2048]{1,0:T(1,128)}) custom-call(s32[4]{0:T(128)} %pad_add_fusion.where_ref, bf16[640,1024]{1,0:T(8,128)(2,1)} %get-tuple-element.120.refs_2_.xo, bf16[640,1024]{1,0:T(8,128)(2,1)} %copy-done.40, ...), custom_call_target="tpu_custom_call" | custom-call | flops 30000001024 | tf_op jit(solution)/shard_map/pallas_call | solution.py:412
  515.6 10.7 %collective-permute-done.20.g = bf16[2,2,1,1,128,768]{5,4,3,2,1,0:T(8,128)(2,1)S(1)} collective-permute-done((bf16[2,2,1,1,128,768]{5,4,3,2,1,0:T(8,128)(2,1)}, bf16[2,2,1,1,128,768]{5,4,3,2,1,0:T(8,128)(2,1)S(1)}, u32[]{:S(2)}, u32[]{:S(2)}) %collective-permute-start.20) | collective-permute-done | bytes 786464 | tf_op jit(solution)/shard_map/ppermute | solution.py:40
  530.8 16.2 %shard_map.288 = (bf16[640,1536]{1,0:T(8,128)(2,1)}, f32[640,1024]{1,0:T(8,128)}) custom-call(s32[4]{0:T(128)} %pad_add_fusion.where_ref, s32[2]{0:T(128)} %copy-done.55, bf16[8,2,64,10368]{3,2,1,0:T(8,128)(2,1)} %bitcast.52, bf16[1024,10368]{1,0:T(8,128)(2,1)} %all-gather.5.cloned.1.call-done.refs_0_.refs_1_.refs_2_.refs_3_, ...), custom_call_target="tpu_custom_call" | custom-call | flops 30000001024 | tf_op jit(solution)/shard_map/pallas_call | solution.py:123
  560.3 19.3 %shard_map.291 = (bf16[640,1536]{1,0:T(8,128)(2,1)}, f32[640,1024]{1,0:T(8,128)}, bf16[640,1024]{1,0:T(8,128)(2,1)}, f32[8,1024]{1,0:T(8,128)}) custom-call(s32[4]{0:T(128)} %pad_add_fusion.where_ref, s32[2]{0:T(128)} %kept_ref.23, bf16[8,2,64,10368]{3,2,1,0:T(8,128)(2,1)} %bitcast.53, ...), custom_call_target="tpu_custom_call" | custom-call | flops 30000001024 | tf_op jit(solution)/shard_map/pallas_call | solution.py:123
  583.3 12.4 %shard_map.293 = (bf16[2,2,1,2,128,384]{5,4,3,2,1,0:T(8,128)(2,1)}, bf16[2,2,1,2,128,384]{5,4,3,2,1,0:T(8,128)(2,1)}, bf16[1,2,2,2,128,384]{5,4,3,2,1,0:T(8,128)...) custom-call(s32[4]{0:T(128)} %pad_add_fusion.where_ref, bf16[640,1024]{1,0:T(8,128)(2,1)} %copy-done.37, ...), custom_call_target="tpu_custom_call" | custom-call | flops 30000001024 | tf_op jit(solution)/shard_map/pallas_call | solution.py:491
  600.4 12.8 %collective-permute-done.26.g = bf16[1,2,2,2,128,1280]{5,4,3,2,1,0:T(8,128)(2,1)} collective-permute-done((bf16[1,2,2,2,128,1280]{5,4,3,2,1,0:T(8,128)(2,1)}, bf16[1,2,2,2,128,1280]{5,4,3,2,1,0:T(8,128)(2,1)}, u32[]{:S(2)}, u32[]{:S(2)}) %collective-permute-start.26) | collective-permute-done | bytes 2621472 | tf_op jit(solution)/shard_map/ppermute | solution.py:40
  633.5 13.1 %collective-permute-done.28.g = bf16[1,2,2,2,128,384]{5,4,3,2,1,0:T(8,128)(2,1)} collective-permute-done((bf16[1,2,2,2,128,384]{5,4,3,2,1,0:T(8,128)(2,1)S(1)}, bf16[1,2,2,2,128,384]{5,4,3,2,1,0:T(8,128)(2,1)}, u32[]{:S(2)}, u32[]{:S(2)}) %collective-permute-start.28) | collective-permute-done | bytes 786464 | tf_op jit(solution)/shard_map/ppermute | solution.py:40
  680.4 10.2 %collective-permute-done.44.refs_3_ = bf16[64,4096]{1,0:T(8,128)(2,1)S(1)} collective-permute-done((bf16[64,4096]{1,0:T(8,128)(2,1)S(1)}, bf16[64,4096]{1,0:T(8,128)(2,1)S(1)}, u32[]{:S(2)}, u32[]{:S(2)}) %collective-permute-start.44) | collective-permute-done | bytes 524320 | tf_op jit(solution)/shard_map/ppermute | solution.py:40
  (411 shorter events, 296.3 us)
Async XLA Ops:
  7.2 118.6 %all-gather.5.cloned.1.call-start = ((), (), s32[]{:S(2)}) async-start(), calls=%async_computation.3 | async-start | bytes 22560768 | tf_op jit(solution)/shard_map/all_gather | solution.py:948
  12.8 223.9 %all-gather.3.cloned.1.call-start = ((), (), s32[]{:S(2)}) async-start(), calls=%async_computation.2 | async-start | bytes 22282240 | tf_op jit(solution)/shard_map/all_gather | solution.py:948
  16.5 484.2 %reduce-scatter.3.cloned.1.call-start = ((), (), s32[]{:S(2)}) async-start(), calls=%async_computation.4 | async-start | bytes 4718592 | tf_op jit(solution)/shard_map/reduce_scatter | solution.py:751
  152.6 47.9 %collective-permute-start.1 = (bf16[1024,1024]{1,0:T(8,128)(2,1)S(1)}, bf16[1024,1024]{1,0:T(8,128)(2,1)}, u32[]{:S(2)}, u32[]{:S(2)}) collective-permute-start(bf16[1024,1024]{1,0:T(8,128)(2,1)S(1)} %copy-done.36), channel_id=1, source_target_pairs={{0,1},{1,0},{2,3},{3,2},{4,5},{5,4},{6,7},{7,6},{8,9},{9,8},{10,11... | collective-permute-start | bytes 6291464 | tf_op jit(solution)/shard_map/ppermute | solution.py:40
  260.0 49.3 %collective-permute-start = (bf16[1024,1024]{1,0:T(8,128)(2,1)}, bf16[1024,1024]{1,0:T(8,128)(2,1)}, u32[]{:S(2)}, u32[]{:S(2)}) collective-permute-start(bf16[1024,1024]{1,0:T(8,128)(2,1)} %constant_dynamic-slice_fusion.2.refs_3_), channel_id=1, source_target_pairs={{0,1},{1,0},{2,3},{3,2},{4,5},{5,4},{6,7},{7,6},{8,9},{9,8},{10,11... | collective-permute-start | bytes 6291464 | tf_op jit(solution)/shard_map/ppermute | solution.py:40
  286.4 22.8 %collective-permute-start.10 = (bf16[640,1024]{1,0:T(8,128)(2,1)}, bf16[640,1024]{1,0:T(8,128)(2,1)S(1)}, u32[]{:S(2)}, u32[]{:S(2)}) collective-permute-start(bf16[640,1024]{1,0:T(8,128)(2,1)} %bitcast_convert_fusion.yo.refs_4_), channel_id=1, source_target_pairs={{0,2},{1,3},{2,0},{3,1},{4,6},{5,7},{6,4},{7,5},{8,10},{9,11},{10,... | collective-permute-start | bytes 3932168 | tf_op jit(solution)/shard_map/ppermute | solution.py:40
  323.6 337.4 %reduce-scatter.5.cloned.1.call-start = ((), (), s32[]{:S(2)}) async-start(), calls=%async_computation.5 | async-start | bytes 4718592 | tf_op jit(solution)/shard_map/reduce_scatter | solution.py:751
  343.2 33.3 %collective-permute-start.11 = (f32[640,1024]{1,0:T(8,128)}, f32[640,1024]{1,0:T(8,128)S(1)}, u32[]{:S(2)}, u32[]{:S(2)}) collective-permute-start(f32[640,1024]{1,0:T(8,128)} %shard_map.272.refs_10_), channel_id=1, source_target_pairs={{0,2},{1,3},{2,0},{3,1},{4,6},{5,7},{6,4},{7,5},{8,10},{9,11},{10,... | collective-permute-start | bytes 7864328 | tf_op jit(solution)/shard_map/ppermute | solution.py:40
  400.6 60.6 %collective-permute-start.17 = (bf16[1,2,2,2,128,1280]{5,4,3,2,1,0:T(8,128)(2,1)}, bf16[1,2,2,2,128,1280]{5,4,3,2,1,0:T(8,128)(2,1)S(1)}, u32[]{:S(2)}, u32[]{:S(2)}) collective-permute-start(bf16[1,2,2,2,128,1280]{5,4,3,2,1,0:T(8,128)(2,1)} %get-tuple-element.146.refs_9_), channel_id=1, source_target_pairs={{0,1},{1,0},{2,3},{3,2},{4,5},{5,4},{6,7},{7,6},{8,9},{9,8},{10,11... | collective-permute-start | bytes 7864328 | tf_op jit(solution)/shard_map/ppermute | solution.py:40
  433.9 49.1 %collective-permute-start.19 = (bf16[2,2,2,1,128,768]{5,4,3,2,1,0:T(8,128)(2,1)}, bf16[2,2,2,1,128,768]{5,4,3,2,1,0:T(8,128)(2,1)}, u32[]{:S(2)}, u32[]{:S(2)}) collective-permute-start(bf16[2,2,2,1,128,768]{5,4,3,2,1,0:T(8,128)(2,1)} %get-tuple-element.151.refs_6_), channel_id=1, source_target_pairs={{0,4},{1,5},{2,6},{3,7},{4,0},{5,1},{6,2},{7,3},{8,12},{9,13},{10,... | collective-permute-start | bytes 4718600 | tf_op jit(solution)/shard_map/ppermute | solution.py:40
  466.5 43.8 %collective-permute-start.21 = (bf16[1,2,2,1,128,1280]{5,4,3,2,1,0:T(8,128)(2,1)}, bf16[1,2,2,1,128,1280]{5,4,3,2,1,0:T(8,128)(2,1)S(1)}, u32[]{:S(2)}, u32[]{:S(2)}) collective-permute-start(bf16[1,2,2,1,128,1280]{5,4,3,2,1,0:T(8,128)(2,1)} %get-tuple-element.156.refs_11_), channel_id=1, source_target_pairs={{0,4},{1,5},{2,6},{3,7},{4,0},{5,1},{6,2},{7,3},{8,12},{9,13},{10,... | collective-permute-start | bytes 3932168 | tf_op jit(solution)/shard_map/ppermute | solution.py:40
  482.7 48.1 %collective-permute-start.18 = (bf16[640,1024]{1,0:T(8,128)(2,1)}, bf16[640,1024]{1,0:T(8,128)(2,1)}, u32[]{:S(2)}, u32[]{:S(2)}) collective-permute-start(bf16[640,1024]{1,0:T(8,128)(2,1)} %get-tuple-element.157.rest_0_.yo.refs_2_), channel_id=1, source_target_pairs={{0,2},{1,3},{2,0},{3,1},{4,6},{5,7},{6,4},{7,5},{8,10},{9,11},{10,... | collective-permute-start | bytes 3932168 | tf_op jit(solution)/shard_map/ppermute | solution.py:40
  485.9 40.3 %collective-permute-start.20 = (bf16[2,2,1,1,128,768]{5,4,3,2,1,0:T(8,128)(2,1)}, bf16[2,2,1,1,128,768]{5,4,3,2,1,0:T(8,128)(2,1)S(1)}, u32[]{:S(2)}, u32[]{:S(2)}) collective-permute-start(bf16[2,2,1,1,128,768]{5,4,3,2,1,0:T(8,128)(2,1)} %get-tuple-element.162.rest_1_), channel_id=1, source_target_pairs={{0,8},{1,9},{2,10},{3,11},{4,12},{5,13},{6,14},{7,15},{8,0},{9,1},... | collective-permute-start | bytes 2359304 | tf_op jit(solution)/shard_map/ppermute | solution.py:40
  508.8 44.8 %collective-permute-start.23 = (bf16[128,1024]{1,0:T(8,128)(2,1)S(1)}, bf16[128,1024]{1,0:T(8,128)(2,1)S(1)}, u32[]{:S(2)}, u32[]{:S(2)}) collective-permute-start(bf16[128,1024]{1,0:T(8,128)(2,1)S(1)} %get-tuple-element.168.refs_8_), channel_id=1, source_target_pairs={{0,2},{1,3},{2,0},{3,1},{4,6},{5,7},{6,4},{7,5},{8,10},{9,11},{10,... | collective-permute-start | bytes 786440 | tf_op jit(solution)/shard_map/ppermute | solution.py:40
  514.0 65.6 %collective-permute-start.25 = (bf16[1,2,1,1,128,1280]{5,4,3,2,1,0:T(8,128)(2,1)}, bf16[1,2,1,1,128,1280]{5,4,3,2,1,0:T(8,128)(2,1)}, u32[]{:S(2)}, u32[]{:S(2)}) collective-permute-start(bf16[1,2,1,1,128,1280]{5,4,3,2,1,0:T(8,128)(2,1)} %get-tuple-element.167.refs_7_), channel_id=1, source_target_pairs={{0,8},{1,9},{2,10},{3,11},{4,12},{5,13},{6,14},{7,15},{8,0},{9,1},... | collective-permute-start | bytes 1966088 | tf_op jit(solution)/shard_map/ppermute | solution.py:40
  529.3 50.3 %collective-permute-start.24 = (bf16[1,2,1,1,128,768]{5,4,3,2,1,0:T(8,128)(2,1)}, bf16[1,2,1,1,128,768]{5,4,3,2,1,0:T(8,128)(2,1)S(1)}, u32[]{:S(2)}, u32[]{:S(2)}) collective-permute-start(bf16[1,2,1,1,128,768]{5,4,3,2,1,0:T(8,128)(2,1)} %get-tuple-element.165.refs_6_), channel_id=1, source_target_pairs={{0,1},{1,0},{2,3},{3,2},{4,5},{5,4},{6,7},{7,6},{8,9},{9,8},{10,11... | collective-permute-start | bytes 1179656 | tf_op jit(solution)/shard_map/ppermute | solution.py:40
  553.1 60.1 %collective-permute-start.26 = (bf16[1,2,2,2,128,1280]{5,4,3,2,1,0:T(8,128)(2,1)}, bf16[1,2,2,2,128,1280]{5,4,3,2,1,0:T(8,128)(2,1)}, u32[]{:S(2)}, u32[]{:S(2)}) collective-permute-start(bf16[1,2,2,2,128,1280]{5,4,3,2,1,0:T(8,128)(2,1)} %get-tuple-element.175.refs_2_.refs_9_), channel_id=1, source_target_pairs={{0,1},{1,0},{2,3},{3,2},{4,5},{5,4},{6,7},{7,6},{8,9},{9,8},{10,11... | collective-permute-start | bytes 7864328 | tf_op jit(solution)/shard_map/ppermute | solution.py:40
  556.8 123.6 %collective-permute-start.43 = (bf16[256,1024]{1,0:T(8,128)(2,1)}, bf16[256,1024]{1,0:T(8,128)(2,1)}, u32[]{:S(2)}, u32[]{:S(2)}) collective-permute-start(bf16[256,1024]{1,0:T(8,128)(2,1)} %shard_map.290.refs_10_.refs_0_), channel_id=1, source_target_pairs={{0,1},{1,0},{2,3},{3,2},{4,5},{5,4},{6,7},{7,6},{8,9},{9,8},{10,11... | collective-permute-start | bytes 1572872 | tf_op jit(solution)/shard_map/ppermute | solution.py:40
  582.6 43.4 %collective-permute-start.30 = (bf16[128,2048]{1,0:T(8,128)(2,1)S(1)}, bf16[128,2048]{1,0:T(8,128)(2,1)S(1)}, u32[]{:S(2)}, u32[]{:S(2)}) collective-permute-start(bf16[128,2048]{1,0:T(8,128)(2,1)S(1)} %get-tuple-element.180.rest_1_), channel_id=1, source_target_pairs={{0,16},{1,17},{2,18},{3,19},{4,20},{5,21},{6,22},{7,23},{8,24},{9,... | collective-permute-start | bytes 1572872 | tf_op jit(solution)/shard_map/ppermute | solution.py:40
  598.5 50.4 %collective-permute-start.27 = (f32[2,16,768]{2,1,0:T(8,128)}, f32[2,16,768]{2,1,0:T(8,128)}, u32[]{:S(2)}, u32[]{:S(2)}) collective-permute-start(f32[2,16,768]{2,1,0:T(8,128)} %bitcast.14.refs_0_), channel_id=1, source_target_pairs={{0,2},{1,3},{2,0},{3,1},{4,6},{5,7},{6,4},{7,5},{8,10},{9,11},{10,... | collective-permute-start | bytes 294920 | tf_op jit(solution)/shard_map/ppermute | solution.py:40
  598.6 29.9 %collective-permute-start.29 = (bf16[2,2,1,2,128,384]{5,4,3,2,1,0:T(8,128)(2,1)}, bf16[2,2,1,2,128,384]{5,4,3,2,1,0:T(8,128)(2,1)S(1)}, u32[]{:S(2)}, u32[]{:S(2)}) collective-permute-start(bf16[2,2,1,2,128,384]{5,4,3,2,1,0:T(8,128)(2,1)} %get-tuple-element.181.rest_0_.refs_6_), channel_id=1, source_target_pairs={{0,8},{1,9},{2,10},{3,11},{4,12},{5,13},{6,14},{7,15},{8,0},{9,1},... | collective-permute-start | bytes 2359304 | tf_op jit(solution)/shard_map/ppermute | solution.py:40
  617.1 39.3 %collective-permute-start.34 = (bf16[1,2,2,1,128,1280]{5,4,3,2,1,0:T(8,128)(2,1)}, bf16[1,2,2,1,128,1280]{5,4,3,2,1,0:T(8,128)(2,1)}, u32[]{:S(2)}, u32[]{:S(2)}) collective-permute-start(bf16[1,2,2,1,128,1280]{5,4,3,2,1,0:T(8,128)(2,1)} %get-tuple-element.183.refs_7_), channel_id=1, source_target_pairs={{0,4},{1,5},{2,6},{3,7},{4,0},{5,1},{6,2},{7,3},{8,12},{9,13},{10,... | collective-permute-start | bytes 3932168 | tf_op jit(solution)/shard_map/ppermute | solution.py:40
  673.8 24.5 %collective-permute-start.42 = (bf16[128,2048]{1,0:T(8,128)(2,1)S(1)}, bf16[128,2048]{1,0:T(8,128)(2,1)S(1)}, u32[]{:S(2)}, u32[]{:S(2)}) collective-permute-start(bf16[128,2048]{1,0:T(8,128)(2,1)S(1)} %get-tuple-element.212.refs_2_), channel_id=1, source_target_pairs={{0,16},{1,17},{2,18},{3,19},{4,20},{5,21},{6,22},{7,23},{8,24},{9,... | collective-permute-start | bytes 1572872 | tf_op jit(solution)/shard_map/ppermute | solution.py:40
  679.0 22.8 %collective-permute-start.41 = (f32[2,16,768]{2,1,0:T(8,128)S(1)}, f32[2,16,768]{2,1,0:T(8,128)S(1)}, u32[]{:S(2)}, u32[]{:S(2)}) collective-permute-start(f32[2,16,768]{2,1,0:T(8,128)S(1)} %shard_map.308.refs_4_.refs_0_), channel_id=1, source_target_pairs={{0,8},{1,9},{2,10},{3,11},{4,12},{5,13},{6,14},{7,15},{8,0},{9,1},... | collective-permute-start | bytes 294920 | tf_op jit(solution)/shard_map/ppermute | solution.py:40
  (100 other events, 860.9 us)
Sparse Core Ops, SparseCore 0:
  12.9 112.7 all-gather.4
  127.9 108.8 all-gather.2
  323.8 87.1 reduce-scatter.2
  461.3 110.2 reduce-scatter.4

commit v9 on v8

--- a/solution.py
+++ b/solution.py
@@ -1044,7 +1044,7 @@
     last_axis, z_axis, x_axis = 1, plan.bits - 1, plan.bits
     y_axis = 0 if plan.ny == 2 else 2
     orders_f1 = [[y_axis, x_axis, z_axis]] * layers
-    orders_q = [[[z_axis, y_axis, x_axis], [y_axis, z_axis, x_axis]]] + [[[x_axis, z_axis, y_axis]]] * (layers - 1)
+    orders_q = [[[z_axis, y_axis, x_axis], [x_axis, z_axis, y_axis]]] + [[[x_axis, z_axis, y_axis]]] * (layers - 1)
     own_rows = 2 * deep
     tail = width // plan.ny * HEAD_DIM // own_rows
     fused = n == HEADS
@@ -1109,7 +1109,6 @@
         prev = tuple(res1[:1]) + ((last_part,) if top else ())
         if not top:
             prev += (terms["q", layer + 1][0].step(prev[:1]),)
-            prev += (terms["f1", layer + 1].step(prev[:1]),)
             prev += (ends["f2", layer + 1].core(prev[:1]),)
         dproj_oth, part = call(
             attend_back_other,
@@ -1138,6 +1137,7 @@
         terms["f1", layer] = Term(plan, keep, send, orders_f1[layer])
         prev = (send,)
         if not top:
+            prev += (terms["f1", layer + 1].step(prev[:1]),)
             prev += (ends["f2", layer + 1].rep(prev[:1]),)
         dproj_own, grad, low_own, sum2 = call(
             attend_back_own,
@@ -1188,13 +1188,13 @@
         got_vec = plan.flip(vec, vec_axes.pop(0)) if vec_axes else None
         return (vec,)
 
-    prev += (terms["f1", 0].step(prev),)
     w = layers - 1
     mixed = call(
         down_last, w, 1, ["fc2"], [saved[w]["hid"][0], last_part, saved[w]["middle"]], [vecs[w]["f2b"]], [low_rows], prev
     )[0]
     qa, qb = terms["q", 0]
-    prev = (ends["rest", 1].core((mixed,)),)
+    prev = (terms["f1", 0].step((mixed,)),)
+    prev = (ends["rest", 1].core(prev),)
     prev = (qa.step(prev),)
     prev = (qb.step(prev + (ends["rest", 1].came,)),)
     prev = step_vec(prev)

time: 735 us -> 740 us (level)
  waiting for transfers between devices: 192 us -> 202 us
    ppermute x49, waiting for transfers between devices: 77.9 us -> 88.2 us  [swap(): return lax.ppermute(v, AX, pairs)]
  transfers between devices with their start and end apart: 53 -> 53, of which waited for: 18 -> 18; matrix products, arithmetic and copies ran while one was open for 6% -> 6% of each run, Pallas kernels for 52% -> 51%
where the time goes in v9:
time: 740 us; the launch traced here: 735 us
  Pallas kernels  416 us (56%)
  waiting for transfers between devices  202 us (27%)
  local copies, waits for them, and re-layouts  62.1 us (8%)
  starting transfers between devices  30 us (4%)
  between operations  14.9 us (2%)
  other arithmetic  10.5 us (1%)
    pallas_call x24, Pallas kernels, row_call(): pl.pallas_call(kernel, grid_spec=pltpu.PrefetchScalarGridSpec(num_scalar_...  275 us
    all_gather x2, waiting for transfers between devices, per_device(): gathered.append(lax.all_gather(done[0], 'shard', axis=0, tiled=True))  114 us
    ppermute x49, waiting for transfers between devices, swap(): return lax.ppermute(v, AX, pairs)  88.2 us
    unnamed x149, local copies, waits for them, and re-layouts  30.3 us
    ppermute x49, starting transfers between devices, swap(): return lax.ppermute(v, AX, pairs)  29.9 us
    pallas_call x10, Pallas kernels, combine(): pl.pallas_call(kernel, grid=(cuts,), in_specs=[pl.BlockSpec(block, index)...  26.9 us
    pallas_call x2, Pallas kernels, chip_grad(): pl.pallas_call(kernel, grid_spec=pltpu.PrefetchScalarGridSpec(num_scalar_...  26.6 us
    pallas_call x2, Pallas kernels, weight_grad(): pl.pallas_call(kernel, grid_spec=pltpu.PrefetchScalarGridSpec(num_scalar_...  26.3 us
  transfers between devices with their start and end apart: 53, of which 18 were waited for; matrix products, arithmetic and copies ran while one was open for 6% of the time, Pallas kernels for 51%

profile of v9, /device:TPU:0, one launch (start us, length us, event | category | flops | bytes accessed | tf_op | source)
XLA Modules:
  0.0 735.3 jit_solution(13265564116085735827)
XLA Ops:
  17.5 108.3 %all-gather.5.cloned.1.call-done.refs_0_.refs_1_.refs_2_.refs_3_ = bf16[1024,10368]{1,0:T(8,128)(2,1)} async-done(((bf16[64,10368]{1,0:T(8,128)(2,1)}), bf16[1024,10368]{1,0:T(8,128)(2,1)}) %all-gather.5.cloned.1.call-update) | async-done | bytes 21233680 | tf_op jit(solution)/shard_map/all_gather | solution.py:948
  140.4 12.0 %shard_map.258 = (bf16[2,8,320,320]{3,2,1,0:T(8,128)(2,1)}, bf16[640,512]{1,0:T(8,128)(2,1)}, f32[640,1024]{1,0:T(8,128)}) custom-call(s32[4]{0:T(128)} %pad_add_fusion.where_ref, s32[2]{0:T(128)} %copy-done.55, bf16[8,2,64,10368]{3,2,1,0:T(8,128)(2,1)} %bitcast.49, bf16[640,1536]{1,0:T(8,128)(2,1)} %shard_map.257.refs_1_.refs_3_), custom_call_target="tpu_custom_call" | custom-call | flops 10000000 | tf_op jit(solution)/shard_map/pallas_call | solution.py:123
  164.2 13.6 %shard_map.259 = (bf16[2,8,320,320]{3,2,1,0:T(8,128)(2,1)}, bf16[640,512]{1,0:T(8,128)(2,1)}, f32[640,1024]{1,0:T(8,128)}, bf16[640,1024]{1,0:T(8,128)(2,1)}) custom-call(s32[4]{0:T(128)} %pad_add_fusion.where_ref, s32[2]{0:T(128)} %kept_ref.23, bf16[8,2,64,10368]{3,2,1,0:T(8,128)(2,1)} %bitcast.50, bf16[640,1536]{1,0:T(8,128)(2,1)} %shard_map.256.refs_1_.refs_3_, ...), custom_call_target="tpu_custom_call" | custom-call | flops 10000000 | tf_op jit(solution)/shard_map/pallas_call | solution.py:123
  182.2 9.7 %shard_map.261 = (bf16[640,2048]{1,0:T(8,128)(2,1)}, bf16[640,2048]{1,0:T(8,128)(2,1)}) custom-call(s32[4]{0:T(128)} %pad_add_fusion.where_ref, s32[2]{0:T(128)} %copy-done.55, bf16[1024,10368]{1,0:T(8,128)(2,1)} %all-gather.5.cloned.1.call-done.refs_0_.refs_1_.refs_2_.refs_3_, ...), custom_call_target="tpu_custom_call" | custom-call | flops 10000000 | tf_op jit(solution)/shard_map/pallas_call | solution.py:123
  210.6 9.7 %shard_map.260 = (bf16[640,2048]{1,0:T(8,128)(2,1)}, bf16[640,2048]{1,0:T(8,128)(2,1)}) custom-call(s32[4]{0:T(128)} %pad_add_fusion.where_ref, s32[2]{0:T(128)} %kept_ref.23, bf16[1024,10368]{1,0:T(8,128)(2,1)} %all-gather.5.cloned.1.call-done.refs_0_.refs_1_.refs_2_.refs_3_, ...), custom_call_target="tpu_custom_call" | custom-call | flops 10000000 | tf_op jit(solution)/shard_map/pallas_call | solution.py:123
  247.7 11.9 %shard_map.266 = (bf16[2,8,320,320]{3,2,1,0:T(8,128)(2,1)}, bf16[640,512]{1,0:T(8,128)(2,1)}, f32[640,1024]{1,0:T(8,128)}) custom-call(s32[4]{0:T(128)} %pad_add_fusion.where_ref, s32[2]{0:T(128)} %copy-done.55, bf16[8,2,64,10240]{3,2,1,0:T(8,128)(2,1)} %bitcast.53, bf16[640,1536]{1,0:T(8,128)(2,1)} %shard_map.265.refs_1_.refs_3_), custom_call_target="tpu_custom_call" | custom-call | flops 10000000 | tf_op jit(solution)/shard_map/pallas_call | solution.py:123
  271.5 13.6 %shard_map.267 = (bf16[2,8,320,320]{3,2,1,0:T(8,128)(2,1)}, bf16[640,512]{1,0:T(8,128)(2,1)}, f32[640,1024]{1,0:T(8,128)}, bf16[640,1024]{1,0:T(8,128)(2,1)}) custom-call(s32[4]{0:T(128)} %pad_add_fusion.where_ref, s32[2]{0:T(128)} %kept_ref.23, bf16[8,2,64,10240]{3,2,1,0:T(8,128)(2,1)} %bitcast.54, bf16[640,1536]{1,0:T(8,128)(2,1)} %shard_map.264.refs_1_.refs_3_, ...), custom_call_target="tpu_custom_call" | custom-call | flops 10000000 | tf_op jit(solution)/shard_map/pallas_call | solution.py:123
  310.3 13.3 %shard_map.270.refs_6_ = bf16[2048,1024]{1,0:T(8,128)(2,1)} custom-call(s32[4]{0:T(128)} %pad_add_fusion.where_ref, bf16[640,2048]{1,0:T(8,128)(2,1)} %get-tuple-element.128.xo.rest_0_.refs_2_, bf16[640,2048]{1,0:T(8,128)(2,1)} %get-tuple-element.129.xt.refs_2_, bf16[640,1024]{1,0:T(8,128)(2,1)} %bitcast_convert_fusion.yo.refs_4_, ...), custom_call_target="tpu_custom_call" | custom-call | flops 30000001024 | tf_op jit(solution)/shard_map/pallas_call | solution.py:534
  323.7 11.9 %shard_map.271 = (bf16[640,2048]{1,0:T(8,128)(2,1)}, f32[640,1024]{1,0:T(8,128)}) custom-call(s32[4]{0:T(128)} %pad_add_fusion.where_ref, s32[2]{0:T(128)} %copy-done.55, bf16[1024,10240]{1,0:T(8,128)(2,1)} %all-gather.3.cloned.1.call-done.refs_0_.refs_1_.refs_2_.refs_3_, bf16[1024,1024]{1,0:T(8,128)(2,1)} %collective-permute-done.rest_1_.refs_1_, ...), custom_call_target="tpu_custom_call" | custom-call | flops 30000001024 | tf_op jit(solution)/shard_map/pallas_call | solution.py:123
  343.7 16.1 %shard_map.273 = (bf16[640,2048]{1,0:T(8,128)(2,1)}, f32[640,1024]{1,0:T(8,128)}, bf16[640,1024]{1,0:T(8,128)(2,1)}, f32[8,1024]{1,0:T(8,128)}) custom-call(s32[4]{0:T(128)} %pad_add_fusion.where_ref, s32[2]{0:T(128)} %kept_ref.23, bf16[1024,10240]{1,0:T(8,128)(2,1)} %all-gather.3.cloned.1.call-done.refs_0_.refs_1_.refs_2_.refs_3_, ...), custom_call_target="tpu_custom_call" | custom-call | flops 30000001024 | tf_op jit(solution)/shard_map/pallas_call | solution.py:123
  359.9 13.1 %shard_map.274 = (bf16[1,2,2,2,128,1280]{5,4,3,2,1,0:T(8,128)(2,1)}, bf16[1,2,2,2,128,1280]{5,4,3,2,1,0:T(8,128)(2,1)}, f32[1,2048]{1,0:T(1,128)}) custom-call(s32[4]{0:T(128)} %pad_add_fusion.where_ref, bf16[640,1024]{1,0:T(8,128)(2,1)} %get-tuple-element.127.refs_2_.xo, bf16[640,1024]{1,0:T(8,128)(2,1)} %collective-permute-done.9.refs_2_.xt, ...), custom_call_target="tpu_custom_call" | custom-call | flops 30000001024 | tf_op jit(solution)/shard_map/pallas_call | solution.py:412
  378.0 16.5 %shard_map.275 = (bf16[640,1536]{1,0:T(8,128)(2,1)}, f32[640,1024]{1,0:T(8,128)}) custom-call(s32[4]{0:T(128)} %pad_add_fusion.where_ref, s32[2]{0:T(128)} %copy-done.55, bf16[8,2,64,10240]{3,2,1,0:T(8,128)(2,1)} %bitcast.55, bf16[1024,10240]{1,0:T(8,128)(2,1)} %all-gather.3.cloned.1.call-done.refs_0_.refs_1_.refs_2_.refs_3_, ...), custom_call_target="tpu_custom_call" | custom-call | flops 30000001024 | tf_op jit(solution)/shard_map/pallas_call | solution.py:123
  401.0 19.2 %shard_map.277 = (bf16[640,1536]{1,0:T(8,128)(2,1)}, f32[640,1024]{1,0:T(8,128)}, bf16[640,1024]{1,0:T(8,128)(2,1)}, f32[8,1024]{1,0:T(8,128)}) custom-call(s32[4]{0:T(128)} %pad_add_fusion.where_ref, s32[2]{0:T(128)} %kept_ref.23, bf16[8,2,64,10240]{3,2,1,0:T(8,128)(2,1)} %bitcast.56, ...), custom_call_target="tpu_custom_call" | custom-call | flops 30000001024 | tf_op jit(solution)/shard_map/pallas_call | solution.py:123
  420.3 10.8 %shard_map.278 = (bf16[2,2,2,1,128,768]{5,4,3,2,1,0:T(8,128)(2,1)}, bf16[2,2,2,1,128,768]{5,4,3,2,1,0:T(8,128)(2,1)}, f32[1,1536]{1,0:T(1,128)}) custom-call(s32[4]{0:T(128)} %pad_add_fusion.where_ref, bf16[640,1024]{1,0:T(8,128)(2,1)} %get-tuple-element.124.refs_1_.xo, bf16[640,1024]{1,0:T(8,128)(2,1)} %copy-done.39, ...), custom_call_target="tpu_custom_call" | custom-call | flops 30000001024 | tf_op jit(solution)/shard_map/pallas_call | solution.py:491
  435.8 11.9 %shard_map.279 = (bf16[640,2048]{1,0:T(8,128)(2,1)}, f32[640,1024]{1,0:T(8,128)}) custom-call(s32[4]{0:T(128)} %pad_add_fusion.where_ref, s32[2]{0:T(128)} %copy-done.55, bf16[1024,10368]{1,0:T(8,128)(2,1)} %all-gather.5.cloned.1.call-done.refs_0_.refs_1_.refs_2_.refs_3_, bf16[1024,1024]{1,0:T(8,128)(2,1)} %collective-permute-done.1.refs_1_, ...), custom_call_target="tpu_custom_call" | custom-call | flops 30000001024 | tf_op jit(solution)/shard_map/pallas_call | solution.py:123
  447.9 13.3 %shard_map.280.rest_0_.refs_10_ = bf16[2048,1024]{1,0:T(8,128)(2,1)} custom-call(s32[4]{0:T(128)} %pad_add_fusion.where_ref, bf16[640,2048]{1,0:T(8,128)(2,1)} %get-tuple-element.121.refs_2_.xo, bf16[640,2048]{1,0:T(8,128)(2,1)} %get-tuple-element.122.refs_2_.xt, bf16[640,1024]{1,0:T(8,128)(2,1)} %get-tuple-element.147.yo.refs_4_, ...), custom_call_target="tpu_custom_call" | custom-call | flops 30000001024 | tf_op jit(solution)/shard_map/pallas_call | solution.py:534
  467.3 15.4 %shard_map.282 = (bf16[640,2048]{1,0:T(8,128)(2,1)}, f32[640,1024]{1,0:T(8,128)}, bf16[640,1024]{1,0:T(8,128)(2,1)}, f32[8,1024]{1,0:T(8,128)}) custom-call(s32[4]{0:T(128)} %pad_add_fusion.where_ref, s32[2]{0:T(128)} %kept_ref.23, bf16[1024,10368]{1,0:T(8,128)(2,1)} %all-gather.5.cloned.1.call-done.refs_0_.refs_1_.refs_2_.refs_3_, ...), custom_call_target="tpu_custom_call" | custom-call | flops 30000001024 | tf_op jit(solution)/shard_map/pallas_call | solution.py:123
  487.5 13.2 %shard_map.284 = (bf16[1,2,2,2,128,1280]{5,4,3,2,1,0:T(8,128)(2,1)}, bf16[1,2,2,2,128,1280]{5,4,3,2,1,0:T(8,128)(2,1)}, f32[1,2048]{1,0:T(1,128)}) custom-call(s32[4]{0:T(128)} %pad_add_fusion.where_ref, bf16[640,1024]{1,0:T(8,128)(2,1)} %get-tuple-element.120.refs_2_.xo, bf16[640,1024]{1,0:T(8,128)(2,1)} %copy-done.40, ...), custom_call_target="tpu_custom_call" | custom-call | flops 30000001024 | tf_op jit(solution)/shard_map/pallas_call | solution.py:412
  509.1 17.1 %collective-permute-done.20.g = bf16[2,2,1,1,128,768]{5,4,3,2,1,0:T(8,128)(2,1)S(1)} collective-permute-done((bf16[2,2,1,1,128,768]{5,4,3,2,1,0:T(8,128)(2,1)}, bf16[2,2,1,1,128,768]{5,4,3,2,1,0:T(8,128)(2,1)S(1)}, u32[]{:S(2)}, u32[]{:S(2)}) %collective-permute-start.20) | collective-permute-done | bytes 786464 | tf_op jit(solution)/shard_map/ppermute | solution.py:40
  531.8 16.1 %shard_map.287 = (bf16[640,1536]{1,0:T(8,128)(2,1)}, f32[640,1024]{1,0:T(8,128)}) custom-call(s32[4]{0:T(128)} %pad_add_fusion.where_ref, s32[2]{0:T(128)} %copy-done.55, bf16[8,2,64,10368]{3,2,1,0:T(8,128)(2,1)} %bitcast.51, bf16[1024,10368]{1,0:T(8,128)(2,1)} %all-gather.5.cloned.1.call-done.refs_0_.refs_1_.refs_2_.refs_3_, bf16[640,1024]{1,0:T(8,128)(2,1)} %copy-done.62, ...), custom_call_target="tpu_custom_call" | custom-call | flops 30000001024 | tf_op jit(solution)/shard_map/pallas_call | solution.py:123
  564.5 19.3 %shard_map.291 = (bf16[640,1536]{1,0:T(8,128)(2,1)}, f32[640,1024]{1,0:T(8,128)}, bf16[640,1024]{1,0:T(8,128)(2,1)}, f32[8,1024]{1,0:T(8,128)}) custom-call(s32[4]{0:T(128)} %pad_add_fusion.where_ref, s32[2]{0:T(128)} %kept_ref.23, bf16[8,2,64,10368]{3,2,1,0:T(8,128)(2,1)} %bitcast.52, ...), custom_call_target="tpu_custom_call" | custom-call | flops 30000001024 | tf_op jit(solution)/shard_map/pallas_call | solution.py:123
  587.6 12.1 %shard_map.293 = (bf16[2,2,1,2,128,384]{5,4,3,2,1,0:T(8,128)(2,1)}, bf16[2,2,1,2,128,384]{5,4,3,2,1,0:T(8,128)(2,1)}, bf16[2,2,2,1,128,384]{5,4,3,2,1,0:T(8,128)...) custom-call(s32[4]{0:T(128)} %pad_add_fusion.where_ref, bf16[640,1024]{1,0:T(8,128)(2,1)} %copy-done.37, ...), custom_call_target="tpu_custom_call" | custom-call | flops 30000001024 | tf_op jit(solution)/shard_map/pallas_call | solution.py:491
  647.2 15.4 %collective-permute-done.34.g = bf16[1,2,2,1,128,1280]{5,4,3,2,1,0:T(8,128)(2,1)} collective-permute-done((bf16[1,2,2,1,128,1280]{5,4,3,2,1,0:T(8,128)(2,1)}, bf16[1,2,2,1,128,1280]{5,4,3,2,1,0:T(8,128)(2,1)}, u32[]{:S(2)}, u32[]{:S(2)}) %collective-permute-start.34) | collective-permute-done | bytes 1310752 | tf_op jit(solution)/shard_map/ppermute | solution.py:40
  686.1 10.2 %collective-permute-done.44.refs_3_ = bf16[64,4096]{1,0:T(8,128)(2,1)S(1)} collective-permute-done((bf16[64,4096]{1,0:T(8,128)(2,1)S(1)}, bf16[64,4096]{1,0:T(8,128)(2,1)S(1)}, u32[]{:S(2)}, u32[]{:S(2)}) %collective-permute-start.44) | collective-permute-done | bytes 524320 | tf_op jit(solution)/shard_map/ppermute | solution.py:40
  (411 shorter events, 296.6 us)
Async XLA Ops:
  7.2 118.6 %all-gather.5.cloned.1.call-start = ((), (), s32[]{:S(2)}) async-start(), calls=%async_computation.3 | async-start | bytes 22560768 | tf_op jit(solution)/shard_map/all_gather | solution.py:948
  12.8 223.9 %all-gather.3.cloned.1.call-start = ((), (), s32[]{:S(2)}) async-start(), calls=%async_computation.2 | async-start | bytes 22282240 | tf_op jit(solution)/shard_map/all_gather | solution.py:948
  16.5 484.2 %reduce-scatter.3.cloned.1.call-start = ((), (), s32[]{:S(2)}) async-start(), calls=%async_computation.4 | async-start | bytes 4718592 | tf_op jit(solution)/shard_map/reduce_scatter | solution.py:751
  152.6 47.9 %collective-permute-start.1 = (bf16[1024,1024]{1,0:T(8,128)(2,1)S(1)}, bf16[1024,1024]{1,0:T(8,128)(2,1)}, u32[]{:S(2)}, u32[]{:S(2)}) collective-permute-start(bf16[1024,1024]{1,0:T(8,128)(2,1)S(1)} %copy-done.36), channel_id=1, source_target_pairs={{0,1},{1,0},{2,3},{3,2},{4,5},{5,4},{6,7},{7,6},{8,9},{9,8},{10,11... | collective-permute-start | bytes 6291464 | tf_op jit(solution)/shard_map/ppermute | solution.py:40
  260.0 49.3 %collective-permute-start = (bf16[1024,1024]{1,0:T(8,128)(2,1)}, bf16[1024,1024]{1,0:T(8,128)(2,1)}, u32[]{:S(2)}, u32[]{:S(2)}) collective-permute-start(bf16[1024,1024]{1,0:T(8,128)(2,1)} %constant_dynamic-slice_fusion.2.refs_3_), channel_id=1, source_target_pairs={{0,1},{1,0},{2,3},{3,2},{4,5},{5,4},{6,7},{7,6},{8,9},{9,8},{10,11... | collective-permute-start | bytes 6291464 | tf_op jit(solution)/shard_map/ppermute | solution.py:40
  323.6 341.7 %reduce-scatter.5.cloned.1.call-start = ((), (), s32[]{:S(2)}) async-start(), calls=%async_computation.5 | async-start | bytes 4718592 | tf_op jit(solution)/shard_map/reduce_scatter | solution.py:751
  343.2 33.3 %collective-permute-start.11 = (f32[640,1024]{1,0:T(8,128)}, f32[640,1024]{1,0:T(8,128)S(1)}, u32[]{:S(2)}, u32[]{:S(2)}) collective-permute-start(f32[640,1024]{1,0:T(8,128)} %shard_map.272.refs_10_), channel_id=1, source_target_pairs={{0,2},{1,3},{2,0},{3,1},{4,6},{5,7},{6,4},{7,5},{8,10},{9,11},{10,... | collective-permute-start | bytes 7864328 | tf_op jit(solution)/shard_map/ppermute | solution.py:40
  400.6 60.6 %collective-permute-start.17 = (bf16[1,2,2,2,128,1280]{5,4,3,2,1,0:T(8,128)(2,1)}, bf16[1,2,2,2,128,1280]{5,4,3,2,1,0:T(8,128)(2,1)S(1)}, u32[]{:S(2)}, u32[]{:S(2)}) collective-permute-start(bf16[1,2,2,2,128,1280]{5,4,3,2,1,0:T(8,128)(2,1)} %get-tuple-element.146.refs_9_), channel_id=1, source_target_pairs={{0,1},{1,0},{2,3},{3,2},{4,5},{5,4},{6,7},{7,6},{8,9},{9,8},{10,11... | collective-permute-start | bytes 7864328 | tf_op jit(solution)/shard_map/ppermute | solution.py:40
  433.9 49.1 %collective-permute-start.19 = (bf16[2,2,2,1,128,768]{5,4,3,2,1,0:T(8,128)(2,1)}, bf16[2,2,2,1,128,768]{5,4,3,2,1,0:T(8,128)(2,1)}, u32[]{:S(2)}, u32[]{:S(2)}) collective-permute-start(bf16[2,2,2,1,128,768]{5,4,3,2,1,0:T(8,128)(2,1)} %get-tuple-element.151.refs_6_), channel_id=1, source_target_pairs={{0,4},{1,5},{2,6},{3,7},{4,0},{5,1},{6,2},{7,3},{8,12},{9,13},{10,... | collective-permute-start | bytes 4718600 | tf_op jit(solution)/shard_map/ppermute | solution.py:40
  466.5 92.9 %collective-permute-start.22 = (bf16[1,2,2,1,128,1280]{5,4,3,2,1,0:T(8,128)(2,1)}, bf16[1,2,2,1,128,1280]{5,4,3,2,1,0:T(8,128)(2,1)}, u32[]{:S(2)}, u32[]{:S(2)}) collective-permute-start(bf16[1,2,2,1,128,1280]{5,4,3,2,1,0:T(8,128)(2,1)} %get-tuple-element.156.refs_11_), channel_id=1, source_target_pairs={{0,4},{1,5},{2,6},{3,7},{4,0},{5,1},{6,2},{7,3},{8,12},{9,13},{10,... | collective-permute-start | bytes 3932168 | tf_op jit(solution)/shard_map/ppermute | solution.py:40
  482.7 48.0 %collective-permute-start.18 = (bf16[640,1024]{1,0:T(8,128)(2,1)}, bf16[640,1024]{1,0:T(8,128)(2,1)S(1)}, u32[]{:S(2)}, u32[]{:S(2)}) collective-permute-start(bf16[640,1024]{1,0:T(8,128)(2,1)} %get-tuple-element.157.rest_0_.yo.refs_2_), channel_id=1, source_target_pairs={{0,2},{1,3},{2,0},{3,1},{4,6},{5,7},{6,4},{7,5},{8,10},{9,11},{10,... | collective-permute-start | bytes 3932168 | tf_op jit(solution)/shard_map/ppermute | solution.py:40
  485.9 40.3 %collective-permute-start.20 = (bf16[2,2,1,1,128,768]{5,4,3,2,1,0:T(8,128)(2,1)}, bf16[2,2,1,1,128,768]{5,4,3,2,1,0:T(8,128)(2,1)S(1)}, u32[]{:S(2)}, u32[]{:S(2)}) collective-permute-start(bf16[2,2,1,1,128,768]{5,4,3,2,1,0:T(8,128)(2,1)} %get-tuple-element.162.rest_1_), channel_id=1, source_target_pairs={{0,8},{1,9},{2,10},{3,11},{4,12},{5,13},{6,14},{7,15},{8,0},{9,1},... | collective-permute-start | bytes 2359304 | tf_op jit(solution)/shard_map/ppermute | solution.py:40
  508.8 45.9 %collective-permute-start.23 = (bf16[128,1024]{1,0:T(8,128)(2,1)S(1)}, bf16[128,1024]{1,0:T(8,128)(2,1)S(1)}, u32[]{:S(2)}, u32[]{:S(2)}) collective-permute-start(bf16[128,1024]{1,0:T(8,128)(2,1)S(1)} %get-tuple-element.166.refs_7_), channel_id=1, source_target_pairs={{0,2},{1,3},{2,0},{3,1},{4,6},{5,7},{6,4},{7,5},{8,10},{9,11},{10,... | collective-permute-start | bytes 786440 | tf_op jit(solution)/shard_map/ppermute | solution.py:40
  529.3 54.5 %collective-permute-start.24 = (bf16[1,2,1,1,128,768]{5,4,3,2,1,0:T(8,128)(2,1)}, bf16[1,2,1,1,128,768]{5,4,3,2,1,0:T(8,128)(2,1)}, u32[]{:S(2)}, u32[]{:S(2)}) collective-permute-start(bf16[1,2,1,1,128,768]{5,4,3,2,1,0:T(8,128)(2,1)} %get-tuple-element.165.refs_6_), channel_id=1, source_target_pairs={{0,1},{1,0},{2,3},{3,2},{4,5},{5,4},{6,7},{7,6},{8,9},{9,8},{10,11... | collective-permute-start | bytes 1179656 | tf_op jit(solution)/shard_map/ppermute | solution.py:40
  554.2 60.1 %collective-permute-start.30 = (bf16[1,2,2,2,128,1280]{5,4,3,2,1,0:T(8,128)(2,1)}, bf16[1,2,2,2,128,1280]{5,4,3,2,1,0:T(8,128)(2,1)}, u32[]{:S(2)}, u32[]{:S(2)}) collective-permute-start(bf16[1,2,2,2,128,1280]{5,4,3,2,1,0:T(8,128)(2,1)} %get-tuple-element.173.rest_0_.refs_2_.refs_9_), channel_id=1, source_target_pairs={{0,1},{1,0},{2,3},{3,2},{4,5},{5,4},{6,7},{7,6},{8,9},{9,8},{10,11... | collective-permute-start | bytes 7864328 | tf_op jit(solution)/shard_map/ppermute | solution.py:40
  557.9 128.2 %collective-permute-start.43 = (bf16[256,1024]{1,0:T(8,128)(2,1)}, bf16[256,1024]{1,0:T(8,128)(2,1)}, u32[]{:S(2)}, u32[]{:S(2)}) collective-permute-start(bf16[256,1024]{1,0:T(8,128)(2,1)} %shard_map.290.refs_11_.refs_0_), channel_id=1, source_target_pairs={{0,1},{1,0},{2,3},{3,2},{4,5},{5,4},{6,7},{7,6},{8,9},{9,8},{10,11... | collective-permute-start | bytes 1572872 | tf_op jit(solution)/shard_map/ppermute | solution.py:40
  586.6 32.0 %collective-permute-start.29 = (bf16[128,2048]{1,0:T(8,128)(2,1)S(1)}, bf16[128,2048]{1,0:T(8,128)(2,1)S(1)}, u32[]{:S(2)}, u32[]{:S(2)}) collective-permute-start(bf16[128,2048]{1,0:T(8,128)(2,1)S(1)} %get-tuple-element.180.rest_1_), channel_id=1, source_target_pairs={{0,16},{1,17},{2,18},{3,19},{4,20},{5,21},{6,22},{7,23},{8,24},{9,... | collective-permute-start | bytes 1572872 | tf_op jit(solution)/shard_map/ppermute | solution.py:40
  602.5 35.5 %collective-permute-start.26 = (f32[2,16,768]{2,1,0:T(8,128)}, f32[2,16,768]{2,1,0:T(8,128)}, u32[]{:S(2)}, u32[]{:S(2)}) collective-permute-start(f32[2,16,768]{2,1,0:T(8,128)} %bitcast.14.refs_0_), channel_id=1, source_target_pairs={{0,2},{1,3},{2,0},{3,1},{4,6},{5,7},{6,4},{7,5},{8,10},{9,11},{10,... | collective-permute-start | bytes 294920 | tf_op jit(solution)/shard_map/ppermute | solution.py:40
  602.5 26.6 %collective-permute-start.28 = (bf16[2,2,1,2,128,384]{5,4,3,2,1,0:T(8,128)(2,1)}, bf16[2,2,1,2,128,384]{5,4,3,2,1,0:T(8,128)(2,1)}, u32[]{:S(2)}, u32[]{:S(2)}) collective-permute-start(bf16[2,2,1,2,128,384]{5,4,3,2,1,0:T(8,128)(2,1)} %get-tuple-element.181.refs_6_), channel_id=1, source_target_pairs={{0,8},{1,9},{2,10},{3,11},{4,12},{5,13},{6,14},{7,15},{8,0},{9,1},... | collective-permute-start | bytes 2359304 | tf_op jit(solution)/shard_map/ppermute | solution.py:40
  618.6 44.0 %collective-permute-start.34 = (bf16[1,2,2,1,128,1280]{5,4,3,2,1,0:T(8,128)(2,1)}, bf16[1,2,2,1,128,1280]{5,4,3,2,1,0:T(8,128)(2,1)}, u32[]{:S(2)}, u32[]{:S(2)}) collective-permute-start(bf16[1,2,2,1,128,1280]{5,4,3,2,1,0:T(8,128)(2,1)} %get-tuple-element.196.refs_2_), channel_id=1, source_target_pairs={{0,4},{1,5},{2,6},{3,7},{4,0},{5,1},{6,2},{7,3},{8,12},{9,13},{10,... | collective-permute-start | bytes 3932168 | tf_op jit(solution)/shard_map/ppermute | solution.py:40
  637.9 30.2 %collective-permute-start.33 = (bf16[2,2,1,1,128,384]{5,4,3,2,1,0:T(8,128)(2,1)}, bf16[2,2,1,1,128,384]{5,4,3,2,1,0:T(8,128)(2,1)S(1)}, u32[]{:S(2)}, u32[]{:S(2)}) collective-permute-start(bf16[2,2,1,1,128,384]{5,4,3,2,1,0:T(8,128)(2,1)} %get-tuple-element.199.refs_2_), channel_id=1, source_target_pairs={{0,8},{1,9},{2,10},{3,11},{4,12},{5,13},{6,14},{7,15},{8,0},{9,1},... | collective-permute-start | bytes 1179656 | tf_op jit(solution)/shard_map/ppermute | solution.py:40
  640.5 30.4 %collective-permute-start.32 = (f32[2,16,768]{2,1,0:T(8,128)S(1)}, f32[2,16,768]{2,1,0:T(8,128)S(1)}, u32[]{:S(2)}, u32[]{:S(2)}) collective-permute-start(f32[2,16,768]{2,1,0:T(8,128)S(1)} %shard_map.299.rest_0_.refs_0_), channel_id=1, source_target_pairs={{0,1},{1,0},{2,3},{3,2},{4,5},{5,4},{6,7},{7,6},{8,9},{9,8},{10,11... | collective-permute-start | bytes 294920 | tf_op jit(solution)/shard_map/ppermute | solution.py:40
  646.5 26.6 %collective-permute-start.38 = (bf16[1,2,1,1,128,384]{5,4,3,2,1,0:T(8,128)(2,1)}, bf16[1,2,1,1,128,384]{5,4,3,2,1,0:T(8,128)(2,1)S(1)}, u32[]{:S(2)}, u32[]{:S(2)}) collective-permute-start(bf16[1,2,1,1,128,384]{5,4,3,2,1,0:T(8,128)(2,1)} %get-tuple-element.203.rest_0_), channel_id=1, source_target_pairs={{0,4},{1,5},{2,6},{3,7},{4,0},{5,1},{6,2},{7,3},{8,12},{9,13},{10,... | collective-permute-start | bytes 589832 | tf_op jit(solution)/shard_map/ppermute | solution.py:40
  680.1 23.1 %collective-permute-start.42 = (bf16[128,2048]{1,0:T(8,128)(2,1)S(1)}, bf16[128,2048]{1,0:T(8,128)(2,1)S(1)}, u32[]{:S(2)}, u32[]{:S(2)}) collective-permute-start(bf16[128,2048]{1,0:T(8,128)(2,1)S(1)} %get-tuple-element.212.refs_2_), channel_id=1, source_target_pairs={{0,16},{1,17},{2,18},{3,19},{4,20},{5,21},{6,22},{7,23},{8,24},{9,... | collective-permute-start | bytes 1572872 | tf_op jit(solution)/shard_map/ppermute | solution.py:40
  (100 other events, 898.9 us)
Sparse Core Ops, SparseCore 0:
  12.9 112.7 all-gather.4
  127.9 108.8 all-gather.2
  323.8 87.1 reduce-scatter.2
  461.3 109.1 reduce-scatter.4

commit v10 on v6

--- a/solution.py
+++ b/solution.py
@@ -964,7 +964,7 @@
     last_axis, z_axis, x_axis = 1, plan.bits - 1, plan.bits
     y_axis = 0 if plan.ny == 2 else 2
     orders_f1 = [[y_axis, x_axis, z_axis]] * layers
-    orders_q = [[[z_axis, y_axis, x_axis], [y_axis, z_axis, x_axis]]] + [[[x_axis, z_axis, y_axis]]] * (layers - 1)
+    orders_q = [[[z_axis, y_axis, x_axis], [x_axis, z_axis, y_axis]]] + [[[x_axis, z_axis, y_axis]]] * (layers - 1)
     own_rows = 2 * deep
     tail = width // plan.ny * HEAD_DIM // own_rows
     fused = n == HEADS

time: 727 us -> 732 us (level)
  no operation moved by 1% of the time
where the time goes in v10:
time: 732 us; the launch traced here: 727 us
  Pallas kernels  403 us (55%)
  waiting for transfers between devices  187 us (26%)
  local copies, waits for them, and re-layouts  75.5 us (10%)
  starting transfers between devices  36.1 us (5%)
  between operations  15.1 us (2%)
  other arithmetic  10.7 us (1%)
    pallas_call x24, Pallas kernels, row_call(): pl.pallas_call(kernel, grid_spec=pltpu.PrefetchScalarGridSpec(num_scalar_...  274 us
    all_gather x2, waiting for transfers between devices, per_device(): gathered.append(lax.all_gather(done[0], 'shard', axis=0, tiled=True))  114 us
    ppermute x49, waiting for transfers between devices, swap(): return lax.ppermute(v, AX, pairs)  73.5 us
    pallas_call x5, Pallas kernels, weight_grad(): pl.pallas_call(kernel, grid_spec=pltpu.PrefetchScalarGridSpec(num_scalar_...  53.2 us
    unnamed x176, local copies, waits for them, and re-layouts  43.3 us
    ppermute x49, starting transfers between devices, swap(): return lax.ppermute(v, AX, pairs)  35.9 us
    pallas_call x2, Pallas kernels, chip_grad(): pl.pallas_call(kernel, grid_spec=pltpu.PrefetchScalarGridSpec(num_scalar_...  26.6 us
  transfers between devices with their start and end apart: 53, of which 16 were waited for; matrix products, arithmetic and copies ran while one was open for 6% of the time, Pallas kernels for 50%

profile of v10, /device:TPU:0, one launch (start us, length us, event | category | flops | bytes accessed | tf_op | source)
XLA Modules:
  0.0 727.3 jit_solution(13756895624157455094)
XLA Ops:
  17.5 108.3 %all-gather.5.cloned.1.call-done.refs_0_.refs_1_.refs_2_.refs_3_ = bf16[1024,10368]{1,0:T(8,128)(2,1)} async-done(((bf16[64,10368]{1,0:T(8,128)(2,1)}), bf16[1024,10368]{1,0:T(8,128)(2,1)}) %all-gather.5.cloned.1.call-update) | async-done | bytes 21233680 | tf_op jit(solution)/shard_map/all_gather | solution.py:868
  140.4 12.0 %shard_map.258 = (bf16[2,8,320,320]{3,2,1,0:T(8,128)(2,1)}, bf16[640,512]{1,0:T(8,128)(2,1)}, f32[640,1024]{1,0:T(8,128)}) custom-call(s32[4]{0:T(128)} %pad_add_fusion.where_ref, s32[2]{0:T(128)} %copy-done.74, bf16[8,2,64,10368]{3,2,1,0:T(8,128)(2,1)} %bitcast.53, bf16[640,1536]{1,0:T(8,128)(2,1)} %shard_map.257.refs_1_.refs_3_), custom_call_target="tpu_custom_call" | custom-call | flops 10000000 | tf_op jit(solution)/shard_map/pallas_call | solution.py:123
  164.3 13.6 %shard_map.259 = (bf16[2,8,320,320]{3,2,1,0:T(8,128)(2,1)}, bf16[640,512]{1,0:T(8,128)(2,1)}, f32[640,1024]{1,0:T(8,128)}, bf16[640,1024]{1,0:T(8,128)(2,1)}) custom-call(s32[4]{0:T(128)} %pad_add_fusion.where_ref, s32[2]{0:T(128)} %kept_ref.23, bf16[8,2,64,10368]{3,2,1,0:T(8,128)(2,1)} %bitcast.54, bf16[640,1536]{1,0:T(8,128)(2,1)} %shard_map.256.refs_1_.refs_3_, ...), custom_call_target="tpu_custom_call" | custom-call | flops 10000000 | tf_op jit(solution)/shard_map/pallas_call | solution.py:123
  182.2 9.7 %shard_map.261 = (bf16[640,2048]{1,0:T(8,128)(2,1)}, bf16[640,2048]{1,0:T(8,128)(2,1)}) custom-call(s32[4]{0:T(128)} %pad_add_fusion.where_ref, s32[2]{0:T(128)} %copy-done.74, bf16[1024,10368]{1,0:T(8,128)(2,1)} %all-gather.5.cloned.1.call-done.refs_0_.refs_1_.refs_2_.refs_3_, ...), custom_call_target="tpu_custom_call" | custom-call | flops 10000000 | tf_op jit(solution)/shard_map/pallas_call | solution.py:123
  210.7 9.7 %shard_map.260 = (bf16[640,2048]{1,0:T(8,128)(2,1)}, bf16[640,2048]{1,0:T(8,128)(2,1)}) custom-call(s32[4]{0:T(128)} %pad_add_fusion.where_ref, s32[2]{0:T(128)} %kept_ref.23, bf16[1024,10368]{1,0:T(8,128)(2,1)} %all-gather.5.cloned.1.call-done.refs_0_.refs_1_.refs_2_.refs_3_, ...), custom_call_target="tpu_custom_call" | custom-call | flops 10000000 | tf_op jit(solution)/shard_map/pallas_call | solution.py:123
  247.7 11.9 %shard_map.266 = (bf16[2,8,320,320]{3,2,1,0:T(8,128)(2,1)}, bf16[640,512]{1,0:T(8,128)(2,1)}, f32[640,1024]{1,0:T(8,128)}) custom-call(s32[4]{0:T(128)} %pad_add_fusion.where_ref, s32[2]{0:T(128)} %copy-done.74, bf16[8,2,64,10240]{3,2,1,0:T(8,128)(2,1)} %bitcast.57, bf16[640,1536]{1,0:T(8,128)(2,1)} %shard_map.265.refs_1_.refs_3_), custom_call_target="tpu_custom_call" | custom-call | flops 10000000 | tf_op jit(solution)/shard_map/pallas_call | solution.py:123
  271.5 13.6 %shard_map.267 = (bf16[2,8,320,320]{3,2,1,0:T(8,128)(2,1)}, bf16[640,512]{1,0:T(8,128)(2,1)}, f32[640,1024]{1,0:T(8,128)}, bf16[640,1024]{1,0:T(8,128)(2,1)}) custom-call(s32[4]{0:T(128)} %pad_add_fusion.where_ref, s32[2]{0:T(128)} %kept_ref.23, bf16[8,2,64,10240]{3,2,1,0:T(8,128)(2,1)} %bitcast.58, bf16[640,1536]{1,0:T(8,128)(2,1)} %shard_map.264.refs_1_.refs_3_, ...), custom_call_target="tpu_custom_call" | custom-call | flops 10000000 | tf_op jit(solution)/shard_map/pallas_call | solution.py:123
  290.0 9.6 %shard_map.268 = (bf16[640,2048]{1,0:T(8,128)(2,1)}, bf16[640,2048]{1,0:T(8,128)(2,1)}) custom-call(s32[4]{0:T(128)} %pad_add_fusion.where_ref, s32[2]{0:T(128)} %kept_ref.23, bf16[1024,10240]{1,0:T(8,128)(2,1)} %all-gather.3.cloned.1.call-done.refs_0_.refs_1_.refs_2_.refs_3_, ...), custom_call_target="tpu_custom_call" | custom-call | flops 10000000 | tf_op jit(solution)/shard_map/pallas_call | solution.py:123
  299.5 9.6 %shard_map.269 = (bf16[640,2048]{1,0:T(8,128)(2,1)}, bf16[640,2048]{1,0:T(8,128)(2,1)}) custom-call(s32[4]{0:T(128)} %pad_add_fusion.where_ref, s32[2]{0:T(128)} %copy-done.74, bf16[1024,10240]{1,0:T(8,128)(2,1)} %all-gather.3.cloned.1.call-done.refs_0_.refs_1_.refs_2_.refs_3_, ...), custom_call_target="tpu_custom_call" | custom-call | flops 10000000 | tf_op jit(solution)/shard_map/pallas_call | solution.py:123
  310.2 13.3 %shard_map.270.refs_6_ = bf16[2048,1024]{1,0:T(8,128)(2,1)} custom-call(s32[4]{0:T(128)} %pad_add_fusion.where_ref, bf16[640,2048]{1,0:T(8,128)(2,1)} %get-tuple-element.129.xo.rest_0_.refs_2_, bf16[640,2048]{1,0:T(8,128)(2,1)} %get-tuple-element.130.xt.refs_2_, bf16[640,1024]{1,0:T(8,128)(2,1)} %bitcast_convert_fusion.yo.refs_4_, ...), custom_call_target="tpu_custom_call" | custom-call | flops 30000001024 | tf_op jit(solution)/shard_map/pallas_call | solution.py:454
  323.5 11.9 %shard_map.271 = (bf16[640,2048]{1,0:T(8,128)(2,1)}, f32[640,1024]{1,0:T(8,128)}) custom-call(s32[4]{0:T(128)} %pad_add_fusion.where_ref, s32[2]{0:T(128)} %copy-done.74, bf16[1024,10240]{1,0:T(8,128)(2,1)} %all-gather.3.cloned.1.call-done.refs_0_.refs_1_.refs_2_.refs_3_, bf16[1024,1024]{1,0:T(8,128)(2,1)} %collective-permute-done.rest_1_.refs_1_, ...), custom_call_target="tpu_custom_call" | custom-call | flops 30000001024 | tf_op jit(solution)/shard_map/pallas_call | solution.py:123
  344.9 16.3 %shard_map.273 = (bf16[640,2048]{1,0:T(8,128)(2,1)}, f32[640,1024]{1,0:T(8,128)}, bf16[640,1024]{1,0:T(8,128)(2,1)}, f32[8,1024]{1,0:T(8,128)}) custom-call(s32[4]{0:T(128)} %pad_add_fusion.where_ref, s32[2]{0:T(128)} %kept_ref.23, bf16[1024,10240]{1,0:T(8,128)(2,1)} %all-gather.3.cloned.1.call-done.refs_0_.refs_1_.refs_2_.refs_3_, ...), custom_call_target="tpu_custom_call" | custom-call | flops 30000001024 | tf_op jit(solution)/shard_map/pallas_call | solution.py:123
  361.2 13.1 %shard_map.274 = (bf16[1,2,2,2,128,1280]{5,4,3,2,1,0:T(8,128)(2,1)}, bf16[1,2,2,2,128,1280]{5,4,3,2,1,0:T(8,128)(2,1)}, f32[1,2048]{1,0:T(1,128)}) custom-call(s32[4]{0:T(128)} %pad_add_fusion.where_ref, bf16[640,1024]{1,0:T(8,128)(2,1)} %get-tuple-element.128.refs_2_.xo, bf16[640,1024]{1,0:T(8,128)(2,1)} %collective-permute-done.9.refs_2_.xt, ...), custom_call_target="tpu_custom_call" | custom-call | flops 30000001024 | tf_op jit(solution)/shard_map/pallas_call | solution.py:412
  378.9 16.6 %shard_map.275 = (bf16[640,1536]{1,0:T(8,128)(2,1)}, f32[640,1024]{1,0:T(8,128)}) custom-call(s32[4]{0:T(128)} %pad_add_fusion.where_ref, s32[2]{0:T(128)} %copy-done.74, bf16[8,2,64,10240]{3,2,1,0:T(8,128)(2,1)} %bitcast.59, bf16[1024,10240]{1,0:T(8,128)(2,1)} %all-gather.3.cloned.1.call-done.refs_0_.refs_1_.refs_2_.refs_3_, bf16[640,1024]{1,0:T(8,128)(2,1)} %copy-done.81, ...), custom_call_target="tpu_custom_call" | custom-call | flops 30000001024 | tf_op jit(solution)/shard_map/pallas_call | solution.py:123
  402.0 19.2 %shard_map.277 = (bf16[640,1536]{1,0:T(8,128)(2,1)}, f32[640,1024]{1,0:T(8,128)}, bf16[640,1024]{1,0:T(8,128)(2,1)}, f32[8,1024]{1,0:T(8,128)}) custom-call(s32[4]{0:T(128)} %pad_add_fusion.where_ref, s32[2]{0:T(128)} %kept_ref.23, bf16[8,2,64,10240]{3,2,1,0:T(8,128)(2,1)} %bitcast.60, ...), custom_call_target="tpu_custom_call" | custom-call | flops 30000001024 | tf_op jit(solution)/shard_map/pallas_call | solution.py:123
  421.3 10.8 %shard_map.278 = (bf16[2,2,2,1,128,768]{5,4,3,2,1,0:T(8,128)(2,1)}, bf16[2,2,2,1,128,768]{5,4,3,2,1,0:T(8,128)(2,1)}, f32[1,1536]{1,0:T(1,128)}) custom-call(s32[4]{0:T(128)} %pad_add_fusion.where_ref, bf16[640,1024]{1,0:T(8,128)(2,1)} %get-tuple-element.125.refs_1_.xo, bf16[640,1024]{1,0:T(8,128)(2,1)} %copy-done.56, ...), custom_call_target="tpu_custom_call" | custom-call | flops 30000001024 | tf_op jit(solution)/shard_map/pallas_call | solution.py:412
  436.7 11.7 %shard_map.279 = (bf16[640,2048]{1,0:T(8,128)(2,1)}, f32[640,1024]{1,0:T(8,128)}) custom-call(s32[4]{0:T(128)} %pad_add_fusion.where_ref, s32[2]{0:T(128)} %copy-done.74, bf16[1024,10368]{1,0:T(8,128)(2,1)} %all-gather.5.cloned.1.call-done.refs_0_.refs_1_.refs_2_.refs_3_, bf16[1024,1024]{1,0:T(8,128)(2,1)} %collective-permute-done.1.refs_1_, ...), custom_call_target="tpu_custom_call" | custom-call | flops 30000001024 | tf_op jit(solution)/shard_map/pallas_call | solution.py:123
  448.7 13.3 %shard_map.280.rest_0_.refs_10_ = bf16[2048,1024]{1,0:T(8,128)(2,1)} custom-call(s32[4]{0:T(128)} %pad_add_fusion.where_ref, bf16[640,2048]{1,0:T(8,128)(2,1)} %get-tuple-element.122.refs_2_.xo, bf16[640,2048]{1,0:T(8,128)(2,1)} %get-tuple-element.123.refs_2_.xt, bf16[640,1024]{1,0:T(8,128)(2,1)} %get-tuple-element.148.yo.refs_4_, ...), custom_call_target="tpu_custom_call" | custom-call | flops 30000001024 | tf_op jit(solution)/shard_map/pallas_call | solution.py:454
  469.7 15.2 %shard_map.282 = (bf16[640,2048]{1,0:T(8,128)(2,1)}, f32[640,1024]{1,0:T(8,128)}, bf16[640,1024]{1,0:T(8,128)(2,1)}, f32[8,1024]{1,0:T(8,128)}) custom-call(s32[4]{0:T(128)} %pad_add_fusion.where_ref, s32[2]{0:T(128)} %kept_ref.23, bf16[1024,10368]{1,0:T(8,128)(2,1)} %all-gather.5.cloned.1.call-done.refs_0_.refs_1_.refs_2_.refs_3_, ...), custom_call_target="tpu_custom_call" | custom-call | flops 30000001024 | tf_op jit(solution)/shard_map/pallas_call | solution.py:123
  491.9 13.3 %shard_map.284 = (bf16[1,2,2,2,128,1280]{5,4,3,2,1,0:T(8,128)(2,1)}, bf16[1,2,2,2,128,1280]{5,4,3,2,1,0:T(8,128)(2,1)}, f32[1,2048]{1,0:T(1,128)}) custom-call(s32[4]{0:T(128)} %pad_add_fusion.where_ref, bf16[640,1024]{1,0:T(8,128)(2,1)} %get-tuple-element.121.refs_2_.xo, bf16[640,1024]{1,0:T(8,128)(2,1)} %copy-done.57, ...), custom_call_target="tpu_custom_call" | custom-call | flops 30000001024 | tf_op jit(solution)/shard_map/pallas_call | solution.py:412
  528.8 16.2 %shard_map.288 = (bf16[640,1536]{1,0:T(8,128)(2,1)}, f32[640,1024]{1,0:T(8,128)}) custom-call(s32[4]{0:T(128)} %pad_add_fusion.where_ref, s32[2]{0:T(128)} %copy-done.74, bf16[8,2,64,10368]{3,2,1,0:T(8,128)(2,1)} %bitcast.55, bf16[1024,10368]{1,0:T(8,128)(2,1)} %all-gather.5.cloned.1.call-done.refs_0_.refs_1_.refs_2_.refs_3_, ...), custom_call_target="tpu_custom_call" | custom-call | flops 30000001024 | tf_op jit(solution)/shard_map/pallas_call | solution.py:123
  558.3 19.3 %shard_map.291 = (bf16[640,1536]{1,0:T(8,128)(2,1)}, f32[640,1024]{1,0:T(8,128)}, bf16[640,1024]{1,0:T(8,128)(2,1)}, f32[8,1024]{1,0:T(8,128)}) custom-call(s32[4]{0:T(128)} %pad_add_fusion.where_ref, s32[2]{0:T(128)} %kept_ref.23, bf16[8,2,64,10368]{3,2,1,0:T(8,128)(2,1)} %bitcast.56, ...), custom_call_target="tpu_custom_call" | custom-call | flops 30000001024 | tf_op jit(solution)/shard_map/pallas_call | solution.py:123
  642.0 14.5 %collective-permute-done.35.g = bf16[1,2,2,1,128,1280]{5,4,3,2,1,0:T(8,128)(2,1)} collective-permute-done((bf16[1,2,2,1,128,1280]{5,4,3,2,1,0:T(8,128)(2,1)}, bf16[1,2,2,1,128,1280]{5,4,3,2,1,0:T(8,128)(2,1)}, u32[]{:S(2)}, u32[]{:S(2)}) %collective-permute-start.35) | collective-permute-done | bytes 1310752 | tf_op jit(solution)/shard_map/ppermute | solution.py:40
  680.8 9.2 %collective-permute-done.44.refs_3_ = bf16[64,4096]{1,0:T(8,128)(2,1)S(1)} collective-permute-done((bf16[64,4096]{1,0:T(8,128)(2,1)S(1)}, bf16[64,4096]{1,0:T(8,128)(2,1)S(1)}, u32[]{:S(2)}, u32[]{:S(2)}) %collective-permute-start.44) | collective-permute-done | bytes 524320 | tf_op jit(solution)/shard_map/ppermute | solution.py:40
  (442 shorter events, 300.4 us)
Async XLA Ops:
  7.2 118.6 %all-gather.5.cloned.1.call-start = ((), (), s32[]{:S(2)}) async-start(), calls=%async_computation.3 | async-start | bytes 22560768 | tf_op jit(solution)/shard_map/all_gather | solution.py:868
  12.9 223.9 %all-gather.3.cloned.1.call-start = ((), (), s32[]{:S(2)}) async-start(), calls=%async_computation.2 | async-start | bytes 22282240 | tf_op jit(solution)/shard_map/all_gather | solution.py:868
  16.5 488.6 %reduce-scatter.3.cloned.1.call-start = ((), (), s32[]{:S(2)}) async-start(), calls=%async_computation.4 | async-start | bytes 4718592 | tf_op jit(solution)/shard_map/reduce_scatter | solution.py:671
  152.7 47.9 %collective-permute-start.1 = (bf16[1024,1024]{1,0:T(8,128)(2,1)S(1)}, bf16[1024,1024]{1,0:T(8,128)(2,1)}, u32[]{:S(2)}, u32[]{:S(2)}) collective-permute-start(bf16[1024,1024]{1,0:T(8,128)(2,1)S(1)} %copy-done.53), channel_id=1, source_target_pairs={{0,1},{1,0},{2,3},{3,2},{4,5},{5,4},{6,7},{7,6},{8,9},{9,8},{10,11... | collective-permute-start | bytes 6291464 | tf_op jit(solution)/shard_map/ppermute | solution.py:40
  260.0 49.1 %collective-permute-start = (bf16[1024,1024]{1,0:T(8,128)(2,1)}, bf16[1024,1024]{1,0:T(8,128)(2,1)}, u32[]{:S(2)}, u32[]{:S(2)}) collective-permute-start(bf16[1024,1024]{1,0:T(8,128)(2,1)} %constant_dynamic-slice_fusion.2.refs_3_), channel_id=1, source_target_pairs={{0,1},{1,0},{2,3},{3,2},{4,5},{5,4},{6,7},{7,6},{8,9},{9,8},{10,11... | collective-permute-start | bytes 6291464 | tf_op jit(solution)/shard_map/ppermute | solution.py:40
  286.5 22.6 %collective-permute-start.10 = (bf16[640,1024]{1,0:T(8,128)(2,1)}, bf16[640,1024]{1,0:T(8,128)(2,1)S(1)}, u32[]{:S(2)}, u32[]{:S(2)}) collective-permute-start(bf16[640,1024]{1,0:T(8,128)(2,1)} %bitcast_convert_fusion.yo.refs_4_), channel_id=1, source_target_pairs={{0,2},{1,3},{2,0},{3,1},{4,6},{5,7},{6,4},{7,5},{8,10},{9,11},{10,... | collective-permute-start | bytes 3932168 | tf_op jit(solution)/shard_map/ppermute | solution.py:40
  323.5 262.1 %reduce-scatter.5.cloned.1.call-start = ((), (), s32[]{:S(2)}) async-start(), calls=%async_computation.5 | async-start | bytes 4718592 | tf_op jit(solution)/shard_map/reduce_scatter | solution.py:671
  342.9 34.9 %collective-permute-start.11 = (f32[640,1024]{1,0:T(8,128)}, f32[640,1024]{1,0:T(8,128)}, u32[]{:S(2)}, u32[]{:S(2)}) collective-permute-start(f32[640,1024]{1,0:T(8,128)} %shard_map.272.refs_10_), channel_id=1, source_target_pairs={{0,2},{1,3},{2,0},{3,1},{4,6},{5,7},{6,4},{7,5},{8,10},{9,11},{10,... | collective-permute-start | bytes 7864328 | tf_op jit(solution)/shard_map/ppermute | solution.py:40
  401.5 60.5 %collective-permute-start.17 = (bf16[1,2,2,2,128,1280]{5,4,3,2,1,0:T(8,128)(2,1)}, bf16[1,2,2,2,128,1280]{5,4,3,2,1,0:T(8,128)(2,1)S(1)}, u32[]{:S(2)}, u32[]{:S(2)}) collective-permute-start(bf16[1,2,2,2,128,1280]{5,4,3,2,1,0:T(8,128)(2,1)} %get-tuple-element.147.refs_9_), channel_id=1, source_target_pairs={{0,1},{1,0},{2,3},{3,2},{4,5},{5,4},{6,7},{7,6},{8,9},{9,8},{10,11... | collective-permute-start | bytes 7864328 | tf_op jit(solution)/shard_map/ppermute | solution.py:40
  434.7 50.2 %collective-permute-start.19 = (bf16[2,2,2,1,128,768]{5,4,3,2,1,0:T(8,128)(2,1)}, bf16[2,2,2,1,128,768]{5,4,3,2,1,0:T(8,128)(2,1)}, u32[]{:S(2)}, u32[]{:S(2)}) collective-permute-start(bf16[2,2,2,1,128,768]{5,4,3,2,1,0:T(8,128)(2,1)} %get-tuple-element.152.refs_6_), channel_id=1, source_target_pairs={{0,4},{1,5},{2,6},{3,7},{4,0},{5,1},{6,2},{7,3},{8,12},{9,13},{10,... | collective-permute-start | bytes 4718600 | tf_op jit(solution)/shard_map/ppermute | solution.py:40
  468.9 44.8 %collective-permute-start.21 = (bf16[1,2,2,1,128,1280]{5,4,3,2,1,0:T(8,128)(2,1)}, bf16[1,2,2,1,128,1280]{5,4,3,2,1,0:T(8,128)(2,1)S(1)}, u32[]{:S(2)}, u32[]{:S(2)}) collective-permute-start(bf16[1,2,2,1,128,1280]{5,4,3,2,1,0:T(8,128)(2,1)} %get-tuple-element.157.refs_11_), channel_id=1, source_target_pairs={{0,4},{1,5},{2,6},{3,7},{4,0},{5,1},{6,2},{7,3},{8,12},{9,13},{10,... | collective-permute-start | bytes 3932168 | tf_op jit(solution)/shard_map/ppermute | solution.py:40
  484.9 43.9 %collective-permute-start.18 = (bf16[640,1024]{1,0:T(8,128)(2,1)}, bf16[640,1024]{1,0:T(8,128)(2,1)}, u32[]{:S(2)}, u32[]{:S(2)}) collective-permute-start(bf16[640,1024]{1,0:T(8,128)(2,1)} %get-tuple-element.158.rest_0_.yo.refs_2_), channel_id=1, source_target_pairs={{0,2},{1,3},{2,0},{3,1},{4,6},{5,7},{6,4},{7,5},{8,10},{9,11},{10,... | collective-permute-start | bytes 3932168 | tf_op jit(solution)/shard_map/ppermute | solution.py:40
  490.3 36.4 %collective-permute-start.20 = (bf16[2,2,1,1,128,768]{5,4,3,2,1,0:T(8,128)(2,1)S(1)}, bf16[2,2,1,1,128,768]{5,4,3,2,1,0:T(8,128)(2,1)S(1)}, u32[]{:S(2)}, u32[]{:S(2)}) collective-permute-start(bf16[2,2,1,1,128,768]{5,4,3,2,1,0:T(8,128)(2,1)S(1)} %get-tuple-element.163.rest_1_), channel_id=1, source_target_pairs={{0,8},{1,9},{2,10},{3,11},{4,12},{5,13},{6,14},{7,15},{8,0},{9,1},... | collective-permute-start | bytes 2359304 | tf_op jit(solution)/shard_map/ppermute | solution.py:40
  513.4 38.4 %collective-permute-start.23 = (bf16[128,1024]{1,0:T(8,128)(2,1)S(1)}, bf16[128,1024]{1,0:T(8,128)(2,1)S(1)}, u32[]{:S(2)}, u32[]{:S(2)}) collective-permute-start(bf16[128,1024]{1,0:T(8,128)(2,1)S(1)} %get-tuple-element.169.refs_8_), channel_id=1, source_target_pairs={{0,2},{1,3},{2,0},{3,1},{4,6},{5,7},{6,4},{7,5},{8,10},{9,11},{10,... | collective-permute-start | bytes 786440 | tf_op jit(solution)/shard_map/ppermute | solution.py:40
  518.8 61.0 %collective-permute-start.25 = (bf16[1,2,1,1,128,1280]{5,4,3,2,1,0:T(8,128)(2,1)}, bf16[1,2,1,1,128,1280]{5,4,3,2,1,0:T(8,128)(2,1)}, u32[]{:S(2)}, u32[]{:S(2)}) collective-permute-start(bf16[1,2,1,1,128,1280]{5,4,3,2,1,0:T(8,128)(2,1)} %get-tuple-element.168.refs_7_), channel_id=1, source_target_pairs={{0,8},{1,9},{2,10},{3,11},{4,12},{5,13},{6,14},{7,15},{8,0},{9,1},... | collective-permute-start | bytes 1966088 | tf_op jit(solution)/shard_map/ppermute | solution.py:40
  527.1 52.7 %collective-permute-start.24 = (bf16[1,2,1,1,128,768]{5,4,3,2,1,0:T(8,128)(2,1)S(1)}, bf16[1,2,1,1,128,768]{5,4,3,2,1,0:T(8,128)(2,1)S(1)}, u32[]{:S(2)}, u32[]{:S(2)}) collective-permute-start(bf16[1,2,1,1,128,768]{5,4,3,2,1,0:T(8,128)(2,1)S(1)} %get-tuple-element.166.refs_6_), channel_id=1, source_target_pairs={{0,1},{1,0},{2,3},{3,2},{4,5},{5,4},{6,7},{7,6},{8,9},{9,8},{10,11... | collective-permute-start | bytes 1179656 | tf_op jit(solution)/shard_map/ppermute | solution.py:40
  551.1 60.3 %collective-permute-start.27 = (bf16[1,2,2,2,128,1280]{5,4,3,2,1,0:T(8,128)(2,1)}, bf16[1,2,2,2,128,1280]{5,4,3,2,1,0:T(8,128)(2,1)}, u32[]{:S(2)}, u32[]{:S(2)}) collective-permute-start(bf16[1,2,2,2,128,1280]{5,4,3,2,1,0:T(8,128)(2,1)} %get-tuple-element.176.refs_2_.refs_9_), channel_id=1, source_target_pairs={{0,1},{1,0},{2,3},{3,2},{4,5},{5,4},{6,7},{7,6},{8,9},{9,8},{10,11... | collective-permute-start | bytes 7864328 | tf_op jit(solution)/shard_map/ppermute | solution.py:40
  554.9 126.0 %collective-permute-start.43 = (bf16[256,1024]{1,0:T(8,128)(2,1)}, bf16[256,1024]{1,0:T(8,128)(2,1)}, u32[]{:S(2)}, u32[]{:S(2)}) collective-permute-start(bf16[256,1024]{1,0:T(8,128)(2,1)} %shard_map.290.refs_10_.refs_0_), channel_id=1, source_target_pairs={{0,1},{1,0},{2,3},{3,2},{4,5},{5,4},{6,7},{7,6},{8,9},{9,8},{10,11... | collective-permute-start | bytes 1572872 | tf_op jit(solution)/shard_map/ppermute | solution.py:40
  583.5 25.9 %collective-permute-start.28 = (bf16[128,2048]{1,0:T(8,128)(2,1)S(1)}, bf16[128,2048]{1,0:T(8,128)(2,1)S(1)}, u32[]{:S(2)}, u32[]{:S(2)}) collective-permute-start(bf16[128,2048]{1,0:T(8,128)(2,1)S(1)} %get-tuple-element.181.rest_1_), channel_id=1, source_target_pairs={{0,16},{1,17},{2,18},{3,19},{4,20},{5,21},{6,22},{7,23},{8,24},{9,... | collective-permute-start | bytes 1572872 | tf_op jit(solution)/shard_map/ppermute | solution.py:40
  598.1 28.1 %collective-permute-start.31 = (bf16[2,2,1,2,128,384]{5,4,3,2,1,0:T(8,128)(2,1)}, bf16[2,2,1,2,128,384]{5,4,3,2,1,0:T(8,128)(2,1)S(1)}, u32[]{:S(2)}, u32[]{:S(2)}) collective-permute-start(bf16[2,2,1,2,128,384]{5,4,3,2,1,0:T(8,128)(2,1)} %get-tuple-element.183.rest_0_), channel_id=1, source_target_pairs={{0,8},{1,9},{2,10},{3,11},{4,12},{5,13},{6,14},{7,15},{8,0},{9,1},... | collective-permute-start | bytes 2359304 | tf_op jit(solution)/shard_map/ppermute | solution.py:40
  616.8 39.7 %collective-permute-start.35 = (bf16[1,2,2,1,128,1280]{5,4,3,2,1,0:T(8,128)(2,1)}, bf16[1,2,2,1,128,1280]{5,4,3,2,1,0:T(8,128)(2,1)}, u32[]{:S(2)}, u32[]{:S(2)}) collective-permute-start(bf16[1,2,2,1,128,1280]{5,4,3,2,1,0:T(8,128)(2,1)} %get-tuple-element.186.refs_8_), channel_id=1, source_target_pairs={{0,4},{1,5},{2,6},{3,7},{4,0},{5,1},{6,2},{7,3},{8,12},{9,13},{10,... | collective-permute-start | bytes 3932168 | tf_op jit(solution)/shard_map/ppermute | solution.py:40
  630.0 29.6 %collective-permute-start.34 = (bf16[2,2,1,1,128,384]{5,4,3,2,1,0:T(8,128)(2,1)S(1)}, bf16[2,2,1,1,128,384]{5,4,3,2,1,0:T(8,128)(2,1)S(1)}, u32[]{:S(2)}, u32[]{:S(2)}) collective-permute-start(bf16[2,2,1,1,128,384]{5,4,3,2,1,0:T(8,128)(2,1)S(1)} %get-tuple-element.202.refs_2_), channel_id=1, source_target_pairs={{0,8},{1,9},{2,10},{3,11},{4,12},{5,13},{6,14},{7,15},{8,0},{9,1},... | collective-permute-start | bytes 1179656 | tf_op jit(solution)/shard_map/ppermute | solution.py:40
  631.9 29.4 %collective-permute-start.33 = (f32[2,16,768]{2,1,0:T(8,128)S(1)}, f32[2,16,768]{2,1,0:T(8,128)S(1)}, u32[]{:S(2)}, u32[]{:S(2)}) collective-permute-start(f32[2,16,768]{2,1,0:T(8,128)S(1)} %shard_map.301.rest_0_.refs_0_), channel_id=1, source_target_pairs={{0,1},{1,0},{2,3},{3,2},{4,5},{5,4},{6,7},{7,6},{8,9},{9,8},{10,11... | collective-permute-start | bytes 294920 | tf_op jit(solution)/shard_map/ppermute | solution.py:40
  640.3 22.5 %collective-permute-start.38 = (bf16[1,2,1,1,128,384]{5,4,3,2,1,0:T(8,128)(2,1)S(1)}, bf16[1,2,1,1,128,384]{5,4,3,2,1,0:T(8,128)(2,1)S(1)}, u32[]{:S(2)}, u32[]{:S(2)}) collective-permute-start(bf16[1,2,1,1,128,384]{5,4,3,2,1,0:T(8,128)(2,1)S(1)} %get-tuple-element.206.rest_0_), channel_id=1, source_target_pairs={{0,4},{1,5},{2,6},{3,7},{4,0},{5,1},{6,2},{7,3},{8,12},{9,13},{10,... | collective-permute-start | bytes 589832 | tf_op jit(solution)/shard_map/ppermute | solution.py:40
  (114 other events, 896.7 us)
Sparse Core Ops, SparseCore 0:
  13.0 112.7 all-gather.4
  128.0 108.8 all-gather.2
  323.6 86.9 reduce-scatter.2
  462.1 106.4 reduce-scatter.4
